TPU v7x, 32 devices: a whole 2x2x4 slice. The times are simulated.
32 devices in a mesh: inp: 4 (over x, core), wt: 4 (over z), out: 2 (over y).
Axes of the slice: x: 2, y: 2, z: 4, core: 2. Of those that a mesh axis runs over, the one named last changes fastest.
Arguments:
- tokens: bfloat16 [2, 4096, 2048], P(None, ('inp', 'wt'), 'out'), may hold values from -6 to 6
- gate_weight: bfloat16 [2048, 4096], P('out', ('wt', 'inp')), may hold values from -0.125 to 0.125
- up_weight: bfloat16 [2048, 4096], P('out', ('wt', 'inp')), may hold values from -0.125 to 0.125
- down_weight: bfloat16 [4096, 2048], P(('wt', 'inp'), 'out'), may hold values from -0.09375 to 0.09375
- cotangent: bfloat16 [2, 4096, 2048], P(None, ('inp', 'wt'), 'out'), may hold values from -3 to 3
Outputs:
- output: bfloat16 [2, 4096, 2048], P(None, ('inp', 'wt'), 'out')
- grad_tokens: bfloat16 [2, 4096, 2048], P(None, ('inp', 'wt'), 'out')
- grad_gate: float32 [2048, 4096], P('out', ('wt', 'inp'))
- grad_up: float32 [2048, 4096], P('out', ('wt', 'inp'))
- grad_down: float32 [4096, 2048], P(('wt', 'inp'), 'out')
All inputs are finite; a program needn't handle non-finite values.
Results may differ from a plain program's by a relative error of at most 0.035.
Values may be sent and summed in bfloat16 or wider, within the bound.
No kernel may reach another device: no remote copies, remote signals or barrier semaphores. Data moves between devices by JAX's collectives and lax.ppermute only.
A program may use at most 128 MiB of HBM per device.

v0:
```python
import functools

import jax
import jax.numpy as jnp
from jax import lax
from jax.experimental import pallas as pl
from jax.experimental.pallas import tpu as pltpu
from jax.sharding import PartitionSpec as P

F32 = jnp.float32
BF16 = jnp.bfloat16
MIB = 1024 * 1024


def matmul(a, b, contract):
    return lax.dot_general(a, b, ((contract[:1], contract[1:]), ((), ())), preferred_element_type=F32)


def gated(gate_sum, up_sum):
    sigmoid_g = jax.nn.sigmoid(gate_sum)
    silu_g = gate_sum * sigmoid_g
    slope = sigmoid_g * (1.0 + gate_sum * (1.0 - sigmoid_g))
    return silu_g, silu_g * up_sum, up_sum * slope


def call(kernel, outs, flops, *args):
    moved = sum(a.size * a.dtype.itemsize for a in args) + sum(o.size * o.dtype.itemsize for o in outs)
    return pl.pallas_call(
        kernel,
        out_shape=outs,
        in_specs=[pl.BlockSpec(memory_space=pltpu.VMEM)] * len(args),
        out_specs=[pl.BlockSpec(memory_space=pltpu.VMEM)] * len(outs),
        compiler_params=pltpu.CompilerParams(vmem_limit_bytes=44 * MIB),
        cost_estimate=pl.CostEstimate(flops=flops, bytes_accessed=moved, transcendentals=0),
    )(*args)


def shape(*dims):
    return jax.ShapeDtypeStruct(dims, BF16)


class Rows:
    def __init__(self, pieces, blocks, step):
        self.pieces, self.blocks, self.step = pieces, blocks, step

    def read(self, refs, at, side):
        piece, first = self.blocks[at][side]
        return refs[piece].at[first : first + self.step]


def hidden_kernel(rows, width, *refs):
    count = len(rows.pieces)
    pieces, (own_ref, other_ref, hidden_ref, turned_ref, silu_ref, rest_ref) = refs[:count], refs[count:]
    groups = own_ref.shape[0] // (2 * width)
    for at in range(len(rows.blocks)):
        span = slice(at * rows.step, (at + 1) * rows.step)
        sums = matmul(rows.read(pieces, at, 0)[...], own_ref[...], (1, 1))
        sums = sums + matmul(rows.read(pieces, at, 1)[...], other_ref[...], (1, 1))
        for group in range(groups):
            low = 2 * group * width
            silu_g, hidden, rest = gated(sums[:, low : low + width], sums[:, low + width : low + 2 * width])
            cols = slice(group * width, (group + 1) * width)
            hidden_ref[span, cols] = hidden.astype(BF16)
            turned_ref[cols, span] = hidden.T.astype(BF16)
            silu_ref[span, cols] = silu_g.astype(BF16)
            rest_ref[span, cols] = rest.astype(BF16)


def grads_kernel(rows, width, *refs):
    count = len(rows.pieces)
    pieces, (down_ref, silu_ref, rest_ref, act_ref, turned_ref) = refs[:count], refs[count:]
    groups = down_ref.shape[0] // width
    half = down_ref.shape[1] // 2
    for at in range(len(rows.blocks)):
        span = slice(at * rows.step, (at + 1) * rows.step)
        back = matmul(rows.read(pieces, at, 0)[...], down_ref[:, :half], (1, 1))
        back = back + matmul(rows.read(pieces, at, 1)[...], down_ref[:, half:], (1, 1))
        for group in range(groups):
            cols = slice(group * width, (group + 1) * width)
            for part, factor in enumerate((rest_ref, silu_ref)):
                grad = back[:, cols] * factor[span, cols].astype(F32)
                low = (2 * group + part) * width
                act_ref[span, low : low + width] = grad.astype(BF16)
                turned_ref[low : low + width, span] = grad.T.astype(BF16)


def weight_kernel(rows, sides, tile, *refs):
    count = len(rows.pieces)
    pieces, (turned_ref, out_ref) = refs[:count], refs[count:]
    half = out_ref.shape[1] // len(sides)
    for place, side in enumerate(sides):

        @pl.loop(0, half // tile)
        def _(index):
            cols = pl.ds(pl.multiple_of(index * tile, tile), tile)
            total = jnp.zeros((out_ref.shape[0], tile), F32)
            for at in range(len(rows.blocks)):
                span = slice(at * rows.step, (at + 1) * rows.step)
                total = total + matmul(turned_ref[:, span], rows.read(pieces, at, side)[:, cols], (1, 0))
            out_ref[:, pl.ds(pl.multiple_of(place * half + index * tile, tile), tile)] = total.astype(BF16)


class Square:
    def core(self, array):
        return lax.ppermute(array, "inp", [(at, at ^ 1) for at in range(4)])

    def chip(self, array):
        return lax.ppermute(array, "inp", [(at, at ^ 2) for at in range(4)])

    def other(self, array):
        return lax.ppermute(array, "out", [(0, 1), (1, 0)])

    def unit_halves(self, weight):
        half = weight.shape[0] // 2
        at = lax.axis_index("out")
        return (
            lax.dynamic_slice_in_dim(weight, at * half, half, 0),
            lax.dynamic_slice_in_dim(weight, (1 - at) * half, half, 0),
        )

    def in_order(self, mine, theirs):
        mine, theirs = mine.astype(F32), theirs.astype(F32)
        first = lax.axis_index("out") == 0
        return jnp.where(first, jnp.concatenate([mine, theirs]), jnp.concatenate([theirs, mine]))

    def gather(self, array):
        step = array.shape[1]
        own = array.reshape(2 * step, array.shape[2])
        by_chip, by_other = self.chip(own), self.other(own)
        corner = [self.other(by_chip[:step]), self.chip(by_other[step:])]
        pieces = [own, by_other, by_chip] + corner
        pieces = pieces + [self.core(piece) for piece in pieces]
        blocks = []
        for base in (0, 5):
            blocks += [((base, 0), (base + 1, 0)), ((base, step), (base + 1, step))]
            blocks += [((base + 2, 0), (base + 3, 0)), ((base + 2, step), (base + 4, 0))]
        return Rows(pieces, blocks, step)

    def scatter(self, product, rows, cols):
        half, quarter = rows // 2, rows // 4
        far = {}
        for chip in (1, 0):
            for other in (1, 0):
                at = slice(half + chip * quarter, half + (chip + 1) * quarter)
                far[chip, other] = self.core(product(at, other).astype(BF16))
        sums = {}
        for chip in (1, 0):
            for other in (1, 0):
                at = slice(chip * quarter, (chip + 1) * quarter)
                sums[chip, other] = product(at, other) + far[chip, other].astype(F32)
        batch = quarter // 2
        corner = sums[1, 1].astype(BF16)
        from_other = self.other(corner[:batch]).astype(F32)
        from_chip = self.chip(corner[batch:]).astype(F32)
        zeros = jnp.zeros_like(from_other)
        to_chip = sums[1, 0] + jnp.concatenate([from_other, zeros])
        to_other = sums[0, 1] + jnp.concatenate([zeros, from_chip])
        total = sums[0, 0] + self.chip(to_chip.astype(BF16)).astype(F32) + self.other(to_other.astype(BF16)).astype(F32)
        return total.astype(BF16).reshape(2, batch, cols // 2)

    def layer(self, tokens, gate_weight, up_weight, down_weight, cotangent):
        def gather_units(array):
            return lax.all_gather(array, "wt", axis=0, tiled=True)

        def scatter_units(array):
            return lax.psum_scatter(array, "wt", scatter_dimension=0, tiled=True)

        gate_mine, gate_theirs = self.unit_halves(gate_weight.T)
        up_mine, up_theirs = self.unit_halves(up_weight.T)
        down_mine, down_theirs = self.unit_halves(down_weight)
        width, half = gate_mine.shape
        own_units = gather_units(jnp.concatenate([gate_mine, up_mine]))
        other_units = gather_units(self.other(jnp.concatenate([gate_theirs, up_theirs])))
        down = gather_units(jnp.concatenate([down_mine, self.other(down_theirs)], axis=1))
        rows_in = self.gather(tokens)
        rows_cot = self.gather(cotangent)
        count = len(rows_in.blocks) * rows_in.step
        units = down.shape[0]

        hidden, hidden_turned, silu, rest = call(
            functools.partial(hidden_kernel, rows_in, width),
            [shape(count, units), shape(units, count), shape(count, units), shape(count, units)],
            8 * count * units * half,
            *rows_in.pieces,
            own_units,
            other_units,
        )
        (down_term,) = call(
            functools.partial(weight_kernel, rows_cot, (0, 1), 256),
            [shape(units, 2 * half)],
            4 * count * units * half,
            *rows_cot.pieces,
            hidden_turned,
        )
        down_sum = scatter_units(down_term)
        act, act_turned = call(
            functools.partial(grads_kernel, rows_cot, width),
            [shape(count, 2 * units), shape(2 * units, count)],
            4 * count * units * half,
            *rows_cot.pieces,
            down,
            silu,
            rest,
        )
        terms = [
            call(
                functools.partial(weight_kernel, rows_in, (side,), 256),
                [shape(2 * units, half)],
                4 * count * units * half,
                *rows_in.pieces,
                act_turned,
            )[0]
            for side in (1, 0)
        ]
        other_sum, own_sum = scatter_units(terms[0]), scatter_units(terms[1])
        down_back = self.other(down_sum[:, half:])
        units_back = self.other(other_sum)
        grad_down = self.in_order(down_sum[:, :half], down_back)
        grad_gate = self.in_order(own_sum[:width], units_back[:width]).T
        grad_up = self.in_order(own_sum[width:], units_back[width:]).T

        def output_block(at, other):
            return matmul(hidden[at], down[:, other * half : (other + 1) * half], (1, 0))

        def input_block(at, other):
            return matmul(act[at], other_units if other else own_units, (1, 0))

        output = self.scatter(output_block, count, 2 * half)
        grad_tokens = self.scatter(input_block, count, 2 * half)
        return (output, grad_tokens, grad_gate, grad_up, grad_down)


class Plain:
    def units(self, weight):
        own = lax.all_to_all(weight, "out", split_axis=0, concat_axis=1, tiled=True)
        return lax.all_gather(own, "wt", axis=0, tiled=True)

    def unit_sums(self, grad):
        own = lax.psum_scatter(grad.astype(BF16), "wt", scatter_dimension=0, tiled=True)
        return lax.all_to_all(own, "out", split_axis=1, concat_axis=0, tiled=True).astype(F32)

    def gather(self, array):
        array = lax.all_gather(lax.all_gather(array, "inp", axis=1, tiled=True), "out", axis=2, tiled=True)
        return array.reshape(-1, array.shape[2])

    def scatter(self, partial, batches):
        partial = partial.astype(BF16).reshape(batches, -1, partial.shape[1])
        partial = lax.psum_scatter(partial, "out", scatter_dimension=2, tiled=True)
        return lax.psum_scatter(partial, "inp", scatter_dimension=1, tiled=True)

    def layer(self, tokens, gate_weight, up_weight, down_weight, cotangent):
        gate, up, down = self.units(gate_weight.T), self.units(up_weight.T), self.units(down_weight)
        rows_in, rows_cot = self.gather(tokens), self.gather(cotangent)
        gate_sum = matmul(rows_in, gate, (1, 1))
        up_sum = matmul(rows_in, up, (1, 1))
        silu_g, hidden, rest = gated(gate_sum, up_sum)
        hidden = hidden.astype(BF16)
        grad_down = self.unit_sums(matmul(hidden, rows_cot, (0, 0)))
        back_sum = matmul(rows_cot, down, (1, 1))
        gate_act, up_act = (back_sum * rest).astype(BF16), (back_sum * silu_g).astype(BF16)
        grad_gate = self.unit_sums(matmul(gate_act, rows_in, (0, 0))).T
        grad_up = self.unit_sums(matmul(up_act, rows_in, (0, 0))).T
        output = self.scatter(matmul(hidden, down, (1, 0)), tokens.shape[0])
        partial = matmul(gate_act, gate, (1, 0)) + matmul(up_act, up, (1, 0))
        grad_tokens = self.scatter(partial, tokens.shape[0])
        return (output, grad_tokens, grad_gate, grad_up, grad_down)


def solution(mesh):
    square = mesh.shape["inp"] == 4 and mesh.shape["out"] == 2

    def on_device(tokens, *others):
        places = Square() if square and tokens.shape[0] == 2 else Plain()
        return places.layer(tokens, *others)

    rows_spec = P(None, ("inp", "wt"), "out")
    in_spec = P("out", ("wt", "inp"))
    down_spec = P(("wt", "inp"), "out")
    return jax.shard_map(
        on_device,
        mesh=mesh,
        in_specs=(rows_spec, in_spec, in_spec, down_spec, rows_spec),
        out_specs=(rows_spec, rows_spec, in_spec, in_spec, down_spec),
        check_vma=False,
    )
```

profile of v0, /device:TPU:0, one launch (start us, length us, event | category | flops | bytes accessed | tf_op | source)
XLA Modules:
  0.0 309.6 jit_solution(1084174316075481968)
XLA Ops:
  10.1 3.0 collective-permute-start.9
  13.1 11.9 %collective-permute-done.9 = bf16[256,1024]{1,0:T(8,128)(2,1)S(1)} collective-permute-done((bf16[256,1024]{1,0:T(8,128)(2,1)S(1)}, bf16[256,1024]{1,0:T(8,128)(2,1)S(1)}, u32[]{:S(2)}, u32[]{:S(2)}) %collective-permute-start.9) | collective-permute-done | bytes 524320 | tf_op jit(solution)/shard_map/ppermute | solution.py:111
  25.9 1.8 collective-permute-start.10
  27.8 1.5 collective-permute-start.1
  30.1 5.2 %collective-permute-done.10 = bf16[128,1024]{1,0:T(8,128)(2,1)S(1)} collective-permute-done((bf16[128,1024]{1,0:T(8,128)(2,1)S(1)}, bf16[128,1024]{1,0:T(8,128)(2,1)S(1)}, u32[]{:S(2)}, u32[]{:S(2)}) %collective-permute-start.10) | collective-permute-done | bytes 262176 | tf_op jit(solution)/shard_map/ppermute | solution.py:111
  35.3 1.7 collective-permute-start.19
  37.9 16.2 %collective-permute-done.1.refs_2_ = bf16[512,1024]{1,0:T(8,128)(2,1)S(1)} collective-permute-done((bf16[512,1024]{1,0:T(8,128)(2,1)}, bf16[512,1024]{1,0:T(8,128)(2,1)S(1)}, u32[]{:S(2)}, u32[]{:S(2)}) %collective-permute-start.1) | collective-permute-done | bytes 1048608 | tf_op jit(solution)/shard_map/ppermute | solution.py:108
  54.4 3.3 %collective-permute-done.refs_1_ = bf16[512,1024]{1,0:T(8,128)(2,1)S(1)} collective-permute-done((bf16[512,1024]{1,0:T(8,128)(2,1)}, bf16[512,1024]{1,0:T(8,128)(2,1)S(1)}, u32[]{:S(2)}, u32[]{:S(2)}) %collective-permute-start) | collective-permute-done | bytes 1048608 | tf_op jit(solution)/shard_map/ppermute | solution.py:111
  57.8 1.8 collective-permute-start.3
  59.5 17.0 %collective-permute-done.20.refs_2_ = bf16[512,1024]{1,0:T(8,128)(2,1)S(1)} collective-permute-done((bf16[512,1024]{1,0:T(8,128)(2,1)}, bf16[512,1024]{1,0:T(8,128)(2,1)S(1)}, u32[]{:S(2)}, u32[]{:S(2)}) %collective-permute-start.20) | collective-permute-done | bytes 1048608 | tf_op jit(solution)/shard_map/ppermute | solution.py:108
  76.9 3.4 %collective-permute-done.19.refs_1_ = bf16[512,1024]{1,0:T(8,128)(2,1)} collective-permute-done((bf16[512,1024]{1,0:T(8,128)(2,1)}, bf16[512,1024]{1,0:T(8,128)(2,1)}, u32[]{:S(2)}, u32[]{:S(2)}) %collective-permute-start.19) | collective-permute-done | bytes 1048608 | tf_op jit(solution)/shard_map/ppermute | solution.py:111
  81.4 10.0 %collective-permute-done.2.refs_3_ = bf16[256,1024]{1,0:T(8,128)(2,1)S(1)} collective-permute-done((bf16[256,1024]{1,0:T(8,128)(2,1)S(1)}, bf16[256,1024]{1,0:T(8,128)(2,1)S(1)}, u32[]{:S(2)}, u32[]{:S(2)}) %collective-permute-start.2) | collective-permute-done | bytes 524320 | tf_op jit(solution)/shard_map/ppermute | solution.py:111
  91.4 1.7 collective-permute-start.22
  94.0 7.2 %collective-permute-done.21.refs_3_ = bf16[256,1024]{1,0:T(8,128)(2,1)} collective-permute-done((bf16[256,1024]{1,0:T(8,128)(2,1)S(1)}, bf16[256,1024]{1,0:T(8,128)(2,1)}, u32[]{:S(2)}, u32[]{:S(2)}) %collective-permute-start.21) | collective-permute-done | bytes 524320 | tf_op jit(solution)/shard_map/ppermute | solution.py:111
  113.7 16.1 %shard_map.92 = (bf16[2048,512]{1,0:T(8,128)(2,1)}, bf16[512,2048]{1,0:T(8,128)(2,1)}, bf16[2048,512]{1,0:T(8,128)(2,1)}, bf16[2048,512]{1,0:T(8,128)(2,1)}) custom-call(bf16[512,1024]{1,0:T(8,128)(2,1)} %bitcast.refs_0_, bf16[512,1024]{1,0:T(8,128)(2,1)S(1)} %collective-permute-done.refs_1_, bf16[512,1024]{1,0:T(8,128)(2,1)S(1)} %collective-permute-done.1.refs_2_, ...), custom_call_target="tpu_custom_call" | custom-call | flops 8589934592 | bytes 20971520 | tf_op jit(solution)/shard_map/pallas_call | solution.py:28
  129.8 11.0 %shard_map.96 = bf16[512,2048]{1,0:T(8,128)(2,1)} custom-call(bf16[512,1024]{1,0:T(8,128)(2,1)} %bitcast.6.refs_0_, bf16[512,1024]{1,0:T(8,128)(2,1)} %collective-permute-done.19.refs_1_, bf16[512,1024]{1,0:T(8,128)(2,1)S(1)} %collective-permute-done.20.refs_2_, bf16[256,1024]{1,0:T(8,128)(2,1)} %collective-permute-done.21.refs_3_, ...), custom_call_target="tpu_custom_call" | custom-call | flops 4294967296 | bytes 12582912 | tf_op jit(solution)/shard_map/pallas_call | solution.py:28
  141.1 11.4 %all-gather.8.cloned.1.call-done.refs_10_ = bf16[512,2048]{1,0:T(8,128)(2,1)} async-done(((bf16[128,2048]{1,0:T(8,128)(2,1)}), bf16[512,2048]{1,0:T(8,128)(2,1)}) %all-gather.8.cloned.1.call-update) | async-done | bytes 2097168 | tf_op jit(solution)/shard_map/all_gather | solution.py:163
  152.5 13.5 %shard_map.93 = (bf16[2048,1024]{1,0:T(8,128)(2,1)}, bf16[1024,2048]{1,0:T(8,128)(2,1)}) custom-call(bf16[512,1024]{1,0:T(8,128)(2,1)} %bitcast.6.refs_0_, bf16[512,1024]{1,0:T(8,128)(2,1)} %collective-permute-done.19.refs_1_, bf16[512,1024]{1,0:T(8,128)(2,1)S(1)} %collective-permute-done.20.refs_2_, bf16[256,1024]{1,0:T(8,128)(2,1)} %collective-permute-done.21.refs_3_, ...), custom_call_target="tpu_custom_call" | custom-call | flops 4294967296 | bytes 23068672 | tf_op jit(solution)/shard_map/pallas_call | solution.py:28
  166.0 9.2 %shard_map.95 = bf16[1024,1024]{1,0:T(8,128)(2,1)} custom-call(bf16[512,1024]{1,0:T(8,128)(2,1)} %bitcast.refs_0_, bf16[512,1024]{1,0:T(8,128)(2,1)S(1)} %collective-permute-done.refs_1_, bf16[512,1024]{1,0:T(8,128)(2,1)S(1)} %collective-permute-done.1.refs_2_, bf16[256,1024]{1,0:T(8,128)(2,1)S(1)} %copy-done.10, bf16[256,1024]{1,0:T(8,128)(2,1)S(1)} %copy-done.14, ...), custom_call_target="tpu_custom_call" | custom-call | flops 4294967296 | bytes 14680064 | tf_op jit(solution)/shard_map/pallas_call | solution.py:28
  175.3 3.2 %convolution_convert_fusion.6 = bf16[512,1024]{1,0:T(8,128)(2,1)} fusion(bf16[512,2048]{1,0:T(8,128)(2,1)} %all-gather.8.cloned.1.call-done.refs_10_, bf16[2048,512]{1,0:T(8,128)(2,1)} %get-tuple-element.11), kind=kOutput, calls=%fused_computation.14 | convolution fusion | flops 537395200 | bytes 2621440 | tf_op jit(solution)/shard_map/dot_general | solution.py:16
  178.5 2.9 convolution_convert_fusion.5
  181.8 3.7 %convolution_convert_fusion.2 = bf16[512,1024]{1,0:T(8,128)(2,1)} fusion(bf16[1024,1024]{1,0:T(8,128)(2,1)S(1)} %copy-done.26, bf16[2048,1024]{1,0:T(8,128)(2,1)} %get-tuple-element.14), kind=kOutput, calls=%fused_computation.10 | convolution fusion | flops 1074266112 | bytes 4194304 | tf_op jit(solution)/shard_map/dot_general | solution.py:16
  185.7 2.3 convolution_convert_fusion.1
  188.4 2.3 convolution_convert_fusion
  190.8 9.3 %shard_map.94 = bf16[1024,1024]{1,0:T(8,128)(2,1)} custom-call(bf16[512,1024]{1,0:T(8,128)(2,1)} %bitcast.refs_0_, bf16[512,1024]{1,0:T(8,128)(2,1)S(1)} %collective-permute-done.refs_1_, bf16[512,1024]{1,0:T(8,128)(2,1)S(1)} %collective-permute-done.1.refs_2_, bf16[256,1024]{1,0:T(8,128)(2,1)S(1)} %copy-done.11, bf16[256,1024]{1,0:T(8,128)(2,1)S(1)} %copy-done.15, ...), custom_call_target="tpu_custom_call" | custom-call | flops 4294967296 | bytes 14680064 | tf_op jit(solution)/shard_map/pallas_call | solution.py:28
  200.2 2.2 convolution_convert_fusion.4
  202.5 2.6 convolution_convert_fusion.3
  205.9 2.7 add_convert_fusion.3
  208.7 1.4 collective-permute-start.31
  210.1 1.4 collective-permute-start.34
  211.6 2.0 add_convert_fusion.7
  213.7 9.2 %collective-permute-done.31 = bf16[256,1024]{1,0:T(8,128)(2,1)S(1)} collective-permute-done((bf16[256,1024]{1,0:T(8,128)(2,1)S(1)}, bf16[256,1024]{1,0:T(8,128)(2,1)S(1)}, u32[]{:S(2)}, u32[]{:S(2)}) %collective-permute-start.31) | collective-permute-done | bytes 524320 | tf_op jit(solution)/shard_map/ppermute | solution.py:111
  222.9 1.4 collective-permute-start.14
  224.3 3.5 %add_convert_fusion.2 = bf16[512,1024]{1,0:T(8,128)(2,1)} fusion(bf16[512,1024]{1,0:T(8,128)(2,1)} %collective-permute-done.29, bf16[1024,1024]{1,0:T(8,128)(2,1)S(1)} %copy-done.27, bf16[256,1024]{1,0:T(8,128)(2,1)S(1)} %collective-permute-done.31, bf16[2048,1024]{1,0:T(8,128)(2,1)S(1)} %copy-done.35), kind=kOutput, calls=%fused_computation.2 | convolution fusion | flops 1076363264 | bytes 5767168 | tf_op jit(solution)/shard_map/dot_general | solution.py:16
  227.9 1.5 collective-permute-start.17
  229.4 3.5 %add_convert_fusion.1 = bf16[512,1024]{1,0:T(8,128)(2,1)} fusion(bf16[512,1024]{1,0:T(8,128)(2,1)} %collective-permute-done.33, bf16[256,1024]{1,0:T(8,128)(2,1)S(1)} %collective-permute-done.34, bf16[1024,1024]{1,0:T(8,128)(2,1)S(1)} %copy-done.31, bf16[2048,1024]{1,0:T(8,128)(2,1)S(1)} %copy-done.35), kind=kOutput, calls=%fused_computation.1 | convolution fusion | flops 1076363264 | bytes 5767168 | tf_op jit(solution)/shard_map/dot_general | solution.py:16
  233.5 2.9 collective-permute-done.14
  236.3 1.5 collective-permute-start.35
  237.8 1.7 convolution_convert_fusion.7
  239.5 1.7 add_convert_fusion.6
  241.2 1.4 collective-permute-done.17
  242.7 1.4 collective-permute-start.15
  244.1 1.7 add_convert_fusion.5
  247.4 17.9 %collective-permute-done.32 = bf16[512,1024]{1,0:T(8,128)(2,1)} collective-permute-done((bf16[512,1024]{1,0:T(8,128)(2,1)}, bf16[512,1024]{1,0:T(8,128)(2,1)}, u32[]{:S(2)}, u32[]{:S(2)}) %collective-permute-start.32) | collective-permute-done | bytes 1048608 | tf_op jit(solution)/shard_map/ppermute | solution.py:108
  265.2 4.6 %add_convert_fusion = bf16[512,1024]{1,0:T(8,128)(2,1)} fusion(bf16[512,1024]{1,0:T(8,128)(2,1)} %collective-permute-done.35, bf16[512,1024]{1,0:T(8,128)(2,1)} %collective-permute-done.32, bf16[512,1024]{1,0:T(8,128)(2,1)} %copy-done.32, bf16[1024,1024]{1,0:T(8,128)(2,1)S(1)} %copy-done.27, bf16[2048,1024]{1,0:T(8,128)(2,1)} %get-tuple-element.14), kind=kOutput, calls=%fused_computation | convolution fusion | flops 1077411840 | bytes 7340032 | tf_op jit(solution)/shard_map/dot_general | solution.py:16
  273.0 14.2 %collective-permute-done.15 = bf16[512,1024]{1,0:T(8,128)(2,1)} collective-permute-done((bf16[512,1024]{1,0:T(8,128)(2,1)}, bf16[512,1024]{1,0:T(8,128)(2,1)}, u32[]{:S(2)}, u32[]{:S(2)}) %collective-permute-start.15) | collective-permute-done | bytes 1048608 | tf_op jit(solution)/shard_map/ppermute | solution.py:108
  287.2 3.9 %add_convert_fusion.4 = bf16[512,1024]{1,0:T(8,128)(2,1)} fusion(bf16[512,1024]{1,0:T(8,128)(2,1)} %collective-permute-done.18, bf16[512,1024]{1,0:T(8,128)(2,1)} %collective-permute-done.15, bf16[512,1024]{1,0:T(8,128)(2,1)S(1)} %collective-permute-done.11, bf16[512,2048]{1,0:T(8,128)(2,1)} %all-gather.8.cloned.1.call-done.refs_10_, ...), kind=kOutput, calls=%fused_computation.4 | convolution fusion | flops 540540928 | bytes 5767168 | tf_op jit(solution)/shard_map/dot_general | solution.py:16
  293.4 6.3 %collective-permute-done.36 = bf16[256,1024]{1,0:T(8,128)(2,1)S(1)} collective-permute-done((bf16[256,1024]{1,0:T(8,128)(2,1)}, bf16[256,1024]{1,0:T(8,128)(2,1)S(1)}, u32[]{:S(2)}, u32[]{:S(2)}) %collective-permute-start.36) | collective-permute-done | bytes 524320 | tf_op jit(solution)/shard_map/ppermute | solution.py:111
  (163 shorter events, 33.8 us)
Async XLA Ops:
  7.2 99.9 %all-gather.4.cloned.1.call-start = ((), (), s32[]{:S(2)}) async-start(), calls=%async_computation.3 | async-start | bytes 2621440 | tf_op jit(solution)/shard_map/all_gather | solution.py:163
  8.8 17.1 %copy-start.24 = (bf16[256,1024]{1,0:T(8,128)(2,1)S(1)}, bf16[256,1024]{1,0:T(8,128)(2,1)}, u32[]{:S(2)}) copy-start(bf16[256,1024]{1,0:T(8,128)(2,1)} %param.8) | copy-start | bytes 1572868
  9.7 97.4 %all-gather.6.cloned.1.call-start = ((), (), s32[]{:S(2)}) async-start(), calls=%async_computation.4 | async-start | bytes 2621440 | tf_op jit(solution)/shard_map/all_gather | solution.py:163
  10.1 15.0 %collective-permute-start.9 = (bf16[256,1024]{1,0:T(8,128)(2,1)S(1)}, bf16[256,1024]{1,0:T(8,128)(2,1)S(1)}, u32[]{:S(2)}, u32[]{:S(2)}) collective-permute-start(bf16[256,1024]{1,0:T(8,128)(2,1)S(1)} %pad_maximum_fusion.1), channel_id=1, source_target_pairs={{0,1},{1,0},{2,3},{3,2},{4,5},{5,4},{6,7},{7,6},{8,9},{9,8},{10,11... | collective-permute-start | bytes 1572872 | tf_op jit(solution)/shard_map/ppermute | solution.py:111
  25.8 126.6 %all-gather.8.cloned.1.call-start = ((), (), s32[]{:S(2)}) async-start(), calls=%async_computation.5 | async-start | bytes 2621440 | tf_op jit(solution)/shard_map/all_gather | solution.py:163
  25.9 9.3 %collective-permute-start.10 = (bf16[128,1024]{1,0:T(8,128)(2,1)S(1)}, bf16[128,1024]{1,0:T(8,128)(2,1)S(1)}, u32[]{:S(2)}, u32[]{:S(2)}) collective-permute-start(bf16[128,1024]{1,0:T(8,128)(2,1)S(1)} %get-tuple-element.37), channel_id=1, source_target_pairs={{0,1},{1,0},{2,3},{3,2},{4,5},{5,4},{6,7},{7,6},{8,9},{9,8},{10,11... | collective-permute-start | bytes 786440 | tf_op jit(solution)/shard_map/ppermute | solution.py:111
  27.8 26.3 %collective-permute-start.1 = (bf16[512,1024]{1,0:T(8,128)(2,1)}, bf16[512,1024]{1,0:T(8,128)(2,1)S(1)}, u32[]{:S(2)}, u32[]{:S(2)}) collective-permute-start(bf16[512,1024]{1,0:T(8,128)(2,1)} %bitcast.refs_0_), channel_id=1, source_target_pairs={{0,16},{8,24},{16,0},{24,8},{1,17},{9,25},{17,1},{25,9},{2,18},{10... | collective-permute-start | bytes 3145736 | tf_op jit(solution)/shard_map/ppermute | solution.py:108
  29.2 28.5 %collective-permute-start = (bf16[512,1024]{1,0:T(8,128)(2,1)}, bf16[512,1024]{1,0:T(8,128)(2,1)S(1)}, u32[]{:S(2)}, u32[]{:S(2)}) collective-permute-start(bf16[512,1024]{1,0:T(8,128)(2,1)} %bitcast.refs_0_), channel_id=1, source_target_pairs={{0,1},{1,0},{2,3},{3,2},{4,5},{5,4},{6,7},{7,6},{8,9},{9,8},{10,11... | collective-permute-start | bytes 3145736 | tf_op jit(solution)/shard_map/ppermute | solution.py:111
  29.8 46.8 %collective-permute-start.20 = (bf16[512,1024]{1,0:T(8,128)(2,1)}, bf16[512,1024]{1,0:T(8,128)(2,1)S(1)}, u32[]{:S(2)}, u32[]{:S(2)}) collective-permute-start(bf16[512,1024]{1,0:T(8,128)(2,1)} %bitcast.6.refs_0_), channel_id=1, source_target_pairs={{0,16},{8,24},{16,0},{24,8},{1,17},{9,25},{17,1},{25,9},{2,18},{10... | collective-permute-start | bytes 3145736 | tf_op jit(solution)/shard_map/ppermute | solution.py:108
  30.1 46.5 %collective-permute-start.4 = (bf16[512,1024]{1,0:T(8,128)(2,1)}, bf16[512,1024]{1,0:T(8,128)(2,1)}, u32[]{:S(2)}, u32[]{:S(2)}) collective-permute-start(bf16[512,1024]{1,0:T(8,128)(2,1)} %bitcast.refs_0_), channel_id=1, source_target_pairs={{0,8},{8,0},{16,24},{24,16},{1,9},{9,1},{17,25},{25,17},{2,10},{10... | collective-permute-start | bytes 3145736 | tf_op jit(solution)/shard_map/ppermute | solution.py:105
  35.3 45.0 %collective-permute-start.19 = (bf16[512,1024]{1,0:T(8,128)(2,1)}, bf16[512,1024]{1,0:T(8,128)(2,1)}, u32[]{:S(2)}, u32[]{:S(2)}) collective-permute-start(bf16[512,1024]{1,0:T(8,128)(2,1)} %bitcast.6.refs_0_), channel_id=1, source_target_pairs={{0,1},{1,0},{2,3},{3,2},{4,5},{5,4},{6,7},{7,6},{8,9},{9,8},{10,11... | collective-permute-start | bytes 3145736 | tf_op jit(solution)/shard_map/ppermute | solution.py:111
  37.8 232.0 %reduce-scatter.8.cloned.1.call-start = ((), (), s32[]{:S(2)}) async-start(), calls=%async_computation.8 | async-start | bytes 2621440 | tf_op jit(solution)/shard_map/reduce_scatter | solution.py:166
  54.1 37.3 %collective-permute-start.2 = (bf16[256,1024]{1,0:T(8,128)(2,1)S(1)}, bf16[256,1024]{1,0:T(8,128)(2,1)S(1)}, u32[]{:S(2)}, u32[]{:S(2)}) collective-permute-start(bf16[256,1024]{1,0:T(8,128)(2,1)S(1)} %slice.110), channel_id=1, source_target_pairs={{0,1},{1,0},{2,3},{3,2},{4,5},{5,4},{6,7},{7,6},{8,9},{9,8},{10,11... | collective-permute-start | bytes 1572872 | tf_op jit(solution)/shard_map/ppermute | solution.py:111
  57.8 35.4 %collective-permute-start.3 = (bf16[256,1024]{1,0:T(8,128)(2,1)S(1)}, bf16[256,1024]{1,0:T(8,128)(2,1)S(1)}, u32[]{:S(2)}, u32[]{:S(2)}) collective-permute-start(bf16[256,1024]{1,0:T(8,128)(2,1)S(1)} %slice.111), channel_id=1, source_target_pairs={{0,16},{8,24},{16,0},{24,8},{1,17},{9,25},{17,1},{25,9},{2,18},{10... | collective-permute-start | bytes 1572872 | tf_op jit(solution)/shard_map/ppermute | solution.py:108
  76.5 27.1 %collective-permute-start.6 = (bf16[512,1024]{1,0:T(8,128)(2,1)S(1)}, bf16[512,1024]{1,0:T(8,128)(2,1)S(1)}, u32[]{:S(2)}, u32[]{:S(2)}) collective-permute-start(bf16[512,1024]{1,0:T(8,128)(2,1)S(1)} %collective-permute-done.1.refs_2_), channel_id=1, source_target_pairs={{0,8},{8,0},{16,24},{24,16},{1,9},{9,1},{17,25},{25,17},{2,10},{10... | collective-permute-start | bytes 3145736 | tf_op jit(solution)/shard_map/ppermute | solution.py:105
  76.6 24.5 %collective-permute-start.21 = (bf16[256,1024]{1,0:T(8,128)(2,1)S(1)}, bf16[256,1024]{1,0:T(8,128)(2,1)}, u32[]{:S(2)}, u32[]{:S(2)}) collective-permute-start(bf16[256,1024]{1,0:T(8,128)(2,1)S(1)} %slice.116), channel_id=1, source_target_pairs={{0,1},{1,0},{2,3},{3,2},{4,5},{5,4},{6,7},{7,6},{8,9},{9,8},{10,11... | collective-permute-start | bytes 1572872 | tf_op jit(solution)/shard_map/ppermute | solution.py:111
  80.3 25.6 %collective-permute-start.5 = (bf16[512,1024]{1,0:T(8,128)(2,1)S(1)}, bf16[512,1024]{1,0:T(8,128)(2,1)S(1)}, u32[]{:S(2)}, u32[]{:S(2)}) collective-permute-start(bf16[512,1024]{1,0:T(8,128)(2,1)S(1)} %collective-permute-done.refs_1_), channel_id=1, source_target_pairs={{0,8},{8,0},{16,24},{24,16},{1,9},{9,1},{17,25},{25,17},{2,10},{10... | collective-permute-start | bytes 3145736 | tf_op jit(solution)/shard_map/ppermute | solution.py:105
  91.4 10.9 %collective-permute-start.22 = (bf16[256,1024]{1,0:T(8,128)(2,1)S(1)}, bf16[256,1024]{1,0:T(8,128)(2,1)}, u32[]{:S(2)}, u32[]{:S(2)}) collective-permute-start(bf16[256,1024]{1,0:T(8,128)(2,1)S(1)} %slice.117), channel_id=1, source_target_pairs={{0,16},{8,24},{16,0},{24,8},{1,17},{9,25},{17,1},{25,9},{2,18},{10... | collective-permute-start | bytes 1572872 | tf_op jit(solution)/shard_map/ppermute | solution.py:108
  93.1 9.3 %collective-permute-start.7 = (bf16[256,1024]{1,0:T(8,128)(2,1)S(1)}, bf16[256,1024]{1,0:T(8,128)(2,1)S(1)}, u32[]{:S(2)}, u32[]{:S(2)}) collective-permute-start(bf16[256,1024]{1,0:T(8,128)(2,1)S(1)} %collective-permute-done.2.refs_3_), channel_id=1, source_target_pairs={{0,8},{8,0},{16,24},{24,16},{1,9},{9,1},{17,25},{25,17},{2,10},{10... | collective-permute-start | bytes 1572872 | tf_op jit(solution)/shard_map/ppermute | solution.py:105
  101.1 3.6 %collective-permute-start.8 = (bf16[256,1024]{1,0:T(8,128)(2,1)S(1)}, bf16[256,1024]{1,0:T(8,128)(2,1)S(1)}, u32[]{:S(2)}, u32[]{:S(2)}) collective-permute-start(bf16[256,1024]{1,0:T(8,128)(2,1)S(1)} %collective-permute-done.3.refs_4_), channel_id=1, source_target_pairs={{0,8},{8,0},{16,24},{24,16},{1,9},{9,1},{17,25},{25,17},{2,10},{10... | collective-permute-start | bytes 1572872 | tf_op jit(solution)/shard_map/ppermute | solution.py:105
  102.3 27.5 %collective-permute-start.23 = (bf16[512,1024]{1,0:T(8,128)(2,1)}, bf16[512,1024]{1,0:T(8,128)(2,1)}, u32[]{:S(2)}, u32[]{:S(2)}) collective-permute-start(bf16[512,1024]{1,0:T(8,128)(2,1)} %bitcast.6.refs_0_), channel_id=1, source_target_pairs={{0,8},{8,0},{16,24},{24,16},{1,9},{9,1},{17,25},{25,17},{2,10},{10... | collective-permute-start | bytes 3145736 | tf_op jit(solution)/shard_map/ppermute | solution.py:105
  103.2 26.6 %collective-permute-start.25 = (bf16[512,1024]{1,0:T(8,128)(2,1)S(1)}, bf16[512,1024]{1,0:T(8,128)(2,1)}, u32[]{:S(2)}, u32[]{:S(2)}) collective-permute-start(bf16[512,1024]{1,0:T(8,128)(2,1)S(1)} %collective-permute-done.20.refs_2_), channel_id=1, source_target_pairs={{0,8},{8,0},{16,24},{24,16},{1,9},{9,1},{17,25},{25,17},{2,10},{10... | collective-permute-start | bytes 3145736 | tf_op jit(solution)/shard_map/ppermute | solution.py:105
  104.6 25.2 %collective-permute-start.24 = (bf16[512,1024]{1,0:T(8,128)(2,1)}, bf16[512,1024]{1,0:T(8,128)(2,1)}, u32[]{:S(2)}, u32[]{:S(2)}) collective-permute-start(bf16[512,1024]{1,0:T(8,128)(2,1)} %collective-permute-done.19.refs_1_), channel_id=1, source_target_pairs={{0,8},{8,0},{16,24},{24,16},{1,9},{9,1},{17,25},{25,17},{2,10},{10... | collective-permute-start | bytes 3145736 | tf_op jit(solution)/shard_map/ppermute | solution.py:105
  105.5 24.3 %collective-permute-start.26 = (bf16[256,1024]{1,0:T(8,128)(2,1)}, bf16[256,1024]{1,0:T(8,128)(2,1)}, u32[]{:S(2)}, u32[]{:S(2)}) collective-permute-start(bf16[256,1024]{1,0:T(8,128)(2,1)} %collective-permute-done.21.refs_3_), channel_id=1, source_target_pairs={{0,8},{8,0},{16,24},{24,16},{1,9},{9,1},{17,25},{25,17},{2,10},{10... | collective-permute-start | bytes 1572872 | tf_op jit(solution)/shard_map/ppermute | solution.py:105
  106.9 22.9 %collective-permute-start.27 = (bf16[256,1024]{1,0:T(8,128)(2,1)}, bf16[256,1024]{1,0:T(8,128)(2,1)}, u32[]{:S(2)}, u32[]{:S(2)}) collective-permute-start(bf16[256,1024]{1,0:T(8,128)(2,1)} %collective-permute-done.22.refs_4_), channel_id=1, source_target_pairs={{0,8},{8,0},{16,24},{24,16},{1,9},{9,1},{17,25},{25,17},{2,10},{10... | collective-permute-start | bytes 1572872 | tf_op jit(solution)/shard_map/ppermute | solution.py:105
  140.8 130.8 %reduce-scatter.6.cloned.1.call-start = ((), (), s32[]{:S(2)}) async-start(), calls=%async_computation.7 | async-start | bytes 2621440 | tf_op jit(solution)/shard_map/reduce_scatter | solution.py:166
  152.5 13.5 %copy-start.14 = (bf16[256,1024]{1,0:T(8,128)(2,1)S(1)}, bf16[256,1024]{1,0:T(8,128)(2,1)}, u32[]{:S(2)}) copy-start(bf16[256,1024]{1,0:T(8,128)(2,1)} %copy-done.12) | copy-start | bytes 1572868
  152.5 13.5 %copy-start.18 = (bf16[256,1024]{1,0:T(8,128)(2,1)S(1)}, bf16[256,1024]{1,0:T(8,128)(2,1)}, u32[]{:S(2)}) copy-start(bf16[256,1024]{1,0:T(8,128)(2,1)} %copy-done.16) | copy-start | bytes 1572868
  152.5 13.5 %copy-start.22 = (bf16[256,1024]{1,0:T(8,128)(2,1)S(1)}, bf16[256,1024]{1,0:T(8,128)(2,1)}, u32[]{:S(2)}) copy-start(bf16[256,1024]{1,0:T(8,128)(2,1)} %copy-done.20) | copy-start | bytes 1572868
  175.3 115.9 %reduce-scatter.4.cloned.1.call-start = ((), (), s32[]{:S(2)}) async-start(), calls=%async_computation.6 | async-start | bytes 2621440 | tf_op jit(solution)/shard_map/reduce_scatter | solution.py:166
  178.5 54.3 %collective-permute-start.12 = (bf16[512,1024]{1,0:T(8,128)(2,1)}, bf16[512,1024]{1,0:T(8,128)(2,1)S(1)}, u32[]{:S(2)}, u32[]{:S(2)}) collective-permute-start(bf16[512,1024]{1,0:T(8,128)(2,1)} %convolution_convert_fusion.6), channel_id=1, source_target_pairs={{0,8},{8,0},{16,24},{24,16},{1,9},{9,1},{17,25},{25,17},{2,10},{10... | collective-permute-start | bytes 3145736 | tf_op jit(solution)/shard_map/ppermute | solution.py:105
  181.4 28.7 %collective-permute-start.13 = (bf16[512,1024]{1,0:T(8,128)(2,1)}, bf16[512,1024]{1,0:T(8,128)(2,1)}, u32[]{:S(2)}, u32[]{:S(2)}) collective-permute-start(bf16[512,1024]{1,0:T(8,128)(2,1)} %convolution_convert_fusion.5), channel_id=1, source_target_pairs={{0,8},{8,0},{16,24},{24,16},{1,9},{9,1},{17,25},{25,17},{2,10},{10... | collective-permute-start | bytes 3145736 | tf_op jit(solution)/shard_map/ppermute | solution.py:105
  185.5 28.1 %collective-permute-start.29 = (bf16[512,1024]{1,0:T(8,128)(2,1)}, bf16[512,1024]{1,0:T(8,128)(2,1)}, u32[]{:S(2)}, u32[]{:S(2)}) collective-permute-start(bf16[512,1024]{1,0:T(8,128)(2,1)} %convolution_convert_fusion.2), channel_id=1, source_target_pairs={{0,8},{8,0},{16,24},{24,16},{1,9},{9,1},{17,25},{25,17},{2,10},{10... | collective-permute-start | bytes 3145736 | tf_op jit(solution)/shard_map/ppermute | solution.py:105
  188.0 17.1 %collective-permute-start.30 = (bf16[512,1024]{1,0:T(8,128)(2,1)}, bf16[512,1024]{1,0:T(8,128)(2,1)}, u32[]{:S(2)}, u32[]{:S(2)}) collective-permute-start(bf16[512,1024]{1,0:T(8,128)(2,1)} %convolution_convert_fusion.1), channel_id=1, source_target_pairs={{0,8},{8,0},{16,24},{24,16},{1,9},{9,1},{17,25},{25,17},{2,10},{10... | collective-permute-start | bytes 3145736 | tf_op jit(solution)/shard_map/ppermute | solution.py:105
  190.6 37.2 %collective-permute-start.33 = (bf16[512,1024]{1,0:T(8,128)(2,1)}, bf16[512,1024]{1,0:T(8,128)(2,1)}, u32[]{:S(2)}, u32[]{:S(2)}) collective-permute-start(bf16[512,1024]{1,0:T(8,128)(2,1)} %convolution_convert_fusion), channel_id=1, source_target_pairs={{0,8},{8,0},{16,24},{24,16},{1,9},{9,1},{17,25},{25,17},{2,10},{10... | collective-permute-start | bytes 3145736 | tf_op jit(solution)/shard_map/ppermute | solution.py:105
  208.7 14.2 %collective-permute-start.31 = (bf16[256,1024]{1,0:T(8,128)(2,1)S(1)}, bf16[256,1024]{1,0:T(8,128)(2,1)S(1)}, u32[]{:S(2)}, u32[]{:S(2)}) collective-permute-start(bf16[256,1024]{1,0:T(8,128)(2,1)S(1)} %get-tuple-element.22), channel_id=1, source_target_pairs={{0,1},{1,0},{2,3},{3,2},{4,5},{5,4},{6,7},{7,6},{8,9},{9,8},{10,11... | collective-permute-start | bytes 1572872 | tf_op jit(solution)/shard_map/ppermute | solution.py:111
  210.1 17.7 %collective-permute-start.34 = (bf16[256,1024]{1,0:T(8,128)(2,1)S(1)}, bf16[256,1024]{1,0:T(8,128)(2,1)S(1)}, u32[]{:S(2)}, u32[]{:S(2)}) collective-permute-start(bf16[256,1024]{1,0:T(8,128)(2,1)S(1)} %get-tuple-element.23), channel_id=1, source_target_pairs={{0,16},{8,24},{16,0},{24,8},{1,17},{9,25},{17,1},{25,9},{2,18},{10... | collective-permute-start | bytes 1572872 | tf_op jit(solution)/shard_map/ppermute | solution.py:108
  213.6 27.6 %collective-permute-start.16 = (bf16[512,1024]{1,0:T(8,128)(2,1)S(1)}, bf16[512,1024]{1,0:T(8,128)(2,1)S(1)}, u32[]{:S(2)}, u32[]{:S(2)}) collective-permute-start(bf16[512,1024]{1,0:T(8,128)(2,1)S(1)} %convolution_convert_fusion.4), channel_id=1, source_target_pairs={{0,8},{8,0},{16,24},{24,16},{1,9},{9,1},{17,25},{25,17},{2,10},{10... | collective-permute-start | bytes 3145736 | tf_op jit(solution)/shard_map/ppermute | solution.py:105
  222.9 13.4 %collective-permute-start.14 = (bf16[256,1024]{1,0:T(8,128)(2,1)S(1)}, bf16[256,1024]{1,0:T(8,128)(2,1)S(1)}, u32[]{:S(2)}, u32[]{:S(2)}) collective-permute-start(bf16[256,1024]{1,0:T(8,128)(2,1)S(1)} %get-tuple-element.24), channel_id=1, source_target_pairs={{0,1},{1,0},{2,3},{3,2},{4,5},{5,4},{6,7},{7,6},{8,9},{9,8},{10,11... | collective-permute-start | bytes 1572872 | tf_op jit(solution)/shard_map/ppermute | solution.py:111
  227.9 18.0 %collective-permute-start.28 = (bf16[512,1024]{1,0:T(8,128)(2,1)S(1)}, bf16[512,1024]{1,0:T(8,128)(2,1)S(1)}, u32[]{:S(2)}, u32[]{:S(2)}) collective-permute-start(bf16[512,1024]{1,0:T(8,128)(2,1)S(1)} %convolution_convert_fusion.3), channel_id=1, source_target_pairs={{0,8},{8,0},{16,24},{24,16},{1,9},{9,1},{17,25},{25,17},{2,10},{10... | collective-permute-start | bytes 3145736 | tf_op jit(solution)/shard_map/ppermute | solution.py:105
  227.9 14.8 %collective-permute-start.17 = (bf16[256,1024]{1,0:T(8,128)(2,1)S(1)}, bf16[256,1024]{1,0:T(8,128)(2,1)S(1)}, u32[]{:S(2)}, u32[]{:S(2)}) collective-permute-start(bf16[256,1024]{1,0:T(8,128)(2,1)S(1)} %get-tuple-element.25), channel_id=1, source_target_pairs={{0,16},{8,24},{16,0},{24,8},{1,17},{9,25},{17,1},{25,9},{2,18},{10... | collective-permute-start | bytes 1572872 | tf_op jit(solution)/shard_map/ppermute | solution.py:108
  232.9 32.4 %collective-permute-start.32 = (bf16[512,1024]{1,0:T(8,128)(2,1)}, bf16[512,1024]{1,0:T(8,128)(2,1)}, u32[]{:S(2)}, u32[]{:S(2)}) collective-permute-start(bf16[512,1024]{1,0:T(8,128)(2,1)} %add_convert_fusion.2), channel_id=1, source_target_pairs={{0,16},{8,24},{16,0},{24,8},{1,17},{9,25},{17,1},{25,9},{2,18},{10... | collective-permute-start | bytes 3145736 | tf_op jit(solution)/shard_map/ppermute | solution.py:108
  236.3 28.9 %collective-permute-start.35 = (bf16[512,1024]{1,0:T(8,128)(2,1)}, bf16[512,1024]{1,0:T(8,128)(2,1)}, u32[]{:S(2)}, u32[]{:S(2)}) collective-permute-start(bf16[512,1024]{1,0:T(8,128)(2,1)} %add_convert_fusion.1), channel_id=1, source_target_pairs={{0,1},{1,0},{2,3},{3,2},{4,5},{5,4},{6,7},{7,6},{8,9},{9,8},{10,11... | collective-permute-start | bytes 3145736 | tf_op jit(solution)/shard_map/ppermute | solution.py:111
  241.2 31.8 %collective-permute-start.11 = (bf16[512,1024]{1,0:T(8,128)(2,1)}, bf16[512,1024]{1,0:T(8,128)(2,1)S(1)}, u32[]{:S(2)}, u32[]{:S(2)}) collective-permute-start(bf16[512,1024]{1,0:T(8,128)(2,1)} %convolution_convert_fusion.7), channel_id=1, source_target_pairs={{0,8},{8,0},{16,24},{24,16},{1,9},{9,1},{17,25},{25,17},{2,10},{10... | collective-permute-start | bytes 3145736 | tf_op jit(solution)/shard_map/ppermute | solution.py:105
  242.7 44.6 %collective-permute-start.15 = (bf16[512,1024]{1,0:T(8,128)(2,1)}, bf16[512,1024]{1,0:T(8,128)(2,1)}, u32[]{:S(2)}, u32[]{:S(2)}) collective-permute-start(bf16[512,1024]{1,0:T(8,128)(2,1)} %add_convert_fusion.6), channel_id=1, source_target_pairs={{0,16},{8,24},{16,0},{24,8},{1,17},{9,25},{17,1},{25,9},{2,18},{10... | collective-permute-start | bytes 3145736 | tf_op jit(solution)/shard_map/ppermute | solution.py:108
  246.8 40.5 %collective-permute-start.18 = (bf16[512,1024]{1,0:T(8,128)(2,1)}, bf16[512,1024]{1,0:T(8,128)(2,1)}, u32[]{:S(2)}, u32[]{:S(2)}) collective-permute-start(bf16[512,1024]{1,0:T(8,128)(2,1)} %add_convert_fusion.5), channel_id=1, source_target_pairs={{0,1},{1,0},{2,3},{3,2},{4,5},{5,4},{6,7},{7,6},{8,9},{9,8},{10,11... | collective-permute-start | bytes 3145736 | tf_op jit(solution)/shard_map/ppermute | solution.py:111
  270.9 21.4 %collective-permute-start.37 = (bf16[128,1024]{1,0:T(8,128)(2,1)S(1)}, bf16[128,1024]{1,0:T(8,128)(2,1)S(1)}, u32[]{:S(2)}, u32[]{:S(2)}) collective-permute-start(bf16[128,1024]{1,0:T(8,128)(2,1)S(1)} %get-tuple-element.27), channel_id=1, source_target_pairs={{0,1},{1,0},{2,3},{3,2},{4,5},{5,4},{6,7},{7,6},{8,9},{9,8},{10,11... | collective-permute-start | bytes 786440 | tf_op jit(solution)/shard_map/ppermute | solution.py:111
  271.7 28.1 %collective-permute-start.36 = (bf16[256,1024]{1,0:T(8,128)(2,1)}, bf16[256,1024]{1,0:T(8,128)(2,1)S(1)}, u32[]{:S(2)}, u32[]{:S(2)}) collective-permute-start(bf16[256,1024]{1,0:T(8,128)(2,1)} %reduce-scatter.6.cloned.1.call-done), channel_id=1, source_target_pairs={{0,1},{1,0},{2,3},{3,2},{4,5},{5,4},{6,7},{7,6},{8,9},{9,8},{10,11... | collective-permute-start | bytes 1572872 | tf_op jit(solution)/shard_map/ppermute | solution.py:111
  (32 other events, 102.4 us)
Sparse Core Ops, SparseCore 0:
  10.1 48.6 all-gather.3
  61.0 44.6 all-gather.5
  107.8 44.6 all-gather.7
  154.6 42.5 reduce-scatter.7
  199.5 43.1 reduce-scatter.5
  244.8 43.1 reduce-scatter.3
where the time goes:
time: 310 us
  waiting for transfers between devices  138 us (45%)
  Pallas kernels  59.1 us (19%)
  matrix products  44.5 us (14%)
  starting transfers between devices  27.9 us (9%)
  local copies, waits for them, and re-layouts  20.3 us (7%)
  between operations  14.6 us (5%)
  other arithmetic  5.32 us (2%)
    ppermute x8, waiting for transfers between devices, chip(): return lax.ppermute(array, 'inp', [(at, at ^ 2) for at in range(4)])  67 us
    ppermute x12, waiting for transfers between devices, other(): return lax.ppermute(array, 'out', [(0, 1), (1, 0)])  59.3 us
    pallas_call x5, Pallas kernels, call(): pl.pallas_call(kernel, out_shape=outs, in_specs=[pl.BlockSpec(memory_spac...  59.1 us
    dot_general x16, matrix products, matmul(): lax.dot_general(a, b, ((contract[:1], contract[1:]), ((), ())), preferred...  44.5 us
    unnamed x78, local copies, waits for them, and re-layouts  17.7 us
    ppermute x12, starting transfers between devices, other(): return lax.ppermute(array, 'out', [(0, 1), (1, 0)])  14.8 us
    all_gather x3, waiting for transfers between devices, gather_units(): return lax.all_gather(array, 'wt', axis=0, tiled=True)  11.4 us
    ppermute x8, starting transfers between devices, chip(): return lax.ppermute(array, 'inp', [(at, at ^ 2) for at in range(4)])  10.3 us
  transfers between devices with their start and end apart: 44, of which 16 were waited for; matrix products, arithmetic and copies ran while one was open for 16% of the time, Pallas kernels for 19%

commit v1 on v0

v1 whole, which is shorter than its diff:
```python
import functools

import jax
import jax.numpy as jnp
from jax import lax
from jax.experimental import pallas as pl
from jax.experimental.pallas import tpu as pltpu
from jax.sharding import PartitionSpec as P

F32 = jnp.float32
BF16 = jnp.bfloat16
MIB = 1024 * 1024


def matmul(a, b, contract):
    return lax.dot_general(a, b, ((contract[:1], contract[1:]), ((), ())), preferred_element_type=F32)


def gated(gate_sum, up_sum):
    sigmoid_g = jax.nn.sigmoid(gate_sum)
    silu_g = gate_sum * sigmoid_g
    slope = sigmoid_g * (1.0 + gate_sum * (1.0 - sigmoid_g))
    return silu_g, silu_g * up_sum, up_sum * slope


def shape(*dims, dtype=BF16):
    return jax.ShapeDtypeStruct(dims, dtype)


def call(kernel, outs, flops, args, after=(), specs=None, scratch=(), limit=24):
    everything = [*args, *after]
    moved = sum(a.size * a.dtype.itemsize for a in args) + sum(o.size * o.dtype.itemsize for o in outs)
    specs = specs or [pl.BlockSpec(memory_space=pltpu.VMEM)] * len(args)

    def body(*refs):
        kernel(*refs[: len(args)], *refs[len(everything) :])

    return pl.pallas_call(
        body,
        out_shape=list(outs),
        in_specs=[*specs, *[pl.BlockSpec(memory_space=pl.ANY)] * len(after)],
        out_specs=[pl.BlockSpec(memory_space=pltpu.VMEM)] * len(outs),
        scratch_shapes=list(scratch),
        compiler_params=pltpu.CompilerParams(vmem_limit_bytes=limit * MIB),
        cost_estimate=pl.CostEstimate(flops=flops, bytes_accessed=moved, transcendentals=0),
    )(*everything)


ANY = pl.BlockSpec(memory_space=pl.ANY)
VMEM = pl.BlockSpec(memory_space=pltpu.VMEM)
SMEM = pl.BlockSpec(memory_space=pltpu.SMEM)


class Rows:
    def __init__(self, pieces, blocks, step):
        self.pieces, self.blocks, self.step = pieces, blocks, step
        self.count, self.half = len(blocks) * step, pieces[0].shape[1]

    def copies(self, refs, sides, scratch, sems):
        found = []
        for at, pair in enumerate(self.blocks):
            found.append([])
            for place, side in enumerate(sides):
                piece, first = pair[side]
                into = scratch.at[pl.ds(at * self.step, self.step), pl.ds(place * self.half, self.half)]
                source = refs[piece].at[pl.ds(first, self.step)]
                found[-1].append(pltpu.make_async_copy(source, into, sems.at[at * len(sides) + place]))
        return found


def hidden_kernel(rows, width, *refs):
    count = len(rows.pieces)
    pieces = refs[:count]
    own_ref, other_ref, hidden_ref, turned_ref, silu_ref, rest_ref, in_ref, unit_ref, sems, unit_sems = refs[count:]
    half = rows.half
    loads = [
        pltpu.make_async_copy(own_ref, unit_ref.at[:, pl.ds(0, half)], unit_sems.at[0]),
        pltpu.make_async_copy(other_ref, unit_ref.at[:, pl.ds(half, half)], unit_sems.at[1]),
    ]
    copies = rows.copies(pieces, (0, 1), in_ref, sems)
    for copy in loads + [copy for block in copies for copy in block]:
        copy.start()
    for copy in loads:
        copy.wait()
    for pair in range(len(copies) // 2):
        for copy in copies[2 * pair] + copies[2 * pair + 1]:
            copy.wait()
        span = slice(2 * pair * rows.step, 2 * (pair + 1) * rows.step)

        @pl.loop(0, unit_ref.shape[0] // (2 * width))
        def _(group):
            units = pl.ds(pl.multiple_of(group * 2 * width, 2 * width), 2 * width)
            sums = matmul(in_ref[span], unit_ref[units], (1, 1))
            silu_g, hidden, rest = gated(sums[:, :width], sums[:, width:])
            cols = pl.ds(pl.multiple_of(group * width, width), width)
            hidden_ref[span, cols] = hidden.astype(BF16)
            turned_ref[cols, span] = hidden.T.astype(BF16)
            silu_ref[span, cols] = silu_g.astype(BF16)
            rest_ref[span, cols] = rest.astype(BF16)


def grads_kernel(rows, width, *refs):
    count = len(rows.pieces)
    pieces = refs[:count]
    down_ref, silu_ref, rest_ref, act_ref, turned_ref, cot_ref, sems = refs[count:]
    copies = rows.copies(pieces, (0, 1), cot_ref, sems)
    for copy in [copy for block in copies for copy in block]:
        copy.start()
    for pair in range(len(copies) // 2):
        for copy in copies[2 * pair] + copies[2 * pair + 1]:
            copy.wait()
        span = slice(2 * pair * rows.step, 2 * (pair + 1) * rows.step)

        @pl.loop(0, down_ref.shape[0] // (2 * width))
        def _(group):
            units = pl.ds(pl.multiple_of(group * 2 * width, 2 * width), 2 * width)
            back = matmul(cot_ref[span], down_ref[units], (1, 1))
            for part, factor in enumerate((rest_ref, silu_ref)):
                grads = back * factor[span, units].astype(F32)
                for side in range(2):
                    grad = grads[:, side * width : (side + 1) * width]
                    low = pl.ds(pl.multiple_of((4 * group + 2 * side + part) * width, width), width)
                    act_ref[span, low] = grad.astype(BF16)
                    turned_ref[low, span] = grad.T.astype(BF16)


def weight_kernel(rows, sides, tile, *refs):
    count = len(rows.pieces)
    pieces, (turned_ref, out_ref, rows_ref, sems) = refs[:count], refs[count:]
    copies = [copy for block in rows.copies(pieces, sides, rows_ref, sems) for copy in block]
    for copy in copies:
        copy.start()
    for copy in copies:
        copy.wait()

    @pl.loop(0, out_ref.shape[1] // tile)
    def _(index):
        cols = pl.ds(pl.multiple_of(index * tile, tile), tile)
        out_ref[:, cols] = matmul(turned_ref[...], rows_ref[:, cols], (1, 0)).astype(BF16)


def block_kernel(first, places, sides, added, *refs):
    rights, many = len(sides), len(places)
    left_any, right_any, refs = refs[0], refs[1 : 1 + rights], refs[1 + rights :]
    adds, refs = refs[: many * added], refs[many * added :]
    outs, (left_ref, right_ref, sems) = refs[:many], refs[many:]
    depth, half = right_ref.shape[1:]
    copies = [pltpu.make_async_copy(left_any.at[pl.ds(first, left_ref.shape[0])], left_ref, sems.at[0])]
    for at, side in enumerate(sides):
        source = right_any[at].at[:, pl.ds(side * half, half)]
        copies.append(pltpu.make_async_copy(source, right_ref.at[at], sems.at[1 + at]))
    for copy in copies:
        copy.start()
    for copy in copies:
        copy.wait()
    for at, (row, right) in enumerate(places):
        total = matmul(left_ref[row : row + outs[at].shape[0]], right_ref[right], (1, 0))
        if added:
            total = total + adds[at][...].astype(F32)
        outs[at][...] = total.astype(BF16)


def halves_kernel(at_ref, gate_ref, up_ref, mine_ref, theirs_ref):
    width = gate_ref.shape[1] // 2
    for part, ref in enumerate((gate_ref, up_ref)):
        span = slice(part * width, (part + 1) * width)
        low, high = ref[:, :width].astype(F32).T.astype(BF16), ref[:, width:].astype(F32).T.astype(BF16)
        first = at_ref[0] == 0
        mine_ref[span] = jnp.where(first, low, high)
        theirs_ref[span] = jnp.where(first, high, low)


def copy_kernel(in_ref, out_ref):
    out_ref[...] = in_ref[...]


def beside_kernel(left_ref, right_ref, out_ref):
    half = left_ref.shape[1]
    out_ref[:, :half] = left_ref[...]
    out_ref[:, half:] = right_ref[...]


def line_kernel(places, at_ref, own_ref, *refs):
    before, after, out_ref = refs[: places - 1], refs[places - 1 : -1], refs[-1]
    step = own_ref.shape[0]
    for block in range(places):
        for at in range(places):
            source = own_ref if at == block else before[at - block - 1] if at > block else after[block - at - 1]

            @pl.when(at_ref[0] == at)
            def _(source=source):
                out_ref[block * step : (block + 1) * step] = source[...]


def finish_kernel(at_ref, mine_ref, theirs_ref, gate_ref, up_ref):
    width = mine_ref.shape[0] // 2
    for part, out_ref in enumerate((gate_ref, up_ref)):
        span = slice(part * width, (part + 1) * width)
        mine, theirs = mine_ref[span].astype(F32).T, theirs_ref[span].astype(F32).T
        first = at_ref[0] == 0
        out_ref[:, :width] = jnp.where(first, mine, theirs)
        out_ref[:, width:] = jnp.where(first, theirs, mine)


class Square:
    def __init__(self, places):
        self.places = places

    def core(self, array):
        return lax.ppermute(array, "inp", [(at, at ^ 1) for at in range(4)])

    def chip(self, array):
        return lax.ppermute(array, "inp", [(at, at ^ 2) for at in range(4)])

    def other(self, array):
        return lax.ppermute(array, "out", [(0, 1), (1, 0)])

    def gather(self, array, split):
        step = array.shape[1]
        own = array.reshape(2 * step, array.shape[2])
        by_chip, by_other = self.chip(own), self.other(own)
        if split:
            corner = [self.other(by_chip[:step]), self.chip(by_other[step:])]
        else:
            corner = [self.chip(by_other)]
        pieces = [own, by_other, by_chip] + corner
        many = len(pieces)
        pieces = pieces + [self.core(piece) for piece in pieces]
        blocks = []
        for base in (0, many):
            blocks += [((base, 0), (base + 1, 0)), ((base, step), (base + 1, step))]
            last = (base + 4, 0) if split else (base + 3, step)
            blocks += [((base + 2, 0), (base + 3, 0)), ((base + 2, step), last)]
        return Rows(pieces, blocks, step)

    def line(self, own, at):
        many = self.places

        def shift(array, by):
            return lax.ppermute(array, "wt", [(i, i + by) for i in range(many) if 0 <= i + by < many])

        near = {by: shift(own, by) for by in (1, -1, 2, -2) if abs(by) < many}
        before, beyond = [near[1], near[2]], [near[-1], near[-2]]
        for by in range(3, many):
            before.append(lax.ppermute(before[-1], "wt", [(i, i + 1) for i in range(by - 1, many - 1)]))
            beyond.append(lax.ppermute(beyond[-1], "wt", [(i, i - 1) for i in range(1, many - by + 1)]))
        (out,) = call(
            functools.partial(line_kernel, many),
            [shape(many * own.shape[0], own.shape[1])],
            0,
            [at, own, *before, *beyond],
            specs=[SMEM] + [VMEM] * (2 * many - 1),
        )
        return out

    def products(self, left, rights, places, adds=(), after=()):
        far = int(not adds)
        quarter, depth = left.shape[0] // 4, left.shape[1]
        half = rights[0][2]
        outs = [shape(quarter, half)] * len(places)
        use = sorted({other for _, other in places})
        chips = sorted({chip for chip, _ in places})
        first = 2 * far * quarter + chips[0] * quarter
        wanted = [((chip - chips[0]) * quarter, use.index(other)) for chip, other in places]
        args = [left] + [rights[other][0] for other in use] + [adds[place] for place in places if adds]
        blocks = call(
            functools.partial(block_kernel, first, wanted, [rights[other][1] for other in use], bool(adds)),
            outs,
            2 * len(places) * quarter * depth * half,
            args,
            after,
            specs=[ANY] * (1 + len(use)) + [VMEM] * (len(args) - 1 - len(use)),
            scratch=[
                pltpu.VMEM((len(chips) * quarter, depth), BF16),
                pltpu.VMEM((len(use), depth, half), BF16),
                pltpu.SemaphoreType.DMA((1 + len(use),)),
            ],
        )
        return dict(zip(places, blocks))

    def scatter_far(self, left, rights):
        first = self.products(left, rights, [(1, 1)])
        second = self.products(left, rights, [(0, 1), (1, 0), (0, 0)], after=list(first.values()))
        return first | second

    def scatter_near(self, left, rights, far, split, after=()):
        far = {place: self.core(block) for place, block in far.items()}
        sums = self.products(left, rights, [(1, 1)], far, after)
        sums |= self.products(left, rights, [(0, 1), (1, 0), (0, 0)], far, list(sums.values()))
        corner = sums[1, 1]
        step = corner.shape[0] // 2
        if split:
            by_other = self.other(corner[:step]).astype(F32)
            by_chip = self.chip(corner[step:]).astype(F32)
            zeros = jnp.zeros_like(by_other)
            to_chip = (sums[1, 0].astype(F32) + jnp.concatenate([by_other, zeros])).astype(BF16)
            to_other = (sums[0, 1].astype(F32) + jnp.concatenate([zeros, by_chip])).astype(BF16)
        else:
            to_chip = sums[1, 0]
            to_other = (sums[0, 1].astype(F32) + self.chip(corner).astype(F32)).astype(BF16)
        return sums[0, 0], self.chip(to_chip), self.other(to_other)

    def scatter_end(self, own, by_chip, by_other):
        total = own.astype(F32) + by_chip.astype(F32) + by_other.astype(F32)
        return total.astype(BF16).reshape(2, own.shape[0] // 2, own.shape[1])

    def layer(self, tokens, gate_weight, up_weight, down_weight, cotangent):
        def gather_units(array):
            return lax.all_gather(array, "wt", axis=0, tiled=True)

        def scatter_units(array):
            return lax.psum_scatter(array, "wt", scatter_dimension=0, tiled=True)

        at_out = lax.axis_index("out").astype(jnp.int32)
        half, width = gate_weight.shape[0], gate_weight.shape[1] // 2
        pair = [shape(2 * width, half)] * 2
        mine, theirs = call(halves_kernel, pair, 0, [at_out.reshape(1), gate_weight, up_weight], specs=[SMEM, VMEM, VMEM])
        own_units = gather_units(mine)
        theirs = self.other(theirs)
        rows_in = self.gather(tokens, True)
        (theirs,) = call(copy_kernel, pair[:1], 0, [theirs], after=[rows_in.pieces[2]])
        other_units = gather_units(theirs)
        down_mine = lax.dynamic_slice_in_dim(down_weight, at_out * width, width, 0)
        down_theirs = self.other(lax.dynamic_slice_in_dim(down_weight, (1 - at_out) * width, width, 0))
        rows_cot = self.gather(cotangent, False)
        (down_own,) = call(
            beside_kernel, [shape(width, 2 * half)], 0, [down_mine, down_theirs], after=[other_units]
        )

        count = rows_in.count
        units = self.places * width
        loads = len(rows_in.blocks)
        both = pltpu.VMEM((count, 2 * half), BF16)
        hidden, hidden_turned, silu, rest = call(
            functools.partial(hidden_kernel, rows_in, width),
            [shape(count, units), shape(units, count), shape(count, units), shape(count, units)],
            8 * count * units * half,
            [*rows_in.pieces, own_units, other_units],
            after=[down_own],
            specs=[ANY] * (len(rows_in.pieces) + 2),
            scratch=[
                both,
                pltpu.VMEM((2 * units, 2 * half), BF16),
                pltpu.SemaphoreType.DMA((2 * loads,)),
                pltpu.SemaphoreType.DMA((2,)),
            ],
            limit=32,
        )
        (down_term,) = call(
            functools.partial(weight_kernel, rows_cot, (0, 1), 256),
            [shape(units, 2 * half)],
            4 * count * units * half,
            [*rows_cot.pieces, hidden_turned],
            specs=[ANY] * len(rows_cot.pieces) + [VMEM],
            scratch=[both, pltpu.SemaphoreType.DMA((2 * loads,))],
        )
        down_sum = scatter_units(down_term)
        at_wt = lax.axis_index("wt").astype(jnp.int32).reshape(1)
        down = self.line(down_own, at_wt)
        down_sides = [(down, 0, half), (down, 1, half)]
        output_far = self.scatter_far(hidden, down_sides)
        act, act_turned = call(
            functools.partial(grads_kernel, rows_cot, width),
            [shape(count, 2 * units), shape(2 * units, count)],
            4 * count * units * half,
            [*rows_cot.pieces, down, silu, rest],
            after=list(output_far.values()),
            specs=[ANY] * len(rows_cot.pieces) + [VMEM] * 3,
            scratch=[both, pltpu.SemaphoreType.DMA((2 * loads,))],
            limit=32,
        )
        terms = [
            call(
                functools.partial(weight_kernel, rows_in, (side,), 256),
                [shape(2 * units, half)],
                4 * count * units * half,
                [*rows_in.pieces, act_turned],
                specs=[ANY] * len(rows_in.pieces) + [VMEM],
                scratch=[pltpu.VMEM((count, half), BF16), pltpu.SemaphoreType.DMA((loads,))],
            )[0]
            for side in (1, 0)
        ]
        other_sum, own_sum = scatter_units(terms[0]), scatter_units(terms[1])
        down_back = self.other(down_sum[:, half:])
        units_back = self.other(other_sum)
        mine, theirs = down_sum[:, :half].astype(F32), down_back.astype(F32)
        grad_down = jnp.where(at_out == 0, jnp.concatenate([mine, theirs]), jnp.concatenate([theirs, mine]))
        grad_gate, grad_up = call(
            finish_kernel,
            [shape(half, 2 * width, dtype=F32)] * 2,
            0,
            [at_out.reshape(1), own_sum, units_back],
            specs=[SMEM, VMEM, VMEM],
        )

        output = self.scatter_end(*self.scatter_near(hidden, down_sides, output_far, True))
        unit_sides = [(own_units, 0, half), (other_units, 0, half)]
        grads_far = self.scatter_far(act, unit_sides)
        grad_tokens = self.scatter_end(*self.scatter_near(act, unit_sides, grads_far, False, [down_back]))
        return (output, grad_tokens, grad_gate, grad_up, grad_down)


class Plain:
    def units(self, weight):
        own = lax.all_to_all(weight, "out", split_axis=0, concat_axis=1, tiled=True)
        return lax.all_gather(own, "wt", axis=0, tiled=True)

    def unit_sums(self, grad):
        own = lax.psum_scatter(grad.astype(BF16), "wt", scatter_dimension=0, tiled=True)
        return lax.all_to_all(own, "out", split_axis=1, concat_axis=0, tiled=True).astype(F32)

    def gather(self, array):
        array = lax.all_gather(lax.all_gather(array, "inp", axis=1, tiled=True), "out", axis=2, tiled=True)
        return array.reshape(-1, array.shape[2])

    def scatter(self, partial, batches):
        partial = partial.astype(BF16).reshape(batches, -1, partial.shape[1])
        partial = lax.psum_scatter(partial, "out", scatter_dimension=2, tiled=True)
        return lax.psum_scatter(partial, "inp", scatter_dimension=1, tiled=True)

    def layer(self, tokens, gate_weight, up_weight, down_weight, cotangent):
        gate, up, down = self.units(gate_weight.T), self.units(up_weight.T), self.units(down_weight)
        rows_in, rows_cot = self.gather(tokens), self.gather(cotangent)
        gate_sum = matmul(rows_in, gate, (1, 1))
        up_sum = matmul(rows_in, up, (1, 1))
        silu_g, hidden, rest = gated(gate_sum, up_sum)
        hidden = hidden.astype(BF16)
        grad_down = self.unit_sums(matmul(hidden, rows_cot, (0, 0)))
        back_sum = matmul(rows_cot, down, (1, 1))
        gate_act, up_act = (back_sum * rest).astype(BF16), (back_sum * silu_g).astype(BF16)
        grad_gate = self.unit_sums(matmul(gate_act, rows_in, (0, 0))).T
        grad_up = self.unit_sums(matmul(up_act, rows_in, (0, 0))).T
        output = self.scatter(matmul(hidden, down, (1, 0)), tokens.shape[0])
        partial = matmul(gate_act, gate, (1, 0)) + matmul(up_act, up, (1, 0))
        grad_tokens = self.scatter(partial, tokens.shape[0])
        return (output, grad_tokens, grad_gate, grad_up, grad_down)


def solution(mesh):
    square = mesh.shape["inp"] == 4 and mesh.shape["out"] == 2 and mesh.shape["wt"] > 2

    def on_device(tokens, *others):
        places = Square(mesh.shape["wt"]) if square and tokens.shape[0] == 2 else Plain()
        return places.layer(tokens, *others)

    rows_spec = P(None, ("inp", "wt"), "out")
    in_spec = P("out", ("wt", "inp"))
    down_spec = P(("wt", "inp"), "out")
    return jax.shard_map(
        on_device,
        mesh=mesh,
        in_specs=(rows_spec, in_spec, in_spec, down_spec, rows_spec),
        out_specs=(rows_spec, rows_spec, in_spec, in_spec, down_spec),
        check_vma=False,
    )
```

time: 310 us -> 413 us (1.33)
  waiting for transfers between devices: 138 us -> 205 us
  matrix products: 44.5 us -> 0 us
  local copies, waits for them, and re-layouts: 20.3 us -> 57.3 us
  Pallas kernels: 59.1 us -> 81.8 us
  starting transfers between devices: 27.9 us -> 38.4 us
  other arithmetic: 5.32 us -> 14.6 us
    ppermute x0 -> x6, waiting for transfers between devices: none -> 59.2 us  [the longest x4 44.5 us: shift(): lax.ppermute(array, 'wt', [(i, i + by) for i in range(many) if 0 <= i + b...]
    dot_general x16 -> x0, matrix products: 44.5 us -> none  [matmul(): lax.dot_general(a, b, ((contract[:1], contract[1:]), ((), ())), preferred...]
    unnamed x78 -> x138, local copies, waits for them, and re-layouts: 17.7 us -> 56.1 us
    ppermute x12 -> x10, waiting for transfers between devices: 59.3 us -> 96.8 us  [other(): return lax.ppermute(array, 'out', [(0, 1), (1, 0)])]
    pallas_call x5 -> x18, Pallas kernels: 59.1 us -> 81.8 us  [call(): pl.pallas_call(body, out_shape=list(outs), in_specs=[*specs, *[pl.BlockSp...]
    ppermute x8, waiting for transfers between devices: 67 us -> 48.3 us  [chip(): return lax.ppermute(array, 'inp', [(at, at ^ 2) for at in range(4)])]
    ppermute x0 -> x6, starting transfers between devices: none -> 12.6 us  [the longest x4 10.6 us: shift(): lax.ppermute(array, 'wt', [(i, i + by) for i in range(many) if 0 <= i + b...]
    all_gather x3 -> x2, waiting for transfers between devices: 11.4 us -> 0.01 us  [gather_units(): return lax.all_gather(array, 'wt', axis=0, tiled=True)]
  transfers between devices with their start and end apart: 44 -> 46, of which waited for: 16 -> 14; matrix products, arithmetic and copies ran while one was open for 16% -> 3% of each run, Pallas kernels for 19% -> 17%
where the time goes in v1:
time: 413 us; the launch traced here: 412 us
  waiting for transfers between devices  205 us (50%)
  Pallas kernels  81.8 us (20%)
  local copies, waits for them, and re-layouts  57.3 us (14%)
  starting transfers between devices  38.4 us (9%)
  other arithmetic  14.6 us (4%)
  between operations  14.4 us (3%)
    ppermute x10, waiting for transfers between devices, other(): return lax.ppermute(array, 'out', [(0, 1), (1, 0)])  96.8 us
    pallas_call x18, Pallas kernels, call(): pl.pallas_call(body, out_shape=list(outs), in_specs=[*specs, *[pl.BlockSp...  81.8 us
    unnamed x138, local copies, waits for them, and re-layouts  56.1 us
    ppermute x8, waiting for transfers between devices, chip(): return lax.ppermute(array, 'inp', [(at, at ^ 2) for at in range(4)])  48.3 us
    ppermute x4, waiting for transfers between devices, shift(): lax.ppermute(array, 'wt', [(i, i + by) for i in range(many) if 0 <= i + b...  44.5 us
    ppermute x1, waiting for transfers between devices, line(): lax.ppermute(beyond[-1], 'wt', [(i, i - 1) for i in range(1, many - by +...  14.7 us
    ppermute x10, starting transfers between devices, other(): return lax.ppermute(array, 'out', [(0, 1), (1, 0)])  11.4 us
    ppermute x8, starting transfers between devices, chip(): return lax.ppermute(array, 'inp', [(at, at ^ 2) for at in range(4)])  11 us
  transfers between devices with their start and end apart: 46, of which 14 were waited for; matrix products, arithmetic and copies ran while one was open for 3% of the time, Pallas kernels for 17%

profile of v1, /device:TPU:0, one launch (start us, length us, event | category | flops | bytes accessed | tf_op | source)
XLA Modules:
  0.0 411.7 jit_solution(17466283334730337022)
XLA Ops:
  7.2 3.0 collective-permute-start.1
  15.0 11.9 %collective-permute-done.9.refs_0_ = bf16[256,1024]{1,0:T(8,128)(2,1)S(1)} collective-permute-done((bf16[256,1024]{1,0:T(8,128)(2,1)S(1)}, bf16[256,1024]{1,0:T(8,128)(2,1)S(1)}, u32[]{:S(2)}, u32[]{:S(2)}) %collective-permute-start.9) | collective-permute-done | bytes 524320 | tf_op jit(solution)/shard_map/ppermute | solution.py:216
  26.8 6.8 %collective-permute-done.1.refs_1_.refs_2_ = bf16[512,1024]{1,0:T(8,128)(2,1)S(1)} collective-permute-done((bf16[512,1024]{1,0:T(8,128)(2,1)}, bf16[512,1024]{1,0:T(8,128)(2,1)S(1)}, u32[]{:S(2)}, u32[]{:S(2)}) %collective-permute-start.1) | collective-permute-done | bytes 1048608 | tf_op jit(solution)/shard_map/ppermute | solution.py:213
  35.3 1.8 collective-permute-start
  37.4 1.7 collective-permute-start.26
  39.2 1.6 collective-permute-start.10
  40.8 20.9 %collective-permute-done.refs_1_ = bf16[512,1024]{1,0:T(8,128)(2,1)S(1)} collective-permute-done((bf16[512,1024]{1,0:T(8,128)(2,1)}, bf16[512,1024]{1,0:T(8,128)(2,1)S(1)}, u32[]{:S(2)}, u32[]{:S(2)}) %collective-permute-start) | collective-permute-done | bytes 1048608 | tf_op jit(solution)/shard_map/ppermute | solution.py:216
  61.7 26.3 %collective-permute-done.10.refs_1_ = bf16[128,1024]{1,0:T(8,128)(2,1)S(1)} collective-permute-done((bf16[128,1024]{1,0:T(8,128)(2,1)S(1)}, bf16[128,1024]{1,0:T(8,128)(2,1)S(1)}, u32[]{:S(2)}, u32[]{:S(2)}) %collective-permute-start.10) | collective-permute-done | bytes 262176 | tf_op jit(solution)/shard_map/ppermute | solution.py:216
  92.6 9.8 %collective-permute-done.2.refs_3_ = bf16[256,1024]{1,0:T(8,128)(2,1)S(1)} collective-permute-done((bf16[256,1024]{1,0:T(8,128)(2,1)S(1)}, bf16[256,1024]{1,0:T(8,128)(2,1)S(1)}, u32[]{:S(2)}, u32[]{:S(2)}) %collective-permute-start.2) | collective-permute-done | bytes 524320 | tf_op jit(solution)/shard_map/ppermute | solution.py:216
  103.2 23.2 %collective-permute-done.3.refs_4_ = bf16[256,1024]{1,0:T(8,128)(2,1)} collective-permute-done((bf16[256,1024]{1,0:T(8,128)(2,1)S(1)}, bf16[256,1024]{1,0:T(8,128)(2,1)}, u32[]{:S(2)}, u32[]{:S(2)}) %collective-permute-start.3) | collective-permute-done | bytes 524320 | tf_op jit(solution)/shard_map/ppermute | solution.py:213
  135.5 1.6 copy-done.23
  142.8 15.4 %shard_map.95 = (bf16[2048,512]{1,0:T(8,128)(2,1)S(1)}, bf16[512,2048]{1,0:T(8,128)(2,1)S(1)}, bf16[2048,512]{1,0:T(8,128)(2,1)S(1)}, bf16[2048,512]{1,0:T(8,128)(2,1)S(1)}) custom-call(bf16[512,1024]{1,0:T(8,128)(2,1)} %bitcast.refs_0_, bf16[512,1024]{1,0:T(8,128)(2,1)S(1)} %copy-done.45, bf16[512,1024]{1,0:T(8,128)(2,1)S(1)} %collective-permute-done.1.refs_1_.refs_2_, ...), custom_call_target="tpu_custom_call" | custom-call | flops 8589934592 | bytes 20971520 | tf_op jit(solution)/shard_map/pallas_call | solution.py:38
  162.2 10.8 %shard_map.104 = bf16[512,2048]{1,0:T(8,128)(2,1)} custom-call(bf16[512,1024]{1,0:T(8,128)(2,1)} %bitcast.4.refs_0_, bf16[512,1024]{1,0:T(8,128)(2,1)} %collective-permute-done.25.refs_1_, bf16[512,1024]{1,0:T(8,128)(2,1)} %collective-permute-done.26.refs_2_, bf16[512,1024]{1,0:T(8,128)(2,1)} %collective-permute-done.27.refs_3_, ...), custom_call_target="tpu_custom_call" | custom-call | flops 4294967296 | bytes 12582912 | tf_op jit(solution)/shard_map/pallas_call | solution.py:38
  174.0 4.5 %collective-permute-start.12 = (bf16[128,2048]{1,0:T(8,128)(2,1)S(1)}, bf16[128,2048]{1,0:T(8,128)(2,1)S(1)}, u32[]{:S(2)}, u32[]{:S(2)}) collective-permute-start(bf16[128,2048]{1,0:T(8,128)(2,1)S(1)} %copy-done.22), channel_id=1, source_target_pairs={{0,4},{2,6},{1,5},{3,7},{8,12},{10,14},{9,13},{11,15},{16,20},{18,... | collective-permute-start | bytes 1572872 | tf_op jit(solution)/shard_map/ppermute | solution.py:240
  179.9 3.5 collective-permute-start.11
  184.7 17.2 %collective-permute-done.12.refs_3_ = bf16[128,2048]{1,0:T(8,128)(2,1)S(1)} collective-permute-done((bf16[128,2048]{1,0:T(8,128)(2,1)S(1)}, bf16[128,2048]{1,0:T(8,128)(2,1)S(1)}, u32[]{:S(2)}, u32[]{:S(2)}) %collective-permute-start.12) | collective-permute-done | bytes 524320 | tf_op jit(solution)/shard_map/ppermute | solution.py:240
  202.6 27.3 %collective-permute-done.15.refs_6_ = bf16[128,2048]{1,0:T(8,128)(2,1)S(1)} collective-permute-done((bf16[128,2048]{1,0:T(8,128)(2,1)S(1)}, bf16[128,2048]{1,0:T(8,128)(2,1)S(1)}, u32[]{:S(2)}, u32[]{:S(2)}) %collective-permute-start.15) | collective-permute-done | bytes 524320 | tf_op jit(solution)/shard_map/ppermute | solution.py:240
  234.4 14.7 %collective-permute-done.16.refs_7_ = bf16[128,2048]{1,0:T(8,128)(2,1)} collective-permute-done((bf16[128,2048]{1,0:T(8,128)(2,1)S(1)}, bf16[128,2048]{1,0:T(8,128)(2,1)}, u32[]{:S(2)}, u32[]{:S(2)}) %collective-permute-start.16) | collective-permute-done | bytes 524320 | tf_op jit(solution)/shard_map/ppermute | solution.py:246
  253.3 1.6 shard_map.96.refs_1_.refs_2_.refs_8_
  256.0 2.3 shard_map.98
  258.5 14.4 %shard_map.101 = (bf16[2048,1024]{1,0:T(8,128)(2,1)}, bf16[1024,2048]{1,0:T(8,128)(2,1)}) custom-call(bf16[512,1024]{1,0:T(8,128)(2,1)} %bitcast.4.refs_0_, bf16[512,1024]{1,0:T(8,128)(2,1)} %collective-permute-done.25.refs_1_, bf16[512,1024]{1,0:T(8,128)(2,1)} %collective-permute-done.26.refs_2_, bf16[512,1024]{1,0:T(8,128)(2,1)} %collective-permute-done.27.refs_3_, ...), custom_call_target="tpu_custom_call" | custom-call | flops 4294967296 | bytes 23068672 | tf_op jit(solution)/shard_map/pallas_call | solution.py:38
  273.0 2.2 copy-done.48
  275.2 6.5 %shard_map.108 = bf16[1024,1024]{1,0:T(8,128)(2,1)S(1)} custom-call(bf16[512,1024]{1,0:T(8,128)(2,1)} %bitcast.refs_0_, bf16[512,1024]{1,0:T(8,128)(2,1)S(1)} %copy-done.46, bf16[512,1024]{1,0:T(8,128)(2,1)S(1)} %copy-done.12, bf16[256,1024]{1,0:T(8,128)(2,1)S(1)} %copy-done.60, bf16[256,1024]{1,0:T(8,128)(2,1)} %collective-permute-done.3.refs_4_, ...), custom_call_target="tpu_custom_call" | custom-call | flops 4294967296 | bytes 14680064 | tf_op jit(solution)/shard_map/pallas_call | solution.py:38
  285.9 2.2 copy-done.49
  292.7 6.7 %shard_map.107 = bf16[1024,1024]{1,0:T(8,128)(2,1)S(1)} custom-call(bf16[512,1024]{1,0:T(8,128)(2,1)} %bitcast.refs_0_, bf16[512,1024]{1,0:T(8,128)(2,1)S(1)} %copy-done.47, bf16[512,1024]{1,0:T(8,128)(2,1)S(1)} %copy-done.13, bf16[256,1024]{1,0:T(8,128)(2,1)S(1)} %copy-done.61, bf16[256,1024]{1,0:T(8,128)(2,1)} %collective-permute-done.3.refs_4_, ...), custom_call_target="tpu_custom_call" | custom-call | flops 4294967296 | bytes 14680064 | tf_op jit(solution)/shard_map/pallas_call | solution.py:38
  301.8 2.2 copy-done
  304.0 1.6 copy-done.9
  305.6 2.5 shard_map.102.refs_3_
  308.2 2.2 shard_map.99.refs_6_
  311.5 1.6 collective-permute-start.23
  313.1 1.9 slice_convert_fusion
  316.4 2.2 copy-done.1
  318.5 1.6 copy-done.10
  320.2 1.6 copy-done.24
  321.8 3.9 shard_map.103
  327.0 2.7 shard_map.105.refs_6_
  330.3 4.2 %shard_map.100 = (bf16[512,1024]{1,0:T(8,128)(2,1)S(1)}, bf16[512,1024]{1,0:T(8,128)(2,1)S(1)}, bf16[512,1024]{1,0:T(8,128)(2,1)S(1)}) custom-call(bf16[2048,512]{1,0:T(8,128)(2,1)S(1)} %copy-done.6, bf16[512,2048]{1,0:T(8,128)(2,1)S(1)} %shard_map.96.refs_1_.refs_2_.refs_8_, bf16[512,2048]{1,0:T(8,128)(2,1)S(1)} %shard_map.96.refs_1_.refs_2_.refs_8_, ...), custom_call_target="tpu_custom_call" | custom-call | flops 1610612736 | bytes 12582912 | tf_op jit(solution)/shard_map/pallas_call | solution.py:38
  334.5 2.7 add_convert_fusion.3
  337.2 3.5 collective-permute-done.21
  343.0 4.1 %shard_map.106 = (bf16[512,1024]{1,0:T(8,128)(2,1)S(1)}, bf16[512,1024]{1,0:T(8,128)(2,1)}, bf16[512,1024]{1,0:T(8,128)(2,1)S(1)}) custom-call(bf16[2048,1024]{1,0:T(8,128)(2,1)S(1)} %copy-done.2, bf16[1024,1024]{1,0:T(8,128)(2,1)S(1)} %copy-done.25, bf16[1024,1024]{1,0:T(8,128)(2,1)S(1)} %copy-done.10, ...), custom_call_target="tpu_custom_call" | custom-call | flops 3221225472 | bytes 14680064 | tf_op jit(solution)/shard_map/pallas_call | solution.py:38
  347.2 1.6 collective-permute-start.37
  348.8 7.0 %collective-permute-done.38 = bf16[512,1024]{1,0:T(8,128)(2,1)S(1)} collective-permute-done((bf16[512,1024]{1,0:T(8,128)(2,1)S(1)}, bf16[512,1024]{1,0:T(8,128)(2,1)S(1)}, u32[]{:S(2)}, u32[]{:S(2)}) %collective-permute-start.38) | collective-permute-done | bytes 1048608 | tf_op jit(solution)/shard_map/ppermute | solution.py:213
  359.2 7.8 %collective-permute-done.24 = bf16[512,1024]{1,0:T(8,128)(2,1)} collective-permute-done((bf16[512,1024]{1,0:T(8,128)(2,1)}, bf16[512,1024]{1,0:T(8,128)(2,1)}, u32[]{:S(2)}, u32[]{:S(2)}) %collective-permute-start.24) | collective-permute-done | bytes 1048608 | tf_op jit(solution)/shard_map/ppermute | solution.py:216
  367.0 11.4 %collective-permute-done.22 = bf16[512,1024]{1,0:T(8,128)(2,1)} collective-permute-done((bf16[512,1024]{1,0:T(8,128)(2,1)}, bf16[512,1024]{1,0:T(8,128)(2,1)}, u32[]{:S(2)}, u32[]{:S(2)}) %collective-permute-start.22) | collective-permute-done | bytes 1048608 | tf_op jit(solution)/shard_map/ppermute | solution.py:213
  378.4 3.2 add_convert_fusion.2
  382.7 16.7 %collective-permute-done.40.refs_2_ = bf16[256,1024]{1,0:T(8,128)(2,1)S(1)} collective-permute-done((bf16[256,1024]{1,0:T(8,128)(2,1)}, bf16[256,1024]{1,0:T(8,128)(2,1)S(1)}, u32[]{:S(2)}, u32[]{:S(2)}) %collective-permute-start.40) | collective-permute-done | bytes 524320 | tf_op jit(solution)/shard_map/ppermute | solution.py:216
  400.4 1.6 shard_map.109
  402.0 3.1 add_convert_fusion
  (217 shorter events, 68.7 us)
Async XLA Ops:
  7.2 122.9 %all-gather.5.cloned.1.call-start = ((), (), s32[]{:S(2)}) async-start(), calls=%async_computation.4 | async-start | bytes 2621440 | tf_op jit(solution)/shard_map/all_gather | solution.py:309
  7.2 26.4 %collective-permute-start.1 = (bf16[512,1024]{1,0:T(8,128)(2,1)}, bf16[512,1024]{1,0:T(8,128)(2,1)S(1)}, u32[]{:S(2)}, u32[]{:S(2)}) collective-permute-start(bf16[512,1024]{1,0:T(8,128)(2,1)} %bitcast.refs_0_), channel_id=1, source_target_pairs={{0,16},{8,24},{16,0},{24,8},{1,17},{9,25},{17,1},{25,9},{2,18},{10... | collective-permute-start | bytes 3145736 | tf_op jit(solution)/shard_map/ppermute | solution.py:213
  13.4 13.4 %collective-permute-start.9 = (bf16[256,1024]{1,0:T(8,128)(2,1)S(1)}, bf16[256,1024]{1,0:T(8,128)(2,1)S(1)}, u32[]{:S(2)}, u32[]{:S(2)}) collective-permute-start(bf16[256,1024]{1,0:T(8,128)(2,1)S(1)} %get-tuple-element.28), channel_id=1, source_target_pairs={{0,1},{1,0},{2,3},{3,2},{4,5},{5,4},{6,7},{7,6},{8,9},{9,8},{10,11... | collective-permute-start | bytes 1572872 | tf_op jit(solution)/shard_map/ppermute | solution.py:216
  33.6 99.9 %copy-start.11 = (bf16[512,1024]{1,0:T(8,128)(2,1)}, bf16[512,1024]{1,0:T(8,128)(2,1)S(1)}, u32[]{:S(2)}) copy-start(bf16[512,1024]{1,0:T(8,128)(2,1)S(1)} %collective-permute-done.1.refs_1_.refs_2_) | copy-start | bytes 3145732
  34.5 99.0 %all-gather.3.cloned.1.call-start = ((), (), s32[]{:S(2)}) async-start(), calls=%async_computation.3 | async-start | bytes 2621440 | tf_op jit(solution)/shard_map/all_gather | solution.py:309
  35.2 277.8 %reduce-scatter.4.cloned.1.call-start = ((), (), s32[]{:S(2)}) async-start(), calls=%async_computation.5 | async-start | bytes 2621440 | tf_op jit(solution)/shard_map/reduce_scatter | solution.py:312
  35.3 26.4 %collective-permute-start = (bf16[512,1024]{1,0:T(8,128)(2,1)}, bf16[512,1024]{1,0:T(8,128)(2,1)S(1)}, u32[]{:S(2)}, u32[]{:S(2)}) collective-permute-start(bf16[512,1024]{1,0:T(8,128)(2,1)} %bitcast.refs_0_), channel_id=1, source_target_pairs={{0,1},{1,0},{2,3},{3,2},{4,5},{5,4},{6,7},{7,6},{8,9},{9,8},{10,11... | collective-permute-start | bytes 3145736 | tf_op jit(solution)/shard_map/ppermute | solution.py:216
  37.1 50.9 %collective-permute-start.4 = (bf16[512,1024]{1,0:T(8,128)(2,1)}, bf16[512,1024]{1,0:T(8,128)(2,1)}, u32[]{:S(2)}, u32[]{:S(2)}) collective-permute-start(bf16[512,1024]{1,0:T(8,128)(2,1)} %bitcast.refs_0_), channel_id=1, source_target_pairs={{0,8},{8,0},{16,24},{24,16},{1,9},{9,1},{17,25},{25,17},{2,10},{10... | collective-permute-start | bytes 3145736 | tf_op jit(solution)/shard_map/ppermute | solution.py:210
  37.1 52.4 %collective-permute-start.25 = (bf16[512,1024]{1,0:T(8,128)(2,1)}, bf16[512,1024]{1,0:T(8,128)(2,1)}, u32[]{:S(2)}, u32[]{:S(2)}) collective-permute-start(bf16[512,1024]{1,0:T(8,128)(2,1)} %bitcast.4.refs_0_), channel_id=1, source_target_pairs={{0,1},{1,0},{2,3},{3,2},{4,5},{5,4},{6,7},{7,6},{8,9},{9,8},{10,11... | collective-permute-start | bytes 3145736 | tf_op jit(solution)/shard_map/ppermute | solution.py:216
  37.4 54.6 %collective-permute-start.26 = (bf16[512,1024]{1,0:T(8,128)(2,1)}, bf16[512,1024]{1,0:T(8,128)(2,1)}, u32[]{:S(2)}, u32[]{:S(2)}) collective-permute-start(bf16[512,1024]{1,0:T(8,128)(2,1)} %bitcast.4.refs_0_), channel_id=1, source_target_pairs={{0,16},{8,24},{16,0},{24,8},{1,17},{9,25},{17,1},{25,9},{2,18},{10... | collective-permute-start | bytes 3145736 | tf_op jit(solution)/shard_map/ppermute | solution.py:213
  39.2 48.8 %collective-permute-start.10 = (bf16[128,1024]{1,0:T(8,128)(2,1)S(1)}, bf16[128,1024]{1,0:T(8,128)(2,1)S(1)}, u32[]{:S(2)}, u32[]{:S(2)}) collective-permute-start(bf16[128,1024]{1,0:T(8,128)(2,1)S(1)} %get-tuple-element.53), channel_id=1, source_target_pairs={{0,1},{1,0},{2,3},{3,2},{4,5},{5,4},{6,7},{7,6},{8,9},{9,8},{10,11... | collective-permute-start | bytes 786440 | tf_op jit(solution)/shard_map/ppermute | solution.py:216
  61.7 64.6 %collective-permute-start.5 = (bf16[512,1024]{1,0:T(8,128)(2,1)S(1)}, bf16[512,1024]{1,0:T(8,128)(2,1)S(1)}, u32[]{:S(2)}, u32[]{:S(2)}) collective-permute-start(bf16[512,1024]{1,0:T(8,128)(2,1)S(1)} %collective-permute-done.refs_1_), channel_id=1, source_target_pairs={{0,8},{8,0},{16,24},{24,16},{1,9},{9,1},{17,25},{25,17},{2,10},{10... | collective-permute-start | bytes 3145736 | tf_op jit(solution)/shard_map/ppermute | solution.py:210
  88.0 42.1 %copy-start.42 = (bf16[128,1024]{1,0:T(8,128)(2,1)}, bf16[128,1024]{1,0:T(8,128)(2,1)S(1)}, u32[]{:S(2)}) copy-start(bf16[128,1024]{1,0:T(8,128)(2,1)S(1)} %collective-permute-done.10.refs_1_) | copy-start | bytes 786436
  88.0 39.8 %collective-permute-start.6 = (bf16[512,1024]{1,0:T(8,128)(2,1)S(1)}, bf16[512,1024]{1,0:T(8,128)(2,1)S(1)}, u32[]{:S(2)}, u32[]{:S(2)}) collective-permute-start(bf16[512,1024]{1,0:T(8,128)(2,1)S(1)} %collective-permute-done.1.refs_1_.refs_2_), channel_id=1, source_target_pairs={{0,8},{8,0},{16,24},{24,16},{1,9},{9,1},{17,25},{25,17},{2,10},{10... | collective-permute-start | bytes 3145736 | tf_op jit(solution)/shard_map/ppermute | solution.py:210
  88.0 14.3 %collective-permute-start.2 = (bf16[256,1024]{1,0:T(8,128)(2,1)S(1)}, bf16[256,1024]{1,0:T(8,128)(2,1)S(1)}, u32[]{:S(2)}, u32[]{:S(2)}) collective-permute-start(bf16[256,1024]{1,0:T(8,128)(2,1)S(1)} %slice.24), channel_id=1, source_target_pairs={{0,1},{1,0},{2,3},{3,2},{4,5},{5,4},{6,7},{7,6},{8,9},{9,8},{10,11... | collective-permute-start | bytes 1572872 | tf_op jit(solution)/shard_map/ppermute | solution.py:216
  89.5 40.6 %collective-permute-start.27 = (bf16[512,1024]{1,0:T(8,128)(2,1)}, bf16[512,1024]{1,0:T(8,128)(2,1)}, u32[]{:S(2)}, u32[]{:S(2)}) collective-permute-start(bf16[512,1024]{1,0:T(8,128)(2,1)} %collective-permute-done.25.refs_1_), channel_id=1, source_target_pairs={{0,16},{8,24},{16,0},{24,8},{1,17},{9,25},{17,1},{25,9},{2,18},{10... | collective-permute-start | bytes 3145736 | tf_op jit(solution)/shard_map/ppermute | solution.py:213
  92.0 34.3 %collective-permute-start.3 = (bf16[256,1024]{1,0:T(8,128)(2,1)S(1)}, bf16[256,1024]{1,0:T(8,128)(2,1)}, u32[]{:S(2)}, u32[]{:S(2)}) collective-permute-start(bf16[256,1024]{1,0:T(8,128)(2,1)S(1)} %slice.25), channel_id=1, source_target_pairs={{0,16},{8,24},{16,0},{24,8},{1,17},{9,25},{17,1},{25,9},{2,18},{10... | collective-permute-start | bytes 1572872 | tf_op jit(solution)/shard_map/ppermute | solution.py:213
  102.4 26.4 %collective-permute-start.7 = (bf16[256,1024]{1,0:T(8,128)(2,1)S(1)}, bf16[256,1024]{1,0:T(8,128)(2,1)S(1)}, u32[]{:S(2)}, u32[]{:S(2)}) collective-permute-start(bf16[256,1024]{1,0:T(8,128)(2,1)S(1)} %collective-permute-done.2.refs_3_), channel_id=1, source_target_pairs={{0,8},{8,0},{16,24},{24,16},{1,9},{9,1},{17,25},{25,17},{2,10},{10... | collective-permute-start | bytes 1572872 | tf_op jit(solution)/shard_map/ppermute | solution.py:210
  126.3 7.2 %collective-permute-start.8 = (bf16[256,1024]{1,0:T(8,128)(2,1)}, bf16[256,1024]{1,0:T(8,128)(2,1)}, u32[]{:S(2)}, u32[]{:S(2)}) collective-permute-start(bf16[256,1024]{1,0:T(8,128)(2,1)} %collective-permute-done.3.refs_4_), channel_id=1, source_target_pairs={{0,8},{8,0},{16,24},{24,16},{1,9},{9,1},{17,25},{25,17},{2,10},{10... | collective-permute-start | bytes 1572872 | tf_op jit(solution)/shard_map/ppermute | solution.py:210
  127.3 34.9 %collective-permute-start.28 = (bf16[512,1024]{1,0:T(8,128)(2,1)}, bf16[512,1024]{1,0:T(8,128)(2,1)}, u32[]{:S(2)}, u32[]{:S(2)}) collective-permute-start(bf16[512,1024]{1,0:T(8,128)(2,1)} %bitcast.4.refs_0_), channel_id=1, source_target_pairs={{0,8},{8,0},{16,24},{24,16},{1,9},{9,1},{17,25},{25,17},{2,10},{10... | collective-permute-start | bytes 3145736 | tf_op jit(solution)/shard_map/ppermute | solution.py:210
  128.8 33.4 %collective-permute-start.29 = (bf16[512,1024]{1,0:T(8,128)(2,1)}, bf16[512,1024]{1,0:T(8,128)(2,1)}, u32[]{:S(2)}, u32[]{:S(2)}) collective-permute-start(bf16[512,1024]{1,0:T(8,128)(2,1)} %collective-permute-done.25.refs_1_), channel_id=1, source_target_pairs={{0,8},{8,0},{16,24},{24,16},{1,9},{9,1},{17,25},{25,17},{2,10},{10... | collective-permute-start | bytes 3145736 | tf_op jit(solution)/shard_map/ppermute | solution.py:210
  129.6 32.6 %collective-permute-start.30 = (bf16[512,1024]{1,0:T(8,128)(2,1)}, bf16[512,1024]{1,0:T(8,128)(2,1)}, u32[]{:S(2)}, u32[]{:S(2)}) collective-permute-start(bf16[512,1024]{1,0:T(8,128)(2,1)} %collective-permute-done.26.refs_2_), channel_id=1, source_target_pairs={{0,8},{8,0},{16,24},{24,16},{1,9},{9,1},{17,25},{25,17},{2,10},{10... | collective-permute-start | bytes 3145736 | tf_op jit(solution)/shard_map/ppermute | solution.py:210
  130.1 32.1 %collective-permute-start.31 = (bf16[512,1024]{1,0:T(8,128)(2,1)}, bf16[512,1024]{1,0:T(8,128)(2,1)}, u32[]{:S(2)}, u32[]{:S(2)}) collective-permute-start(bf16[512,1024]{1,0:T(8,128)(2,1)} %collective-permute-done.27.refs_3_), channel_id=1, source_target_pairs={{0,8},{8,0},{16,24},{24,16},{1,9},{9,1},{17,25},{25,17},{2,10},{10... | collective-permute-start | bytes 3145736 | tf_op jit(solution)/shard_map/ppermute | solution.py:210
  173.0 185.6 %reduce-scatter.8.cloned.1.call-start = ((), (), s32[]{:S(2)}) async-start(), calls=%async_computation.7 | async-start | bytes 2621440 | tf_op jit(solution)/shard_map/reduce_scatter | solution.py:312
  174.0 27.8 %collective-permute-start.12 = (bf16[128,2048]{1,0:T(8,128)(2,1)S(1)}, bf16[128,2048]{1,0:T(8,128)(2,1)S(1)}, u32[]{:S(2)}, u32[]{:S(2)}) collective-permute-start(bf16[128,2048]{1,0:T(8,128)(2,1)S(1)} %copy-done.22), channel_id=1, source_target_pairs={{0,4},{2,6},{1,5},{3,7},{8,12},{10,14},{9,13},{11,15},{16,20},{18,... | collective-permute-start | bytes 1572872 | tf_op jit(solution)/shard_map/ppermute | solution.py:240
  178.6 51.3 %collective-permute-start.15 = (bf16[128,2048]{1,0:T(8,128)(2,1)S(1)}, bf16[128,2048]{1,0:T(8,128)(2,1)S(1)}, u32[]{:S(2)}, u32[]{:S(2)}) collective-permute-start(bf16[128,2048]{1,0:T(8,128)(2,1)S(1)} %copy-done.22), channel_id=1, source_target_pairs={{4,0},{6,2},{5,1},{7,3},{12,8},{14,10},{13,9},{15,11},{20,16},{22,... | collective-permute-start | bytes 1572872 | tf_op jit(solution)/shard_map/ppermute | solution.py:240
  179.9 52.2 %collective-permute-start.11 = (bf16[128,2048]{1,0:T(8,128)(2,1)S(1)}, bf16[128,2048]{1,0:T(8,128)(2,1)S(1)}, u32[]{:S(2)}, u32[]{:S(2)}) collective-permute-start(bf16[128,2048]{1,0:T(8,128)(2,1)S(1)} %copy-done.22), channel_id=1, source_target_pairs={{0,2},{2,4},{4,6},{1,3},{3,5},{5,7},{8,10},{10,12},{12,14},{9,11},... | collective-permute-start | bytes 1572872 | tf_op jit(solution)/shard_map/ppermute | solution.py:240
  183.4 49.4 %collective-permute-start.14 = (bf16[128,2048]{1,0:T(8,128)(2,1)S(1)}, bf16[128,2048]{1,0:T(8,128)(2,1)S(1)}, u32[]{:S(2)}, u32[]{:S(2)}) collective-permute-start(bf16[128,2048]{1,0:T(8,128)(2,1)S(1)} %copy-done.22), channel_id=1, source_target_pairs={{2,0},{4,2},{6,4},{3,1},{5,3},{7,5},{10,8},{12,10},{14,12},{11,9},... | collective-permute-start | bytes 1572872 | tf_op jit(solution)/shard_map/ppermute | solution.py:240
  201.9 31.8 %collective-permute-start.13 = (bf16[128,2048]{1,0:T(8,128)(2,1)S(1)}, bf16[128,2048]{1,0:T(8,128)(2,1)S(1)}, u32[]{:S(2)}, u32[]{:S(2)}) collective-permute-start(bf16[128,2048]{1,0:T(8,128)(2,1)S(1)} %collective-permute-done.12.refs_3_), channel_id=1, source_target_pairs={{4,6},{5,7},{12,14},{13,15},{20,22},{21,23},{28,30},{29,31}} | collective-permute-start | bytes 1572872 | tf_op jit(solution)/shard_map/ppermute | solution.py:245
  229.9 19.2 %collective-permute-start.16 = (bf16[128,2048]{1,0:T(8,128)(2,1)S(1)}, bf16[128,2048]{1,0:T(8,128)(2,1)}, u32[]{:S(2)}, u32[]{:S(2)}) collective-permute-start(bf16[128,2048]{1,0:T(8,128)(2,1)S(1)} %collective-permute-done.15.refs_6_), channel_id=1, source_target_pairs={{2,0},{3,1},{10,8},{11,9},{18,16},{19,17},{26,24},{27,25}} | collective-permute-start | bytes 1572872 | tf_op jit(solution)/shard_map/ppermute | solution.py:246
  283.0 99.7 %reduce-scatter.6.cloned.1.call-start = ((), (), s32[]{:S(2)}) async-start(), calls=%async_computation.6 | async-start | bytes 2621440 | tf_op jit(solution)/shard_map/reduce_scatter | solution.py:312
  283.2 25.0 %collective-permute-start.20 = (bf16[512,1024]{1,0:T(8,128)(2,1)S(1)}, bf16[512,1024]{1,0:T(8,128)(2,1)}, u32[]{:S(2)}, u32[]{:S(2)}) collective-permute-start(bf16[512,1024]{1,0:T(8,128)(2,1)S(1)} %shard_map.97.refs_3_.refs_11_), channel_id=1, source_target_pairs={{0,8},{8,0},{16,24},{24,16},{1,9},{9,1},{17,25},{25,17},{2,10},{10... | collective-permute-start | bytes 3145736 | tf_op jit(solution)/shard_map/ppermute | solution.py:210
  300.8 14.2 %collective-permute-start.17 = (bf16[512,1024]{1,0:T(8,128)(2,1)}, bf16[512,1024]{1,0:T(8,128)(2,1)}, u32[]{:S(2)}, u32[]{:S(2)}) collective-permute-start(bf16[512,1024]{1,0:T(8,128)(2,1)} %copy-done.28), channel_id=1, source_target_pairs={{0,8},{8,0},{16,24},{24,16},{1,9},{9,1},{17,25},{25,17},{2,10},{10... | collective-permute-start | bytes 3145736 | tf_op jit(solution)/shard_map/ppermute | solution.py:210
  301.2 24.4 %collective-permute-start.18 = (bf16[512,1024]{1,0:T(8,128)(2,1)}, bf16[512,1024]{1,0:T(8,128)(2,1)}, u32[]{:S(2)}, u32[]{:S(2)}) collective-permute-start(bf16[512,1024]{1,0:T(8,128)(2,1)} %copy-done.27), channel_id=1, source_target_pairs={{0,8},{8,0},{16,24},{24,16},{1,9},{9,1},{17,25},{25,17},{2,10},{10... | collective-permute-start | bytes 3145736 | tf_op jit(solution)/shard_map/ppermute | solution.py:210
  301.4 24.3 %collective-permute-start.19 = (bf16[512,1024]{1,0:T(8,128)(2,1)}, bf16[512,1024]{1,0:T(8,128)(2,1)}, u32[]{:S(2)}, u32[]{:S(2)}) collective-permute-start(bf16[512,1024]{1,0:T(8,128)(2,1)} %copy-done.26), channel_id=1, source_target_pairs={{0,8},{8,0},{16,24},{24,16},{1,9},{9,1},{17,25},{25,17},{2,10},{10... | collective-permute-start | bytes 3145736 | tf_op jit(solution)/shard_map/ppermute | solution.py:210
  308.1 18.2 %collective-permute-start.35 = (bf16[512,1024]{1,0:T(8,128)(2,1)}, bf16[512,1024]{1,0:T(8,128)(2,1)}, u32[]{:S(2)}, u32[]{:S(2)}) collective-permute-start(bf16[512,1024]{1,0:T(8,128)(2,1)} %shard_map.102.refs_3_), channel_id=1, source_target_pairs={{0,8},{8,0},{16,24},{24,16},{1,9},{9,1},{17,25},{25,17},{2,10},{10... | collective-permute-start | bytes 3145736 | tf_op jit(solution)/shard_map/ppermute | solution.py:210
  311.5 18.3 %collective-permute-start.23 = (bf16[256,1024]{1,0:T(8,128)(2,1)}, bf16[256,1024]{1,0:T(8,128)(2,1)}, u32[]{:S(2)}, u32[]{:S(2)}) collective-permute-start(bf16[256,1024]{1,0:T(8,128)(2,1)} %get-tuple-element.50), channel_id=1, source_target_pairs={{0,16},{8,24},{16,0},{24,8},{1,17},{9,25},{17,1},{25,9},{2,18},{10... | collective-permute-start | bytes 1572872 | tf_op jit(solution)/shard_map/ppermute | solution.py:213
  315.0 11.4 %collective-permute-start.36 = (bf16[128,1024]{1,0:T(8,128)(2,1)S(1)}, bf16[128,1024]{1,0:T(8,128)(2,1)S(1)}, u32[]{:S(2)}, u32[]{:S(2)}) collective-permute-start(bf16[128,1024]{1,0:T(8,128)(2,1)S(1)} %get-tuple-element.52), channel_id=1, source_target_pairs={{0,1},{1,0},{2,3},{3,2},{4,5},{5,4},{6,7},{7,6},{8,9},{9,8},{10,11... | collective-permute-start | bytes 786440 | tf_op jit(solution)/shard_map/ppermute | solution.py:216
  325.6 16.9 %collective-permute-start.32 = (bf16[512,1024]{1,0:T(8,128)(2,1)S(1)}, bf16[512,1024]{1,0:T(8,128)(2,1)S(1)}, u32[]{:S(2)}, u32[]{:S(2)}) collective-permute-start(bf16[512,1024]{1,0:T(8,128)(2,1)S(1)} %get-tuple-element.39), channel_id=1, source_target_pairs={{0,8},{8,0},{16,24},{24,16},{1,9},{9,1},{17,25},{25,17},{2,10},{10... | collective-permute-start | bytes 3145736 | tf_op jit(solution)/shard_map/ppermute | solution.py:210
  325.7 17.3 %collective-permute-start.33 = (bf16[512,1024]{1,0:T(8,128)(2,1)S(1)}, bf16[512,1024]{1,0:T(8,128)(2,1)S(1)}, u32[]{:S(2)}, u32[]{:S(2)}) collective-permute-start(bf16[512,1024]{1,0:T(8,128)(2,1)S(1)} %get-tuple-element.40), channel_id=1, source_target_pairs={{0,8},{8,0},{16,24},{24,16},{1,9},{9,1},{17,25},{25,17},{2,10},{10... | collective-permute-start | bytes 3145736 | tf_op jit(solution)/shard_map/ppermute | solution.py:210
  326.2 16.8 %collective-permute-start.34 = (bf16[512,1024]{1,0:T(8,128)(2,1)S(1)}, bf16[512,1024]{1,0:T(8,128)(2,1)S(1)}, u32[]{:S(2)}, u32[]{:S(2)}) collective-permute-start(bf16[512,1024]{1,0:T(8,128)(2,1)S(1)} %get-tuple-element.41), channel_id=1, source_target_pairs={{0,8},{8,0},{16,24},{24,16},{1,9},{9,1},{17,25},{25,17},{2,10},{10... | collective-permute-start | bytes 3145736 | tf_op jit(solution)/shard_map/ppermute | solution.py:210
  326.3 14.3 %collective-permute-start.21 = (bf16[256,1024]{1,0:T(8,128)(2,1)S(1)}, bf16[256,1024]{1,0:T(8,128)(2,1)S(1)}, u32[]{:S(2)}, u32[]{:S(2)}) collective-permute-start(bf16[256,1024]{1,0:T(8,128)(2,1)S(1)} %copy-done.68), channel_id=1, source_target_pairs={{0,1},{1,0},{2,3},{3,2},{4,5},{5,4},{6,7},{7,6},{8,9},{9,8},{10,11... | collective-permute-start | bytes 1572872 | tf_op jit(solution)/shard_map/ppermute | solution.py:216
  329.8 26.1 %collective-permute-start.38 = (bf16[512,1024]{1,0:T(8,128)(2,1)S(1)}, bf16[512,1024]{1,0:T(8,128)(2,1)S(1)}, u32[]{:S(2)}, u32[]{:S(2)}) collective-permute-start(bf16[512,1024]{1,0:T(8,128)(2,1)S(1)} %shard_map.105.refs_6_), channel_id=1, source_target_pairs={{0,16},{8,24},{16,0},{24,8},{1,17},{9,25},{17,1},{25,9},{2,18},{10... | collective-permute-start | bytes 3145736 | tf_op jit(solution)/shard_map/ppermute | solution.py:213
  340.6 26.4 %collective-permute-start.24 = (bf16[512,1024]{1,0:T(8,128)(2,1)}, bf16[512,1024]{1,0:T(8,128)(2,1)}, u32[]{:S(2)}, u32[]{:S(2)}) collective-permute-start(bf16[512,1024]{1,0:T(8,128)(2,1)} %add_convert_fusion.3), channel_id=1, source_target_pairs={{0,1},{1,0},{2,3},{3,2},{4,5},{5,4},{6,7},{7,6},{8,9},{9,8},{10,11... | collective-permute-start | bytes 3145736 | tf_op jit(solution)/shard_map/ppermute | solution.py:216
  342.5 35.9 %collective-permute-start.22 = (bf16[512,1024]{1,0:T(8,128)(2,1)}, bf16[512,1024]{1,0:T(8,128)(2,1)}, u32[]{:S(2)}, u32[]{:S(2)}) collective-permute-start(bf16[512,1024]{1,0:T(8,128)(2,1)} %add_convert_fusion.4), channel_id=1, source_target_pairs={{0,16},{8,24},{16,0},{24,8},{1,17},{9,25},{17,1},{25,9},{2,18},{10... | collective-permute-start | bytes 3145736 | tf_op jit(solution)/shard_map/ppermute | solution.py:213
  347.2 54.9 %collective-permute-start.37 = (bf16[512,1024]{1,0:T(8,128)(2,1)}, bf16[512,1024]{1,0:T(8,128)(2,1)}, u32[]{:S(2)}, u32[]{:S(2)}) collective-permute-start(bf16[512,1024]{1,0:T(8,128)(2,1)} %get-tuple-element.44), channel_id=1, source_target_pairs={{0,16},{8,24},{16,0},{24,8},{1,17},{9,25},{17,1},{25,9},{2,18},{10... | collective-permute-start | bytes 3145736 | tf_op jit(solution)/shard_map/ppermute | solution.py:213
  357.2 44.8 %collective-permute-start.39 = (bf16[512,1024]{1,0:T(8,128)(2,1)}, bf16[512,1024]{1,0:T(8,128)(2,1)}, u32[]{:S(2)}, u32[]{:S(2)}) collective-permute-start(bf16[512,1024]{1,0:T(8,128)(2,1)} %add_convert_fusion.1), channel_id=1, source_target_pairs={{0,1},{1,0},{2,3},{3,2},{4,5},{5,4},{6,7},{7,6},{8,9},{9,8},{10,11... | collective-permute-start | bytes 3145736 | tf_op jit(solution)/shard_map/ppermute | solution.py:216
  358.6 40.8 %collective-permute-start.40 = (bf16[256,1024]{1,0:T(8,128)(2,1)}, bf16[256,1024]{1,0:T(8,128)(2,1)S(1)}, u32[]{:S(2)}, u32[]{:S(2)}) collective-permute-start(bf16[256,1024]{1,0:T(8,128)(2,1)} %reduce-scatter.8.cloned.1.call-done), channel_id=1, source_target_pairs={{0,1},{1,0},{2,3},{3,2},{4,5},{5,4},{6,7},{7,6},{8,9},{9,8},{10,11... | collective-permute-start | bytes 1572872 | tf_op jit(solution)/shard_map/ppermute | solution.py:216
  (67 other events, 288.3 us)
Sparse Core Ops, SparseCore 0:
  34.6 47.4 all-gather.4
  84.2 44.6 all-gather.2
  173.2 66.6 reduce-scatter.3
  283.1 44.4 reduce-scatter.7
  329.7 43.1 reduce-scatter.5

commit v2 on v1

v2 whole, which is shorter than its diff:
```python
import functools

import jax
import jax.numpy as jnp
from jax import lax
from jax.experimental import pallas as pl
from jax.experimental.pallas import tpu as pltpu
from jax.sharding import PartitionSpec as P

F32 = jnp.float32
BF16 = jnp.bfloat16
MIB = 1024 * 1024


def matmul(a, b, contract):
    return lax.dot_general(a, b, ((contract[:1], contract[1:]), ((), ())), preferred_element_type=F32)


def gated(gate_sum, up_sum):
    sigmoid_g = jax.nn.sigmoid(gate_sum)
    silu_g = gate_sum * sigmoid_g
    slope = sigmoid_g * (1.0 + gate_sum * (1.0 - sigmoid_g))
    return silu_g, silu_g * up_sum, up_sum * slope


def shape(*dims, dtype=BF16):
    return jax.ShapeDtypeStruct(dims, dtype)


def call(kernel, outs, flops, args, after=(), specs=None, scratch=(), limit=24):
    everything = [*args, *after]
    moved = sum(a.size * a.dtype.itemsize for a in args) + sum(o.size * o.dtype.itemsize for o in outs)
    specs = specs or [pl.BlockSpec(memory_space=pltpu.VMEM)] * len(args)

    def body(*refs):
        kernel(*refs[: len(args)], *refs[len(everything) :])

    return pl.pallas_call(
        body,
        out_shape=list(outs),
        in_specs=[*specs, *[pl.BlockSpec(memory_space=pl.ANY)] * len(after)],
        out_specs=[pl.BlockSpec(memory_space=pltpu.VMEM)] * len(outs),
        scratch_shapes=list(scratch),
        compiler_params=pltpu.CompilerParams(vmem_limit_bytes=limit * MIB),
        cost_estimate=pl.CostEstimate(flops=flops, bytes_accessed=moved, transcendentals=0),
    )(*everything)


ANY = pl.BlockSpec(memory_space=pl.ANY)
VMEM = pl.BlockSpec(memory_space=pltpu.VMEM)
SMEM = pl.BlockSpec(memory_space=pltpu.SMEM)


def hidden_kernel(width, step, rows_ref, unit_ref, hidden_ref, turned_ref, silu_ref, rest_ref):
    @pl.loop(0, rows_ref.shape[0] // step)
    def _(at):
        span = pl.ds(pl.multiple_of(at * step, step), step)
        for group in range(unit_ref.shape[0] // (2 * width)):
            units = slice(2 * group * width, 2 * (group + 1) * width)
            sums = matmul(rows_ref[span], unit_ref[units], (1, 1))
            silu_g, hidden, rest = gated(sums[:, :width], sums[:, width:])
            cols = slice(group * width, (group + 1) * width)
            hidden_ref[span, cols] = hidden.astype(BF16)
            turned_ref[cols, span] = hidden.T.astype(BF16)
            silu_ref[span, cols] = silu_g.astype(BF16)
            rest_ref[span, cols] = rest.astype(BF16)


def grads_kernel(width, step, rows_ref, down_ref, silu_ref, rest_ref, act_ref, turned_ref):
    @pl.loop(0, rows_ref.shape[0] // step)
    def _(at):
        span = pl.ds(pl.multiple_of(at * step, step), step)
        for pair in range(down_ref.shape[0] // (2 * width)):
            units = slice(2 * pair * width, 2 * (pair + 1) * width)
            back = matmul(rows_ref[span], down_ref[units], (1, 1))
            for part, factor in enumerate((rest_ref, silu_ref)):
                grads = back * factor[span, units].astype(F32)
                for side in range(2):
                    grad = grads[:, side * width : (side + 1) * width]
                    first = (4 * pair + 2 * side + part) * width
                    low = slice(first, first + width)
                    act_ref[span, low] = grad.astype(BF16)
                    turned_ref[low, span] = grad.T.astype(BF16)


def weight_kernel(first, tile, turned_ref, rows_ref, away_ref, stay_ref):
    half = away_ref.shape[0]

    @pl.loop(0, away_ref.shape[1] // tile)
    def _(index):
        cols = pl.ds(pl.multiple_of(index * tile, tile), tile)
        right = rows_ref[:, pl.ds(pl.multiple_of(first + index * tile, tile), tile)]
        away_ref[:, cols] = matmul(turned_ref[:half], right, (1, 0)).astype(BF16)
        stay_ref[:, cols] = matmul(turned_ref[half:], right, (1, 0)).astype(BF16)


def block_kernel(first, places, sides, added, *refs):
    rights, many = len(sides), len(places)
    left_any, right_any, refs = refs[0], refs[1 : 1 + rights], refs[1 + rights :]
    adds, refs = refs[: many * added], refs[many * added :]
    outs, (left_ref, right_ref, sems) = refs[:many], refs[many:]
    depth, half = right_ref.shape[1:]
    copies = [pltpu.make_async_copy(left_any.at[pl.ds(first, left_ref.shape[0])], left_ref, sems.at[0])]
    for at, side in enumerate(sides):
        source = right_any[at].at[:, pl.ds(side * half, half)]
        copies.append(pltpu.make_async_copy(source, right_ref.at[at], sems.at[1 + at]))
    for copy in copies:
        copy.start()
    for copy in copies:
        copy.wait()
    for at, (row, right) in enumerate(places):
        total = matmul(left_ref[row : row + outs[at].shape[0]], right_ref[right], (1, 0))
        if added:
            total = total + adds[at][...].astype(F32)
        outs[at][...] = total.astype(BF16)


def halves_kernel(at_ref, gate_ref, up_ref, mine_ref, theirs_ref):
    width = gate_ref.shape[1] // 2
    for part, ref in enumerate((gate_ref, up_ref)):
        span = slice(part * width, (part + 1) * width)
        low, high = ref[:, :width].astype(F32).T.astype(BF16), ref[:, width:].astype(F32).T.astype(BF16)
        first = at_ref[0] == 0
        mine_ref[span] = jnp.where(first, low, high)
        theirs_ref[span] = jnp.where(first, high, low)


def finish_kernel(at_ref, mine_ref, theirs_ref, gate_ref, up_ref):
    width = mine_ref.shape[0] // 2
    for part, out_ref in enumerate((gate_ref, up_ref)):
        span = slice(part * width, (part + 1) * width)
        mine, theirs = mine_ref[span].astype(F32).T, theirs_ref[span].astype(F32).T
        first = at_ref[0] == 0
        out_ref[:, :width] = jnp.where(first, mine, theirs)
        out_ref[:, width:] = jnp.where(first, theirs, mine)


class Square:
    def core(self, array):
        return lax.ppermute(array, "inp", [(at, at ^ 1) for at in range(4)])

    def across(self, array):
        return lax.ppermute(array, "inp", [(at, at ^ 2) for at in range(4)])

    def other(self, array):
        return lax.ppermute(array, "out", [(0, 1), (1, 0)])

    def near(self, array):
        return lax.ppermute(array, "wt", [(at, at ^ 1) for at in range(4)])

    def far(self, array):
        return lax.ppermute(array, "wt", [(at, at ^ 2) for at in range(4)])

    def gather(self, array, split):
        step = array.shape[1]
        own = array.reshape(2 * step, array.shape[2])
        by_near, by_other = self.near(own), self.other(own)
        if split:
            corner = jnp.concatenate([self.other(by_near[:step]), self.near(by_other[step:])])
        else:
            corner = self.other(by_near)
        pieces = [own, by_other, by_near, corner]
        pieces += [self.core(piece) for piece in pieces]
        rows = [jnp.concatenate(pieces[at : at + 2], axis=1) for at in range(0, 8, 2)]
        return jnp.concatenate(rows)

    def gather_units(self, own):
        by_far = self.far(own)
        return [self.across(own), self.across(by_far), own, by_far]

    def scatter_units(self, away, stay):
        total = stay.astype(F32) + self.across(away).astype(F32)
        half = total.shape[0] // 2
        return total[:half] + self.far(total[half:].astype(BF16)).astype(F32)

    def products(self, left, rights, places, adds=(), after=()):
        far = int(not adds)
        quarter, depth = left.shape[0] // 4, left.shape[1]
        half = rights[0][2]
        outs = [shape(quarter, half)] * len(places)
        use = sorted({other for _, other in places})
        chips = sorted({chip for chip, _ in places})
        first = 2 * far * quarter + chips[0] * quarter
        wanted = [((chip - chips[0]) * quarter, use.index(other)) for chip, other in places]
        args = [left] + [rights[other][0] for other in use] + [adds[place] for place in places if adds]
        blocks = call(
            functools.partial(block_kernel, first, wanted, [rights[other][1] for other in use], bool(adds)),
            outs,
            2 * len(places) * quarter * depth * half,
            args,
            after,
            specs=[ANY] * (1 + len(use)) + [VMEM] * (len(args) - 1 - len(use)),
            scratch=[
                pltpu.VMEM((len(chips) * quarter, depth), BF16),
                pltpu.VMEM((len(use), depth, half), BF16),
                pltpu.SemaphoreType.DMA((1 + len(use),)),
            ],
        )
        return dict(zip(places, blocks))

    def scatter_far(self, left, rights, after=()):
        first = self.products(left, rights, [(1, 1)], after=after)
        second = self.products(left, rights, [(0, 1), (1, 0), (0, 0)], after=list(first.values()))
        return first | second

    def scatter_near(self, left, rights, far, after=()):
        far = {place: self.core(block) for place, block in far.items()}
        sums = self.products(left, rights, [(1, 1)], far, after)
        sums |= self.products(left, rights, [(0, 1), (1, 0), (0, 0)], far, list(sums.values()))
        return sums

    def scatter_end(self, sums, split):
        corner = sums[1, 1]
        step = corner.shape[0] // 2
        if split:
            by_other = self.other(corner[:step]).astype(F32)
            by_near = self.near(corner[step:]).astype(F32)
            zeros = jnp.zeros_like(by_other)
            to_near = (sums[1, 0].astype(F32) + jnp.concatenate([by_other, zeros])).astype(BF16)
            to_other = (sums[0, 1].astype(F32) + jnp.concatenate([zeros, by_near])).astype(BF16)
        else:
            to_near = (sums[1, 0].astype(F32) + self.other(corner).astype(F32)).astype(BF16)
            to_other = sums[0, 1]
        total = sums[0, 0].astype(F32) + self.near(to_near).astype(F32) + self.other(to_other).astype(F32)
        return total.astype(BF16).reshape(2, step, corner.shape[1])

    def layer(self, tokens, gate_weight, up_weight, down_weight, cotangent):
        at_out = lax.axis_index("out").astype(jnp.int32)
        half, width = gate_weight.shape[0], gate_weight.shape[1] // 2
        pair = [shape(2 * width, half)] * 2
        mine, theirs = call(halves_kernel, pair, 0, [at_out.reshape(1), gate_weight, up_weight], specs=[SMEM, VMEM, VMEM])
        theirs = self.other(theirs)
        down_mine = lax.dynamic_slice_in_dim(down_weight, at_out * width, width, 0)
        down_theirs = self.other(lax.dynamic_slice_in_dim(down_weight, (1 - at_out) * width, width, 0))
        down_own = jnp.concatenate([down_mine, down_theirs], axis=1)

        rows_in = self.gather(tokens, False)
        sides = [jnp.concatenate(self.gather_units(own)) for own in (mine, theirs)]
        gate_up = jnp.concatenate(sides, axis=1)
        rows_cot = self.gather(cotangent, True)
        down = jnp.concatenate(self.gather_units(down_own))

        count, units = rows_in.shape[0], down.shape[0]
        step = count // 4
        hidden, hidden_turned, silu, rest = call(
            functools.partial(hidden_kernel, width, step),
            [shape(count, units), shape(units, count), shape(count, units), shape(count, units)],
            8 * count * units * half,
            [rows_in, gate_up],
            limit=28,
        )
        down_terms = call(
            functools.partial(weight_kernel, 0, 256),
            [shape(units // 2, 2 * half)] * 2,
            4 * count * units * half,
            [hidden_turned, rows_cot],
        )
        down_sum = self.scatter_units(*down_terms)
        down_sides = [(down, 0, half), (down, 1, half)]
        output_far = self.scatter_far(hidden, down_sides)
        act, act_turned = call(
            functools.partial(grads_kernel, width, step),
            [shape(count, 2 * units), shape(2 * units, count)],
            4 * count * units * half,
            [rows_cot, down, silu, rest],
            after=list(output_far.values()),
            limit=28,
        )
        output_sums = self.scatter_near(hidden, down_sides, output_far)

        def unit_terms(side, after):
            return call(
                functools.partial(weight_kernel, side * half, 256),
                [shape(units, half)] * 2,
                4 * count * units * half,
                [act_turned, rows_in],
                after=after,
            )

        other_terms = unit_terms(1, list(output_sums.values()))
        other_sum = self.scatter_units(*other_terms).astype(BF16)
        unit_sides = [(gate_up, 0, half), (gate_up, 1, half)]
        grads_far = self.scatter_far(act, unit_sides, other_terms)
        own_terms = unit_terms(0, list(grads_far.values()))
        own_sum = self.scatter_units(*own_terms).astype(BF16)
        grads_sums = self.scatter_near(act, unit_sides, grads_far, own_terms)
        output = self.scatter_end(output_sums, True)
        grad_tokens = self.scatter_end(grads_sums, False)

        down_back = self.other(down_sum[:, half:].astype(BF16))
        units_back = self.other(other_sum)
        mine, theirs = down_sum[:, :half], down_back.astype(F32)
        grad_down = jnp.where(at_out == 0, jnp.concatenate([mine, theirs]), jnp.concatenate([theirs, mine]))
        grad_gate, grad_up = call(
            finish_kernel,
            [shape(half, 2 * width, dtype=F32)] * 2,
            0,
            [at_out.reshape(1), own_sum, units_back],
            specs=[SMEM, VMEM, VMEM],
        )
        return (output, grad_tokens, grad_gate, grad_up, grad_down)


class Plain:
    def units(self, weight):
        own = lax.all_to_all(weight, "out", split_axis=0, concat_axis=1, tiled=True)
        return lax.all_gather(own, "wt", axis=0, tiled=True)

    def unit_sums(self, grad):
        own = lax.psum_scatter(grad.astype(BF16), "wt", scatter_dimension=0, tiled=True)
        return lax.all_to_all(own, "out", split_axis=1, concat_axis=0, tiled=True).astype(F32)

    def gather(self, array):
        array = lax.all_gather(lax.all_gather(array, "inp", axis=1, tiled=True), "out", axis=2, tiled=True)
        return array.reshape(-1, array.shape[2])

    def scatter(self, partial, batches):
        partial = partial.astype(BF16).reshape(batches, -1, partial.shape[1])
        partial = lax.psum_scatter(partial, "out", scatter_dimension=2, tiled=True)
        return lax.psum_scatter(partial, "inp", scatter_dimension=1, tiled=True)

    def layer(self, tokens, gate_weight, up_weight, down_weight, cotangent):
        gate, up, down = self.units(gate_weight.T), self.units(up_weight.T), self.units(down_weight)
        rows_in, rows_cot = self.gather(tokens), self.gather(cotangent)
        gate_sum = matmul(rows_in, gate, (1, 1))
        up_sum = matmul(rows_in, up, (1, 1))
        silu_g, hidden, rest = gated(gate_sum, up_sum)
        hidden = hidden.astype(BF16)
        grad_down = self.unit_sums(matmul(hidden, rows_cot, (0, 0)))
        back_sum = matmul(rows_cot, down, (1, 1))
        gate_act, up_act = (back_sum * rest).astype(BF16), (back_sum * silu_g).astype(BF16)
        grad_gate = self.unit_sums(matmul(gate_act, rows_in, (0, 0))).T
        grad_up = self.unit_sums(matmul(up_act, rows_in, (0, 0))).T
        output = self.scatter(matmul(hidden, down, (1, 0)), tokens.shape[0])
        partial = matmul(gate_act, gate, (1, 0)) + matmul(up_act, up, (1, 0))
        grad_tokens = self.scatter(partial, tokens.shape[0])
        return (output, grad_tokens, grad_gate, grad_up, grad_down)


def solution(mesh):
    square = mesh.shape["inp"] == 4 and mesh.shape["out"] == 2 and mesh.shape["wt"] == 4

    def on_device(tokens, *others):
        places = Square() if square and tokens.shape[0] == 2 else Plain()
        return places.layer(tokens, *others)

    rows_spec = P(None, ("inp", "wt"), "out")
    in_spec = P("out", ("wt", "inp"))
    down_spec = P(("wt", "inp"), "out")
    return jax.shard_map(
        on_device,
        mesh=mesh,
        in_specs=(rows_spec, in_spec, in_spec, down_spec, rows_spec),
        out_specs=(rows_spec, rows_spec, in_spec, in_spec, down_spec),
        check_vma=False,
    )
```

time: 413 us -> 377 us (0.913)
  other arithmetic: 14.6 us -> 58.6 us
  local copies, waits for them, and re-layouts: 57.3 us -> 13.6 us
  waiting for transfers between devices: 205 us -> 186 us
  Pallas kernels: 81.8 us -> 63.3 us
  between operations: 14.4 us -> 1.58 us
  starting transfers between devices: 38.4 us -> 50.8 us
    ppermute x10 -> x12, waiting for transfers between devices: 96.8 us -> 40.7 us  [other(): return lax.ppermute(array, 'out', [(0, 1), (1, 0)])]
    unnamed x138 -> x69, local copies, waits for them, and re-layouts: 56.1 us -> 10.1 us
    concatenate x0 -> x5, other arithmetic: none -> 43.7 us  [the longest x2 22.9 us: gather(): return jnp.concatenate(rows)]
    ppermute x14 -> x21, waiting for transfers between devices: 108 us -> 145 us  [the longest x6 113 us: far(): return lax.ppermute(array, 'wt', [(at, at ^ 2) for at in range(4)])]
    pallas_call x18 -> x15, Pallas kernels: 81.8 us -> 63.3 us  [call(): pl.pallas_call(body, out_shape=list(outs), in_specs=[*specs, *[pl.BlockSp...]
    ppermute x14 -> x21, starting transfers between devices: 23.6 us -> 31.1 us  [the longest x6 12.8 us: far(): return lax.ppermute(array, 'wt', [(at, at ^ 2) for at in range(4)])]
    ppermute x10 -> x12, starting transfers between devices: 11.4 us -> 16.2 us  [other(): return lax.ppermute(array, 'out', [(0, 1), (1, 0)])]
    convert_element_type x7 -> x8, other arithmetic: 13.6 us -> 12.6 us  [the longest x2 6.28 us: scatter_end(): return total.astype(BF16).reshape(2, step, corner.shape[1])]
  transfers between devices with their start and end apart: 46 -> 49, of which waited for: 14 -> 13; matrix products, arithmetic and copies ran while one was open for 3% -> 16% of each run, Pallas kernels for 17% -> 17%
where the time goes in v2:
time: 377 us; the launch traced here: 374 us
  waiting for transfers between devices  186 us (49%)
  Pallas kernels  63.3 us (17%)
  other arithmetic  58.6 us (16%)
  starting transfers between devices  50.8 us (13%)
  local copies, waits for them, and re-layouts  13.6 us (4%)
    ppermute x6, waiting for transfers between devices, far(): return lax.ppermute(array, 'wt', [(at, at ^ 2) for at in range(4)])  113 us
    pallas_call x15, Pallas kernels, call(): pl.pallas_call(body, out_shape=list(outs), in_specs=[*specs, *[pl.BlockSp...  63.3 us
    ppermute x12, waiting for transfers between devices, other(): return lax.ppermute(array, 'out', [(0, 1), (1, 0)])  40.7 us
    ppermute x9, waiting for transfers between devices, across(): return lax.ppermute(array, 'inp', [(at, at ^ 2) for at in range(4)])  30.7 us
    concatenate x2, other arithmetic, gather(): return jnp.concatenate(rows)  22.9 us
    ppermute x12, starting transfers between devices, other(): return lax.ppermute(array, 'out', [(0, 1), (1, 0)])  16.2 us
    concatenate x1, other arithmetic, layer(): gate_up = jnp.concatenate(sides, axis=1)  16.1 us
    ppermute x6, starting transfers between devices, far(): return lax.ppermute(array, 'wt', [(at, at ^ 2) for at in range(4)])  12.8 us
  transfers between devices with their start and end apart: 49, of which 13 were waited for; matrix products, arithmetic and copies ran while one was open for 16% of the time, Pallas kernels for 17%

profile of v2, /device:TPU:0, one launch (start us, length us, event | category | flops | bytes accessed | tf_op | source)
XLA Modules:
  0.0 373.9 jit_solution(4198771768333823010)
XLA Ops:
  3.1 3.0 collective-permute-start.10
  7.3 3.1 collective-permute-start.8
  11.8 1.6 collective-permute-start.1
  13.4 10.2 %collective-permute-done.14 = bf16[128,1024]{1,0:T(8,128)(2,1)S(1)} collective-permute-done((bf16[128,1024]{1,0:T(8,128)(2,1)S(1)}, bf16[128,1024]{1,0:T(8,128)(2,1)S(1)}, u32[]{:S(2)}, u32[]{:S(2)}) %collective-permute-start.14) | collective-permute-done | bytes 262176 | tf_op jit(solution)/shard_map/ppermute | solution.py:146
  23.7 1.8 collective-permute-start.27
  25.5 1.5 collective-permute-start.26
  27.0 6.0 %collective-permute-done.8 = bf16[256,1024]{1,0:T(8,128)(2,1)S(1)} collective-permute-done((bf16[256,1024]{1,0:T(8,128)(2,1)S(1)}, bf16[256,1024]{1,0:T(8,128)(2,1)S(1)}, u32[]{:S(2)}, u32[]{:S(2)}) %collective-permute-start.8) | collective-permute-done | bytes 524320 | tf_op jit(solution)/shard_map/ppermute | solution.py:152
  33.0 1.5 collective-permute-start.15
  34.6 42.6 %collective-permute-done.16 = bf16[128,2048]{1,0:T(8,128)(2,1)S(1)} collective-permute-done((bf16[128,2048]{1,0:T(8,128)(2,1)S(1)}, bf16[128,2048]{1,0:T(8,128)(2,1)S(1)}, u32[]{:S(2)}, u32[]{:S(2)}) %collective-permute-start.16) | collective-permute-done | bytes 524320 | tf_op jit(solution)/shard_map/ppermute | solution.py:152
  78.7 3.4 collective-permute-start.12
  84.7 18.8 %collective-permute-done.12 = bf16[256,1024]{1,0:T(8,128)(2,1)S(1)} collective-permute-done((bf16[256,1024]{1,0:T(8,128)(2,1)S(1)}, bf16[256,1024]{1,0:T(8,128)(2,1)S(1)}, u32[]{:S(2)}, u32[]{:S(2)}) %collective-permute-start.12) | collective-permute-done | bytes 524320 | tf_op jit(solution)/shard_map/ppermute | solution.py:152
  106.2 9.9 %collective-permute-done.17 = bf16[128,2048]{1,0:T(8,128)(2,1)S(1)} collective-permute-done((bf16[128,2048]{1,0:T(8,128)(2,1)S(1)}, bf16[128,2048]{1,0:T(8,128)(2,1)S(1)}, u32[]{:S(2)}, u32[]{:S(2)}) %collective-permute-start.17) | collective-permute-done | bytes 524320 | tf_op jit(solution)/shard_map/ppermute | solution.py:143
  116.2 18.3 %collective-permute-done.28 = bf16[256,1024]{1,0:T(8,128)(2,1)S(1)} collective-permute-done((bf16[256,1024]{1,0:T(8,128)(2,1)S(1)}, bf16[256,1024]{1,0:T(8,128)(2,1)S(1)}, u32[]{:S(2)}, u32[]{:S(2)}) %collective-permute-start.28) | collective-permute-done | bytes 524320 | tf_op jit(solution)/shard_map/ppermute | solution.py:146
  136.5 4.7 %pad_maximum_fusion.refs_1_.refs_2_ = bf16[512,2048]{1,0:T(8,128)(2,1)S(1)} fusion(bf16[128,2048]{1,0:T(8,128)(2,1)S(1)} %collective-permute-done.16, bf16[128,1024]{1,0:T(8,128)(2,1)S(1)} %collective-permute-done.14, bf16[128,1024]{1,0:T(8,128)(2,1)S(1)} %get-tuple-element.63, bf16[128,2048]{1,0:T(8,128)(2,1)S(1)} %collective-permute-done.17, ...), kind=kLoop, calls=%fused_computation.3 | loop fusion | flops 10485760 | bytes 4194304 | tf_op jit(solution)/shard_map/concatenate | solution.py:241
  141.3 4.5 %collective-permute-done.13 = bf16[256,1024]{1,0:T(8,128)(2,1)S(1)} collective-permute-done((bf16[256,1024]{1,0:T(8,128)(2,1)S(1)}, bf16[256,1024]{1,0:T(8,128)(2,1)S(1)}, u32[]{:S(2)}, u32[]{:S(2)}) %collective-permute-start.13) | collective-permute-done | bytes 524320 | tf_op jit(solution)/shard_map/ppermute | solution.py:143
  145.8 16.1 %maximum_maximum_fusion.2.refs_1_.refs_2_ = bf16[1024,2048]{1,0:T(8,128)(2,1)S(1)} fusion(bf16[256,1024]{1,0:T(8,128)(2,1)S(1)} %collective-permute-done.12, bf16[256,1024]{1,0:T(8,128)(2,1)S(1)} %copy-done.32, bf16[256,1024]{1,0:T(8,128)(2,1)S(1)} %collective-permute-done.13, bf16[256,1024]{1,0:T(8,128)(2,1)S(1)} %collective-permute-done.11, ...), kind=kLoop, calls=%fused_computation.2 | loop fusion | flops 33554432 | bytes 8388608 | tf_op jit(solution)/shard_map/concatenate | solution.py:239
  163.8 12.8 %maximum_maximum_fusion.refs_0_.refs_1_ = bf16[2048,2048]{1,0:T(8,128)(2,1)S(1)} fusion(bf16[512,1024]{1,0:T(8,128)(2,1)} %collective-permute-done.6, bf16[512,1024]{1,0:T(8,128)(2,1)} %copy-done.28, bf16[512,1024]{1,0:T(8,128)(2,1)} %copy-done.30, bf16[512,1024]{1,0:T(8,128)(2,1)S(1)} %collective-permute-done.3, ...), kind=kLoop, calls=%fused_computation | loop fusion | flops 67108864 | bytes 16777216 | tf_op jit(solution)/shard_map/concatenate | solution.py:165
  176.6 11.1 %shard_map.93 = (bf16[2048,512]{1,0:T(8,128)(2,1)S(1)}, bf16[512,2048]{1,0:T(8,128)(2,1)S(1)}, bf16[2048,512]{1,0:T(8,128)(2,1)S(1)}, bf16[2048,512]{1,0:T(8,128)(2,1)S(1)}) custom-call(bf16[2048,2048]{1,0:T(8,128)(2,1)S(1)} %maximum_maximum_fusion.refs_0_.refs_1_, bf16[1024,2048]{1,0:T(8,128)(2,1)S(1)} %maximum_maximum_fusion.2.refs_1_.refs_2_), custom_call_target="tpu_custom_call" | custom-call | flops 8589934592 | bytes 20971520 | tf_op jit(solution)/shard_map/pallas_call | solution.py:38
  190.4 3.3 shard_map.95
  195.0 10.0 %maximum_maximum_fusion.1.refs_0_.refs_1_ = bf16[2048,2048]{1,0:T(8,128)(2,1)S(1)} fusion(bf16[512,1024]{1,0:T(8,128)(2,1)} %collective-permute-done.33, bf16[512,1024]{1,0:T(8,128)(2,1)} %collective-permute-done.32, bf16[512,1024]{1,0:T(8,128)(2,1)} %copy-done.29, bf16[512,1024]{1,0:T(8,128)(2,1)} %collective-permute-done.30, ...), kind=kLoop, calls=%fused_computation.1 | loop fusion | flops 67108864 | bytes 16777216 | tf_op jit(solution)/shard_map/concatenate | solution.py:165
  205.1 5.7 %shard_map.106 = (bf16[256,2048]{1,0:T(8,128)(2,1)S(1)}, bf16[256,2048]{1,0:T(8,128)(2,1)S(1)}) custom-call(bf16[512,2048]{1,0:T(8,128)(2,1)S(1)} %copy-done.17, bf16[2048,2048]{1,0:T(8,128)(2,1)S(1)} %maximum_maximum_fusion.1.refs_0_.refs_1_), custom_call_target="tpu_custom_call" | custom-call | flops 4294967296 | bytes 12582912 | tf_op jit(solution)/shard_map/pallas_call | solution.py:38
  210.9 1.6 collective-permute-start.46
  212.4 10.5 %shard_map.98 = (bf16[2048,1024]{1,0:T(8,128)(2,1)S(1)}, bf16[1024,2048]{1,0:T(8,128)(2,1)S(1)}) custom-call(bf16[2048,2048]{1,0:T(8,128)(2,1)} %copy-done.4, bf16[512,2048]{1,0:T(8,128)(2,1)S(1)} %pad_maximum_fusion.refs_1_.refs_2_, bf16[2048,512]{1,0:T(8,128)(2,1)S(1)} %copy-done.11, bf16[2048,512]{1,0:T(8,128)(2,1)S(1)} %copy-done.13, ...), custom_call_target="tpu_custom_call" | custom-call | flops 4294967296 | bytes 23068672 | tf_op jit(solution)/shard_map/pallas_call | solution.py:38
  222.9 2.0 copy-done.5
  224.9 3.0 shard_map.96.refs_6_.refs_2_
  227.9 4.2 %shard_map.97 = (bf16[512,1024]{1,0:T(8,128)(2,1)S(1)}, bf16[512,1024]{1,0:T(8,128)(2,1)S(1)}, bf16[512,1024]{1,0:T(8,128)(2,1)S(1)}) custom-call(bf16[2048,512]{1,0:T(8,128)(2,1)S(1)} %copy-done.3, bf16[512,2048]{1,0:T(8,128)(2,1)S(1)} %pad_maximum_fusion.refs_1_.refs_2_, bf16[512,2048]{1,0:T(8,128)(2,1)S(1)} %pad_maximum_fusion.refs_1_.refs_2_, ...), custom_call_target="tpu_custom_call" | custom-call | flops 1610612736 | bytes 12582912 | tf_op jit(solution)/shard_map/pallas_call | solution.py:38
  232.1 2.6 copy-done.6
  234.7 5.0 %shard_map.99 = (bf16[512,1024]{1,0:T(8,128)(2,1)S(1)}, bf16[512,1024]{1,0:T(8,128)(2,1)S(1)}) custom-call(bf16[1024,2048]{1,0:T(8,128)(2,1)S(1)} %copy-done.6, bf16[2048,2048]{1,0:T(8,128)(2,1)S(1)} %maximum_maximum_fusion.refs_0_.refs_1_, bf16[512,1024]{1,0:T(8,128)(2,1)S(1)} %shard_map.96.refs_6_.refs_2_, ...), custom_call_target="tpu_custom_call" | custom-call | flops 4294967296 | bytes 14680064 | tf_op jit(solution)/shard_map/pallas_call | solution.py:38
  240.3 1.9 shard_map.100.refs_3_.refs_2_
  242.3 4.4 %shard_map.101 = (bf16[512,1024]{1,0:T(8,128)(2,1)S(1)}, bf16[512,1024]{1,0:T(8,128)(2,1)S(1)}, bf16[512,1024]{1,0:T(8,128)(2,1)S(1)}) custom-call(bf16[2048,1024]{1,0:T(8,128)(2,1)S(1)} %copy-done.1, bf16[1024,2048]{1,0:T(8,128)(2,1)S(1)} %maximum_maximum_fusion.2.refs_1_.refs_2_, bf16[1024,2048]{1,0:T(8,128)(2,1)S(1)} %maximum_maximum_fusion.2.refs_1_.refs_2_, ...), custom_call_target="tpu_custom_call" | custom-call | flops 3221225472 | bytes 15728640 | tf_op jit(solution)/shard_map/pallas_call | solution.py:38
  247.2 3.4 collective-permute-start.47
  250.7 1.6 collective-permute-start.22
  252.3 5.0 %shard_map.102 = (bf16[512,1024]{1,0:T(8,128)(2,1)S(1)}, bf16[512,1024]{1,0:T(8,128)(2,1)S(1)}) custom-call(bf16[1024,2048]{1,0:T(8,128)(2,1)S(1)} %copy-done.7, bf16[2048,2048]{1,0:T(8,128)(2,1)S(1)} %maximum_maximum_fusion.refs_0_.refs_1_, bf16[512,1024]{1,0:T(8,128)(2,1)S(1)} %shard_map.100.refs_3_.refs_2_, ...), custom_call_target="tpu_custom_call" | custom-call | flops 4294967296 | bytes 14680064 | tf_op jit(solution)/shard_map/pallas_call | solution.py:38
  257.3 17.3 %collective-permute-done.47 = bf16[128,2048]{1,0:T(8,128)(2,1)S(1)} collective-permute-done((bf16[128,2048]{1,0:T(8,128)(2,1)S(1)}, bf16[128,2048]{1,0:T(8,128)(2,1)S(1)}, u32[]{:S(2)}, u32[]{:S(2)}) %collective-permute-start.47) | collective-permute-done | bytes 524320 | tf_op jit(solution)/shard_map/ppermute | solution.py:152
  278.1 1.7 shard_map.103.refs_6_
  279.8 1.6 collective-permute-start.38
  283.2 16.3 %collective-permute-done.41 = bf16[512,1024]{1,0:T(8,128)(2,1)S(1)} collective-permute-done((bf16[512,1024]{1,0:T(8,128)(2,1)S(1)}, bf16[512,1024]{1,0:T(8,128)(2,1)S(1)}, u32[]{:S(2)}, u32[]{:S(2)}) %collective-permute-start.41) | collective-permute-done | bytes 1048608 | tf_op jit(solution)/shard_map/ppermute | solution.py:143
  302.1 1.9 collective-permute-start.44
  304.0 4.6 %shard_map.104 = (bf16[512,1024]{1,0:T(8,128)(2,1)S(1)}, bf16[512,1024]{1,0:T(8,128)(2,1)S(1)}, bf16[512,1024]{1,0:T(8,128)(2,1)S(1)}) custom-call(bf16[2048,1024]{1,0:T(8,128)(2,1)S(1)} %copy-done.1, bf16[1024,2048]{1,0:T(8,128)(2,1)S(1)} %maximum_maximum_fusion.2.refs_1_.refs_2_, bf16[1024,2048]{1,0:T(8,128)(2,1)S(1)} %maximum_maximum_fusion.2.refs_1_.refs_2_, ...), custom_call_target="tpu_custom_call" | custom-call | flops 3221225472 | bytes 18874368 | tf_op jit(solution)/shard_map/pallas_call | solution.py:38
  313.5 23.1 %collective-permute-done.44 = bf16[256,1024]{1,0:T(8,128)(2,1)S(1)} collective-permute-done((bf16[256,1024]{1,0:T(8,128)(2,1)S(1)}, bf16[256,1024]{1,0:T(8,128)(2,1)S(1)}, u32[]{:S(2)}, u32[]{:S(2)}) %collective-permute-start.44) | collective-permute-done | bytes 524320 | tf_op jit(solution)/shard_map/ppermute | solution.py:152
  337.4 2.5 collective-permute-start.39
  343.4 5.0 %collective-permute-done.42 = bf16[256,1024]{1,0:T(8,128)(2,1)} collective-permute-done((bf16[256,1024]{1,0:T(8,128)(2,1)}, bf16[256,1024]{1,0:T(8,128)(2,1)}, u32[]{:S(2)}, u32[]{:S(2)}) %collective-permute-start.42) | collective-permute-done | bytes 524320 | tf_op jit(solution)/shard_map/ppermute | solution.py:152
  348.4 2.3 collective-permute-start.45
  351.9 3.1 add_convert_fusion.2
  355.1 12.1 %collective-permute-done.45.refs_2_ = bf16[256,1024]{1,0:T(8,128)(2,1)S(1)} collective-permute-done((bf16[256,1024]{1,0:T(8,128)(2,1)S(1)}, bf16[256,1024]{1,0:T(8,128)(2,1)S(1)}, u32[]{:S(2)}, u32[]{:S(2)}) %collective-permute-start.45) | collective-permute-done | bytes 524320 | tf_op jit(solution)/shard_map/ppermute | solution.py:146
  367.2 1.6 shard_map.105
  368.8 1.7 collective-permute-done.39
  370.5 3.1 add_convert_fusion
  (162 shorter events, 39.3 us)
Async XLA Ops:
  3.1 22.4 %collective-permute-start.10 = (bf16[256,1024]{1,0:T(8,128)(2,1)S(1)}, bf16[256,1024]{1,0:T(8,128)(2,1)S(1)}, u32[]{:S(2)}, u32[]{:S(2)}) collective-permute-start(bf16[256,1024]{1,0:T(8,128)(2,1)S(1)} %get-tuple-element.34), channel_id=1, source_target_pairs={{0,1},{1,0},{2,3},{3,2},{4,5},{5,4},{6,7},{7,6},{8,9},{9,8},{10,11... | collective-permute-start | bytes 1572872 | tf_op jit(solution)/shard_map/ppermute | solution.py:146
  7.2 16.5 %collective-permute-start.14 = (bf16[128,1024]{1,0:T(8,128)(2,1)S(1)}, bf16[128,1024]{1,0:T(8,128)(2,1)S(1)}, u32[]{:S(2)}, u32[]{:S(2)}) collective-permute-start(bf16[128,1024]{1,0:T(8,128)(2,1)S(1)} %get-tuple-element.64), channel_id=1, source_target_pairs={{0,1},{1,0},{2,3},{3,2},{4,5},{5,4},{6,7},{7,6},{8,9},{9,8},{10,11... | collective-permute-start | bytes 786440 | tf_op jit(solution)/shard_map/ppermute | solution.py:146
  7.3 25.8 %collective-permute-start.8 = (bf16[256,1024]{1,0:T(8,128)(2,1)S(1)}, bf16[256,1024]{1,0:T(8,128)(2,1)S(1)}, u32[]{:S(2)}, u32[]{:S(2)}) collective-permute-start(bf16[256,1024]{1,0:T(8,128)(2,1)S(1)} %get-tuple-element.33), channel_id=1, source_target_pairs={{0,4},{2,6},{4,0},{6,2},{1,5},{3,7},{5,1},{7,3},{8,12},{10,14},{12... | collective-permute-start | bytes 1572872 | tf_op jit(solution)/shard_map/ppermute | solution.py:152
  10.3 22.7 %collective-permute-start.7 = (bf16[256,1024]{1,0:T(8,128)(2,1)S(1)}, bf16[256,1024]{1,0:T(8,128)(2,1)S(1)}, u32[]{:S(2)}, u32[]{:S(2)}) collective-permute-start(bf16[256,1024]{1,0:T(8,128)(2,1)S(1)} %get-tuple-element.33), channel_id=1, source_target_pairs={{0,16},{8,24},{16,0},{24,8},{1,17},{9,25},{17,1},{25,9},{2,18},{10... | collective-permute-start | bytes 1572872 | tf_op jit(solution)/shard_map/ppermute | solution.py:143
  11.8 70.3 %collective-permute-start.1 = (bf16[512,1024]{1,0:T(8,128)(2,1)}, bf16[512,1024]{1,0:T(8,128)(2,1)S(1)}, u32[]{:S(2)}, u32[]{:S(2)}) collective-permute-start(bf16[512,1024]{1,0:T(8,128)(2,1)} %bitcast.5), channel_id=1, source_target_pairs={{0,2},{2,0},{4,6},{6,4},{1,3},{3,1},{5,7},{7,5},{8,10},{10,8},{12,... | collective-permute-start | bytes 3145736 | tf_op jit(solution)/shard_map/ppermute | solution.py:149
  23.7 59.9 %collective-permute-start.27 = (bf16[512,1024]{1,0:T(8,128)(2,1)}, bf16[512,1024]{1,0:T(8,128)(2,1)S(1)}, u32[]{:S(2)}, u32[]{:S(2)}) collective-permute-start(bf16[512,1024]{1,0:T(8,128)(2,1)} %bitcast.9), channel_id=1, source_target_pairs={{0,2},{2,0},{4,6},{6,4},{1,3},{3,1},{5,7},{7,5},{8,10},{10,8},{12,... | collective-permute-start | bytes 3145736 | tf_op jit(solution)/shard_map/ppermute | solution.py:149
  25.5 58.7 %collective-permute-start.26 = (bf16[512,1024]{1,0:T(8,128)(2,1)}, bf16[512,1024]{1,0:T(8,128)(2,1)S(1)}, u32[]{:S(2)}, u32[]{:S(2)}) collective-permute-start(bf16[512,1024]{1,0:T(8,128)(2,1)} %bitcast.10), channel_id=1, source_target_pairs={{0,1},{1,0},{2,3},{3,2},{4,5},{5,4},{6,7},{7,6},{8,9},{9,8},{10,11... | collective-permute-start | bytes 3145736 | tf_op jit(solution)/shard_map/ppermute | solution.py:146
  33.0 44.1 %collective-permute-start.16 = (bf16[128,2048]{1,0:T(8,128)(2,1)S(1)}, bf16[128,2048]{1,0:T(8,128)(2,1)S(1)}, u32[]{:S(2)}, u32[]{:S(2)}) collective-permute-start(bf16[128,2048]{1,0:T(8,128)(2,1)S(1)} %pad_maximum_fusion.1), channel_id=1, source_target_pairs={{0,4},{2,6},{4,0},{6,2},{1,5},{3,7},{5,1},{7,3},{8,12},{10,14},{12... | collective-permute-start | bytes 1572872 | tf_op jit(solution)/shard_map/ppermute | solution.py:152
  33.0 45.7 %collective-permute-start.15 = (bf16[128,2048]{1,0:T(8,128)(2,1)S(1)}, bf16[128,2048]{1,0:T(8,128)(2,1)S(1)}, u32[]{:S(2)}, u32[]{:S(2)}) collective-permute-start(bf16[128,2048]{1,0:T(8,128)(2,1)S(1)} %pad_maximum_fusion.1), channel_id=1, source_target_pairs={{0,16},{8,24},{16,0},{24,8},{1,17},{9,25},{17,1},{25,9},{2,18},{10... | collective-permute-start | bytes 1572872 | tf_op jit(solution)/shard_map/ppermute | solution.py:143
  77.2 29.0 %collective-permute-start = (bf16[512,1024]{1,0:T(8,128)(2,1)}, bf16[512,1024]{1,0:T(8,128)(2,1)S(1)}, u32[]{:S(2)}, u32[]{:S(2)}) collective-permute-start(bf16[512,1024]{1,0:T(8,128)(2,1)} %bitcast.6), channel_id=1, source_target_pairs={{0,1},{1,0},{2,3},{3,2},{4,5},{5,4},{6,7},{7,6},{8,9},{9,8},{10,11... | collective-permute-start | bytes 3145736 | tf_op jit(solution)/shard_map/ppermute | solution.py:146
  78.7 24.8 %collective-permute-start.12 = (bf16[256,1024]{1,0:T(8,128)(2,1)S(1)}, bf16[256,1024]{1,0:T(8,128)(2,1)S(1)}, u32[]{:S(2)}, u32[]{:S(2)}) collective-permute-start(bf16[256,1024]{1,0:T(8,128)(2,1)S(1)} %collective-permute-done.10), channel_id=1, source_target_pairs={{0,4},{2,6},{4,0},{6,2},{1,5},{3,7},{5,1},{7,3},{8,12},{10,14},{12... | collective-permute-start | bytes 1572872 | tf_op jit(solution)/shard_map/ppermute | solution.py:152
  82.1 22.9 %collective-permute-start.9 = (bf16[256,1024]{1,0:T(8,128)(2,1)S(1)}, bf16[256,1024]{1,0:T(8,128)(2,1)S(1)}, u32[]{:S(2)}, u32[]{:S(2)}) collective-permute-start(bf16[256,1024]{1,0:T(8,128)(2,1)S(1)} %collective-permute-done.8), channel_id=1, source_target_pairs={{0,16},{8,24},{16,0},{24,8},{1,17},{9,25},{17,1},{25,9},{2,18},{10... | collective-permute-start | bytes 1572872 | tf_op jit(solution)/shard_map/ppermute | solution.py:143
  83.6 21.9 %collective-permute-start.11 = (bf16[256,1024]{1,0:T(8,128)(2,1)S(1)}, bf16[256,1024]{1,0:T(8,128)(2,1)S(1)}, u32[]{:S(2)}, u32[]{:S(2)}) collective-permute-start(bf16[256,1024]{1,0:T(8,128)(2,1)S(1)} %collective-permute-done.10), channel_id=1, source_target_pairs={{0,16},{8,24},{16,0},{24,8},{1,17},{9,25},{17,1},{25,9},{2,18},{10... | collective-permute-start | bytes 1572872 | tf_op jit(solution)/shard_map/ppermute | solution.py:143
  84.1 51.9 %collective-permute-start.2 = (bf16[512,1024]{1,0:T(8,128)(2,1)S(1)}, bf16[512,1024]{1,0:T(8,128)(2,1)S(1)}, u32[]{:S(2)}, u32[]{:S(2)}) collective-permute-start(bf16[512,1024]{1,0:T(8,128)(2,1)S(1)} %collective-permute-done.1), channel_id=1, source_target_pairs={{0,1},{1,0},{2,3},{3,2},{4,5},{5,4},{6,7},{7,6},{8,9},{9,8},{10,11... | collective-permute-start | bytes 3145736 | tf_op jit(solution)/shard_map/ppermute | solution.py:146
  103.5 12.7 %collective-permute-start.17 = (bf16[128,2048]{1,0:T(8,128)(2,1)S(1)}, bf16[128,2048]{1,0:T(8,128)(2,1)S(1)}, u32[]{:S(2)}, u32[]{:S(2)}) collective-permute-start(bf16[128,2048]{1,0:T(8,128)(2,1)S(1)} %collective-permute-done.16), channel_id=1, source_target_pairs={{0,16},{8,24},{16,0},{24,8},{1,17},{9,25},{17,1},{25,9},{2,18},{10... | collective-permute-start | bytes 1572872 | tf_op jit(solution)/shard_map/ppermute | solution.py:143
  105.0 29.5 %collective-permute-start.28 = (bf16[256,1024]{1,0:T(8,128)(2,1)S(1)}, bf16[256,1024]{1,0:T(8,128)(2,1)S(1)}, u32[]{:S(2)}, u32[]{:S(2)}) collective-permute-start(bf16[256,1024]{1,0:T(8,128)(2,1)S(1)} %slice.54), channel_id=1, source_target_pairs={{0,1},{1,0},{2,3},{3,2},{4,5},{5,4},{6,7},{7,6},{8,9},{9,8},{10,11... | collective-permute-start | bytes 1572872 | tf_op jit(solution)/shard_map/ppermute | solution.py:146
  105.5 30.5 %collective-permute-start.29 = (bf16[256,1024]{1,0:T(8,128)(2,1)S(1)}, bf16[256,1024]{1,0:T(8,128)(2,1)S(1)}, u32[]{:S(2)}, u32[]{:S(2)}) collective-permute-start(bf16[256,1024]{1,0:T(8,128)(2,1)S(1)} %slice.55), channel_id=1, source_target_pairs={{0,2},{2,0},{4,6},{6,4},{1,3},{3,1},{5,7},{7,5},{8,10},{10,8},{12,... | collective-permute-start | bytes 1572872 | tf_op jit(solution)/shard_map/ppermute | solution.py:149
  106.2 55.8 %collective-permute-start.3 = (bf16[512,1024]{1,0:T(8,128)(2,1)S(1)}, bf16[512,1024]{1,0:T(8,128)(2,1)S(1)}, u32[]{:S(2)}, u32[]{:S(2)}) collective-permute-start(bf16[512,1024]{1,0:T(8,128)(2,1)S(1)} %bitcast.7), channel_id=1, source_target_pairs={{0,8},{8,0},{16,24},{24,16},{1,9},{9,1},{17,25},{25,17},{2,10},{10... | collective-permute-start | bytes 3145736 | tf_op jit(solution)/shard_map/ppermute | solution.py:140
  116.2 46.3 %collective-permute-start.5 = (bf16[512,1024]{1,0:T(8,128)(2,1)S(1)}, bf16[512,1024]{1,0:T(8,128)(2,1)S(1)}, u32[]{:S(2)}, u32[]{:S(2)}) collective-permute-start(bf16[512,1024]{1,0:T(8,128)(2,1)S(1)} %collective-permute-done.1), channel_id=1, source_target_pairs={{0,8},{8,0},{16,24},{24,16},{1,9},{9,1},{17,25},{25,17},{2,10},{10... | collective-permute-start | bytes 3145736 | tf_op jit(solution)/shard_map/ppermute | solution.py:140
  136.0 26.6 %collective-permute-start.4 = (bf16[512,1024]{1,0:T(8,128)(2,1)S(1)}, bf16[512,1024]{1,0:T(8,128)(2,1)S(1)}, u32[]{:S(2)}, u32[]{:S(2)}) collective-permute-start(bf16[512,1024]{1,0:T(8,128)(2,1)S(1)} %collective-permute-done), channel_id=1, source_target_pairs={{0,8},{8,0},{16,24},{24,16},{1,9},{9,1},{17,25},{25,17},{2,10},{10... | collective-permute-start | bytes 3145736 | tf_op jit(solution)/shard_map/ppermute | solution.py:140
  136.0 27.8 %collective-permute-start.6 = (bf16[512,1024]{1,0:T(8,128)(2,1)S(1)}, bf16[512,1024]{1,0:T(8,128)(2,1)}, u32[]{:S(2)}, u32[]{:S(2)}) collective-permute-start(bf16[512,1024]{1,0:T(8,128)(2,1)S(1)} %collective-permute-done.2), channel_id=1, source_target_pairs={{0,8},{8,0},{16,24},{24,16},{1,9},{9,1},{17,25},{25,17},{2,10},{10... | collective-permute-start | bytes 3145736 | tf_op jit(solution)/shard_map/ppermute | solution.py:140
  145.8 47.9 %collective-permute-start.30 = (bf16[512,1024]{1,0:T(8,128)(2,1)S(1)}, bf16[512,1024]{1,0:T(8,128)(2,1)}, u32[]{:S(2)}, u32[]{:S(2)}) collective-permute-start(bf16[512,1024]{1,0:T(8,128)(2,1)S(1)} %bitcast.12), channel_id=1, source_target_pairs={{0,8},{8,0},{16,24},{24,16},{1,9},{9,1},{17,25},{25,17},{2,10},{10... | collective-permute-start | bytes 3145736 | tf_op jit(solution)/shard_map/ppermute | solution.py:140
  162.0 32.1 %collective-permute-start.31 = (bf16[512,1024]{1,0:T(8,128)(2,1)S(1)}, bf16[512,1024]{1,0:T(8,128)(2,1)S(1)}, u32[]{:S(2)}, u32[]{:S(2)}) collective-permute-start(bf16[512,1024]{1,0:T(8,128)(2,1)S(1)} %collective-permute-done.26), channel_id=1, source_target_pairs={{0,8},{8,0},{16,24},{24,16},{1,9},{9,1},{17,25},{25,17},{2,10},{10... | collective-permute-start | bytes 3145736 | tf_op jit(solution)/shard_map/ppermute | solution.py:140
  162.5 31.8 %collective-permute-start.32 = (bf16[512,1024]{1,0:T(8,128)(2,1)S(1)}, bf16[512,1024]{1,0:T(8,128)(2,1)}, u32[]{:S(2)}, u32[]{:S(2)}) collective-permute-start(bf16[512,1024]{1,0:T(8,128)(2,1)S(1)} %collective-permute-done.27), channel_id=1, source_target_pairs={{0,8},{8,0},{16,24},{24,16},{1,9},{9,1},{17,25},{25,17},{2,10},{10... | collective-permute-start | bytes 3145736 | tf_op jit(solution)/shard_map/ppermute | solution.py:140
  162.6 32.4 %collective-permute-start.33 = (bf16[512,1024]{1,0:T(8,128)(2,1)S(1)}, bf16[512,1024]{1,0:T(8,128)(2,1)}, u32[]{:S(2)}, u32[]{:S(2)}) collective-permute-start(bf16[512,1024]{1,0:T(8,128)(2,1)S(1)} %constant_dynamic-update-slice_fusion), channel_id=1, source_target_pairs={{0,8},{8,0},{16,24},{24,16},{1,9},{9,1},{17,25},{25,17},{2,10},{10... | collective-permute-start | bytes 3145736 | tf_op jit(solution)/shard_map/ppermute | solution.py:140
  190.1 34.8 %collective-permute-start.21 = (bf16[512,1024]{1,0:T(8,128)(2,1)S(1)}, bf16[512,1024]{1,0:T(8,128)(2,1)}, u32[]{:S(2)}, u32[]{:S(2)}) collective-permute-start(bf16[512,1024]{1,0:T(8,128)(2,1)S(1)} %shard_map.94.refs_3_.refs_4_), channel_id=1, source_target_pairs={{0,8},{8,0},{16,24},{24,16},{1,9},{9,1},{17,25},{25,17},{2,10},{10... | collective-permute-start | bytes 3145736 | tf_op jit(solution)/shard_map/ppermute | solution.py:140
  193.7 34.2 %collective-permute-start.18 = (bf16[512,1024]{1,0:T(8,128)(2,1)}, bf16[512,1024]{1,0:T(8,128)(2,1)}, u32[]{:S(2)}, u32[]{:S(2)}) collective-permute-start(bf16[512,1024]{1,0:T(8,128)(2,1)} %get-tuple-element.36.refs_5_), channel_id=1, source_target_pairs={{0,8},{8,0},{16,24},{24,16},{1,9},{9,1},{17,25},{25,17},{2,10},{10... | collective-permute-start | bytes 3145736 | tf_op jit(solution)/shard_map/ppermute | solution.py:140
  194.0 33.9 %collective-permute-start.19 = (bf16[512,1024]{1,0:T(8,128)(2,1)}, bf16[512,1024]{1,0:T(8,128)(2,1)}, u32[]{:S(2)}, u32[]{:S(2)}) collective-permute-start(bf16[512,1024]{1,0:T(8,128)(2,1)} %get-tuple-element.37.refs_6_), channel_id=1, source_target_pairs={{0,8},{8,0},{16,24},{24,16},{1,9},{9,1},{17,25},{25,17},{2,10},{10... | collective-permute-start | bytes 3145736 | tf_op jit(solution)/shard_map/ppermute | solution.py:140
  194.3 33.6 %collective-permute-start.20 = (bf16[512,1024]{1,0:T(8,128)(2,1)}, bf16[512,1024]{1,0:T(8,128)(2,1)}, u32[]{:S(2)}, u32[]{:S(2)}) collective-permute-start(bf16[512,1024]{1,0:T(8,128)(2,1)} %get-tuple-element.38.refs_7_), channel_id=1, source_target_pairs={{0,8},{8,0},{16,24},{24,16},{1,9},{9,1},{17,25},{25,17},{2,10},{10... | collective-permute-start | bytes 3145736 | tf_op jit(solution)/shard_map/ppermute | solution.py:140
  210.9 35.9 %collective-permute-start.46 = (bf16[256,2048]{1,0:T(8,128)(2,1)S(1)}, bf16[256,2048]{1,0:T(8,128)(2,1)S(1)}, u32[]{:S(2)}, u32[]{:S(2)}) collective-permute-start(bf16[256,2048]{1,0:T(8,128)(2,1)S(1)} %get-tuple-element.60), channel_id=1, source_target_pairs={{0,16},{8,24},{16,0},{24,8},{1,17},{9,25},{17,1},{25,9},{2,18},{10... | collective-permute-start | bytes 3145736 | tf_op jit(solution)/shard_map/ppermute | solution.py:143
  239.7 40.1 %collective-permute-start.43 = (bf16[512,1024]{1,0:T(8,128)(2,1)S(1)}, bf16[512,1024]{1,0:T(8,128)(2,1)S(1)}, u32[]{:S(2)}, u32[]{:S(2)}) collective-permute-start(bf16[512,1024]{1,0:T(8,128)(2,1)S(1)} %get-tuple-element.46.refs_2_), channel_id=1, source_target_pairs={{0,16},{8,24},{16,0},{24,8},{1,17},{9,25},{17,1},{25,9},{2,18},{10... | collective-permute-start | bytes 3145736 | tf_op jit(solution)/shard_map/ppermute | solution.py:143
  242.2 34.5 %collective-permute-start.37 = (bf16[512,1024]{1,0:T(8,128)(2,1)S(1)}, bf16[512,1024]{1,0:T(8,128)(2,1)S(1)}, u32[]{:S(2)}, u32[]{:S(2)}) collective-permute-start(bf16[512,1024]{1,0:T(8,128)(2,1)S(1)} %shard_map.100.refs_3_.refs_2_), channel_id=1, source_target_pairs={{0,8},{8,0},{16,24},{24,16},{1,9},{9,1},{17,25},{25,17},{2,10},{10... | collective-permute-start | bytes 3145736 | tf_op jit(solution)/shard_map/ppermute | solution.py:140
  247.2 27.4 %collective-permute-start.47 = (bf16[128,2048]{1,0:T(8,128)(2,1)S(1)}, bf16[128,2048]{1,0:T(8,128)(2,1)S(1)}, u32[]{:S(2)}, u32[]{:S(2)}) collective-permute-start(bf16[128,2048]{1,0:T(8,128)(2,1)S(1)} %slice.75), channel_id=1, source_target_pairs={{0,4},{2,6},{4,0},{6,2},{1,5},{3,7},{5,1},{7,3},{8,12},{10,14},{12... | collective-permute-start | bytes 1572872 | tf_op jit(solution)/shard_map/ppermute | solution.py:152
  250.7 25.5 %collective-permute-start.22 = (bf16[256,1024]{1,0:T(8,128)(2,1)S(1)}, bf16[256,1024]{1,0:T(8,128)(2,1)S(1)}, u32[]{:S(2)}, u32[]{:S(2)}) collective-permute-start(bf16[256,1024]{1,0:T(8,128)(2,1)S(1)} %get-tuple-element.61), channel_id=1, source_target_pairs={{0,1},{1,0},{2,3},{3,2},{4,5},{5,4},{6,7},{7,6},{8,9},{9,8},{10,11... | collective-permute-start | bytes 1572872 | tf_op jit(solution)/shard_map/ppermute | solution.py:146
  252.3 24.0 %collective-permute-start.24 = (bf16[256,1024]{1,0:T(8,128)(2,1)S(1)}, bf16[256,1024]{1,0:T(8,128)(2,1)S(1)}, u32[]{:S(2)}, u32[]{:S(2)}) collective-permute-start(bf16[256,1024]{1,0:T(8,128)(2,1)S(1)} %get-tuple-element.62), channel_id=1, source_target_pairs={{0,2},{2,0},{4,6},{6,4},{1,3},{3,1},{5,7},{7,5},{8,10},{10,8},{12,... | collective-permute-start | bytes 1572872 | tf_op jit(solution)/shard_map/ppermute | solution.py:149
  274.6 24.9 %collective-permute-start.41 = (bf16[512,1024]{1,0:T(8,128)(2,1)S(1)}, bf16[512,1024]{1,0:T(8,128)(2,1)S(1)}, u32[]{:S(2)}, u32[]{:S(2)}) collective-permute-start(bf16[512,1024]{1,0:T(8,128)(2,1)S(1)} %get-tuple-element.51.refs_3_), channel_id=1, source_target_pairs={{0,16},{8,24},{16,0},{24,8},{1,17},{9,25},{17,1},{25,9},{2,18},{10... | collective-permute-start | bytes 3145736 | tf_op jit(solution)/shard_map/ppermute | solution.py:143
  276.2 25.2 %collective-permute-start.34 = (bf16[512,1024]{1,0:T(8,128)(2,1)S(1)}, bf16[512,1024]{1,0:T(8,128)(2,1)S(1)}, u32[]{:S(2)}, u32[]{:S(2)}) collective-permute-start(bf16[512,1024]{1,0:T(8,128)(2,1)S(1)} %get-tuple-element.48.refs_3_), channel_id=1, source_target_pairs={{0,8},{8,0},{16,24},{24,16},{1,9},{9,1},{17,25},{25,17},{2,10},{10... | collective-permute-start | bytes 3145736 | tf_op jit(solution)/shard_map/ppermute | solution.py:140
  276.3 25.2 %collective-permute-start.35 = (bf16[512,1024]{1,0:T(8,128)(2,1)S(1)}, bf16[512,1024]{1,0:T(8,128)(2,1)S(1)}, u32[]{:S(2)}, u32[]{:S(2)}) collective-permute-start(bf16[512,1024]{1,0:T(8,128)(2,1)S(1)} %get-tuple-element.49.refs_4_), channel_id=1, source_target_pairs={{0,8},{8,0},{16,24},{24,16},{1,9},{9,1},{17,25},{25,17},{2,10},{10... | collective-permute-start | bytes 3145736 | tf_op jit(solution)/shard_map/ppermute | solution.py:140
  276.8 25.3 %collective-permute-start.36 = (bf16[512,1024]{1,0:T(8,128)(2,1)S(1)}, bf16[512,1024]{1,0:T(8,128)(2,1)S(1)}, u32[]{:S(2)}, u32[]{:S(2)}) collective-permute-start(bf16[512,1024]{1,0:T(8,128)(2,1)S(1)} %get-tuple-element.50.refs_5_), channel_id=1, source_target_pairs={{0,8},{8,0},{16,24},{24,16},{1,9},{9,1},{17,25},{25,17},{2,10},{10... | collective-permute-start | bytes 3145736 | tf_op jit(solution)/shard_map/ppermute | solution.py:140
  279.8 29.7 %collective-permute-start.38 = (bf16[512,1024]{1,0:T(8,128)(2,1)S(1)}, bf16[512,1024]{1,0:T(8,128)(2,1)S(1)}, u32[]{:S(2)}, u32[]{:S(2)}) collective-permute-start(bf16[512,1024]{1,0:T(8,128)(2,1)S(1)} %shard_map.103.refs_6_), channel_id=1, source_target_pairs={{0,1},{1,0},{2,3},{3,2},{4,5},{5,4},{6,7},{7,6},{8,9},{9,8},{10,11... | collective-permute-start | bytes 3145736 | tf_op jit(solution)/shard_map/ppermute | solution.py:146
  299.5 12.5 %collective-permute-start.48 = (bf16[128,1024]{1,0:T(8,128)(2,1)S(1)}, bf16[128,1024]{1,0:T(8,128)(2,1)S(1)}, u32[]{:S(2)}, u32[]{:S(2)}) collective-permute-start(bf16[128,1024]{1,0:T(8,128)(2,1)S(1)} %slice.78), channel_id=1, source_target_pairs={{0,1},{1,0},{2,3},{3,2},{4,5},{5,4},{6,7},{7,6},{8,9},{9,8},{10,11... | collective-permute-start | bytes 786440 | tf_op jit(solution)/shard_map/ppermute | solution.py:146
  301.4 50.5 %collective-permute-start.23 = (bf16[512,1024]{1,0:T(8,128)(2,1)}, bf16[512,1024]{1,0:T(8,128)(2,1)}, u32[]{:S(2)}, u32[]{:S(2)}) collective-permute-start(bf16[512,1024]{1,0:T(8,128)(2,1)} %add_convert_fusion.4), channel_id=1, source_target_pairs={{0,2},{2,0},{4,6},{6,4},{1,3},{3,1},{5,7},{7,5},{8,10},{10,8},{12,... | collective-permute-start | bytes 3145736 | tf_op jit(solution)/shard_map/ppermute | solution.py:149
  301.5 50.4 %collective-permute-start.25 = (bf16[512,1024]{1,0:T(8,128)(2,1)}, bf16[512,1024]{1,0:T(8,128)(2,1)}, u32[]{:S(2)}, u32[]{:S(2)}) collective-permute-start(bf16[512,1024]{1,0:T(8,128)(2,1)} %add_convert_fusion.3), channel_id=1, source_target_pairs={{0,1},{1,0},{2,3},{3,2},{4,5},{5,4},{6,7},{7,6},{8,9},{9,8},{10,11... | collective-permute-start | bytes 3145736 | tf_op jit(solution)/shard_map/ppermute | solution.py:146
  302.1 34.5 %collective-permute-start.44 = (bf16[256,1024]{1,0:T(8,128)(2,1)S(1)}, bf16[256,1024]{1,0:T(8,128)(2,1)S(1)}, u32[]{:S(2)}, u32[]{:S(2)}) collective-permute-start(bf16[256,1024]{1,0:T(8,128)(2,1)S(1)} %slice.76), channel_id=1, source_target_pairs={{0,4},{2,6},{4,0},{6,2},{1,5},{3,7},{5,1},{7,3},{8,12},{10,14},{12... | collective-permute-start | bytes 1572872 | tf_op jit(solution)/shard_map/ppermute | solution.py:152
  309.5 38.9 %collective-permute-start.42 = (bf16[256,1024]{1,0:T(8,128)(2,1)}, bf16[256,1024]{1,0:T(8,128)(2,1)}, u32[]{:S(2)}, u32[]{:S(2)}) collective-permute-start(bf16[256,1024]{1,0:T(8,128)(2,1)} %slice.77), channel_id=1, source_target_pairs={{0,4},{2,6},{4,0},{6,2},{1,5},{3,7},{5,1},{7,3},{8,12},{10,14},{12... | collective-permute-start | bytes 1572872 | tf_op jit(solution)/shard_map/ppermute | solution.py:152
  312.0 56.8 %collective-permute-start.40 = (bf16[512,1024]{1,0:T(8,128)(2,1)S(1)}, bf16[512,1024]{1,0:T(8,128)(2,1)}, u32[]{:S(2)}, u32[]{:S(2)}) collective-permute-start(bf16[512,1024]{1,0:T(8,128)(2,1)S(1)} %get-tuple-element.55), channel_id=1, source_target_pairs={{0,1},{1,0},{2,3},{3,2},{4,5},{5,4},{6,7},{7,6},{8,9},{9,8},{10,11... | collective-permute-start | bytes 3145736 | tf_op jit(solution)/shard_map/ppermute | solution.py:146
  337.4 33.1 %collective-permute-start.39 = (bf16[512,1024]{1,0:T(8,128)(2,1)}, bf16[512,1024]{1,0:T(8,128)(2,1)}, u32[]{:S(2)}, u32[]{:S(2)}) collective-permute-start(bf16[512,1024]{1,0:T(8,128)(2,1)} %add_convert_fusion.1), channel_id=1, source_target_pairs={{0,2},{2,0},{4,6},{6,4},{1,3},{3,1},{5,7},{7,5},{8,10},{10,8},{12,... | collective-permute-start | bytes 3145736 | tf_op jit(solution)/shard_map/ppermute | solution.py:149
  348.4 18.8 %collective-permute-start.45 = (bf16[256,1024]{1,0:T(8,128)(2,1)S(1)}, bf16[256,1024]{1,0:T(8,128)(2,1)S(1)}, u32[]{:S(2)}, u32[]{:S(2)}) collective-permute-start(bf16[256,1024]{1,0:T(8,128)(2,1)S(1)} %fusion), channel_id=1, source_target_pairs={{0,1},{1,0},{2,3},{3,2},{4,5},{5,4},{6,7},{7,6},{8,9},{9,8},{10,11... | collective-permute-start | bytes 1572872 | tf_op jit(solution)/shard_map/ppermute | solution.py:146
  (35 other events, 748.4 us)

commit v3 on v2

--- a/solution.py
+++ b/solution.py
@@ -51,13 +51,14 @@
 SMEM = pl.BlockSpec(memory_space=pltpu.SMEM)
 
 
-def hidden_kernel(width, step, rows_ref, unit_ref, hidden_ref, turned_ref, silu_ref, rest_ref):
-    @pl.loop(0, rows_ref.shape[0] // step)
-    def _(at):
-        span = pl.ds(pl.multiple_of(at * step, step), step)
-        for group in range(unit_ref.shape[0] // (2 * width)):
-            units = slice(2 * group * width, 2 * (group + 1) * width)
-            sums = matmul(rows_ref[span], unit_ref[units], (1, 1))
+def hidden_kernel(width, rows, groups, *refs):
+    row_refs, unit_refs = refs[:rows], refs[rows : rows + groups]
+    hidden_ref, turned_ref, silu_ref, rest_ref = refs[rows + groups :]
+    step = row_refs[0].shape[0]
+    for at, row_ref in enumerate(row_refs):
+        span = slice(at * step, (at + 1) * step)
+        for group, unit_ref in enumerate(unit_refs):
+            sums = matmul(row_ref[...], unit_ref[...], (1, 1))
             silu_g, hidden, rest = gated(sums[:, :width], sums[:, width:])
             cols = slice(group * width, (group + 1) * width)
             hidden_ref[span, cols] = hidden.astype(BF16)
@@ -66,13 +67,14 @@
             rest_ref[span, cols] = rest.astype(BF16)
 
 
-def grads_kernel(width, step, rows_ref, down_ref, silu_ref, rest_ref, act_ref, turned_ref):
-    @pl.loop(0, rows_ref.shape[0] // step)
-    def _(at):
-        span = pl.ds(pl.multiple_of(at * step, step), step)
+def grads_kernel(width, rows, *refs):
+    row_refs, (down_ref, silu_ref, rest_ref, act_ref, turned_ref) = refs[:rows], refs[rows:]
+    step = row_refs[0].shape[0]
+    for at, row_ref in enumerate(row_refs):
+        span = slice(at * step, (at + 1) * step)
         for pair in range(down_ref.shape[0] // (2 * width)):
             units = slice(2 * pair * width, 2 * (pair + 1) * width)
-            back = matmul(rows_ref[span], down_ref[units], (1, 1))
+            back = matmul(row_ref[...], down_ref[units], (1, 1))
             for part, factor in enumerate((rest_ref, silu_ref)):
                 grads = back * factor[span, units].astype(F32)
                 for side in range(2):
@@ -83,15 +85,20 @@
                     turned_ref[low, span] = grad.T.astype(BF16)
 
 
-def weight_kernel(first, tile, turned_ref, rows_ref, away_ref, stay_ref):
-    half = away_ref.shape[0]
+def weight_kernel(first, tile, rows, *refs):
+    row_refs, (turned_ref, away_ref, stay_ref) = refs[:rows], refs[rows:]
+    half, step = away_ref.shape[0], row_refs[0].shape[0]
 
     @pl.loop(0, away_ref.shape[1] // tile)
     def _(index):
         cols = pl.ds(pl.multiple_of(index * tile, tile), tile)
-        right = rows_ref[:, pl.ds(pl.multiple_of(first + index * tile, tile), tile)]
-        away_ref[:, cols] = matmul(turned_ref[:half], right, (1, 0)).astype(BF16)
-        stay_ref[:, cols] = matmul(turned_ref[half:], right, (1, 0)).astype(BF16)
+        here = pl.ds(pl.multiple_of(first + index * tile, tile), tile)
+        for out_ref, low in ((away_ref, 0), (stay_ref, half)):
+            total = jnp.zeros((half, tile), F32)
+            for at, row_ref in enumerate(row_refs):
+                left = turned_ref[low : low + half, at * step : (at + 1) * step]
+                total = total + matmul(left, row_ref[:, here], (1, 0))
+            out_ref[:, cols] = total.astype(BF16)
 
 
 def block_kernel(first, places, sides, added, *refs):
@@ -115,14 +122,36 @@
         outs[at][...] = total.astype(BF16)
 
 
-def halves_kernel(at_ref, gate_ref, up_ref, mine_ref, theirs_ref):
-    width = gate_ref.shape[1] // 2
+def halves_kernel(at_ref, gate_ref, up_ref, down_ref, mine_ref, down_mine_ref, theirs_ref):
+    width = down_mine_ref.shape[0]
+    first = at_ref[0] == 0
     for part, ref in enumerate((gate_ref, up_ref)):
         span = slice(part * width, (part + 1) * width)
         low, high = ref[:, :width].astype(F32).T.astype(BF16), ref[:, width:].astype(F32).T.astype(BF16)
-        first = at_ref[0] == 0
         mine_ref[span] = jnp.where(first, low, high)
         theirs_ref[span] = jnp.where(first, high, low)
+    low, high = down_ref[:width], down_ref[width:]
+    down_mine_ref[...] = jnp.where(first, low, high)
+    theirs_ref[2 * width :] = jnp.where(first, high, low)
+
+
+def beside_kernel(first, left_ref, right_ref, out_ref):
+    rows, half = left_ref.shape
+    out_ref[:, :half] = left_ref[...]
+    out_ref[:, half:] = right_ref[first : first + rows]
+
+
+def halves_beside_kernel(left_ref, top_ref, low_ref, out_ref):
+    half, step = left_ref.shape[1], top_ref.shape[0]
+    out_ref[:, :half] = left_ref[...]
+    out_ref[:step, half:] = top_ref[...]
+    out_ref[step:, half:] = low_ref[...]
+
+
+def stack_kernel(*refs):
+    out_ref, step = refs[-1], refs[0].shape[0]
+    for at, ref in enumerate(refs[:-1]):
+        out_ref[at * step : (at + 1) * step] = ref[...]
 
 
 def finish_kernel(at_ref, mine_ref, theirs_ref, gate_ref, up_ref):
@@ -135,6 +164,15 @@
         out_ref[:, width:] = jnp.where(first, theirs, mine)
 
 
+def beside(left, right, first=0, after=()):
+    out = [shape(left.shape[0], 2 * left.shape[1])]
+    return call(functools.partial(beside_kernel, first), out, 0, [left, right], after)[0]
+
+
+def stacked(parts, after=()):
+    return call(stack_kernel, [shape(len(parts) * parts[0].shape[0], parts[0].shape[1])], 0, parts, after)[0]
+
+
 class Square:
     def core(self, array):
         return lax.ppermute(array, "inp", [(at, at ^ 1) for at in range(4)])
@@ -150,23 +188,6 @@
 
     def far(self, array):
         return lax.ppermute(array, "wt", [(at, at ^ 2) for at in range(4)])
-
-    def gather(self, array, split):
-        step = array.shape[1]
-        own = array.reshape(2 * step, array.shape[2])
-        by_near, by_other = self.near(own), self.other(own)
-        if split:
-            corner = jnp.concatenate([self.other(by_near[:step]), self.near(by_other[step:])])
-        else:
-            corner = self.other(by_near)
-        pieces = [own, by_other, by_near, corner]
-        pieces += [self.core(piece) for piece in pieces]
-        rows = [jnp.concatenate(pieces[at : at + 2], axis=1) for at in range(0, 8, 2)]
-        return jnp.concatenate(rows)
-
-    def gather_units(self, own):
-        by_far = self.far(own)
-        return [self.across(own), self.across(by_far), own, by_far]
 
     def scatter_units(self, away, stay):
         total = stay.astype(F32) + self.across(away).astype(F32)
@@ -203,99 +224,121 @@
         second = self.products(left, rights, [(0, 1), (1, 0), (0, 0)], after=list(first.values()))
         return first | second
 
-    def scatter_near(self, left, rights, far, after=()):
-        far = {place: self.core(block) for place, block in far.items()}
-        sums = self.products(left, rights, [(1, 1)], far, after)
-        sums |= self.products(left, rights, [(0, 1), (1, 0), (0, 0)], far, list(sums.values()))
-        return sums
-
-    def scatter_end(self, sums, split):
-        corner = sums[1, 1]
-        step = corner.shape[0] // 2
-        if split:
-            by_other = self.other(corner[:step]).astype(F32)
-            by_near = self.near(corner[step:]).astype(F32)
-            zeros = jnp.zeros_like(by_other)
-            to_near = (sums[1, 0].astype(F32) + jnp.concatenate([by_other, zeros])).astype(BF16)
-            to_other = (sums[0, 1].astype(F32) + jnp.concatenate([zeros, by_near])).astype(BF16)
-        else:
-            to_near = (sums[1, 0].astype(F32) + self.other(corner).astype(F32)).astype(BF16)
-            to_other = sums[0, 1]
-        total = sums[0, 0].astype(F32) + self.near(to_near).astype(F32) + self.other(to_other).astype(F32)
-        return total.astype(BF16).reshape(2, step, corner.shape[1])
+    def near_first(self, left, rights, far, after):
+        return self.products(left, rights, [(1, 1)], far, after)
+
+    def near_rest(self, left, rights, far, after):
+        return self.products(left, rights, [(0, 1), (1, 0), (0, 0)], far, after)
 
     def layer(self, tokens, gate_weight, up_weight, down_weight, cotangent):
-        at_out = lax.axis_index("out").astype(jnp.int32)
+        at_out = lax.axis_index("out").astype(jnp.int32).reshape(1)
         half, width = gate_weight.shape[0], gate_weight.shape[1] // 2
-        pair = [shape(2 * width, half)] * 2
-        mine, theirs = call(halves_kernel, pair, 0, [at_out.reshape(1), gate_weight, up_weight], specs=[SMEM, VMEM, VMEM])
+        mine, down_mine, theirs = call(
+            halves_kernel,
+            [shape(2 * width, half), shape(width, half), shape(3 * width, half)],
+            0,
+            [at_out, gate_weight, up_weight, down_weight],
+            specs=[SMEM, VMEM, VMEM, VMEM],
+        )
         theirs = self.other(theirs)
-        down_mine = lax.dynamic_slice_in_dim(down_weight, at_out * width, width, 0)
-        down_theirs = self.other(lax.dynamic_slice_in_dim(down_weight, (1 - at_out) * width, width, 0))
-        down_own = jnp.concatenate([down_mine, down_theirs], axis=1)
-
-        rows_in = self.gather(tokens, False)
-        sides = [jnp.concatenate(self.gather_units(own)) for own in (mine, theirs)]
-        gate_up = jnp.concatenate(sides, axis=1)
-        rows_cot = self.gather(cotangent, True)
-        down = jnp.concatenate(self.gather_units(down_own))
-
-        count, units = rows_in.shape[0], down.shape[0]
-        step = count // 4
+        step = tokens.shape[1]
+        tok, cot = tokens.reshape(2 * step, half), cotangent.reshape(2 * step, half)
+
+        tok_near, tok_other = self.near(tok), self.other(tok)
+        own_units = beside(mine, theirs)
+        far_units = self.far(own_units)
+        tok_corner = self.other(tok_near)
+        tok_top = beside(tok, tok_other)
+        across_units = self.across(own_units)
+        own_down = beside(down_mine, theirs, 2 * width, [far_units, across_units])
+        far_down = self.far(own_down)
+        unit_groups = [across_units, self.across(far_units), own_units, far_units]
+        (cot,) = call(stack_kernel, [shape(*cot.shape)], 0, [cot], after=[tok_near, tok_other])
+        cot_near, cot_other = self.near(cot), self.other(cot)
+        tok_low = beside(tok_near, tok_corner)
+        rows_in = [tok_top, tok_low, self.core(tok_top), self.core(tok_low)]
+        cot_corner = [self.other(cot_near[:step]), self.near(cot_other[step:])]
+        cot_top = beside(cot, cot_other)
+        (cot_low,) = call(halves_beside_kernel, [shape(2 * step, 2 * half)], 0, [cot_near, *cot_corner])
+        rows_cot = [cot_top, cot_low, self.core(cot_top), self.core(cot_low)]
+        down_groups = [self.across(own_down), self.across(far_down), own_down, far_down]
+
+        count, units = 8 * step, 4 * width
         hidden, hidden_turned, silu, rest = call(
-            functools.partial(hidden_kernel, width, step),
+            functools.partial(hidden_kernel, width, 4, 4),
             [shape(count, units), shape(units, count), shape(count, units), shape(count, units)],
             8 * count * units * half,
-            [rows_in, gate_up],
+            [*rows_in, *unit_groups],
+            after=[far_down, cot_top],
             limit=28,
         )
+        down = stacked(down_groups)
+        down_sides = [(down, 0, half), (down, 1, half)]
+        output_far = self.scatter_far(hidden, down_sides)
         down_terms = call(
-            functools.partial(weight_kernel, 0, 256),
+            functools.partial(weight_kernel, 0, 256, 4),
             [shape(units // 2, 2 * half)] * 2,
             4 * count * units * half,
-            [hidden_turned, rows_cot],
+            [*rows_cot, hidden_turned],
+            list(output_far.values()),
         )
         down_sum = self.scatter_units(*down_terms)
-        down_sides = [(down, 0, half), (down, 1, half)]
-        output_far = self.scatter_far(hidden, down_sides)
         act, act_turned = call(
-            functools.partial(grads_kernel, width, step),
+            functools.partial(grads_kernel, width, 4),
             [shape(count, 2 * units), shape(2 * units, count)],
             4 * count * units * half,
-            [rows_cot, down, silu, rest],
-            after=list(output_far.values()),
+            [*rows_cot, down, silu, rest],
+            after=down_terms,
             limit=28,
         )
-        output_sums = self.scatter_near(hidden, down_sides, output_far)
+        output_far = {place: self.core(block) for place, block in output_far.items()}
+        sums = self.near_first(hidden, down_sides, output_far, [act])
+        corner = sums[1, 1]
+        by_other, by_near = self.other(corner[:step]), self.near(corner[step:])
+        sums |= self.near_rest(hidden, down_sides, output_far, [corner])
 
         def unit_terms(side, after):
             return call(
-                functools.partial(weight_kernel, side * half, 256),
+                functools.partial(weight_kernel, side * half, 256, 4),
                 [shape(units, half)] * 2,
                 4 * count * units * half,
-                [act_turned, rows_in],
+                [*rows_in, act_turned],
                 after=after,
             )
 
-        other_terms = unit_terms(1, list(output_sums.values()))
+        other_terms = unit_terms(1, [sums[0, 0]])
         other_sum = self.scatter_units(*other_terms).astype(BF16)
+        gate_up = stacked(unit_groups, [other_terms[0]])
         unit_sides = [(gate_up, 0, half), (gate_up, 1, half)]
-        grads_far = self.scatter_far(act, unit_sides, other_terms)
+        grads_far = self.scatter_far(act, unit_sides, [by_other, by_near])
+        zeros = jnp.zeros((step, half), F32)
+        to_near = (sums[1, 0].astype(F32) + jnp.concatenate([by_other.astype(F32), zeros])).astype(BF16)
+        to_other = (sums[0, 1].astype(F32) + jnp.concatenate([zeros, by_near.astype(F32)])).astype(BF16)
+        by_near, by_other = self.near(to_near), self.other(to_other)
+        total = sums[0, 0].astype(F32) + by_near.astype(F32) + by_other.astype(F32)
+        output = total.astype(BF16).reshape(2, step, half)
+
         own_terms = unit_terms(0, list(grads_far.values()))
         own_sum = self.scatter_units(*own_terms).astype(BF16)
-        grads_sums = self.scatter_near(act, unit_sides, grads_far, own_terms)
-        output = self.scatter_end(output_sums, True)
-        grad_tokens = self.scatter_end(grads_sums, False)
+        grads_far = {place: self.core(block) for place, block in grads_far.items()}
+        sums = self.near_first(act, unit_sides, grads_far, [own_terms[0], by_near, by_other])
+        by_other = self.other(sums[1, 1])
+        sums |= self.near_rest(act, unit_sides, grads_far, [sums[1, 1]])
+        to_near = (sums[1, 0].astype(F32) + by_other.astype(F32)).astype(BF16)
+        by_near, by_other = self.near(to_near), self.other(sums[0, 1])
+        total = sums[0, 0].astype(F32) + by_near.astype(F32) + by_other.astype(F32)
+        grad_tokens = total.astype(BF16).reshape(2, step, half)
 
         down_back = self.other(down_sum[:, half:].astype(BF16))
         units_back = self.other(other_sum)
         mine, theirs = down_sum[:, :half], down_back.astype(F32)
-        grad_down = jnp.where(at_out == 0, jnp.concatenate([mine, theirs]), jnp.concatenate([theirs, mine]))
+        first = at_out[0] == 0
+        grad_down = jnp.where(first, jnp.concatenate([mine, theirs]), jnp.concatenate([theirs, mine]))
         grad_gate, grad_up = call(
             finish_kernel,
             [shape(half, 2 * width, dtype=F32)] * 2,
             0,
-            [at_out.reshape(1), own_sum, units_back],
+            [at_out, own_sum, units_back],
             specs=[SMEM, VMEM, VMEM],
         )
         return (output, grad_tokens, grad_gate, grad_up, grad_down)

time: 377 us -> 344 us (0.912)
  other arithmetic: 58.6 us -> 10.6 us
  waiting for transfers between devices: 186 us -> 211 us
  starting transfers between devices: 50.8 us -> 38.5 us
  local copies, waits for them, and re-layouts: 13.6 us -> 21.2 us
    ppermute x6, waiting for transfers between devices: 1.68 us -> 53.6 us  [near(): return lax.ppermute(array, 'wt', [(at, at ^ 1) for at in range(4)])]
    ppermute x6 -> x5, waiting for transfers between devices: 113 us -> 63 us  [far(): return lax.ppermute(array, 'wt', [(at, at ^ 2) for at in range(4)])]
    concatenate x5 -> x0, other arithmetic: 43.7 us -> none  [the longest x2 22.9 us: gather(): return jnp.concatenate(rows)]
    ppermute x12 -> x11, waiting for transfers between devices: 40.7 us -> 64.2 us  [other(): return lax.ppermute(array, 'out', [(0, 1), (1, 0)])]
    unnamed x69 -> x108, local copies, waits for them, and re-layouts: 10.1 us -> 20 us
    ppermute x6 -> x5, starting transfers between devices: 12.8 us -> 6.31 us  [far(): return lax.ppermute(array, 'wt', [(at, at ^ 2) for at in range(4)])]
    convert_element_type x5, other arithmetic: 10.2 us -> 5.34 us  [the longest x1 1.63 us: layer(): to_near = (sums[1, 0].astype(F32) + by_other.astype(F32)).astype(BF16)]
    ppermute x9 -> x7, starting transfers between devices: 11.7 us -> 7.17 us  [across(): return lax.ppermute(array, 'inp', [(at, at ^ 2) for at in range(4)])]
  transfers between devices with their start and end apart: 49 -> 41, of which waited for: 13 -> 16; matrix products, arithmetic and copies ran while one was open for 16% -> 3% of each run, Pallas kernels for 17% -> 18%
where the time goes in v3:
time: 344 us
  waiting for transfers between devices  211 us (61%)
  Pallas kernels  61.1 us (18%)
  starting transfers between devices  38.5 us (11%)
  local copies, waits for them, and re-layouts  21.2 us (6%)
  other arithmetic  10.6 us (3%)
    ppermute x11, waiting for transfers between devices, other(): return lax.ppermute(array, 'out', [(0, 1), (1, 0)])  64.2 us
    ppermute x5, waiting for transfers between devices, far(): return lax.ppermute(array, 'wt', [(at, at ^ 2) for at in range(4)])  63 us
    pallas_call x24, Pallas kernels, call(): pl.pallas_call(body, out_shape=list(outs), in_specs=[*specs, *[pl.BlockSp...  61.1 us
    ppermute x6, waiting for transfers between devices, near(): return lax.ppermute(array, 'wt', [(at, at ^ 1) for at in range(4)])  53.6 us
    ppermute x7, waiting for transfers between devices, across(): return lax.ppermute(array, 'inp', [(at, at ^ 2) for at in range(4)])  30 us
    unnamed x108, local copies, waits for them, and re-layouts  20 us
    ppermute x11, starting transfers between devices, other(): return lax.ppermute(array, 'out', [(0, 1), (1, 0)])  14.5 us
    ppermute x6, starting transfers between devices, near(): return lax.ppermute(array, 'wt', [(at, at ^ 1) for at in range(4)])  8.26 us
  transfers between devices with their start and end apart: 41, of which 16 were waited for; matrix products, arithmetic and copies ran while one was open for 3% of the time, Pallas kernels for 18%

profile of v3, /device:TPU:0, one launch (start us, length us, event | category | flops | bytes accessed | tf_op | source)
XLA Modules:
  0.0 343.8 jit_solution(8358921426453638279)
XLA Ops:
  0.6 3.1 collective-permute-start.1
  9.4 17.8 %collective-permute-done.1.refs_0_.refs_1_ = bf16[512,1024]{1,0:T(8,128)(2,1)} collective-permute-done((bf16[512,1024]{1,0:T(8,128)(2,1)}, bf16[512,1024]{1,0:T(8,128)(2,1)}, u32[]{:S(2)}, u32[]{:S(2)}) %collective-permute-start.1) | collective-permute-done | bytes 1048608 | tf_op jit(solution)/shard_map/ppermute | solution.py:187
  27.2 1.7 collective-permute-start.2
  28.9 18.0 %collective-permute-done.5.refs_1_ = bf16[384,1024]{1,0:T(8,128)(2,1)S(1)} collective-permute-done((bf16[384,1024]{1,0:T(8,128)(2,1)S(1)}, bf16[384,1024]{1,0:T(8,128)(2,1)S(1)}, u32[]{:S(2)}, u32[]{:S(2)}) %collective-permute-start.5) | collective-permute-done | bytes 786464 | tf_op jit(solution)/shard_map/ppermute | solution.py:184
  48.5 2.6 collective-permute-start.7
  55.4 13.9 %collective-permute-done.2.refs_1_ = bf16[512,1024]{1,0:T(8,128)(2,1)S(1)} collective-permute-done((bf16[512,1024]{1,0:T(8,128)(2,1)}, bf16[512,1024]{1,0:T(8,128)(2,1)S(1)}, u32[]{:S(2)}, u32[]{:S(2)}) %collective-permute-start.2) | collective-permute-done | bytes 1048608 | tf_op jit(solution)/shard_map/ppermute | solution.py:184
  71.3 22.5 %collective-permute-done.7.refs_2_.refs_7_.refs_3_ = bf16[256,2048]{1,0:T(8,128)(2,1)S(1)} collective-permute-done((bf16[256,2048]{1,0:T(8,128)(2,1)S(1)}, bf16[256,2048]{1,0:T(8,128)(2,1)S(1)}, u32[]{:S(2)}, u32[]{:S(2)}) %collective-permute-start.7) | collective-permute-done | bytes 1048608 | tf_op jit(solution)/shard_map/ppermute | solution.py:190
  94.0 2.2 collective-permute-done.17.refs_0_
  96.6 1.7 collective-permute-start.18
  98.3 20.3 %collective-permute-done.9.refs_8_.refs_3_ = bf16[128,2048]{1,0:T(8,128)(2,1)S(1)} collective-permute-done((bf16[128,2048]{1,0:T(8,128)(2,1)S(1)}, bf16[128,2048]{1,0:T(8,128)(2,1)S(1)}, u32[]{:S(2)}, u32[]{:S(2)}) %collective-permute-start.9) | collective-permute-done | bytes 524320 | tf_op jit(solution)/shard_map/ppermute | solution.py:190
  120.9 11.7 %collective-permute-done.19.refs_2_ = bf16[256,1024]{1,0:T(8,128)(2,1)S(1)} collective-permute-done((bf16[256,1024]{1,0:T(8,128)(2,1)S(1)}, bf16[256,1024]{1,0:T(8,128)(2,1)S(1)}, u32[]{:S(2)}, u32[]{:S(2)}) %collective-permute-start.19) | collective-permute-done | bytes 524320 | tf_op jit(solution)/shard_map/ppermute | solution.py:187
  133.6 21.4 %collective-permute-done.8.refs_5_.refs_1_ = bf16[256,2048]{1,0:T(8,128)(2,1)S(1)} collective-permute-done((bf16[256,2048]{1,0:T(8,128)(2,1)S(1)}, bf16[256,2048]{1,0:T(8,128)(2,1)S(1)}, u32[]{:S(2)}, u32[]{:S(2)}) %collective-permute-start.8) | collective-permute-done | bytes 1048608 | tf_op jit(solution)/shard_map/ppermute | solution.py:181
  155.1 9.7 %shard_map.99 = (bf16[2048,512]{1,0:T(8,128)(2,1)S(1)}, bf16[512,2048]{1,0:T(8,128)(2,1)S(1)}, bf16[2048,512]{1,0:T(8,128)(2,1)S(1)}, bf16[2048,512]{1,0:T(8,128)(2,1)S(1)}) custom-call(bf16[512,2048]{1,0:T(8,128)(2,1)S(1)} %shard_map.92.refs_0_, bf16[512,2048]{1,0:T(8,128)(2,1)S(1)} %shard_map.93.refs_1_, ...), custom_call_target="tpu_custom_call" | custom-call | flops 8589934592 | bytes 20971520 | tf_op jit(solution)/shard_map/pallas_call | solution.py:38
  166.9 2.3 shard_map.102
  170.3 5.7 %shard_map.104 = (bf16[256,2048]{1,0:T(8,128)(2,1)S(1)}, bf16[256,2048]{1,0:T(8,128)(2,1)S(1)}) custom-call(bf16[512,2048]{1,0:T(8,128)(2,1)S(1)} %shard_map.98.refs_9_.refs_0_, bf16[512,2048]{1,0:T(8,128)(2,1)S(1)} %shard_map.103.refs_1_, bf16[512,2048]{1,0:T(8,128)(2,1)S(1)} %collective-permute-done.20.refs_2_, ...), custom_call_target="tpu_custom_call" | custom-call | flops 4294967296 | bytes 12582912 | tf_op jit(solution)/shard_map/pallas_call | solution.py:38
  176.6 1.6 copy-done.7
  178.2 1.6 copy-done.9
  179.8 1.6 copy-done.29
  181.4 1.6 copy-done.31
  183.0 1.6 copy-done.33
  184.6 1.6 copy-done.35
  186.2 5.4 %shard_map.105 = (bf16[2048,1024]{1,0:T(8,128)(2,1)S(1)}, bf16[1024,2048]{1,0:T(8,128)(2,1)S(1)}) custom-call(bf16[512,2048]{1,0:T(8,128)(2,1)S(1)} %copy-done.7, bf16[512,2048]{1,0:T(8,128)(2,1)S(1)} %copy-done.9, bf16[512,2048]{1,0:T(8,128)(2,1)S(1)} %copy-done.29, bf16[512,2048]{1,0:T(8,128)(2,1)S(1)} %copy-done.31, ...), custom_call_target="tpu_custom_call" | custom-call | flops 4294967296 | bytes 23068672 | tf_op jit(solution)/shard_map/pallas_call | solution.py:38
  191.7 3.0 shard_map.106.refs_6_
  194.7 1.8 collective-permute-start.24
  197.5 1.6 collective-permute-start.22
  199.1 1.9 copy-done.39
  201.1 3.8 %shard_map.107 = (bf16[512,1024]{1,0:T(8,128)(2,1)S(1)}, bf16[512,1024]{1,0:T(8,128)(2,1)S(1)}, bf16[512,1024]{1,0:T(8,128)(2,1)S(1)}) custom-call(bf16[2048,512]{1,0:T(8,128)(2,1)S(1)} %get-tuple-element.37.refs_0_, bf16[512,2048]{1,0:T(8,128)(2,1)S(1)} %shard_map.100.refs_1_.refs_2_.refs_4_, bf16[512,2048]{1,0:T(8,128)(2,1)S(1)} %shard_map.100.refs_1_.refs_2_.refs_4_, ...), custom_call_target="tpu_custom_call" | custom-call | flops 1610612736 | bytes 12582912 | tf_op jit(solution)/shard_map/pallas_call | solution.py:38
  205.0 5.0 %shard_map.108 = (bf16[512,1024]{1,0:T(8,128)(2,1)S(1)}, bf16[512,1024]{1,0:T(8,128)(2,1)S(1)}) custom-call(bf16[512,2048]{1,0:T(8,128)(2,1)S(1)} %shard_map.92.refs_0_, bf16[512,2048]{1,0:T(8,128)(2,1)S(1)} %copy-done.5, bf16[512,2048]{1,0:T(8,128)(2,1)S(1)} %copy-done.24, bf16[512,2048]{1,0:T(8,128)(2,1)S(1)} %copy-done.26, ...), custom_call_target="tpu_custom_call" | custom-call | flops 4294967296 | bytes 14680064 | tf_op jit(solution)/shard_map/pallas_call | solution.py:38
  213.7 2.0 shard_map.110.refs_3_.refs_5_
  215.8 1.6 convert_add_fusion
  217.5 2.7 collective-permute-start.39
  220.2 5.4 %shard_map.111 = (bf16[512,1024]{1,0:T(8,128)(2,1)}, bf16[512,1024]{1,0:T(8,128)(2,1)}, bf16[512,1024]{1,0:T(8,128)(2,1)}) custom-call(bf16[2048,1024]{1,0:T(8,128)(2,1)S(1)} %get-tuple-element.46.refs_3_.refs_0_, bf16[1024,2048]{1,0:T(8,128)(2,1)S(1)} %shard_map.109.refs_1_.refs_2_, bf16[1024,2048]{1,0:T(8,128)(2,1)S(1)} %shard_map.109.refs_1_.refs_2_, ...), custom_call_target="tpu_custom_call" | custom-call | flops 3221225472 | bytes 15728640 | tf_op jit(solution)/shard_map/pallas_call | solution.py:38
  225.6 5.0 %shard_map.112 = (bf16[512,1024]{1,0:T(8,128)(2,1)S(1)}, bf16[512,1024]{1,0:T(8,128)(2,1)S(1)}) custom-call(bf16[512,2048]{1,0:T(8,128)(2,1)S(1)} %shard_map.92.refs_0_, bf16[512,2048]{1,0:T(8,128)(2,1)S(1)} %copy-done.5, bf16[512,2048]{1,0:T(8,128)(2,1)S(1)} %copy-done.24, bf16[512,2048]{1,0:T(8,128)(2,1)S(1)} %copy-done.27, ...), custom_call_target="tpu_custom_call" | custom-call | flops 4294967296 | bytes 14680064 | tf_op jit(solution)/shard_map/pallas_call | solution.py:38
  230.6 5.7 %collective-permute-done.25.refs_5_ = bf16[512,1024]{1,0:T(8,128)(2,1)S(1)} collective-permute-done((bf16[512,1024]{1,0:T(8,128)(2,1)S(1)}, bf16[512,1024]{1,0:T(8,128)(2,1)S(1)}, u32[]{:S(2)}, u32[]{:S(2)}) %collective-permute-start.25) | collective-permute-done | bytes 1048608 | tf_op jit(solution)/shard_map/ppermute | solution.py:184
  236.4 11.9 %collective-permute-done.23.refs_4_ = bf16[512,1024]{1,0:T(8,128)(2,1)S(1)} collective-permute-done((bf16[512,1024]{1,0:T(8,128)(2,1)S(1)}, bf16[512,1024]{1,0:T(8,128)(2,1)S(1)}, u32[]{:S(2)}, u32[]{:S(2)}) %collective-permute-start.23) | collective-permute-done | bytes 1048608 | tf_op jit(solution)/shard_map/ppermute | solution.py:187
  248.8 1.7 shard_map.113.refs_6_
  254.8 26.6 %collective-permute-done.40 = bf16[128,1024]{1,0:T(8,128)(2,1)S(1)} collective-permute-done((bf16[128,1024]{1,0:T(8,128)(2,1)}, bf16[128,1024]{1,0:T(8,128)(2,1)S(1)}, u32[]{:S(2)}, u32[]{:S(2)}) %collective-permute-start.40) | collective-permute-done | bytes 262176 | tf_op jit(solution)/shard_map/ppermute | solution.py:184
  282.4 1.8 convert_add_fusion.1
  285.9 6.5 %shard_map.114 = (bf16[512,1024]{1,0:T(8,128)(2,1)S(1)}, bf16[512,1024]{1,0:T(8,128)(2,1)S(1)}, bf16[512,1024]{1,0:T(8,128)(2,1)S(1)}) custom-call(bf16[2048,1024]{1,0:T(8,128)(2,1)S(1)} %copy-done.3, bf16[1024,2048]{1,0:T(8,128)(2,1)S(1)} %copy-done.1, bf16[1024,2048]{1,0:T(8,128)(2,1)S(1)} %copy-done.1, bf16[512,1024]{1,0:T(8,128)(2,1)} %collective-permute-done.26.refs_3_, ...), custom_call_target="tpu_custom_call" | custom-call | flops 3221225472 | bytes 18874368 | tf_op jit(solution)/shard_map/pallas_call | solution.py:38
  293.9 1.6 add_convert_fusion.1
  295.6 2.6 collective-permute-start.31
  298.1 7.8 %collective-permute-done.33 = bf16[512,1024]{1,0:T(8,128)(2,1)S(1)} collective-permute-done((bf16[512,1024]{1,0:T(8,128)(2,1)}, bf16[512,1024]{1,0:T(8,128)(2,1)S(1)}, u32[]{:S(2)}, u32[]{:S(2)}) %collective-permute-start.33) | collective-permute-done | bytes 1048608 | tf_op jit(solution)/shard_map/ppermute | solution.py:181
  306.9 3.4 collective-permute-done.36
  311.9 1.6 add_convert_fusion.2
  313.5 16.8 %collective-permute-done.34 = bf16[256,1024]{1,0:T(8,128)(2,1)S(1)} collective-permute-done((bf16[256,1024]{1,0:T(8,128)(2,1)S(1)}, bf16[256,1024]{1,0:T(8,128)(2,1)S(1)}, u32[]{:S(2)}, u32[]{:S(2)}) %collective-permute-start.34) | collective-permute-done | bytes 524320 | tf_op jit(solution)/shard_map/ppermute | solution.py:190
  330.5 1.6 shard_map.115
  332.1 10.1 %collective-permute-done.31 = bf16[512,1024]{1,0:T(8,128)(2,1)S(1)} collective-permute-done((bf16[512,1024]{1,0:T(8,128)(2,1)S(1)}, bf16[512,1024]{1,0:T(8,128)(2,1)S(1)}, u32[]{:S(2)}, u32[]{:S(2)}) %collective-permute-start.31) | collective-permute-done | bytes 1048608 | tf_op jit(solution)/shard_map/ppermute | solution.py:187
  342.2 1.6 add_convert_fusion
  (188 shorter events, 37.7 us)
Async XLA Ops:
  0.6 26.6 %collective-permute-start.1 = (bf16[512,1024]{1,0:T(8,128)(2,1)}, bf16[512,1024]{1,0:T(8,128)(2,1)}, u32[]{:S(2)}, u32[]{:S(2)}) collective-permute-start(bf16[512,1024]{1,0:T(8,128)(2,1)} %bitcast.6), channel_id=1, source_target_pairs={{0,2},{2,0},{4,6},{6,4},{1,3},{3,1},{5,7},{7,5},{8,10},{10,8},{12,... | collective-permute-start | bytes 3145736 | tf_op jit(solution)/shard_map/ppermute | solution.py:187
  3.7 47.4 %collective-permute-start = (bf16[512,1024]{1,0:T(8,128)(2,1)}, bf16[512,1024]{1,0:T(8,128)(2,1)S(1)}, u32[]{:S(2)}, u32[]{:S(2)}) collective-permute-start(bf16[512,1024]{1,0:T(8,128)(2,1)} %bitcast.7), channel_id=1, source_target_pairs={{0,1},{1,0},{2,3},{3,2},{4,5},{5,4},{6,7},{7,6},{8,9},{9,8},{10,11... | collective-permute-start | bytes 3145736 | tf_op jit(solution)/shard_map/ppermute | solution.py:184
  5.2 45.9 %copy-start.40 = (bf16[2,256,1024]{2,1,0:T(8,128)(2,1)S(1)}, bf16[2,256,1024]{2,1,0:T(8,128)(2,1)}, u32[]{:S(2)}) copy-start(bf16[2,256,1024]{2,1,0:T(8,128)(2,1)} %param.9) | copy-start | bytes 3145732
  8.9 38.0 %collective-permute-start.5 = (bf16[384,1024]{1,0:T(8,128)(2,1)S(1)}, bf16[384,1024]{1,0:T(8,128)(2,1)S(1)}, u32[]{:S(2)}, u32[]{:S(2)}) collective-permute-start(bf16[384,1024]{1,0:T(8,128)(2,1)S(1)} %get-tuple-element.35), channel_id=1, source_target_pairs={{0,1},{1,0},{2,3},{3,2},{4,5},{5,4},{6,7},{7,6},{8,9},{9,8},{10,11... | collective-permute-start | bytes 2359304 | tf_op jit(solution)/shard_map/ppermute | solution.py:184
  27.2 42.1 %collective-permute-start.2 = (bf16[512,1024]{1,0:T(8,128)(2,1)}, bf16[512,1024]{1,0:T(8,128)(2,1)S(1)}, u32[]{:S(2)}, u32[]{:S(2)}) collective-permute-start(bf16[512,1024]{1,0:T(8,128)(2,1)} %collective-permute-done.1.refs_0_.refs_1_), channel_id=1, source_target_pairs={{0,1},{1,0},{2,3},{3,2},{4,5},{5,4},{6,7},{7,6},{8,9},{9,8},{10,11... | collective-permute-start | bytes 3145736 | tf_op jit(solution)/shard_map/ppermute | solution.py:184
  46.9 108.1 %copy-start.12 = (bf16[256,2048]{1,0:T(8,128)(2,1)}, bf16[256,2048]{1,0:T(8,128)(2,1)S(1)}, u32[]{:S(2)}) copy-start(bf16[256,2048]{1,0:T(8,128)(2,1)S(1)} %shard_map.95.refs_6_.refs_2_) | copy-start | bytes 3145732
  47.0 23.8 %collective-permute-start.6 = (bf16[256,2048]{1,0:T(8,128)(2,1)S(1)}, bf16[256,2048]{1,0:T(8,128)(2,1)S(1)}, u32[]{:S(2)}, u32[]{:S(2)}) collective-permute-start(bf16[256,2048]{1,0:T(8,128)(2,1)S(1)} %shard_map.95.refs_6_.refs_2_), channel_id=1, source_target_pairs={{0,16},{8,24},{16,0},{24,8},{1,17},{9,25},{17,1},{25,9},{2,18},{10... | collective-permute-start | bytes 3145736 | tf_op jit(solution)/shard_map/ppermute | solution.py:181
  48.5 45.3 %collective-permute-start.7 = (bf16[256,2048]{1,0:T(8,128)(2,1)S(1)}, bf16[256,2048]{1,0:T(8,128)(2,1)S(1)}, u32[]{:S(2)}, u32[]{:S(2)}) collective-permute-start(bf16[256,2048]{1,0:T(8,128)(2,1)S(1)} %shard_map.95.refs_6_.refs_2_), channel_id=1, source_target_pairs={{0,4},{2,6},{4,0},{6,2},{1,5},{3,7},{5,1},{7,3},{8,12},{10,14},{12... | collective-permute-start | bytes 3145736 | tf_op jit(solution)/shard_map/ppermute | solution.py:190
  52.1 44.1 %collective-permute-start.17 = (bf16[512,1024]{1,0:T(8,128)(2,1)S(1)}, bf16[512,1024]{1,0:T(8,128)(2,1)S(1)}, u32[]{:S(2)}, u32[]{:S(2)}) collective-permute-start(bf16[512,1024]{1,0:T(8,128)(2,1)S(1)} %shard_map.97.refs_0_), channel_id=1, source_target_pairs={{0,2},{2,0},{4,6},{6,4},{1,3},{3,1},{5,7},{7,5},{8,10},{10,8},{12,... | collective-permute-start | bytes 3145736 | tf_op jit(solution)/shard_map/ppermute | solution.py:187
  52.5 44.1 %collective-permute-start.10 = (bf16[512,1024]{1,0:T(8,128)(2,1)S(1)}, bf16[512,1024]{1,0:T(8,128)(2,1)S(1)}, u32[]{:S(2)}, u32[]{:S(2)}) collective-permute-start(bf16[512,1024]{1,0:T(8,128)(2,1)S(1)} %shard_map.97.refs_0_), channel_id=1, source_target_pairs={{0,1},{1,0},{2,3},{3,2},{4,5},{5,4},{6,7},{7,6},{8,9},{9,8},{10,11... | collective-permute-start | bytes 3145736 | tf_op jit(solution)/shard_map/ppermute | solution.py:184
  69.3 85.7 %collective-permute-start.3 = (bf16[512,2048]{1,0:T(8,128)(2,1)S(1)}, bf16[512,2048]{1,0:T(8,128)(2,1)S(1)}, u32[]{:S(2)}, u32[]{:S(2)}) collective-permute-start(bf16[512,2048]{1,0:T(8,128)(2,1)S(1)} %shard_map.92.refs_0_), channel_id=1, source_target_pairs={{0,8},{8,0},{16,24},{24,16},{1,9},{9,1},{17,25},{25,17},{2,10},{10... | collective-permute-start | bytes 6291464 | tf_op jit(solution)/shard_map/ppermute | solution.py:178
  70.7 84.3 %copy-start.4 = (bf16[512,2048]{1,0:T(8,128)(2,1)}, bf16[512,2048]{1,0:T(8,128)(2,1)S(1)}, u32[]{:S(2)}) copy-start(bf16[512,2048]{1,0:T(8,128)(2,1)S(1)} %shard_map.93.refs_1_) | copy-start | bytes 6291460
  70.7 84.3 %collective-permute-start.4 = (bf16[512,2048]{1,0:T(8,128)(2,1)S(1)}, bf16[512,2048]{1,0:T(8,128)(2,1)S(1)}, u32[]{:S(2)}, u32[]{:S(2)}) collective-permute-start(bf16[512,2048]{1,0:T(8,128)(2,1)S(1)} %shard_map.93.refs_1_), channel_id=1, source_target_pairs={{0,8},{8,0},{16,24},{24,16},{1,9},{9,1},{17,25},{25,17},{2,10},{10... | collective-permute-start | bytes 6291464 | tf_op jit(solution)/shard_map/ppermute | solution.py:178
  93.8 61.2 %copy-start.10 = (bf16[256,2048]{1,0:T(8,128)(2,1)}, bf16[256,2048]{1,0:T(8,128)(2,1)S(1)}, u32[]{:S(2)}) copy-start(bf16[256,2048]{1,0:T(8,128)(2,1)S(1)} %collective-permute-done.7.refs_2_.refs_7_.refs_3_) | copy-start | bytes 3145732
  93.9 24.8 %collective-permute-start.9 = (bf16[128,2048]{1,0:T(8,128)(2,1)S(1)}, bf16[128,2048]{1,0:T(8,128)(2,1)S(1)}, u32[]{:S(2)}, u32[]{:S(2)}) collective-permute-start(bf16[128,2048]{1,0:T(8,128)(2,1)S(1)} %shard_map.96.refs_2_), channel_id=1, source_target_pairs={{0,4},{2,6},{4,0},{6,2},{1,5},{3,7},{5,1},{7,3},{8,12},{10,14},{12... | collective-permute-start | bytes 1572872 | tf_op jit(solution)/shard_map/ppermute | solution.py:190
  96.1 22.6 %collective-permute-start.11 = (bf16[128,2048]{1,0:T(8,128)(2,1)S(1)}, bf16[128,2048]{1,0:T(8,128)(2,1)S(1)}, u32[]{:S(2)}, u32[]{:S(2)}) collective-permute-start(bf16[128,2048]{1,0:T(8,128)(2,1)S(1)} %shard_map.96.refs_2_), channel_id=1, source_target_pairs={{0,16},{8,24},{16,0},{24,8},{1,17},{9,25},{17,1},{25,9},{2,18},{10... | collective-permute-start | bytes 1572872 | tf_op jit(solution)/shard_map/ppermute | solution.py:181
  96.6 22.6 %collective-permute-start.18 = (bf16[256,1024]{1,0:T(8,128)(2,1)S(1)}, bf16[256,1024]{1,0:T(8,128)(2,1)S(1)}, u32[]{:S(2)}, u32[]{:S(2)}) collective-permute-start(bf16[256,1024]{1,0:T(8,128)(2,1)S(1)} %slice.52), channel_id=1, source_target_pairs={{0,1},{1,0},{2,3},{3,2},{4,5},{5,4},{6,7},{7,6},{8,9},{9,8},{10,11... | collective-permute-start | bytes 1572872 | tf_op jit(solution)/shard_map/ppermute | solution.py:184
  118.7 13.8 %collective-permute-start.19 = (bf16[256,1024]{1,0:T(8,128)(2,1)S(1)}, bf16[256,1024]{1,0:T(8,128)(2,1)S(1)}, u32[]{:S(2)}, u32[]{:S(2)}) collective-permute-start(bf16[256,1024]{1,0:T(8,128)(2,1)S(1)} %slice.53), channel_id=1, source_target_pairs={{0,2},{2,0},{4,6},{6,4},{1,3},{3,1},{5,7},{7,5},{8,10},{10,8},{12,... | collective-permute-start | bytes 1572872 | tf_op jit(solution)/shard_map/ppermute | solution.py:187
  118.7 14.8 %collective-permute-start.12 = (bf16[128,2048]{1,0:T(8,128)(2,1)S(1)}, bf16[128,2048]{1,0:T(8,128)(2,1)S(1)}, u32[]{:S(2)}, u32[]{:S(2)}) collective-permute-start(bf16[128,2048]{1,0:T(8,128)(2,1)S(1)} %collective-permute-done.9.refs_8_.refs_3_), channel_id=1, source_target_pairs={{0,16},{8,24},{16,0},{24,8},{1,17},{9,25},{17,1},{25,9},{2,18},{10... | collective-permute-start | bytes 1572872 | tf_op jit(solution)/shard_map/ppermute | solution.py:181
  119.2 35.8 %collective-permute-start.8 = (bf16[256,2048]{1,0:T(8,128)(2,1)S(1)}, bf16[256,2048]{1,0:T(8,128)(2,1)S(1)}, u32[]{:S(2)}, u32[]{:S(2)}) collective-permute-start(bf16[256,2048]{1,0:T(8,128)(2,1)S(1)} %collective-permute-done.7.refs_2_.refs_7_.refs_3_), channel_id=1, source_target_pairs={{0,16},{8,24},{16,0},{24,8},{1,17},{9,25},{17,1},{25,9},{2,18},{10... | collective-permute-start | bytes 3145736 | tf_op jit(solution)/shard_map/ppermute | solution.py:181
  120.9 49.4 %copy-start.6 = (bf16[512,2048]{1,0:T(8,128)(2,1)}, bf16[512,2048]{1,0:T(8,128)(2,1)S(1)}, u32[]{:S(2)}) copy-start(bf16[512,2048]{1,0:T(8,128)(2,1)S(1)} %shard_map.98.refs_9_.refs_0_) | copy-start | bytes 6291460
  132.5 37.3 %collective-permute-start.20 = (bf16[512,2048]{1,0:T(8,128)(2,1)S(1)}, bf16[512,2048]{1,0:T(8,128)(2,1)S(1)}, u32[]{:S(2)}, u32[]{:S(2)}) collective-permute-start(bf16[512,2048]{1,0:T(8,128)(2,1)S(1)} %shard_map.98.refs_9_.refs_0_), channel_id=1, source_target_pairs={{0,8},{8,0},{16,24},{24,16},{1,9},{9,1},{17,25},{25,17},{2,10},{10... | collective-permute-start | bytes 6291464 | tf_op jit(solution)/shard_map/ppermute | solution.py:178
  132.7 37.6 %copy-start.8 = (bf16[512,2048]{1,0:T(8,128)(2,1)}, bf16[512,2048]{1,0:T(8,128)(2,1)S(1)}, u32[]{:S(2)}) copy-start(bf16[512,2048]{1,0:T(8,128)(2,1)S(1)} %shard_map.103.refs_1_) | copy-start | bytes 6291460
  133.5 36.8 %collective-permute-start.21 = (bf16[512,2048]{1,0:T(8,128)(2,1)S(1)}, bf16[512,2048]{1,0:T(8,128)(2,1)S(1)}, u32[]{:S(2)}, u32[]{:S(2)}) collective-permute-start(bf16[512,2048]{1,0:T(8,128)(2,1)S(1)} %shard_map.103.refs_1_), channel_id=1, source_target_pairs={{0,8},{8,0},{16,24},{24,16},{1,9},{9,1},{17,25},{25,17},{2,10},{10... | collective-permute-start | bytes 6291464 | tf_op jit(solution)/shard_map/ppermute | solution.py:178
  166.9 24.8 %collective-permute-start.16 = (bf16[512,1024]{1,0:T(8,128)(2,1)S(1)}, bf16[512,1024]{1,0:T(8,128)(2,1)}, u32[]{:S(2)}, u32[]{:S(2)}) collective-permute-start(bf16[512,1024]{1,0:T(8,128)(2,1)S(1)} %shard_map.101.refs_3_.refs_5_), channel_id=1, source_target_pairs={{0,8},{8,0},{16,24},{24,16},{1,9},{9,1},{17,25},{25,17},{2,10},{10... | collective-permute-start | bytes 3145736 | tf_op jit(solution)/shard_map/ppermute | solution.py:178
  169.2 27.4 %collective-permute-start.13 = (bf16[512,1024]{1,0:T(8,128)(2,1)S(1)}, bf16[512,1024]{1,0:T(8,128)(2,1)S(1)}, u32[]{:S(2)}, u32[]{:S(2)}) collective-permute-start(bf16[512,1024]{1,0:T(8,128)(2,1)S(1)} %get-tuple-element.38.refs_6_), channel_id=1, source_target_pairs={{0,8},{8,0},{16,24},{24,16},{1,9},{9,1},{17,25},{25,17},{2,10},{10... | collective-permute-start | bytes 3145736 | tf_op jit(solution)/shard_map/ppermute | solution.py:178
  169.7 29.4 %collective-permute-start.14 = (bf16[512,1024]{1,0:T(8,128)(2,1)S(1)}, bf16[512,1024]{1,0:T(8,128)(2,1)}, u32[]{:S(2)}, u32[]{:S(2)}) collective-permute-start(bf16[512,1024]{1,0:T(8,128)(2,1)S(1)} %get-tuple-element.39.refs_7_), channel_id=1, source_target_pairs={{0,8},{8,0},{16,24},{24,16},{1,9},{9,1},{17,25},{25,17},{2,10},{10... | collective-permute-start | bytes 3145736 | tf_op jit(solution)/shard_map/ppermute | solution.py:178
  169.8 29.3 %collective-permute-start.15 = (bf16[512,1024]{1,0:T(8,128)(2,1)S(1)}, bf16[512,1024]{1,0:T(8,128)(2,1)}, u32[]{:S(2)}, u32[]{:S(2)}) collective-permute-start(bf16[512,1024]{1,0:T(8,128)(2,1)S(1)} %get-tuple-element.40.refs_8_), channel_id=1, source_target_pairs={{0,8},{8,0},{16,24},{24,16},{1,9},{9,1},{17,25},{25,17},{2,10},{10... | collective-permute-start | bytes 3145736 | tf_op jit(solution)/shard_map/ppermute | solution.py:178
  176.0 39.7 %collective-permute-start.38 = (bf16[256,2048]{1,0:T(8,128)(2,1)S(1)}, bf16[256,2048]{1,0:T(8,128)(2,1)}, u32[]{:S(2)}, u32[]{:S(2)}) collective-permute-start(bf16[256,2048]{1,0:T(8,128)(2,1)S(1)} %get-tuple-element.44.refs_7_), channel_id=1, source_target_pairs={{0,16},{8,24},{16,0},{24,8},{1,17},{9,25},{17,1},{25,9},{2,18},{10... | collective-permute-start | bytes 3145736 | tf_op jit(solution)/shard_map/ppermute | solution.py:181
  191.6 57.2 %copy-start.2 = (bf16[2048,1024]{1,0:T(8,128)(2,1)}, bf16[2048,1024]{1,0:T(8,128)(2,1)S(1)}, u32[]{:S(2)}) copy-start(bf16[2048,1024]{1,0:T(8,128)(2,1)S(1)} %get-tuple-element.46.refs_3_.refs_0_) | copy-start | bytes 12582916
  194.7 17.2 %collective-permute-start.24 = (bf16[256,1024]{1,0:T(8,128)(2,1)S(1)}, bf16[256,1024]{1,0:T(8,128)(2,1)S(1)}, u32[]{:S(2)}, u32[]{:S(2)}) collective-permute-start(bf16[256,1024]{1,0:T(8,128)(2,1)S(1)} %get-tuple-element.64), channel_id=1, source_target_pairs={{0,2},{2,0},{4,6},{6,4},{1,3},{3,1},{5,7},{7,5},{8,10},{10,8},{12,... | collective-permute-start | bytes 1572872 | tf_op jit(solution)/shard_map/ppermute | solution.py:187
  197.5 15.6 %collective-permute-start.22 = (bf16[256,1024]{1,0:T(8,128)(2,1)S(1)}, bf16[256,1024]{1,0:T(8,128)(2,1)S(1)}, u32[]{:S(2)}, u32[]{:S(2)}) collective-permute-start(bf16[256,1024]{1,0:T(8,128)(2,1)S(1)} %get-tuple-element.63), channel_id=1, source_target_pairs={{0,1},{1,0},{2,3},{3,2},{4,5},{5,4},{6,7},{7,6},{8,9},{9,8},{10,11... | collective-permute-start | bytes 1572872 | tf_op jit(solution)/shard_map/ppermute | solution.py:184
  210.0 43.0 %collective-permute-start.35 = (bf16[512,1024]{1,0:T(8,128)(2,1)S(1)}, bf16[512,1024]{1,0:T(8,128)(2,1)S(1)}, u32[]{:S(2)}, u32[]{:S(2)}) collective-permute-start(bf16[512,1024]{1,0:T(8,128)(2,1)S(1)} %get-tuple-element.51.refs_4_), channel_id=1, source_target_pairs={{0,16},{8,24},{16,0},{24,8},{1,17},{9,25},{17,1},{25,9},{2,18},{10... | collective-permute-start | bytes 3145736 | tf_op jit(solution)/shard_map/ppermute | solution.py:181
  212.2 24.2 %collective-permute-start.25 = (bf16[512,1024]{1,0:T(8,128)(2,1)S(1)}, bf16[512,1024]{1,0:T(8,128)(2,1)S(1)}, u32[]{:S(2)}, u32[]{:S(2)}) collective-permute-start(bf16[512,1024]{1,0:T(8,128)(2,1)S(1)} %add_convert_fusion.3), channel_id=1, source_target_pairs={{0,1},{1,0},{2,3},{3,2},{4,5},{5,4},{6,7},{7,6},{8,9},{9,8},{10,11... | collective-permute-start | bytes 3145736 | tf_op jit(solution)/shard_map/ppermute | solution.py:184
  213.4 34.9 %collective-permute-start.23 = (bf16[512,1024]{1,0:T(8,128)(2,1)S(1)}, bf16[512,1024]{1,0:T(8,128)(2,1)S(1)}, u32[]{:S(2)}, u32[]{:S(2)}) collective-permute-start(bf16[512,1024]{1,0:T(8,128)(2,1)S(1)} %add_convert_fusion.4), channel_id=1, source_target_pairs={{0,2},{2,0},{4,6},{6,4},{1,3},{3,1},{5,7},{7,5},{8,10},{10,8},{12,... | collective-permute-start | bytes 3145736 | tf_op jit(solution)/shard_map/ppermute | solution.py:187
  215.7 32.6 %collective-permute-start.29 = (bf16[512,1024]{1,0:T(8,128)(2,1)S(1)}, bf16[512,1024]{1,0:T(8,128)(2,1)S(1)}, u32[]{:S(2)}, u32[]{:S(2)}) collective-permute-start(bf16[512,1024]{1,0:T(8,128)(2,1)S(1)} %shard_map.110.refs_3_.refs_5_), channel_id=1, source_target_pairs={{0,8},{8,0},{16,24},{24,16},{1,9},{9,1},{17,25},{25,17},{2,10},{10... | collective-permute-start | bytes 3145736 | tf_op jit(solution)/shard_map/ppermute | solution.py:178
  217.5 33.1 %collective-permute-start.39 = (bf16[128,2048]{1,0:T(8,128)(2,1)S(1)}, bf16[128,2048]{1,0:T(8,128)(2,1)S(1)}, u32[]{:S(2)}, u32[]{:S(2)}) collective-permute-start(bf16[128,2048]{1,0:T(8,128)(2,1)S(1)} %slice.75), channel_id=1, source_target_pairs={{0,4},{2,6},{4,0},{6,2},{1,5},{3,7},{5,1},{7,3},{8,12},{10,14},{12... | collective-permute-start | bytes 1572872 | tf_op jit(solution)/shard_map/ppermute | solution.py:190
  236.4 49.1 %collective-permute-start.26 = (bf16[512,1024]{1,0:T(8,128)(2,1)}, bf16[512,1024]{1,0:T(8,128)(2,1)}, u32[]{:S(2)}, u32[]{:S(2)}) collective-permute-start(bf16[512,1024]{1,0:T(8,128)(2,1)} %get-tuple-element.52.refs_6_), channel_id=1, source_target_pairs={{0,8},{8,0},{16,24},{24,16},{1,9},{9,1},{17,25},{25,17},{2,10},{10... | collective-permute-start | bytes 3145736 | tf_op jit(solution)/shard_map/ppermute | solution.py:178
  248.3 37.6 %collective-permute-start.27 = (bf16[512,1024]{1,0:T(8,128)(2,1)}, bf16[512,1024]{1,0:T(8,128)(2,1)}, u32[]{:S(2)}, u32[]{:S(2)}) collective-permute-start(bf16[512,1024]{1,0:T(8,128)(2,1)} %get-tuple-element.53.refs_7_), channel_id=1, source_target_pairs={{0,8},{8,0},{16,24},{24,16},{1,9},{9,1},{17,25},{25,17},{2,10},{10... | collective-permute-start | bytes 3145736 | tf_op jit(solution)/shard_map/ppermute | solution.py:178
  248.3 37.6 %collective-permute-start.28 = (bf16[512,1024]{1,0:T(8,128)(2,1)}, bf16[512,1024]{1,0:T(8,128)(2,1)}, u32[]{:S(2)}, u32[]{:S(2)}) collective-permute-start(bf16[512,1024]{1,0:T(8,128)(2,1)} %get-tuple-element.54.refs_8_), channel_id=1, source_target_pairs={{0,8},{8,0},{16,24},{24,16},{1,9},{9,1},{17,25},{25,17},{2,10},{10... | collective-permute-start | bytes 3145736 | tf_op jit(solution)/shard_map/ppermute | solution.py:178
  250.6 43.3 %collective-permute-start.30 = (bf16[512,1024]{1,0:T(8,128)(2,1)S(1)}, bf16[512,1024]{1,0:T(8,128)(2,1)}, u32[]{:S(2)}, u32[]{:S(2)}) collective-permute-start(bf16[512,1024]{1,0:T(8,128)(2,1)S(1)} %shard_map.113.refs_6_), channel_id=1, source_target_pairs={{0,1},{1,0},{2,3},{3,2},{4,5},{5,4},{6,7},{7,6},{8,9},{9,8},{10,11... | collective-permute-start | bytes 3145736 | tf_op jit(solution)/shard_map/ppermute | solution.py:184
  254.2 27.2 %collective-permute-start.40 = (bf16[128,1024]{1,0:T(8,128)(2,1)}, bf16[128,1024]{1,0:T(8,128)(2,1)S(1)}, u32[]{:S(2)}, u32[]{:S(2)}) collective-permute-start(bf16[128,1024]{1,0:T(8,128)(2,1)} %slice.78), channel_id=1, source_target_pairs={{0,1},{1,0},{2,3},{3,2},{4,5},{5,4},{6,7},{7,6},{8,9},{9,8},{10,11... | collective-permute-start | bytes 786440 | tf_op jit(solution)/shard_map/ppermute | solution.py:184
  281.4 24.5 %collective-permute-start.33 = (bf16[512,1024]{1,0:T(8,128)(2,1)}, bf16[512,1024]{1,0:T(8,128)(2,1)S(1)}, u32[]{:S(2)}, u32[]{:S(2)}) collective-permute-start(bf16[512,1024]{1,0:T(8,128)(2,1)} %copy-done.48), channel_id=1, source_target_pairs={{0,16},{8,24},{16,0},{24,8},{1,17},{9,25},{17,1},{25,9},{2,18},{10... | collective-permute-start | bytes 3145736 | tf_op jit(solution)/shard_map/ppermute | solution.py:181
  285.5 24.8 %collective-permute-start.36 = (bf16[256,1024]{1,0:T(8,128)(2,1)S(1)}, bf16[256,1024]{1,0:T(8,128)(2,1)S(1)}, u32[]{:S(2)}, u32[]{:S(2)}) collective-permute-start(bf16[256,1024]{1,0:T(8,128)(2,1)S(1)} %slice.76), channel_id=1, source_target_pairs={{0,4},{2,6},{4,0},{6,2},{1,5},{3,7},{5,1},{7,3},{8,12},{10,14},{12... | collective-permute-start | bytes 1572872 | tf_op jit(solution)/shard_map/ppermute | solution.py:190
  292.4 39.6 %collective-permute-start.32 = (bf16[512,1024]{1,0:T(8,128)(2,1)S(1)}, bf16[512,1024]{1,0:T(8,128)(2,1)S(1)}, u32[]{:S(2)}, u32[]{:S(2)}) collective-permute-start(bf16[512,1024]{1,0:T(8,128)(2,1)S(1)} %get-tuple-element.58), channel_id=1, source_target_pairs={{0,1},{1,0},{2,3},{3,2},{4,5},{5,4},{6,7},{7,6},{8,9},{9,8},{10,11... | collective-permute-start | bytes 3145736 | tf_op jit(solution)/shard_map/ppermute | solution.py:184
  295.6 46.6 %collective-permute-start.31 = (bf16[512,1024]{1,0:T(8,128)(2,1)S(1)}, bf16[512,1024]{1,0:T(8,128)(2,1)S(1)}, u32[]{:S(2)}, u32[]{:S(2)}) collective-permute-start(bf16[512,1024]{1,0:T(8,128)(2,1)S(1)} %add_convert_fusion.1), channel_id=1, source_target_pairs={{0,2},{2,0},{4,6},{6,4},{1,3},{3,1},{5,7},{7,5},{8,10},{10,8},{12,... | collective-permute-start | bytes 3145736 | tf_op jit(solution)/shard_map/ppermute | solution.py:187
  306.4 23.9 %collective-permute-start.34 = (bf16[256,1024]{1,0:T(8,128)(2,1)S(1)}, bf16[256,1024]{1,0:T(8,128)(2,1)S(1)}, u32[]{:S(2)}, u32[]{:S(2)}) collective-permute-start(bf16[256,1024]{1,0:T(8,128)(2,1)S(1)} %slice.77), channel_id=1, source_target_pairs={{0,4},{2,6},{4,0},{6,2},{1,5},{3,7},{5,1},{7,3},{8,12},{10,14},{12... | collective-permute-start | bytes 1572872 | tf_op jit(solution)/shard_map/ppermute | solution.py:190
  310.4 20.0 %collective-permute-start.37 = (bf16[256,1024]{1,0:T(8,128)(2,1)S(1)}, bf16[256,1024]{1,0:T(8,128)(2,1)S(1)}, u32[]{:S(2)}, u32[]{:S(2)}) collective-permute-start(bf16[256,1024]{1,0:T(8,128)(2,1)S(1)} %fusion), channel_id=1, source_target_pairs={{0,1},{1,0},{2,3},{3,2},{4,5},{5,4},{6,7},{7,6},{8,9},{9,8},{10,11... | collective-permute-start | bytes 1572872 | tf_op jit(solution)/shard_map/ppermute | solution.py:184
  (48 other events, 333.3 us)

commit v4 on v0

--- a/solution.py
+++ b/solution.py
@@ -23,20 +23,33 @@
     return silu_g, silu_g * up_sum, up_sum * slope
 
 
-def call(kernel, outs, flops, *args):
+def shape(*dims, dtype=BF16):
+    return jax.ShapeDtypeStruct(dims, dtype)
+
+
+def call(kernel, outs, flops, args, after=(), specs=None, scratch=(), limit=24):
+    everything = [*args, *after]
     moved = sum(a.size * a.dtype.itemsize for a in args) + sum(o.size * o.dtype.itemsize for o in outs)
+    specs = specs or [pl.BlockSpec(memory_space=pltpu.VMEM)] * len(args)
+
+    def body(*refs):
+        kernel(*refs[: len(args)], *refs[len(everything) :])
+
     return pl.pallas_call(
-        kernel,
-        out_shape=outs,
-        in_specs=[pl.BlockSpec(memory_space=pltpu.VMEM)] * len(args),
+        body,
+        out_shape=list(outs),
+        in_specs=[*specs, *[pl.BlockSpec(memory_space=pl.ANY)] * len(after)],
         out_specs=[pl.BlockSpec(memory_space=pltpu.VMEM)] * len(outs),
-        compiler_params=pltpu.CompilerParams(vmem_limit_bytes=44 * MIB),
+        scratch_shapes=list(scratch),
+        compiler_params=pltpu.CompilerParams(vmem_limit_bytes=limit * MIB),
         cost_estimate=pl.CostEstimate(flops=flops, bytes_accessed=moved, transcendentals=0),
-    )(*args)
-
-
-def shape(*dims):
-    return jax.ShapeDtypeStruct(dims, BF16)
+    )(*everything)
+
+
+ANY = pl.BlockSpec(memory_space=pl.ANY)
+HBM = pl.BlockSpec(memory_space=pltpu.HBM)
+VMEM = pl.BlockSpec(memory_space=pltpu.VMEM)
+SMEM = pl.BlockSpec(memory_space=pltpu.SMEM)
 
 
 class Rows:
@@ -100,6 +113,41 @@
             out_ref[:, pl.ds(pl.multiple_of(place * half + index * tile, tile), tile)] = total.astype(BF16)
 
 
+def block_kernel(first, places, sides, added, *refs):
+    rights, many = len(sides), len(places)
+    left_any, right_any, refs = refs[0], refs[1 : 1 + rights], refs[1 + rights :]
+    adds, refs = refs[: many * added], refs[many * added :]
+    outs, (left_ref, right_ref, sems) = refs[:many], refs[many:]
+    depth, half = right_ref.shape[1:]
+    copies = [pltpu.make_async_copy(left_any.at[pl.ds(first, left_ref.shape[0])], left_ref, sems.at[0])]
+    for at, side in enumerate(sides):
+        source = right_any[at].at[:, pl.ds(side * half, half)]
+        copies.append(pltpu.make_async_copy(source, right_ref.at[at], sems.at[1 + at]))
+    for copy in copies:
+        copy.start()
+    for copy in copies:
+        copy.wait()
+    for at, (row, right) in enumerate(places):
+        total = matmul(left_ref[row : row + outs[at].shape[0]], right_ref[right], (1, 0))
+        if added:
+            total = total + adds[at][...].astype(F32)
+        outs[at][...] = total.astype(BF16)
+
+
+def sum_kernel(left_ref, right_ref, out_ref):
+    out_ref[...] = (left_ref[...].astype(F32) + right_ref[...].astype(F32)).astype(BF16)
+
+
+def finish_kernel(at_ref, mine_ref, theirs_ref, gate_ref, up_ref):
+    width = mine_ref.shape[0] // 2
+    for part, out_ref in enumerate((gate_ref, up_ref)):
+        span = slice(part * width, (part + 1) * width)
+        mine, theirs = mine_ref[span].astype(F32).T, theirs_ref[span].astype(F32).T
+        first = at_ref[0] == 0
+        out_ref[:, :width] = jnp.where(first, mine, theirs)
+        out_ref[:, width:] = jnp.where(first, theirs, mine)
+
+
 class Square:
     def core(self, array):
         return lax.ppermute(array, "inp", [(at, at ^ 1) for at in range(4)])
@@ -136,27 +184,42 @@
             blocks += [((base + 2, 0), (base + 3, 0)), ((base + 2, step), (base + 4, 0))]
         return Rows(pieces, blocks, step)
 
-    def scatter(self, product, rows, cols):
-        half, quarter = rows // 2, rows // 4
-        far = {}
-        for chip in (1, 0):
-            for other in (1, 0):
-                at = slice(half + chip * quarter, half + (chip + 1) * quarter)
-                far[chip, other] = self.core(product(at, other).astype(BF16))
-        sums = {}
-        for chip in (1, 0):
-            for other in (1, 0):
-                at = slice(chip * quarter, (chip + 1) * quarter)
-                sums[chip, other] = product(at, other) + far[chip, other].astype(F32)
-        batch = quarter // 2
-        corner = sums[1, 1].astype(BF16)
-        from_other = self.other(corner[:batch]).astype(F32)
-        from_chip = self.chip(corner[batch:]).astype(F32)
-        zeros = jnp.zeros_like(from_other)
-        to_chip = sums[1, 0] + jnp.concatenate([from_other, zeros])
-        to_other = sums[0, 1] + jnp.concatenate([zeros, from_chip])
-        total = sums[0, 0] + self.chip(to_chip.astype(BF16)).astype(F32) + self.other(to_other.astype(BF16)).astype(F32)
-        return total.astype(BF16).reshape(2, batch, cols // 2)
+    def products(self, left, rights, places, adds=(), after=()):
+        far = int(not adds)
+        quarter, depth = left.shape[0] // 4, left.shape[1]
+        half = rights[0][2]
+        outs = [shape(quarter, half)] * len(places)
+        use = sorted({other for _, other in places})
+        chips = sorted({chip for chip, _ in places})
+        first = 2 * far * quarter + chips[0] * quarter
+        wanted = [((chip - chips[0]) * quarter, use.index(other)) for chip, other in places]
+        args = [left] + [rights[other][0] for other in use] + [adds[place] for place in places if adds]
+        blocks = call(
+            functools.partial(block_kernel, first, wanted, [rights[other][1] for other in use], bool(adds)),
+            outs,
+            2 * len(places) * quarter * depth * half,
+            args,
+            after,
+            specs=[ANY] * (1 + len(use)) + [VMEM] * (len(args) - 1 - len(use)),
+            scratch=[
+                pltpu.VMEM((len(chips) * quarter, depth), BF16),
+                pltpu.VMEM((len(use), depth, half), BF16),
+                pltpu.SemaphoreType.DMA((1 + len(use),)),
+            ],
+        )
+        return dict(zip(places, blocks))
+
+    def far_first(self, left, rights, after):
+        return self.products(left, rights, [(1, 1)], after=after)
+
+    def far_rest(self, left, rights, after):
+        return self.products(left, rights, [(0, 1), (1, 0), (0, 0)], after=after)
+
+    def near_first(self, left, rights, far, after):
+        return self.products(left, rights, [(1, 1)], far, after)
+
+    def near_rest(self, left, rights, far, after):
+        return self.products(left, rights, [(0, 1), (1, 0), (0, 0)], far, after)
 
     def layer(self, tokens, gate_weight, up_weight, down_weight, cotangent):
         def gather_units(array):
@@ -174,59 +237,90 @@
         down = gather_units(jnp.concatenate([down_mine, self.other(down_theirs)], axis=1))
         rows_in = self.gather(tokens)
         rows_cot = self.gather(cotangent)
-        count = len(rows_in.blocks) * rows_in.step
+        step = rows_in.step
+        count = len(rows_in.blocks) * step
         units = down.shape[0]
 
         hidden, hidden_turned, silu, rest = call(
             functools.partial(hidden_kernel, rows_in, width),
             [shape(count, units), shape(units, count), shape(count, units), shape(count, units)],
             8 * count * units * half,
-            *rows_in.pieces,
-            own_units,
-            other_units,
+            [*rows_in.pieces, own_units, other_units],
+            limit=44,
         )
         (down_term,) = call(
             functools.partial(weight_kernel, rows_cot, (0, 1), 256),
             [shape(units, 2 * half)],
             4 * count * units * half,
-            *rows_cot.pieces,
-            hidden_turned,
+            [*rows_cot.pieces, hidden_turned],
+            limit=44,
         )
         down_sum = scatter_units(down_term)
+        down_sides = [(down, 0, half), (down, 1, half)]
+        output_far = self.far_first(hidden, down_sides, [])
+        output_far |= self.far_rest(hidden, down_sides, [output_far[1, 1]])
         act, act_turned = call(
             functools.partial(grads_kernel, rows_cot, width),
             [shape(count, 2 * units), shape(2 * units, count)],
             4 * count * units * half,
-            *rows_cot.pieces,
-            down,
-            silu,
-            rest,
-        )
-        terms = [
-            call(
+            [*rows_cot.pieces, down, silu, rest],
+            after=list(output_far.values()),
+            limit=44,
+        )
+
+        def unit_term(side, after):
+            return call(
                 functools.partial(weight_kernel, rows_in, (side,), 256),
                 [shape(2 * units, half)],
                 4 * count * units * half,
-                *rows_in.pieces,
-                act_turned,
+                [*rows_in.pieces, act_turned],
+                after,
+                limit=44,
             )[0]
-            for side in (1, 0)
-        ]
-        other_sum, own_sum = scatter_units(terms[0]), scatter_units(terms[1])
+
+        output_far = {place: self.core(block) for place, block in output_far.items()}
+        sums = self.near_first(hidden, down_sides, output_far, [act])
+        corner = sums[1, 1]
+        by_other, by_chip = self.other(corner[:step]), self.chip(corner[step:])
+        sums |= self.near_rest(hidden, down_sides, output_far, [corner])
+        other_term = unit_term(1, [sums[0, 0]])
+        other_sum = scatter_units(other_term)
+        unit_sides = [(own_units, 0, half), (other_units, 0, half)]
+        grads_far = self.far_first(act, unit_sides, [other_term, by_other, by_chip])
+        grads_far |= self.far_rest(act, unit_sides, [grads_far[1, 1]])
+        zeros = jnp.zeros((step, half), F32)
+        to_chip = (sums[1, 0].astype(F32) + jnp.concatenate([by_other.astype(F32), zeros])).astype(BF16)
+        to_other = (sums[0, 1].astype(F32) + jnp.concatenate([zeros, by_chip.astype(F32)])).astype(BF16)
+        output_chip, output_other = self.chip(to_chip), self.other(to_other)
+        own_term = unit_term(0, list(grads_far.values()))
+        own_sum = scatter_units(own_term)
+        grads_far = {place: self.core(block) for place, block in grads_far.items()}
+        grads = self.near_first(act, unit_sides, grads_far, [own_term])
+        corner = self.chip(grads[1, 1])
         down_back = self.other(down_sum[:, half:])
+        grads |= self.near_rest(act, unit_sides, grads_far, [grads[1, 1], output_chip, output_other])
+        by_chip = self.chip(grads[1, 0])
+        (to_other,) = call(sum_kernel, [shape(2 * step, half)], 0, [grads[0, 1], corner])
+        by_other = self.other(to_other)
+        total = sums[0, 0].astype(F32) + output_chip.astype(F32) + output_other.astype(F32)
+        output = total.astype(BF16).reshape(2, step, half)
         units_back = self.other(other_sum)
-        grad_down = self.in_order(down_sum[:, :half], down_back)
-        grad_gate = self.in_order(own_sum[:width], units_back[:width]).T
-        grad_up = self.in_order(own_sum[width:], units_back[width:]).T
-
-        def output_block(at, other):
-            return matmul(hidden[at], down[:, other * half : (other + 1) * half], (1, 0))
-
-        def input_block(at, other):
-            return matmul(act[at], other_units if other else own_units, (1, 0))
-
-        output = self.scatter(output_block, count, 2 * half)
-        grad_tokens = self.scatter(input_block, count, 2 * half)
+        (partial,) = call(sum_kernel, [shape(2 * step, half)], 0, [grads[0, 0], by_chip], [down_back])
+        (total,) = call(sum_kernel, [shape(2 * step, half)], 0, [partial, by_other], [units_back])
+        grad_tokens = total.reshape(2, step, half)
+
+        at_out = lax.axis_index("out").astype(jnp.int32).reshape(1)
+        mine, theirs = down_sum[:, :half].astype(F32), down_back.astype(F32)
+        first = at_out[0] == 0
+        grad_down = jnp.where(first, jnp.concatenate([mine, theirs]), jnp.concatenate([theirs, mine]))
+        grad_gate, grad_up = call(
+            finish_kernel,
+            [shape(half, 2 * width, dtype=F32)] * 2,
+            0,
+            [at_out, own_sum, units_back],
+            [total],
+            specs=[SMEM, VMEM, VMEM],
+        )
         return (output, grad_tokens, grad_gate, grad_up, grad_down)
 
 

time: 310 us -> 353 us (1.14)
  matrix products: 44.5 us -> 0 us
  waiting for transfers between devices: 138 us -> 177 us
  Pallas kernels: 59.1 us -> 85.5 us
  local copies, waits for them, and re-layouts: 20.3 us -> 36.8 us
  other arithmetic: 5.32 us -> 9.86 us
    dot_general x16 -> x0, matrix products: 44.5 us -> none  [matmul(): lax.dot_general(a, b, ((contract[:1], contract[1:]), ((), ())), preferred...]
    pallas_call x5 -> x17, Pallas kernels: 59.1 us -> 85.5 us  [call(): pl.pallas_call(body, out_shape=list(outs), in_specs=[*specs, *[pl.BlockSp...]
    ppermute x12 -> x11, waiting for transfers between devices: 59.3 us -> 81.3 us  [other(): return lax.ppermute(array, 'out', [(0, 1), (1, 0)])]
    unnamed x78 -> x134, local copies, waits for them, and re-layouts: 17.7 us -> 34.3 us
    ppermute x8, waiting for transfers between devices: 67 us -> 77.5 us  [chip(): return lax.ppermute(array, 'inp', [(at, at ^ 2) for at in range(4)])]
    all_gather x3, waiting for transfers between devices: 11.4 us -> 18.1 us  [gather_units(): return lax.all_gather(array, 'wt', axis=0, tiled=True)]
    convert_element_type x4 -> x5, other arithmetic: 2.31 us -> 7.07 us  [the longest x1 2.82 us: layer(): output = total.astype(BF16).reshape(2, step, half)]
    ppermute x12 -> x11, starting transfers between devices: 14.8 us -> 15 us  [other(): return lax.ppermute(array, 'out', [(0, 1), (1, 0)])]
  transfers between devices with their start and end apart: 44 -> 43, of which waited for: 16 -> 14; matrix products, arithmetic and copies ran while one was open for 16% -> 3% of each run, Pallas kernels for 19% -> 20%
where the time goes in v4:
time: 353 us; the launch traced here: 352 us
  waiting for transfers between devices  177 us (50%)
  Pallas kernels  85.5 us (24%)
  local copies, waits for them, and re-layouts  36.8 us (10%)
  starting transfers between devices  27.8 us (8%)
  between operations  14.8 us (4%)
  other arithmetic  9.86 us (3%)
    pallas_call x17, Pallas kernels, call(): pl.pallas_call(body, out_shape=list(outs), in_specs=[*specs, *[pl.BlockSp...  85.5 us
    ppermute x11, waiting for transfers between devices, other(): return lax.ppermute(array, 'out', [(0, 1), (1, 0)])  81.3 us
    ppermute x8, waiting for transfers between devices, chip(): return lax.ppermute(array, 'inp', [(at, at ^ 2) for at in range(4)])  77.5 us
    unnamed x134, local copies, waits for them, and re-layouts  34.3 us
    all_gather x3, waiting for transfers between devices, gather_units(): return lax.all_gather(array, 'wt', axis=0, tiled=True)  18.1 us
    ppermute x11, starting transfers between devices, other(): return lax.ppermute(array, 'out', [(0, 1), (1, 0)])  15 us
    ppermute x8, starting transfers between devices, chip(): return lax.ppermute(array, 'inp', [(at, at ^ 2) for at in range(4)])  8.44 us
  transfers between devices with their start and end apart: 43, of which 14 were waited for; matrix products, arithmetic and copies ran while one was open for 3% of the time, Pallas kernels for 20%

profile of v4, /device:TPU:0, one launch (start us, length us, event | category | flops | bytes accessed | tf_op | source)
XLA Modules:
  0.0 351.7 jit_solution(9293321071168761552)
XLA Ops:
  10.1 3.0 collective-permute-start.9
  13.1 11.9 %collective-permute-done.9 = bf16[256,1024]{1,0:T(8,128)(2,1)S(1)} collective-permute-done((bf16[256,1024]{1,0:T(8,128)(2,1)S(1)}, bf16[256,1024]{1,0:T(8,128)(2,1)S(1)}, u32[]{:S(2)}, u32[]{:S(2)}) %collective-permute-start.9) | collective-permute-done | bytes 524320 | tf_op jit(solution)/shard_map/ppermute | solution.py:159
  25.9 1.8 collective-permute-start.10
  27.8 5.9 %collective-permute-done.10 = bf16[128,1024]{1,0:T(8,128)(2,1)S(1)} collective-permute-done((bf16[128,1024]{1,0:T(8,128)(2,1)S(1)}, bf16[128,1024]{1,0:T(8,128)(2,1)S(1)}, u32[]{:S(2)}, u32[]{:S(2)}) %collective-permute-start.10) | collective-permute-done | bytes 262176 | tf_op jit(solution)/shard_map/ppermute | solution.py:159
  34.5 1.5 collective-permute-start.1
  36.0 1.5 collective-permute-start
  38.6 22.3 %collective-permute-done.1.refs_2_ = bf16[512,1024]{1,0:T(8,128)(2,1)S(1)} collective-permute-done((bf16[512,1024]{1,0:T(8,128)(2,1)}, bf16[512,1024]{1,0:T(8,128)(2,1)S(1)}, u32[]{:S(2)}, u32[]{:S(2)}) %collective-permute-start.1) | collective-permute-done | bytes 1048608 | tf_op jit(solution)/shard_map/ppermute | solution.py:156
  60.9 1.5 collective-permute-start.2
  62.5 1.6 collective-permute-start.3
  64.0 19.3 %collective-permute-done.16.refs_2_ = bf16[512,1024]{1,0:T(8,128)(2,1)S(1)} collective-permute-done((bf16[512,1024]{1,0:T(8,128)(2,1)}, bf16[512,1024]{1,0:T(8,128)(2,1)S(1)}, u32[]{:S(2)}, u32[]{:S(2)}) %collective-permute-start.16) | collective-permute-done | bytes 1048608 | tf_op jit(solution)/shard_map/ppermute | solution.py:156
  83.4 1.5 collective-permute-start.17
  86.5 9.5 %collective-permute-done.2.refs_3_ = bf16[256,1024]{1,0:T(8,128)(2,1)S(1)} collective-permute-done((bf16[256,1024]{1,0:T(8,128)(2,1)S(1)}, bf16[256,1024]{1,0:T(8,128)(2,1)S(1)}, u32[]{:S(2)}, u32[]{:S(2)}) %collective-permute-start.2) | collective-permute-done | bytes 524320 | tf_op jit(solution)/shard_map/ppermute | solution.py:159
  97.5 6.8 %collective-permute-done.17.refs_3_ = bf16[256,1024]{1,0:T(8,128)(2,1)} collective-permute-done((bf16[256,1024]{1,0:T(8,128)(2,1)S(1)}, bf16[256,1024]{1,0:T(8,128)(2,1)}, u32[]{:S(2)}, u32[]{:S(2)}) %collective-permute-start.17) | collective-permute-done | bytes 524320 | tf_op jit(solution)/shard_map/ppermute | solution.py:159
  111.4 1.3 copy-done.29
  112.7 1.3 copy-done.33
  118.3 15.6 %shard_map.92 = (bf16[2048,512]{1,0:T(8,128)(2,1)}, bf16[512,2048]{1,0:T(8,128)(2,1)}, bf16[2048,512]{1,0:T(8,128)(2,1)}, bf16[2048,512]{1,0:T(8,128)(2,1)}) custom-call(bf16[512,1024]{1,0:T(8,128)(2,1)} %bitcast.refs_0_, bf16[512,1024]{1,0:T(8,128)(2,1)S(1)} %collective-permute-done.refs_1_, bf16[512,1024]{1,0:T(8,128)(2,1)S(1)} %collective-permute-done.1.refs_2_, ...), custom_call_target="tpu_custom_call" | custom-call | flops 8589934592 | bytes 20971520 | tf_op jit(solution)/shard_map/pallas_call | solution.py:38
  133.8 18.1 %all-gather.8.cloned.1.call-done.refs_1_.refs_2_.refs_10_ = bf16[512,2048]{1,0:T(8,128)(2,1)} async-done(((bf16[128,2048]{1,0:T(8,128)(2,1)}), bf16[512,2048]{1,0:T(8,128)(2,1)}) %all-gather.8.cloned.1.call-update) | async-done | bytes 2097168 | tf_op jit(solution)/shard_map/all_gather | solution.py:226
  151.9 1.6 copy-done
  153.5 1.6 copy-done.6
  156.2 2.3 shard_map.94
  159.8 13.5 %shard_map.95 = (bf16[2048,1024]{1,0:T(8,128)(2,1)}, bf16[1024,2048]{1,0:T(8,128)(2,1)}) custom-call(bf16[512,1024]{1,0:T(8,128)(2,1)} %bitcast.5.refs_0_, bf16[512,1024]{1,0:T(8,128)(2,1)} %collective-permute-done.15.refs_1_, bf16[512,1024]{1,0:T(8,128)(2,1)S(1)} %collective-permute-done.16.refs_2_, bf16[256,1024]{1,0:T(8,128)(2,1)} %collective-permute-done.17.refs_3_, ...), custom_call_target="tpu_custom_call" | custom-call | flops 4294967296 | bytes 23068672 | tf_op jit(solution)/shard_map/pallas_call | solution.py:38
  173.3 2.2 copy-done.2
  175.5 2.2 shard_map.96.refs_6_
  177.8 3.7 %shard_map.97 = (bf16[512,1024]{1,0:T(8,128)(2,1)S(1)}, bf16[512,1024]{1,0:T(8,128)(2,1)S(1)}, bf16[512,1024]{1,0:T(8,128)(2,1)S(1)}) custom-call(bf16[2048,512]{1,0:T(8,128)(2,1)S(1)} %copy-done.7, bf16[512,2048]{1,0:T(8,128)(2,1)S(1)} %copy-done.1, bf16[512,2048]{1,0:T(8,128)(2,1)S(1)} %copy-done.1, bf16[512,1024]{1,0:T(8,128)(2,1)S(1)} %collective-permute-done.11.refs_3_, ...), custom_call_target="tpu_custom_call" | custom-call | flops 1610612736 | bytes 12582912 | tf_op jit(solution)/shard_map/pallas_call | solution.py:38
  183.4 8.9 %shard_map.98.refs_2_ = bf16[1024,1024]{1,0:T(8,128)(2,1)} custom-call(bf16[512,1024]{1,0:T(8,128)(2,1)} %bitcast.refs_0_, bf16[512,1024]{1,0:T(8,128)(2,1)S(1)} %collective-permute-done.refs_1_, bf16[512,1024]{1,0:T(8,128)(2,1)S(1)} %collective-permute-done.1.refs_2_, bf16[256,1024]{1,0:T(8,128)(2,1)S(1)} %copy-done.48, bf16[256,1024]{1,0:T(8,128)(2,1)S(1)} %copy-done.52, ...), custom_call_target="tpu_custom_call" | custom-call | flops 4294967296 | bytes 14680064 | tf_op jit(solution)/shard_map/pallas_call | solution.py:38
  194.6 11.0 %shard_map.104 = bf16[512,2048]{1,0:T(8,128)(2,1)} custom-call(bf16[512,1024]{1,0:T(8,128)(2,1)} %bitcast.5.refs_0_, bf16[512,1024]{1,0:T(8,128)(2,1)} %collective-permute-done.15.refs_1_, bf16[512,1024]{1,0:T(8,128)(2,1)S(1)} %copy-done.19, bf16[256,1024]{1,0:T(8,128)(2,1)} %collective-permute-done.17.refs_3_, ...), custom_call_target="tpu_custom_call" | custom-call | flops 4294967296 | bytes 12582912 | tf_op jit(solution)/shard_map/pallas_call | solution.py:38
  205.7 1.5 collective-permute-start.24
  207.3 1.4 collective-permute-start.26
  208.7 11.5 %collective-permute-done.24.refs_3_ = bf16[256,1024]{1,0:T(8,128)(2,1)S(1)} collective-permute-done((bf16[256,1024]{1,0:T(8,128)(2,1)S(1)}, bf16[256,1024]{1,0:T(8,128)(2,1)S(1)}, u32[]{:S(2)}, u32[]{:S(2)}) %collective-permute-start.24) | collective-permute-done | bytes 524320 | tf_op jit(solution)/shard_map/ppermute | solution.py:159
  221.3 2.2 copy-done.3
  223.6 2.5 shard_map.99.refs_3_.refs_11_
  227.0 3.9 %shard_map.100 = (bf16[512,1024]{1,0:T(8,128)(2,1)S(1)}, bf16[512,1024]{1,0:T(8,128)(2,1)S(1)}, bf16[512,1024]{1,0:T(8,128)(2,1)S(1)}) custom-call(bf16[2048,1024]{1,0:T(8,128)(2,1)S(1)} %copy-done.4, bf16[1024,1024]{1,0:T(8,128)(2,1)S(1)} %copy-done.20, bf16[1024,1024]{1,0:T(8,128)(2,1)S(1)} %copy-done.8, bf16[512,1024]{1,0:T(8,128)(2,1)} %shard_map.99.refs_3_.refs_11_), custom_call_target="tpu_custom_call" | custom-call | flops 3221225472 | bytes 11534336 | tf_op jit(solution)/shard_map/pallas_call | solution.py:38
  233.8 9.0 %shard_map.101.refs_3_ = bf16[1024,1024]{1,0:T(8,128)(2,1)} custom-call(bf16[512,1024]{1,0:T(8,128)(2,1)} %bitcast.refs_0_, bf16[512,1024]{1,0:T(8,128)(2,1)S(1)} %copy-done.17, bf16[512,1024]{1,0:T(8,128)(2,1)S(1)} %copy-done.15, bf16[256,1024]{1,0:T(8,128)(2,1)S(1)} %copy-done.49, bf16[256,1024]{1,0:T(8,128)(2,1)S(1)} %copy-done.53, ...), custom_call_target="tpu_custom_call" | custom-call | flops 4294967296 | bytes 14680064 | tf_op jit(solution)/shard_map/pallas_call | solution.py:38
  243.9 1.7 add_convert_fusion.2
  245.6 1.5 collective-permute-start.25
  247.1 1.5 add_convert_fusion.1
  249.3 1.6 copy-done.9
  250.9 1.5 shard_map.102.refs_6_
  253.2 18.5 %collective-permute-done.25.refs_7_ = bf16[512,1024]{1,0:T(8,128)(2,1)S(1)} collective-permute-done((bf16[512,1024]{1,0:T(8,128)(2,1)S(1)}, bf16[512,1024]{1,0:T(8,128)(2,1)S(1)}, u32[]{:S(2)}, u32[]{:S(2)}) %collective-permute-start.25) | collective-permute-done | bytes 1048608 | tf_op jit(solution)/shard_map/ppermute | solution.py:156
  271.7 1.9 collective-permute-done.27.refs_8_
  273.6 3.9 %shard_map.103 = (bf16[512,1024]{1,0:T(8,128)(2,1)S(1)}, bf16[512,1024]{1,0:T(8,128)(2,1)}, bf16[512,1024]{1,0:T(8,128)(2,1)S(1)}) custom-call(bf16[2048,1024]{1,0:T(8,128)(2,1)S(1)} %copy-done.5, bf16[1024,1024]{1,0:T(8,128)(2,1)S(1)} %copy-done.21, bf16[1024,1024]{1,0:T(8,128)(2,1)S(1)} %copy-done.8, ...), custom_call_target="tpu_custom_call" | custom-call | flops 3221225472 | bytes 14680064 | tf_op jit(solution)/shard_map/pallas_call | solution.py:38
  278.1 16.1 %collective-permute-done.34.refs_1_ = bf16[512,1024]{1,0:T(8,128)(2,1)S(1)} collective-permute-done((bf16[512,1024]{1,0:T(8,128)(2,1)S(1)}, bf16[512,1024]{1,0:T(8,128)(2,1)S(1)}, u32[]{:S(2)}, u32[]{:S(2)}) %collective-permute-start.34) | collective-permute-done | bytes 1048608 | tf_op jit(solution)/shard_map/ppermute | solution.py:156
  296.1 1.3 collective-permute-start.36
  299.3 2.8 add_convert_fusion
  302.2 33.8 %collective-permute-done.33.refs_2_ = bf16[128,1024]{1,0:T(8,128)(2,1)S(1)} collective-permute-done((bf16[128,1024]{1,0:T(8,128)(2,1)S(1)}, bf16[128,1024]{1,0:T(8,128)(2,1)S(1)}, u32[]{:S(2)}, u32[]{:S(2)}) %collective-permute-start.33) | collective-permute-done | bytes 262176 | tf_op jit(solution)/shard_map/ppermute | solution.py:159
  336.0 1.5 shard_map.105.refs_0_
  338.6 2.4 shard_map.107.refs_3_
  343.3 1.6 shard_map.108
  (211 shorter events, 42.3 us)
Async XLA Ops:
  7.2 103.1 %all-gather.4.cloned.1.call-start = ((), (), s32[]{:S(2)}) async-start(), calls=%async_computation.3 | async-start | bytes 2621440 | tf_op jit(solution)/shard_map/all_gather | solution.py:226
  9.7 100.6 %all-gather.6.cloned.1.call-start = ((), (), s32[]{:S(2)}) async-start(), calls=%async_computation.4 | async-start | bytes 2621440 | tf_op jit(solution)/shard_map/all_gather | solution.py:226
  10.1 15.0 %collective-permute-start.9 = (bf16[256,1024]{1,0:T(8,128)(2,1)S(1)}, bf16[256,1024]{1,0:T(8,128)(2,1)S(1)}, u32[]{:S(2)}, u32[]{:S(2)}) collective-permute-start(bf16[256,1024]{1,0:T(8,128)(2,1)S(1)} %pad_maximum_fusion.1), channel_id=1, source_target_pairs={{0,1},{1,0},{2,3},{3,2},{4,5},{5,4},{6,7},{7,6},{8,9},{9,8},{10,11... | collective-permute-start | bytes 1572872 | tf_op jit(solution)/shard_map/ppermute | solution.py:159
  25.8 126.1 %all-gather.8.cloned.1.call-start = ((), (), s32[]{:S(2)}) async-start(), calls=%async_computation.5 | async-start | bytes 2621440 | tf_op jit(solution)/shard_map/all_gather | solution.py:226
  25.9 7.7 %collective-permute-start.10 = (bf16[128,1024]{1,0:T(8,128)(2,1)S(1)}, bf16[128,1024]{1,0:T(8,128)(2,1)S(1)}, u32[]{:S(2)}, u32[]{:S(2)}) collective-permute-start(bf16[128,1024]{1,0:T(8,128)(2,1)S(1)} %get-tuple-element.50), channel_id=1, source_target_pairs={{0,1},{1,0},{2,3},{3,2},{4,5},{5,4},{6,7},{7,6},{8,9},{9,8},{10,11... | collective-permute-start | bytes 786440 | tf_op jit(solution)/shard_map/ppermute | solution.py:159
  34.5 261.6 %reduce-scatter.6.cloned.1.call-start = ((), (), s32[]{:S(2)}) async-start(), calls=%async_computation.7 | async-start | bytes 2621440 | tf_op jit(solution)/shard_map/reduce_scatter | solution.py:229
  34.5 26.4 %collective-permute-start.1 = (bf16[512,1024]{1,0:T(8,128)(2,1)}, bf16[512,1024]{1,0:T(8,128)(2,1)S(1)}, u32[]{:S(2)}, u32[]{:S(2)}) collective-permute-start(bf16[512,1024]{1,0:T(8,128)(2,1)} %bitcast.refs_0_), channel_id=1, source_target_pairs={{0,16},{8,24},{16,0},{24,8},{1,17},{9,25},{17,1},{25,9},{2,18},{10... | collective-permute-start | bytes 3145736 | tf_op jit(solution)/shard_map/ppermute | solution.py:156
  36.0 26.4 %collective-permute-start = (bf16[512,1024]{1,0:T(8,128)(2,1)}, bf16[512,1024]{1,0:T(8,128)(2,1)S(1)}, u32[]{:S(2)}, u32[]{:S(2)}) collective-permute-start(bf16[512,1024]{1,0:T(8,128)(2,1)} %bitcast.refs_0_), channel_id=1, source_target_pairs={{0,1},{1,0},{2,3},{3,2},{4,5},{5,4},{6,7},{7,6},{8,9},{9,8},{10,11... | collective-permute-start | bytes 3145736 | tf_op jit(solution)/shard_map/ppermute | solution.py:159
  37.5 45.9 %collective-permute-start.16 = (bf16[512,1024]{1,0:T(8,128)(2,1)}, bf16[512,1024]{1,0:T(8,128)(2,1)S(1)}, u32[]{:S(2)}, u32[]{:S(2)}) collective-permute-start(bf16[512,1024]{1,0:T(8,128)(2,1)} %bitcast.5.refs_0_), channel_id=1, source_target_pairs={{0,16},{8,24},{16,0},{24,8},{1,17},{9,25},{17,1},{25,9},{2,18},{10... | collective-permute-start | bytes 3145736 | tf_op jit(solution)/shard_map/ppermute | solution.py:156
  38.0 46.9 %collective-permute-start.4 = (bf16[512,1024]{1,0:T(8,128)(2,1)}, bf16[512,1024]{1,0:T(8,128)(2,1)S(1)}, u32[]{:S(2)}, u32[]{:S(2)}) collective-permute-start(bf16[512,1024]{1,0:T(8,128)(2,1)} %bitcast.refs_0_), channel_id=1, source_target_pairs={{0,8},{8,0},{16,24},{24,16},{1,9},{9,1},{17,25},{25,17},{2,10},{10... | collective-permute-start | bytes 3145736 | tf_op jit(solution)/shard_map/ppermute | solution.py:153
  38.0 46.9 %collective-permute-start.15 = (bf16[512,1024]{1,0:T(8,128)(2,1)}, bf16[512,1024]{1,0:T(8,128)(2,1)}, u32[]{:S(2)}, u32[]{:S(2)}) collective-permute-start(bf16[512,1024]{1,0:T(8,128)(2,1)} %bitcast.5.refs_0_), channel_id=1, source_target_pairs={{0,1},{1,0},{2,3},{3,2},{4,5},{5,4},{6,7},{7,6},{8,9},{9,8},{10,11... | collective-permute-start | bytes 3145736 | tf_op jit(solution)/shard_map/ppermute | solution.py:159
  60.9 122.5 %copy-start.14 = (bf16[512,1024]{1,0:T(8,128)(2,1)}, bf16[512,1024]{1,0:T(8,128)(2,1)S(1)}, u32[]{:S(2)}) copy-start(bf16[512,1024]{1,0:T(8,128)(2,1)S(1)} %collective-permute-done.1.refs_2_) | copy-start | bytes 3145732
  60.9 35.1 %collective-permute-start.2 = (bf16[256,1024]{1,0:T(8,128)(2,1)S(1)}, bf16[256,1024]{1,0:T(8,128)(2,1)S(1)}, u32[]{:S(2)}, u32[]{:S(2)}) collective-permute-start(bf16[256,1024]{1,0:T(8,128)(2,1)S(1)} %slice.32), channel_id=1, source_target_pairs={{0,1},{1,0},{2,3},{3,2},{4,5},{5,4},{6,7},{7,6},{8,9},{9,8},{10,11... | collective-permute-start | bytes 1572872 | tf_op jit(solution)/shard_map/ppermute | solution.py:159
  62.4 121.0 %copy-start.16 = (bf16[512,1024]{1,0:T(8,128)(2,1)}, bf16[512,1024]{1,0:T(8,128)(2,1)S(1)}, u32[]{:S(2)}) copy-start(bf16[512,1024]{1,0:T(8,128)(2,1)S(1)} %collective-permute-done.refs_1_) | copy-start | bytes 3145732
  62.5 34.2 %collective-permute-start.3 = (bf16[256,1024]{1,0:T(8,128)(2,1)S(1)}, bf16[256,1024]{1,0:T(8,128)(2,1)S(1)}, u32[]{:S(2)}, u32[]{:S(2)}) collective-permute-start(bf16[256,1024]{1,0:T(8,128)(2,1)S(1)} %slice.33), channel_id=1, source_target_pairs={{0,16},{8,24},{16,0},{24,8},{1,17},{9,25},{17,1},{25,9},{2,18},{10... | collective-permute-start | bytes 1572872 | tf_op jit(solution)/shard_map/ppermute | solution.py:156
  83.4 76.2 %copy-start.18 = (bf16[512,1024]{1,0:T(8,128)(2,1)}, bf16[512,1024]{1,0:T(8,128)(2,1)S(1)}, u32[]{:S(2)}) copy-start(bf16[512,1024]{1,0:T(8,128)(2,1)S(1)} %collective-permute-done.16.refs_2_) | copy-start | bytes 3145732
  83.4 20.9 %collective-permute-start.17 = (bf16[256,1024]{1,0:T(8,128)(2,1)S(1)}, bf16[256,1024]{1,0:T(8,128)(2,1)}, u32[]{:S(2)}, u32[]{:S(2)}) collective-permute-start(bf16[256,1024]{1,0:T(8,128)(2,1)S(1)} %slice.34), channel_id=1, source_target_pairs={{0,1},{1,0},{2,3},{3,2},{4,5},{5,4},{6,7},{7,6},{8,9},{9,8},{10,11... | collective-permute-start | bytes 1572872 | tf_op jit(solution)/shard_map/ppermute | solution.py:159
  84.9 24.0 %copy-start.24 = (bf16[512,1024]{1,0:T(8,128)(2,1)}, bf16[512,1024]{1,0:T(8,128)(2,1)S(1)}, u32[]{:S(2)}) copy-start(bf16[512,1024]{1,0:T(8,128)(2,1)S(1)} %collective-permute-done.4.refs_5_) | copy-start | bytes 3145732
  84.9 22.9 %collective-permute-start.5 = (bf16[512,1024]{1,0:T(8,128)(2,1)S(1)}, bf16[512,1024]{1,0:T(8,128)(2,1)S(1)}, u32[]{:S(2)}, u32[]{:S(2)}) collective-permute-start(bf16[512,1024]{1,0:T(8,128)(2,1)S(1)} %collective-permute-done.refs_1_), channel_id=1, source_target_pairs={{0,8},{8,0},{16,24},{24,16},{1,9},{9,1},{17,25},{25,17},{2,10},{10... | collective-permute-start | bytes 3145736 | tf_op jit(solution)/shard_map/ppermute | solution.py:153
  84.9 24.0 %collective-permute-start.6 = (bf16[512,1024]{1,0:T(8,128)(2,1)S(1)}, bf16[512,1024]{1,0:T(8,128)(2,1)S(1)}, u32[]{:S(2)}, u32[]{:S(2)}) collective-permute-start(bf16[512,1024]{1,0:T(8,128)(2,1)S(1)} %collective-permute-done.1.refs_2_), channel_id=1, source_target_pairs={{0,8},{8,0},{16,24},{24,16},{1,9},{9,1},{17,25},{25,17},{2,10},{10... | collective-permute-start | bytes 3145736 | tf_op jit(solution)/shard_map/ppermute | solution.py:153
  96.0 9.3 %collective-permute-start.18 = (bf16[256,1024]{1,0:T(8,128)(2,1)S(1)}, bf16[256,1024]{1,0:T(8,128)(2,1)}, u32[]{:S(2)}, u32[]{:S(2)}) collective-permute-start(bf16[256,1024]{1,0:T(8,128)(2,1)S(1)} %slice.35), channel_id=1, source_target_pairs={{0,16},{8,24},{16,0},{24,8},{1,17},{9,25},{17,1},{25,9},{2,18},{10... | collective-permute-start | bytes 1572872 | tf_op jit(solution)/shard_map/ppermute | solution.py:156
  96.6 9.0 %collective-permute-start.7 = (bf16[256,1024]{1,0:T(8,128)(2,1)S(1)}, bf16[256,1024]{1,0:T(8,128)(2,1)S(1)}, u32[]{:S(2)}, u32[]{:S(2)}) collective-permute-start(bf16[256,1024]{1,0:T(8,128)(2,1)S(1)} %collective-permute-done.2.refs_3_), channel_id=1, source_target_pairs={{0,8},{8,0},{16,24},{24,16},{1,9},{9,1},{17,25},{25,17},{2,10},{10... | collective-permute-start | bytes 1572872 | tf_op jit(solution)/shard_map/ppermute | solution.py:153
  104.3 2.3 collective-permute-start.8
  105.3 50.8 %collective-permute-start.19 = (bf16[512,1024]{1,0:T(8,128)(2,1)}, bf16[512,1024]{1,0:T(8,128)(2,1)}, u32[]{:S(2)}, u32[]{:S(2)}) collective-permute-start(bf16[512,1024]{1,0:T(8,128)(2,1)} %bitcast.5.refs_0_), channel_id=1, source_target_pairs={{0,8},{8,0},{16,24},{24,16},{1,9},{9,1},{17,25},{25,17},{2,10},{10... | collective-permute-start | bytes 3145736 | tf_op jit(solution)/shard_map/ppermute | solution.py:153
  106.4 52.7 %collective-permute-start.20 = (bf16[512,1024]{1,0:T(8,128)(2,1)}, bf16[512,1024]{1,0:T(8,128)(2,1)}, u32[]{:S(2)}, u32[]{:S(2)}) collective-permute-start(bf16[512,1024]{1,0:T(8,128)(2,1)} %collective-permute-done.15.refs_1_), channel_id=1, source_target_pairs={{0,8},{8,0},{16,24},{24,16},{1,9},{9,1},{17,25},{25,17},{2,10},{10... | collective-permute-start | bytes 3145736 | tf_op jit(solution)/shard_map/ppermute | solution.py:153
  107.4 52.1 %collective-permute-start.21 = (bf16[512,1024]{1,0:T(8,128)(2,1)S(1)}, bf16[512,1024]{1,0:T(8,128)(2,1)}, u32[]{:S(2)}, u32[]{:S(2)}) collective-permute-start(bf16[512,1024]{1,0:T(8,128)(2,1)S(1)} %collective-permute-done.16.refs_2_), channel_id=1, source_target_pairs={{0,8},{8,0},{16,24},{24,16},{1,9},{9,1},{17,25},{25,17},{2,10},{10... | collective-permute-start | bytes 3145736 | tf_op jit(solution)/shard_map/ppermute | solution.py:153
  108.7 49.8 %collective-permute-start.22 = (bf16[256,1024]{1,0:T(8,128)(2,1)}, bf16[256,1024]{1,0:T(8,128)(2,1)}, u32[]{:S(2)}, u32[]{:S(2)}) collective-permute-start(bf16[256,1024]{1,0:T(8,128)(2,1)} %collective-permute-done.17.refs_3_), channel_id=1, source_target_pairs={{0,8},{8,0},{16,24},{24,16},{1,9},{9,1},{17,25},{25,17},{2,10},{10... | collective-permute-start | bytes 1572872 | tf_op jit(solution)/shard_map/ppermute | solution.py:153
  109.9 49.2 %collective-permute-start.23 = (bf16[256,1024]{1,0:T(8,128)(2,1)}, bf16[256,1024]{1,0:T(8,128)(2,1)}, u32[]{:S(2)}, u32[]{:S(2)}) collective-permute-start(bf16[256,1024]{1,0:T(8,128)(2,1)} %collective-permute-done.18.refs_4_), channel_id=1, source_target_pairs={{0,8},{8,0},{16,24},{24,16},{1,9},{9,1},{17,25},{25,17},{2,10},{10... | collective-permute-start | bytes 1572872 | tf_op jit(solution)/shard_map/ppermute | solution.py:153
  156.1 17.2 %collective-permute-start.14 = (bf16[512,1024]{1,0:T(8,128)(2,1)S(1)}, bf16[512,1024]{1,0:T(8,128)(2,1)}, u32[]{:S(2)}, u32[]{:S(2)}) collective-permute-start(bf16[512,1024]{1,0:T(8,128)(2,1)S(1)} %shard_map.93.refs_3_.refs_13_), channel_id=1, source_target_pairs={{0,8},{8,0},{16,24},{24,16},{1,9},{9,1},{17,25},{25,17},{2,10},{10... | collective-permute-start | bytes 3145736 | tf_op jit(solution)/shard_map/ppermute | solution.py:153
  158.5 19.2 %collective-permute-start.11 = (bf16[512,1024]{1,0:T(8,128)(2,1)}, bf16[512,1024]{1,0:T(8,128)(2,1)S(1)}, u32[]{:S(2)}, u32[]{:S(2)}) collective-permute-start(bf16[512,1024]{1,0:T(8,128)(2,1)} %get-tuple-element.26.refs_14_), channel_id=1, source_target_pairs={{0,8},{8,0},{16,24},{24,16},{1,9},{9,1},{17,25},{25,17},{2,10},{10... | collective-permute-start | bytes 3145736 | tf_op jit(solution)/shard_map/ppermute | solution.py:153
  159.1 18.7 %collective-permute-start.12 = (bf16[512,1024]{1,0:T(8,128)(2,1)S(1)}, bf16[512,1024]{1,0:T(8,128)(2,1)S(1)}, u32[]{:S(2)}, u32[]{:S(2)}) collective-permute-start(bf16[512,1024]{1,0:T(8,128)(2,1)S(1)} %get-tuple-element.27.refs_15_), channel_id=1, source_target_pairs={{0,8},{8,0},{16,24},{24,16},{1,9},{9,1},{17,25},{25,17},{2,10},{10... | collective-permute-start | bytes 3145736 | tf_op jit(solution)/shard_map/ppermute | solution.py:153
  159.1 18.6 %collective-permute-start.13 = (bf16[512,1024]{1,0:T(8,128)(2,1)S(1)}, bf16[512,1024]{1,0:T(8,128)(2,1)}, u32[]{:S(2)}, u32[]{:S(2)}) collective-permute-start(bf16[512,1024]{1,0:T(8,128)(2,1)S(1)} %get-tuple-element.28.refs_16_), channel_id=1, source_target_pairs={{0,8},{8,0},{16,24},{24,16},{1,9},{9,1},{17,25},{25,17},{2,10},{10... | collective-permute-start | bytes 3145736 | tf_op jit(solution)/shard_map/ppermute | solution.py:153
  193.4 104.0 %reduce-scatter.4.cloned.1.call-start = ((), (), s32[]{:S(2)}) async-start(), calls=%async_computation.6 | async-start | bytes 2621440 | tf_op jit(solution)/shard_map/reduce_scatter | solution.py:229
  205.6 135.4 %reduce-scatter.8.cloned.1.call-start = ((), (), s32[]{:S(2)}) async-start(), calls=%async_computation.8 | async-start | bytes 2621440 | tf_op jit(solution)/shard_map/reduce_scatter | solution.py:229
  205.7 14.4 %collective-permute-start.24 = (bf16[256,1024]{1,0:T(8,128)(2,1)S(1)}, bf16[256,1024]{1,0:T(8,128)(2,1)S(1)}, u32[]{:S(2)}, u32[]{:S(2)}) collective-permute-start(bf16[256,1024]{1,0:T(8,128)(2,1)S(1)} %get-tuple-element.45), channel_id=1, source_target_pairs={{0,1},{1,0},{2,3},{3,2},{4,5},{5,4},{6,7},{7,6},{8,9},{9,8},{10,11... | collective-permute-start | bytes 1572872 | tf_op jit(solution)/shard_map/ppermute | solution.py:159
  207.3 14.1 %collective-permute-start.26 = (bf16[256,1024]{1,0:T(8,128)(2,1)S(1)}, bf16[256,1024]{1,0:T(8,128)(2,1)S(1)}, u32[]{:S(2)}, u32[]{:S(2)}) collective-permute-start(bf16[256,1024]{1,0:T(8,128)(2,1)S(1)} %get-tuple-element.46), channel_id=1, source_target_pairs={{0,16},{8,24},{16,0},{24,8},{1,17},{9,25},{17,1},{25,9},{2,18},{10... | collective-permute-start | bytes 1572872 | tf_op jit(solution)/shard_map/ppermute | solution.py:156
  242.8 5.7 %collective-permute-start.31 = (bf16[512,1024]{1,0:T(8,128)(2,1)}, bf16[512,1024]{1,0:T(8,128)(2,1)S(1)}, u32[]{:S(2)}, u32[]{:S(2)}) collective-permute-start(bf16[512,1024]{1,0:T(8,128)(2,1)} %shard_map.99.refs_3_.refs_11_), channel_id=1, source_target_pairs={{0,8},{8,0},{16,24},{24,16},{1,9},{9,1},{17,25},{25,17},{2,10},{10... | collective-permute-start | bytes 3145736 | tf_op jit(solution)/shard_map/ppermute | solution.py:153
  242.9 9.5 %collective-permute-start.28 = (bf16[512,1024]{1,0:T(8,128)(2,1)}, bf16[512,1024]{1,0:T(8,128)(2,1)S(1)}, u32[]{:S(2)}, u32[]{:S(2)}) collective-permute-start(bf16[512,1024]{1,0:T(8,128)(2,1)} %copy-done.38), channel_id=1, source_target_pairs={{0,8},{8,0},{16,24},{24,16},{1,9},{9,1},{17,25},{25,17},{2,10},{10... | collective-permute-start | bytes 3145736 | tf_op jit(solution)/shard_map/ppermute | solution.py:153
  243.4 9.7 %collective-permute-start.29 = (bf16[512,1024]{1,0:T(8,128)(2,1)}, bf16[512,1024]{1,0:T(8,128)(2,1)S(1)}, u32[]{:S(2)}, u32[]{:S(2)}) collective-permute-start(bf16[512,1024]{1,0:T(8,128)(2,1)} %copy-done.37), channel_id=1, source_target_pairs={{0,8},{8,0},{16,24},{24,16},{1,9},{9,1},{17,25},{25,17},{2,10},{10... | collective-permute-start | bytes 3145736 | tf_op jit(solution)/shard_map/ppermute | solution.py:153
  243.5 9.7 %collective-permute-start.30 = (bf16[512,1024]{1,0:T(8,128)(2,1)}, bf16[512,1024]{1,0:T(8,128)(2,1)S(1)}, u32[]{:S(2)}, u32[]{:S(2)}) collective-permute-start(bf16[512,1024]{1,0:T(8,128)(2,1)} %copy-done.36), channel_id=1, source_target_pairs={{0,8},{8,0},{16,24},{24,16},{1,9},{9,1},{17,25},{25,17},{2,10},{10... | collective-permute-start | bytes 3145736 | tf_op jit(solution)/shard_map/ppermute | solution.py:153
  245.6 26.1 %collective-permute-start.25 = (bf16[512,1024]{1,0:T(8,128)(2,1)S(1)}, bf16[512,1024]{1,0:T(8,128)(2,1)S(1)}, u32[]{:S(2)}, u32[]{:S(2)}) collective-permute-start(bf16[512,1024]{1,0:T(8,128)(2,1)S(1)} %add_convert_fusion.2), channel_id=1, source_target_pairs={{0,16},{8,24},{16,0},{24,8},{1,17},{9,25},{17,1},{25,9},{2,18},{10... | collective-permute-start | bytes 3145736 | tf_op jit(solution)/shard_map/ppermute | solution.py:156
  248.6 25.0 %collective-permute-start.27 = (bf16[512,1024]{1,0:T(8,128)(2,1)S(1)}, bf16[512,1024]{1,0:T(8,128)(2,1)S(1)}, u32[]{:S(2)}, u32[]{:S(2)}) collective-permute-start(bf16[512,1024]{1,0:T(8,128)(2,1)S(1)} %add_convert_fusion.1), channel_id=1, source_target_pairs={{0,1},{1,0},{2,3},{3,2},{4,5},{5,4},{6,7},{7,6},{8,9},{9,8},{10,11... | collective-permute-start | bytes 3145736 | tf_op jit(solution)/shard_map/ppermute | solution.py:159
  252.4 41.7 %collective-permute-start.34 = (bf16[512,1024]{1,0:T(8,128)(2,1)S(1)}, bf16[512,1024]{1,0:T(8,128)(2,1)S(1)}, u32[]{:S(2)}, u32[]{:S(2)}) collective-permute-start(bf16[512,1024]{1,0:T(8,128)(2,1)S(1)} %shard_map.102.refs_6_), channel_id=1, source_target_pairs={{0,16},{8,24},{16,0},{24,8},{1,17},{9,25},{17,1},{25,9},{2,18},{10... | collective-permute-start | bytes 3145736 | tf_op jit(solution)/shard_map/ppermute | solution.py:156
  277.5 58.5 %collective-permute-start.32 = (bf16[512,1024]{1,0:T(8,128)(2,1)}, bf16[512,1024]{1,0:T(8,128)(2,1)}, u32[]{:S(2)}, u32[]{:S(2)}) collective-permute-start(bf16[512,1024]{1,0:T(8,128)(2,1)} %get-tuple-element.40), channel_id=1, source_target_pairs={{0,16},{8,24},{16,0},{24,8},{1,17},{9,25},{17,1},{25,9},{2,18},{10... | collective-permute-start | bytes 3145736 | tf_op jit(solution)/shard_map/ppermute | solution.py:156
  295.4 43.2 %collective-permute-start.35 = (bf16[512,1024]{1,0:T(8,128)(2,1)}, bf16[512,1024]{1,0:T(8,128)(2,1)}, u32[]{:S(2)}, u32[]{:S(2)}) collective-permute-start(bf16[512,1024]{1,0:T(8,128)(2,1)} %shard_map.106), channel_id=1, source_target_pairs={{0,1},{1,0},{2,3},{3,2},{4,5},{5,4},{6,7},{7,6},{8,9},{9,8},{10,11... | collective-permute-start | bytes 3145736 | tf_op jit(solution)/shard_map/ppermute | solution.py:159
  296.1 42.5 %collective-permute-start.36 = (bf16[256,1024]{1,0:T(8,128)(2,1)}, bf16[256,1024]{1,0:T(8,128)(2,1)S(1)}, u32[]{:S(2)}, u32[]{:S(2)}) collective-permute-start(bf16[256,1024]{1,0:T(8,128)(2,1)} %reduce-scatter.6.cloned.1.call-done), channel_id=1, source_target_pairs={{0,1},{1,0},{2,3},{3,2},{4,5},{5,4},{6,7},{7,6},{8,9},{9,8},{10,11... | collective-permute-start | bytes 1572872 | tf_op jit(solution)/shard_map/ppermute | solution.py:159
  298.5 37.5 %copy-start.44 = (bf16[512,1024]{1,0:T(8,128)(2,1)S(1)}, bf16[512,1024]{1,0:T(8,128)(2,1)}, u32[]{:S(2)}) copy-start(bf16[512,1024]{1,0:T(8,128)(2,1)} %copy-done.43) | copy-start | bytes 3145732
  298.5 37.5 %collective-permute-start.33 = (bf16[128,1024]{1,0:T(8,128)(2,1)S(1)}, bf16[128,1024]{1,0:T(8,128)(2,1)S(1)}, u32[]{:S(2)}, u32[]{:S(2)}) collective-permute-start(bf16[128,1024]{1,0:T(8,128)(2,1)S(1)} %get-tuple-element.48), channel_id=1, source_target_pairs={{0,1},{1,0},{2,3},{3,2},{4,5},{5,4},{6,7},{7,6},{8,9},{9,8},{10,11... | collective-permute-start | bytes 786440 | tf_op jit(solution)/shard_map/ppermute | solution.py:159
  (60 other events, 279.4 us)
Sparse Core Ops, SparseCore 0:
  10.1 48.6 all-gather.3
  61.0 44.6 all-gather.5
  107.2 44.6 all-gather.7
  193.5 42.7 reduce-scatter.5
  238.5 43.1 reduce-scatter.3
  283.9 43.1 reduce-scatter.7

commit v5 on v4

--- a/solution.py
+++ b/solution.py
@@ -257,7 +257,7 @@
         )
         down_sum = scatter_units(down_term)
         down_sides = [(down, 0, half), (down, 1, half)]
-        output_far = self.far_first(hidden, down_sides, [])
+        output_far = self.far_first(hidden, down_sides, [down_term])
         output_far |= self.far_rest(hidden, down_sides, [output_far[1, 1]])
         act, act_turned = call(
             functools.partial(grads_kernel, rows_cot, width),

time: 353 us -> 340 us (0.963)
  waiting for transfers between devices: 177 us -> 169 us
    ppermute x8, waiting for transfers between devices: 77.5 us -> 69.5 us  [chip(): return lax.ppermute(array, 'inp', [(at, at ^ 2) for at in range(4)])]
    all_gather x3, waiting for transfers between devices: 18.1 us -> 11.3 us  [gather_units(): return lax.all_gather(array, 'wt', axis=0, tiled=True)]
    ppermute x11, waiting for transfers between devices: 81.3 us -> 87.8 us  [other(): return lax.ppermute(array, 'out', [(0, 1), (1, 0)])]
    unnamed x134 -> x128, local copies, waits for them, and re-layouts: 34.3 us -> 33 us
  transfers between devices with their start and end apart: 43 -> 43, of which waited for: 14 -> 16; matrix products, arithmetic and copies ran while one was open for 3% -> 3% of each run, Pallas kernels for 20% -> 21%
where the time goes in v5:
time: 340 us; the launch traced here: 339 us
  waiting for transfers between devices  169 us (50%)
  Pallas kernels  84.4 us (25%)
  local copies, waits for them, and re-layouts  35.6 us (10%)
  starting transfers between devices  25.3 us (7%)
  between operations  14.8 us (4%)
  other arithmetic  9.82 us (3%)
    ppermute x11, waiting for transfers between devices, other(): return lax.ppermute(array, 'out', [(0, 1), (1, 0)])  87.8 us
    pallas_call x17, Pallas kernels, call(): pl.pallas_call(body, out_shape=list(outs), in_specs=[*specs, *[pl.BlockSp...  84.4 us
    ppermute x8, waiting for transfers between devices, chip(): return lax.ppermute(array, 'inp', [(at, at ^ 2) for at in range(4)])  69.5 us
    unnamed x128, local copies, waits for them, and re-layouts  33 us
    ppermute x11, starting transfers between devices, other(): return lax.ppermute(array, 'out', [(0, 1), (1, 0)])  12.5 us
    all_gather x3, waiting for transfers between devices, gather_units(): return lax.all_gather(array, 'wt', axis=0, tiled=True)  11.3 us
    ppermute x8, starting transfers between devices, chip(): return lax.ppermute(array, 'inp', [(at, at ^ 2) for at in range(4)])  9.58 us
  transfers between devices with their start and end apart: 43, of which 16 were waited for; matrix products, arithmetic and copies ran while one was open for 3% of the time, Pallas kernels for 21%

profile of v5, /device:TPU:0, one launch (start us, length us, event | category | flops | bytes accessed | tf_op | source)
XLA Modules:
  0.0 339.1 jit_solution(13643350771344499071)
XLA Ops:
  7.2 1.3 constant_dynamic-slice_fusion.2
  10.1 3.0 collective-permute-start.9
  13.1 11.9 %collective-permute-done.9 = bf16[256,1024]{1,0:T(8,128)(2,1)S(1)} collective-permute-done((bf16[256,1024]{1,0:T(8,128)(2,1)S(1)}, bf16[256,1024]{1,0:T(8,128)(2,1)S(1)}, u32[]{:S(2)}, u32[]{:S(2)}) %collective-permute-start.9) | collective-permute-done | bytes 524320 | tf_op jit(solution)/shard_map/ppermute | solution.py:159
  25.9 1.8 collective-permute-start.10
  27.8 1.5 collective-permute-start.1
  30.1 5.2 %collective-permute-done.10 = bf16[128,1024]{1,0:T(8,128)(2,1)S(1)} collective-permute-done((bf16[128,1024]{1,0:T(8,128)(2,1)S(1)}, bf16[128,1024]{1,0:T(8,128)(2,1)S(1)}, u32[]{:S(2)}, u32[]{:S(2)}) %collective-permute-start.10) | collective-permute-done | bytes 262176 | tf_op jit(solution)/shard_map/ppermute | solution.py:159
  35.3 1.7 collective-permute-start.11
  37.9 16.2 %collective-permute-done.1.refs_2_ = bf16[512,1024]{1,0:T(8,128)(2,1)S(1)} collective-permute-done((bf16[512,1024]{1,0:T(8,128)(2,1)}, bf16[512,1024]{1,0:T(8,128)(2,1)S(1)}, u32[]{:S(2)}, u32[]{:S(2)}) %collective-permute-start.1) | collective-permute-done | bytes 1048608 | tf_op jit(solution)/shard_map/ppermute | solution.py:156
  54.5 3.3 collective-permute-done.refs_1_
  57.8 1.8 collective-permute-start.3
  59.5 17.0 %collective-permute-done.12.refs_2_ = bf16[512,1024]{1,0:T(8,128)(2,1)S(1)} collective-permute-done((bf16[512,1024]{1,0:T(8,128)(2,1)}, bf16[512,1024]{1,0:T(8,128)(2,1)S(1)}, u32[]{:S(2)}, u32[]{:S(2)}) %collective-permute-start.12) | collective-permute-done | bytes 1048608 | tf_op jit(solution)/shard_map/ppermute | solution.py:156
  76.9 3.4 collective-permute-done.11.refs_1_
  81.4 10.0 %collective-permute-done.2.refs_3_ = bf16[256,1024]{1,0:T(8,128)(2,1)S(1)} collective-permute-done((bf16[256,1024]{1,0:T(8,128)(2,1)S(1)}, bf16[256,1024]{1,0:T(8,128)(2,1)S(1)}, u32[]{:S(2)}, u32[]{:S(2)}) %collective-permute-start.2) | collective-permute-done | bytes 524320 | tf_op jit(solution)/shard_map/ppermute | solution.py:159
  91.4 1.7 collective-permute-start.14
  93.9 7.2 %collective-permute-done.13.refs_3_ = bf16[256,1024]{1,0:T(8,128)(2,1)} collective-permute-done((bf16[256,1024]{1,0:T(8,128)(2,1)S(1)}, bf16[256,1024]{1,0:T(8,128)(2,1)}, u32[]{:S(2)}, u32[]{:S(2)}) %collective-permute-start.13) | collective-permute-done | bytes 524320 | tf_op jit(solution)/shard_map/ppermute | solution.py:159
  113.7 16.2 %shard_map.92 = (bf16[2048,512]{1,0:T(8,128)(2,1)}, bf16[512,2048]{1,0:T(8,128)(2,1)}, bf16[2048,512]{1,0:T(8,128)(2,1)}, bf16[2048,512]{1,0:T(8,128)(2,1)}) custom-call(bf16[512,1024]{1,0:T(8,128)(2,1)} %bitcast.refs_0_, bf16[512,1024]{1,0:T(8,128)(2,1)S(1)} %collective-permute-done.refs_1_, bf16[512,1024]{1,0:T(8,128)(2,1)S(1)} %collective-permute-done.1.refs_2_, ...), custom_call_target="tpu_custom_call" | custom-call | flops 8589934592 | bytes 20971520 | tf_op jit(solution)/shard_map/pallas_call | solution.py:38
  130.0 11.2 %shard_map.93.refs_2_ = bf16[512,2048]{1,0:T(8,128)(2,1)} custom-call(bf16[512,1024]{1,0:T(8,128)(2,1)} %bitcast.5.refs_0_, bf16[512,1024]{1,0:T(8,128)(2,1)} %collective-permute-done.11.refs_1_, bf16[512,1024]{1,0:T(8,128)(2,1)S(1)} %collective-permute-done.12.refs_2_, bf16[256,1024]{1,0:T(8,128)(2,1)} %collective-permute-done.13.refs_3_, ...), custom_call_target="tpu_custom_call" | custom-call | flops 4294967296 | bytes 12582912 | tf_op jit(solution)/shard_map/pallas_call | solution.py:38
  141.2 11.3 %all-gather.8.cloned.1.call-done.refs_1_.refs_2_.refs_10_ = bf16[512,2048]{1,0:T(8,128)(2,1)} async-done(((bf16[128,2048]{1,0:T(8,128)(2,1)}), bf16[512,2048]{1,0:T(8,128)(2,1)}) %all-gather.8.cloned.1.call-update) | async-done | bytes 2097168 | tf_op jit(solution)/shard_map/all_gather | solution.py:226
  152.5 1.6 copy-done
  154.1 1.6 copy-done.10
  157.3 2.3 shard_map.95
  160.9 13.5 %shard_map.96 = (bf16[2048,1024]{1,0:T(8,128)(2,1)}, bf16[1024,2048]{1,0:T(8,128)(2,1)}) custom-call(bf16[512,1024]{1,0:T(8,128)(2,1)} %bitcast.5.refs_0_, bf16[512,1024]{1,0:T(8,128)(2,1)} %collective-permute-done.11.refs_1_, bf16[512,1024]{1,0:T(8,128)(2,1)S(1)} %collective-permute-done.12.refs_2_, bf16[256,1024]{1,0:T(8,128)(2,1)} %collective-permute-done.13.refs_3_, ...), custom_call_target="tpu_custom_call" | custom-call | flops 4294967296 | bytes 23068672 | tf_op jit(solution)/shard_map/pallas_call | solution.py:38
  174.4 2.2 copy-done.3
  177.6 2.3 shard_map.98
  183.0 9.2 %shard_map.99.refs_2_ = bf16[1024,1024]{1,0:T(8,128)(2,1)} custom-call(bf16[512,1024]{1,0:T(8,128)(2,1)} %bitcast.refs_0_, bf16[512,1024]{1,0:T(8,128)(2,1)S(1)} %copy-done.19, bf16[512,1024]{1,0:T(8,128)(2,1)S(1)} %copy-done.16, bf16[256,1024]{1,0:T(8,128)(2,1)S(1)} %copy-done.45, bf16[256,1024]{1,0:T(8,128)(2,1)S(1)} %copy-done.49, ...), custom_call_target="tpu_custom_call" | custom-call | flops 4294967296 | bytes 14680064 | tf_op jit(solution)/shard_map/pallas_call | solution.py:38
  193.9 1.5 collective-permute-start.24
  195.5 1.4 collective-permute-start.26
  196.9 10.9 %collective-permute-done.24.refs_3_ = bf16[256,1024]{1,0:T(8,128)(2,1)S(1)} collective-permute-done((bf16[256,1024]{1,0:T(8,128)(2,1)S(1)}, bf16[256,1024]{1,0:T(8,128)(2,1)S(1)}, u32[]{:S(2)}, u32[]{:S(2)}) %collective-permute-start.24) | collective-permute-done | bytes 524320 | tf_op jit(solution)/shard_map/ppermute | solution.py:159
  209.0 2.2 copy-done.4
  211.2 2.5 shard_map.100.refs_3_.refs_11_
  214.6 3.9 %shard_map.101 = (bf16[512,1024]{1,0:T(8,128)(2,1)S(1)}, bf16[512,1024]{1,0:T(8,128)(2,1)S(1)}, bf16[512,1024]{1,0:T(8,128)(2,1)S(1)}) custom-call(bf16[2048,1024]{1,0:T(8,128)(2,1)S(1)} %copy-done.5, bf16[1024,1024]{1,0:T(8,128)(2,1)S(1)} %copy-done.21, bf16[1024,1024]{1,0:T(8,128)(2,1)S(1)} %copy-done.8, bf16[512,1024]{1,0:T(8,128)(2,1)} %shard_map.100.refs_3_.refs_11_), custom_call_target="tpu_custom_call" | custom-call | flops 3221225472 | bytes 11534336 | tf_op jit(solution)/shard_map/pallas_call | solution.py:38
  220.9 9.3 %shard_map.102.refs_3_ = bf16[1024,1024]{1,0:T(8,128)(2,1)} custom-call(bf16[512,1024]{1,0:T(8,128)(2,1)} %bitcast.refs_0_, bf16[512,1024]{1,0:T(8,128)(2,1)S(1)} %copy-done.20, bf16[512,1024]{1,0:T(8,128)(2,1)S(1)} %copy-done.17, bf16[256,1024]{1,0:T(8,128)(2,1)S(1)} %copy-done.46, bf16[256,1024]{1,0:T(8,128)(2,1)S(1)} %copy-done.50, ...), custom_call_target="tpu_custom_call" | custom-call | flops 4294967296 | bytes 14680064 | tf_op jit(solution)/shard_map/pallas_call | solution.py:38
  231.3 1.6 add_convert_fusion.2
  232.9 1.5 collective-permute-start.25
  234.4 1.5 add_convert_fusion.1
  236.5 1.6 copy-done.9
  238.1 1.5 shard_map.103.refs_6_
  240.3 18.7 %collective-permute-done.25.refs_7_ = bf16[512,1024]{1,0:T(8,128)(2,1)S(1)} collective-permute-done((bf16[512,1024]{1,0:T(8,128)(2,1)S(1)}, bf16[512,1024]{1,0:T(8,128)(2,1)S(1)}, u32[]{:S(2)}, u32[]{:S(2)}) %collective-permute-start.25) | collective-permute-done | bytes 1048608 | tf_op jit(solution)/shard_map/ppermute | solution.py:156
  259.0 1.8 collective-permute-done.27.refs_8_
  260.8 3.9 %shard_map.104 = (bf16[512,1024]{1,0:T(8,128)(2,1)S(1)}, bf16[512,1024]{1,0:T(8,128)(2,1)}, bf16[512,1024]{1,0:T(8,128)(2,1)S(1)}) custom-call(bf16[2048,1024]{1,0:T(8,128)(2,1)S(1)} %copy-done.6, bf16[1024,1024]{1,0:T(8,128)(2,1)S(1)} %copy-done.22, bf16[1024,1024]{1,0:T(8,128)(2,1)S(1)} %copy-done.8, ...), custom_call_target="tpu_custom_call" | custom-call | flops 3221225472 | bytes 14680064 | tf_op jit(solution)/shard_map/pallas_call | solution.py:38
  265.4 16.1 %collective-permute-done.34.refs_1_ = bf16[512,1024]{1,0:T(8,128)(2,1)S(1)} collective-permute-done((bf16[512,1024]{1,0:T(8,128)(2,1)S(1)}, bf16[512,1024]{1,0:T(8,128)(2,1)S(1)}, u32[]{:S(2)}, u32[]{:S(2)}) %collective-permute-start.34) | collective-permute-done | bytes 1048608 | tf_op jit(solution)/shard_map/ppermute | solution.py:156
  283.2 1.5 collective-permute-start.36
  286.4 2.8 add_convert_fusion
  289.2 34.1 %collective-permute-done.33.refs_2_ = bf16[128,1024]{1,0:T(8,128)(2,1)S(1)} collective-permute-done((bf16[128,1024]{1,0:T(8,128)(2,1)S(1)}, bf16[128,1024]{1,0:T(8,128)(2,1)S(1)}, u32[]{:S(2)}, u32[]{:S(2)}) %collective-permute-start.33) | collective-permute-done | bytes 262176 | tf_op jit(solution)/shard_map/ppermute | solution.py:159
  323.3 1.5 shard_map.105.refs_0_
  325.9 2.5 shard_map.107.refs_3_
  328.4 1.2 copy-done.14
  330.6 1.6 shard_map.108
  (205 shorter events, 40.9 us)
Async XLA Ops:
  7.2 99.9 %all-gather.4.cloned.1.call-start = ((), (), s32[]{:S(2)}) async-start(), calls=%async_computation.3 | async-start | bytes 2621440 | tf_op jit(solution)/shard_map/all_gather | solution.py:226
  9.7 97.4 %all-gather.6.cloned.1.call-start = ((), (), s32[]{:S(2)}) async-start(), calls=%async_computation.4 | async-start | bytes 2621440 | tf_op jit(solution)/shard_map/all_gather | solution.py:226
  10.1 15.0 %collective-permute-start.9 = (bf16[256,1024]{1,0:T(8,128)(2,1)S(1)}, bf16[256,1024]{1,0:T(8,128)(2,1)S(1)}, u32[]{:S(2)}, u32[]{:S(2)}) collective-permute-start(bf16[256,1024]{1,0:T(8,128)(2,1)S(1)} %pad_maximum_fusion.1), channel_id=1, source_target_pairs={{0,1},{1,0},{2,3},{3,2},{4,5},{5,4},{6,7},{7,6},{8,9},{9,8},{10,11... | collective-permute-start | bytes 1572872 | tf_op jit(solution)/shard_map/ppermute | solution.py:159
  25.8 126.6 %all-gather.8.cloned.1.call-start = ((), (), s32[]{:S(2)}) async-start(), calls=%async_computation.5 | async-start | bytes 2621440 | tf_op jit(solution)/shard_map/all_gather | solution.py:226
  25.9 9.3 %collective-permute-start.10 = (bf16[128,1024]{1,0:T(8,128)(2,1)S(1)}, bf16[128,1024]{1,0:T(8,128)(2,1)S(1)}, u32[]{:S(2)}, u32[]{:S(2)}) collective-permute-start(bf16[128,1024]{1,0:T(8,128)(2,1)S(1)} %get-tuple-element.50), channel_id=1, source_target_pairs={{0,1},{1,0},{2,3},{3,2},{4,5},{5,4},{6,7},{7,6},{8,9},{9,8},{10,11... | collective-permute-start | bytes 786440 | tf_op jit(solution)/shard_map/ppermute | solution.py:159
  27.8 26.3 %collective-permute-start.1 = (bf16[512,1024]{1,0:T(8,128)(2,1)}, bf16[512,1024]{1,0:T(8,128)(2,1)S(1)}, u32[]{:S(2)}, u32[]{:S(2)}) collective-permute-start(bf16[512,1024]{1,0:T(8,128)(2,1)} %bitcast.refs_0_), channel_id=1, source_target_pairs={{0,16},{8,24},{16,0},{24,8},{1,17},{9,25},{17,1},{25,9},{2,18},{10... | collective-permute-start | bytes 3145736 | tf_op jit(solution)/shard_map/ppermute | solution.py:156
  29.2 28.5 %collective-permute-start = (bf16[512,1024]{1,0:T(8,128)(2,1)}, bf16[512,1024]{1,0:T(8,128)(2,1)S(1)}, u32[]{:S(2)}, u32[]{:S(2)}) collective-permute-start(bf16[512,1024]{1,0:T(8,128)(2,1)} %bitcast.refs_0_), channel_id=1, source_target_pairs={{0,1},{1,0},{2,3},{3,2},{4,5},{5,4},{6,7},{7,6},{8,9},{9,8},{10,11... | collective-permute-start | bytes 3145736 | tf_op jit(solution)/shard_map/ppermute | solution.py:159
  29.8 46.8 %collective-permute-start.12 = (bf16[512,1024]{1,0:T(8,128)(2,1)}, bf16[512,1024]{1,0:T(8,128)(2,1)S(1)}, u32[]{:S(2)}, u32[]{:S(2)}) collective-permute-start(bf16[512,1024]{1,0:T(8,128)(2,1)} %bitcast.5.refs_0_), channel_id=1, source_target_pairs={{0,16},{8,24},{16,0},{24,8},{1,17},{9,25},{17,1},{25,9},{2,18},{10... | collective-permute-start | bytes 3145736 | tf_op jit(solution)/shard_map/ppermute | solution.py:156
  30.1 46.9 %collective-permute-start.4 = (bf16[512,1024]{1,0:T(8,128)(2,1)}, bf16[512,1024]{1,0:T(8,128)(2,1)}, u32[]{:S(2)}, u32[]{:S(2)}) collective-permute-start(bf16[512,1024]{1,0:T(8,128)(2,1)} %bitcast.refs_0_), channel_id=1, source_target_pairs={{0,8},{8,0},{16,24},{24,16},{1,9},{9,1},{17,25},{25,17},{2,10},{10... | collective-permute-start | bytes 3145736 | tf_op jit(solution)/shard_map/ppermute | solution.py:153
  35.3 45.0 %collective-permute-start.11 = (bf16[512,1024]{1,0:T(8,128)(2,1)}, bf16[512,1024]{1,0:T(8,128)(2,1)}, u32[]{:S(2)}, u32[]{:S(2)}) collective-permute-start(bf16[512,1024]{1,0:T(8,128)(2,1)} %bitcast.5.refs_0_), channel_id=1, source_target_pairs={{0,1},{1,0},{2,3},{3,2},{4,5},{5,4},{6,7},{7,6},{8,9},{9,8},{10,11... | collective-permute-start | bytes 3145736 | tf_op jit(solution)/shard_map/ppermute | solution.py:159
  37.9 245.3 %reduce-scatter.6.cloned.1.call-start = ((), (), s32[]{:S(2)}) async-start(), calls=%async_computation.7 | async-start | bytes 2621440 | tf_op jit(solution)/shard_map/reduce_scatter | solution.py:229
  54.1 53.0 %copy-start.15 = (bf16[512,1024]{1,0:T(8,128)(2,1)}, bf16[512,1024]{1,0:T(8,128)(2,1)S(1)}, u32[]{:S(2)}) copy-start(bf16[512,1024]{1,0:T(8,128)(2,1)S(1)} %collective-permute-done.1.refs_2_) | copy-start | bytes 3145732
  54.1 37.3 %collective-permute-start.2 = (bf16[256,1024]{1,0:T(8,128)(2,1)S(1)}, bf16[256,1024]{1,0:T(8,128)(2,1)S(1)}, u32[]{:S(2)}, u32[]{:S(2)}) collective-permute-start(bf16[256,1024]{1,0:T(8,128)(2,1)S(1)} %slice.32), channel_id=1, source_target_pairs={{0,1},{1,0},{2,3},{3,2},{4,5},{5,4},{6,7},{7,6},{8,9},{9,8},{10,11... | collective-permute-start | bytes 1572872 | tf_op jit(solution)/shard_map/ppermute | solution.py:159
  57.7 72.2 %copy-start.18 = (bf16[512,1024]{1,0:T(8,128)(2,1)}, bf16[512,1024]{1,0:T(8,128)(2,1)S(1)}, u32[]{:S(2)}) copy-start(bf16[512,1024]{1,0:T(8,128)(2,1)S(1)} %collective-permute-done.refs_1_) | copy-start | bytes 3145732
  57.8 35.4 %collective-permute-start.3 = (bf16[256,1024]{1,0:T(8,128)(2,1)S(1)}, bf16[256,1024]{1,0:T(8,128)(2,1)S(1)}, u32[]{:S(2)}, u32[]{:S(2)}) collective-permute-start(bf16[256,1024]{1,0:T(8,128)(2,1)S(1)} %slice.33), channel_id=1, source_target_pairs={{0,16},{8,24},{16,0},{24,8},{1,17},{9,25},{17,1},{25,9},{2,18},{10... | collective-permute-start | bytes 1572872 | tf_op jit(solution)/shard_map/ppermute | solution.py:156
  76.6 24.6 %collective-permute-start.13 = (bf16[256,1024]{1,0:T(8,128)(2,1)S(1)}, bf16[256,1024]{1,0:T(8,128)(2,1)}, u32[]{:S(2)}, u32[]{:S(2)}) collective-permute-start(bf16[256,1024]{1,0:T(8,128)(2,1)S(1)} %slice.34), channel_id=1, source_target_pairs={{0,1},{1,0},{2,3},{3,2},{4,5},{5,4},{6,7},{7,6},{8,9},{9,8},{10,11... | collective-permute-start | bytes 1572872 | tf_op jit(solution)/shard_map/ppermute | solution.py:159
  76.9 27.7 %collective-permute-start.5 = (bf16[512,1024]{1,0:T(8,128)(2,1)S(1)}, bf16[512,1024]{1,0:T(8,128)(2,1)S(1)}, u32[]{:S(2)}, u32[]{:S(2)}) collective-permute-start(bf16[512,1024]{1,0:T(8,128)(2,1)S(1)} %collective-permute-done.refs_1_), channel_id=1, source_target_pairs={{0,8},{8,0},{16,24},{24,16},{1,9},{9,1},{17,25},{25,17},{2,10},{10... | collective-permute-start | bytes 3145736 | tf_op jit(solution)/shard_map/ppermute | solution.py:153
  80.3 25.6 %collective-permute-start.6 = (bf16[512,1024]{1,0:T(8,128)(2,1)S(1)}, bf16[512,1024]{1,0:T(8,128)(2,1)S(1)}, u32[]{:S(2)}, u32[]{:S(2)}) collective-permute-start(bf16[512,1024]{1,0:T(8,128)(2,1)S(1)} %collective-permute-done.1.refs_2_), channel_id=1, source_target_pairs={{0,8},{8,0},{16,24},{24,16},{1,9},{9,1},{17,25},{25,17},{2,10},{10... | collective-permute-start | bytes 3145736 | tf_op jit(solution)/shard_map/ppermute | solution.py:153
  91.4 10.9 %collective-permute-start.14 = (bf16[256,1024]{1,0:T(8,128)(2,1)S(1)}, bf16[256,1024]{1,0:T(8,128)(2,1)}, u32[]{:S(2)}, u32[]{:S(2)}) collective-permute-start(bf16[256,1024]{1,0:T(8,128)(2,1)S(1)} %slice.35), channel_id=1, source_target_pairs={{0,16},{8,24},{16,0},{24,8},{1,17},{9,25},{17,1},{25,9},{2,18},{10... | collective-permute-start | bytes 1572872 | tf_op jit(solution)/shard_map/ppermute | solution.py:156
  93.1 9.3 %collective-permute-start.7 = (bf16[256,1024]{1,0:T(8,128)(2,1)S(1)}, bf16[256,1024]{1,0:T(8,128)(2,1)S(1)}, u32[]{:S(2)}, u32[]{:S(2)}) collective-permute-start(bf16[256,1024]{1,0:T(8,128)(2,1)S(1)} %collective-permute-done.2.refs_3_), channel_id=1, source_target_pairs={{0,8},{8,0},{16,24},{24,16},{1,9},{9,1},{17,25},{25,17},{2,10},{10... | collective-permute-start | bytes 1572872 | tf_op jit(solution)/shard_map/ppermute | solution.py:153
  101.1 2.5 collective-permute-start.8
  102.3 27.7 %collective-permute-start.15 = (bf16[512,1024]{1,0:T(8,128)(2,1)}, bf16[512,1024]{1,0:T(8,128)(2,1)}, u32[]{:S(2)}, u32[]{:S(2)}) collective-permute-start(bf16[512,1024]{1,0:T(8,128)(2,1)} %bitcast.5.refs_0_), channel_id=1, source_target_pairs={{0,8},{8,0},{16,24},{24,16},{1,9},{9,1},{17,25},{25,17},{2,10},{10... | collective-permute-start | bytes 3145736 | tf_op jit(solution)/shard_map/ppermute | solution.py:153
  103.3 26.7 %collective-permute-start.16 = (bf16[512,1024]{1,0:T(8,128)(2,1)}, bf16[512,1024]{1,0:T(8,128)(2,1)}, u32[]{:S(2)}, u32[]{:S(2)}) collective-permute-start(bf16[512,1024]{1,0:T(8,128)(2,1)} %collective-permute-done.11.refs_1_), channel_id=1, source_target_pairs={{0,8},{8,0},{16,24},{24,16},{1,9},{9,1},{17,25},{25,17},{2,10},{10... | collective-permute-start | bytes 3145736 | tf_op jit(solution)/shard_map/ppermute | solution.py:153
  104.4 25.6 %collective-permute-start.17 = (bf16[512,1024]{1,0:T(8,128)(2,1)S(1)}, bf16[512,1024]{1,0:T(8,128)(2,1)}, u32[]{:S(2)}, u32[]{:S(2)}) collective-permute-start(bf16[512,1024]{1,0:T(8,128)(2,1)S(1)} %collective-permute-done.12.refs_2_), channel_id=1, source_target_pairs={{0,8},{8,0},{16,24},{24,16},{1,9},{9,1},{17,25},{25,17},{2,10},{10... | collective-permute-start | bytes 3145736 | tf_op jit(solution)/shard_map/ppermute | solution.py:153
  105.6 24.4 %collective-permute-start.18 = (bf16[256,1024]{1,0:T(8,128)(2,1)}, bf16[256,1024]{1,0:T(8,128)(2,1)}, u32[]{:S(2)}, u32[]{:S(2)}) collective-permute-start(bf16[256,1024]{1,0:T(8,128)(2,1)} %collective-permute-done.13.refs_3_), channel_id=1, source_target_pairs={{0,8},{8,0},{16,24},{24,16},{1,9},{9,1},{17,25},{25,17},{2,10},{10... | collective-permute-start | bytes 1572872 | tf_op jit(solution)/shard_map/ppermute | solution.py:153
  106.9 23.1 %collective-permute-start.19 = (bf16[256,1024]{1,0:T(8,128)(2,1)}, bf16[256,1024]{1,0:T(8,128)(2,1)}, u32[]{:S(2)}, u32[]{:S(2)}) collective-permute-start(bf16[256,1024]{1,0:T(8,128)(2,1)} %collective-permute-done.14.refs_4_), channel_id=1, source_target_pairs={{0,8},{8,0},{16,24},{24,16},{1,9},{9,1},{17,25},{25,17},{2,10},{10... | collective-permute-start | bytes 1572872 | tf_op jit(solution)/shard_map/ppermute | solution.py:153
  130.0 22.5 %copy-start.7 = (bf16[2048,512]{1,0:T(8,128)(2,1)S(1)}, bf16[2048,512]{1,0:T(8,128)(2,1)}, u32[]{:S(2)}) copy-start(bf16[2048,512]{1,0:T(8,128)(2,1)} %get-tuple-element.25.refs_0_) | copy-start | bytes 6291460
  156.6 17.7 %collective-permute-start.23 = (bf16[512,1024]{1,0:T(8,128)(2,1)S(1)}, bf16[512,1024]{1,0:T(8,128)(2,1)S(1)}, u32[]{:S(2)}, u32[]{:S(2)}) collective-permute-start(bf16[512,1024]{1,0:T(8,128)(2,1)S(1)} %shard_map.94.refs_3_.refs_13_), channel_id=1, source_target_pairs={{0,8},{8,0},{16,24},{24,16},{1,9},{9,1},{17,25},{25,17},{2,10},{10... | collective-permute-start | bytes 3145736 | tf_op jit(solution)/shard_map/ppermute | solution.py:153
  159.6 18.0 %collective-permute-start.20 = (bf16[512,1024]{1,0:T(8,128)(2,1)}, bf16[512,1024]{1,0:T(8,128)(2,1)S(1)}, u32[]{:S(2)}, u32[]{:S(2)}) collective-permute-start(bf16[512,1024]{1,0:T(8,128)(2,1)} %get-tuple-element.27.refs_14_), channel_id=1, source_target_pairs={{0,8},{8,0},{16,24},{24,16},{1,9},{9,1},{17,25},{25,17},{2,10},{10... | collective-permute-start | bytes 3145736 | tf_op jit(solution)/shard_map/ppermute | solution.py:153
  159.7 18.0 %collective-permute-start.21 = (bf16[512,1024]{1,0:T(8,128)(2,1)S(1)}, bf16[512,1024]{1,0:T(8,128)(2,1)S(1)}, u32[]{:S(2)}, u32[]{:S(2)}) collective-permute-start(bf16[512,1024]{1,0:T(8,128)(2,1)S(1)} %get-tuple-element.28.refs_15_), channel_id=1, source_target_pairs={{0,8},{8,0},{16,24},{24,16},{1,9},{9,1},{17,25},{25,17},{2,10},{10... | collective-permute-start | bytes 3145736 | tf_op jit(solution)/shard_map/ppermute | solution.py:153
  160.2 17.5 %collective-permute-start.22 = (bf16[512,1024]{1,0:T(8,128)(2,1)S(1)}, bf16[512,1024]{1,0:T(8,128)(2,1)S(1)}, u32[]{:S(2)}, u32[]{:S(2)}) collective-permute-start(bf16[512,1024]{1,0:T(8,128)(2,1)S(1)} %get-tuple-element.29.refs_16_), channel_id=1, source_target_pairs={{0,8},{8,0},{16,24},{24,16},{1,9},{9,1},{17,25},{25,17},{2,10},{10... | collective-permute-start | bytes 3145736 | tf_op jit(solution)/shard_map/ppermute | solution.py:153
  193.2 91.5 %reduce-scatter.4.cloned.1.call-start = ((), (), s32[]{:S(2)}) async-start(), calls=%async_computation.6 | async-start | bytes 2621440 | tf_op jit(solution)/shard_map/reduce_scatter | solution.py:229
  193.8 134.6 %reduce-scatter.8.cloned.1.call-start = ((), (), s32[]{:S(2)}) async-start(), calls=%async_computation.8 | async-start | bytes 2621440 | tf_op jit(solution)/shard_map/reduce_scatter | solution.py:229
  193.9 13.9 %collective-permute-start.24 = (bf16[256,1024]{1,0:T(8,128)(2,1)S(1)}, bf16[256,1024]{1,0:T(8,128)(2,1)S(1)}, u32[]{:S(2)}, u32[]{:S(2)}) collective-permute-start(bf16[256,1024]{1,0:T(8,128)(2,1)S(1)} %get-tuple-element.45), channel_id=1, source_target_pairs={{0,1},{1,0},{2,3},{3,2},{4,5},{5,4},{6,7},{7,6},{8,9},{9,8},{10,11... | collective-permute-start | bytes 1572872 | tf_op jit(solution)/shard_map/ppermute | solution.py:159
  195.5 13.5 %collective-permute-start.26 = (bf16[256,1024]{1,0:T(8,128)(2,1)S(1)}, bf16[256,1024]{1,0:T(8,128)(2,1)S(1)}, u32[]{:S(2)}, u32[]{:S(2)}) collective-permute-start(bf16[256,1024]{1,0:T(8,128)(2,1)S(1)} %get-tuple-element.46), channel_id=1, source_target_pairs={{0,16},{8,24},{16,0},{24,8},{1,17},{9,25},{17,1},{25,9},{2,18},{10... | collective-permute-start | bytes 1572872 | tf_op jit(solution)/shard_map/ppermute | solution.py:156
  230.2 5.7 %collective-permute-start.31 = (bf16[512,1024]{1,0:T(8,128)(2,1)}, bf16[512,1024]{1,0:T(8,128)(2,1)S(1)}, u32[]{:S(2)}, u32[]{:S(2)}) collective-permute-start(bf16[512,1024]{1,0:T(8,128)(2,1)} %shard_map.100.refs_3_.refs_11_), channel_id=1, source_target_pairs={{0,8},{8,0},{16,24},{24,16},{1,9},{9,1},{17,25},{25,17},{2,10},{10... | collective-permute-start | bytes 3145736 | tf_op jit(solution)/shard_map/ppermute | solution.py:153
  230.2 9.3 %collective-permute-start.28 = (bf16[512,1024]{1,0:T(8,128)(2,1)}, bf16[512,1024]{1,0:T(8,128)(2,1)S(1)}, u32[]{:S(2)}, u32[]{:S(2)}) collective-permute-start(bf16[512,1024]{1,0:T(8,128)(2,1)} %copy-done.35), channel_id=1, source_target_pairs={{0,8},{8,0},{16,24},{24,16},{1,9},{9,1},{17,25},{25,17},{2,10},{10... | collective-permute-start | bytes 3145736 | tf_op jit(solution)/shard_map/ppermute | solution.py:153
  230.7 9.5 %collective-permute-start.29 = (bf16[512,1024]{1,0:T(8,128)(2,1)}, bf16[512,1024]{1,0:T(8,128)(2,1)S(1)}, u32[]{:S(2)}, u32[]{:S(2)}) collective-permute-start(bf16[512,1024]{1,0:T(8,128)(2,1)} %copy-done.34), channel_id=1, source_target_pairs={{0,8},{8,0},{16,24},{24,16},{1,9},{9,1},{17,25},{25,17},{2,10},{10... | collective-permute-start | bytes 3145736 | tf_op jit(solution)/shard_map/ppermute | solution.py:153
  230.8 9.4 %collective-permute-start.30 = (bf16[512,1024]{1,0:T(8,128)(2,1)}, bf16[512,1024]{1,0:T(8,128)(2,1)S(1)}, u32[]{:S(2)}, u32[]{:S(2)}) collective-permute-start(bf16[512,1024]{1,0:T(8,128)(2,1)} %copy-done.33), channel_id=1, source_target_pairs={{0,8},{8,0},{16,24},{24,16},{1,9},{9,1},{17,25},{25,17},{2,10},{10... | collective-permute-start | bytes 3145736 | tf_op jit(solution)/shard_map/ppermute | solution.py:153
  232.9 26.1 %collective-permute-start.25 = (bf16[512,1024]{1,0:T(8,128)(2,1)S(1)}, bf16[512,1024]{1,0:T(8,128)(2,1)S(1)}, u32[]{:S(2)}, u32[]{:S(2)}) collective-permute-start(bf16[512,1024]{1,0:T(8,128)(2,1)S(1)} %add_convert_fusion.2), channel_id=1, source_target_pairs={{0,16},{8,24},{16,0},{24,8},{1,17},{9,25},{17,1},{25,9},{2,18},{10... | collective-permute-start | bytes 3145736 | tf_op jit(solution)/shard_map/ppermute | solution.py:156
  235.9 24.9 %collective-permute-start.27 = (bf16[512,1024]{1,0:T(8,128)(2,1)S(1)}, bf16[512,1024]{1,0:T(8,128)(2,1)S(1)}, u32[]{:S(2)}, u32[]{:S(2)}) collective-permute-start(bf16[512,1024]{1,0:T(8,128)(2,1)S(1)} %add_convert_fusion.1), channel_id=1, source_target_pairs={{0,1},{1,0},{2,3},{3,2},{4,5},{5,4},{6,7},{7,6},{8,9},{9,8},{10,11... | collective-permute-start | bytes 3145736 | tf_op jit(solution)/shard_map/ppermute | solution.py:159
  238.1 22.7 %copy-start.22 = (bf16[1024,1024]{1,0:T(8,128)(2,1)S(1)}, bf16[1024,1024]{1,0:T(8,128)(2,1)}, u32[]{:S(2)}) copy-start(bf16[1024,1024]{1,0:T(8,128)(2,1)} %all-gather.4.cloned.1.call-done.refs_10_.refs_1_) | copy-start | bytes 6291460
  239.6 41.9 %collective-permute-start.34 = (bf16[512,1024]{1,0:T(8,128)(2,1)S(1)}, bf16[512,1024]{1,0:T(8,128)(2,1)S(1)}, u32[]{:S(2)}, u32[]{:S(2)}) collective-permute-start(bf16[512,1024]{1,0:T(8,128)(2,1)S(1)} %shard_map.103.refs_6_), channel_id=1, source_target_pairs={{0,16},{8,24},{16,0},{24,8},{1,17},{9,25},{17,1},{25,9},{2,18},{10... | collective-permute-start | bytes 3145736 | tf_op jit(solution)/shard_map/ppermute | solution.py:156
  264.7 58.6 %collective-permute-start.32 = (bf16[512,1024]{1,0:T(8,128)(2,1)}, bf16[512,1024]{1,0:T(8,128)(2,1)}, u32[]{:S(2)}, u32[]{:S(2)}) collective-permute-start(bf16[512,1024]{1,0:T(8,128)(2,1)} %get-tuple-element.41), channel_id=1, source_target_pairs={{0,16},{8,24},{16,0},{24,8},{1,17},{9,25},{17,1},{25,9},{2,18},{10... | collective-permute-start | bytes 3145736 | tf_op jit(solution)/shard_map/ppermute | solution.py:156
  282.7 43.2 %collective-permute-start.35 = (bf16[512,1024]{1,0:T(8,128)(2,1)}, bf16[512,1024]{1,0:T(8,128)(2,1)}, u32[]{:S(2)}, u32[]{:S(2)}) collective-permute-start(bf16[512,1024]{1,0:T(8,128)(2,1)} %shard_map.106), channel_id=1, source_target_pairs={{0,1},{1,0},{2,3},{3,2},{4,5},{5,4},{6,7},{7,6},{8,9},{9,8},{10,11... | collective-permute-start | bytes 3145736 | tf_op jit(solution)/shard_map/ppermute | solution.py:159
  283.2 42.7 %collective-permute-start.36 = (bf16[256,1024]{1,0:T(8,128)(2,1)}, bf16[256,1024]{1,0:T(8,128)(2,1)S(1)}, u32[]{:S(2)}, u32[]{:S(2)}) collective-permute-start(bf16[256,1024]{1,0:T(8,128)(2,1)} %reduce-scatter.6.cloned.1.call-done), channel_id=1, source_target_pairs={{0,1},{1,0},{2,3},{3,2},{4,5},{5,4},{6,7},{7,6},{8,9},{9,8},{10,11... | collective-permute-start | bytes 1572872 | tf_op jit(solution)/shard_map/ppermute | solution.py:159
  285.8 37.5 %copy-start.41 = (bf16[512,1024]{1,0:T(8,128)(2,1)S(1)}, bf16[512,1024]{1,0:T(8,128)(2,1)}, u32[]{:S(2)}) copy-start(bf16[512,1024]{1,0:T(8,128)(2,1)} %copy-done.40) | copy-start | bytes 3145732
  285.8 37.5 %collective-permute-start.33 = (bf16[128,1024]{1,0:T(8,128)(2,1)S(1)}, bf16[128,1024]{1,0:T(8,128)(2,1)S(1)}, u32[]{:S(2)}, u32[]{:S(2)}) collective-permute-start(bf16[128,1024]{1,0:T(8,128)(2,1)S(1)} %get-tuple-element.48), channel_id=1, source_target_pairs={{0,1},{1,0},{2,3},{3,2},{4,5},{5,4},{6,7},{7,6},{8,9},{9,8},{10,11... | collective-permute-start | bytes 786440 | tf_op jit(solution)/shard_map/ppermute | solution.py:159
  (57 other events, 220.8 us)
Sparse Core Ops, SparseCore 0:
  10.1 48.6 all-gather.3
  61.0 44.6 all-gather.5
  107.8 44.6 all-gather.7
  193.3 42.5 reduce-scatter.5
  238.2 43.1 reduce-scatter.3
  283.5 43.1 reduce-scatter.7

commit v6 on v5

--- a/solution.py
+++ b/solution.py
@@ -132,6 +132,10 @@
         if added:
             total = total + adds[at][...].astype(F32)
         outs[at][...] = total.astype(BF16)
+
+
+def copy_kernel(in_ref, out_ref):
+    out_ref[...] = in_ref[...]
 
 
 def sum_kernel(left_ref, right_ref, out_ref):
@@ -284,7 +288,7 @@
         by_other, by_chip = self.other(corner[:step]), self.chip(corner[step:])
         sums |= self.near_rest(hidden, down_sides, output_far, [corner])
         other_term = unit_term(1, [sums[0, 0]])
-        other_sum = scatter_units(other_term)
+        other_sum = scatter_units(call(copy_kernel, [shape(*other_term.shape)], 0, [other_term], [down_sum])[0])
         unit_sides = [(own_units, 0, half), (other_units, 0, half)]
         grads_far = self.far_first(act, unit_sides, [other_term, by_other, by_chip])
         grads_far |= self.far_rest(act, unit_sides, [grads_far[1, 1]])
@@ -293,7 +297,7 @@
         to_other = (sums[0, 1].astype(F32) + jnp.concatenate([zeros, by_chip.astype(F32)])).astype(BF16)
         output_chip, output_other = self.chip(to_chip), self.other(to_other)
         own_term = unit_term(0, list(grads_far.values()))
-        own_sum = scatter_units(own_term)
+        own_sum = scatter_units(call(copy_kernel, [shape(*own_term.shape)], 0, [own_term], [other_sum])[0])
         grads_far = {place: self.core(block) for place, block in grads_far.items()}
         grads = self.near_first(act, unit_sides, grads_far, [own_term])
         corner = self.chip(grads[1, 1])

time: 340 us -> 359 us (1.056)
  local copies, waits for them, and re-layouts: 35.6 us -> 44 us
  waiting for transfers between devices: 169 us -> 176 us
    reduce_scatter x3, waiting for transfers between devices: 0.01 us -> 8.85 us  [scatter_units(): return lax.psum_scatter(array, 'wt', scatter_dimension=0, tiled=True)]
    unnamed x128 -> x140, local copies, waits for them, and re-layouts: 33 us -> 41.4 us
    pallas_call x17 -> x19, Pallas kernels: 84.4 us -> 86.4 us  [call(): pl.pallas_call(body, out_shape=list(outs), in_specs=[*specs, *[pl.BlockSp...]
  transfers between devices with their start and end apart: 43 -> 43, of which waited for: 16 -> 18; matrix products, arithmetic and copies ran while one was open for 3% -> 3% of each run, Pallas kernels for 21% -> 24%
where the time goes in v6:
time: 359 us; the launch traced here: 358 us
  waiting for transfers between devices  176 us (49%)
  Pallas kernels  86.4 us (24%)
  local copies, waits for them, and re-layouts  44 us (12%)
  starting transfers between devices  27.5 us (8%)
  between operations  14.8 us (4%)
  other arithmetic  8.89 us (2%)
    ppermute x11, waiting for transfers between devices, other(): return lax.ppermute(array, 'out', [(0, 1), (1, 0)])  87.4 us
    pallas_call x19, Pallas kernels, call(): pl.pallas_call(body, out_shape=list(outs), in_specs=[*specs, *[pl.BlockSp...  86.4 us
    ppermute x8, waiting for transfers between devices, chip(): return lax.ppermute(array, 'inp', [(at, at ^ 2) for at in range(4)])  68.6 us
    unnamed x140, local copies, waits for them, and re-layouts  41.4 us
    ppermute x11, starting transfers between devices, other(): return lax.ppermute(array, 'out', [(0, 1), (1, 0)])  14.4 us
    all_gather x3, waiting for transfers between devices, gather_units(): return lax.all_gather(array, 'wt', axis=0, tiled=True)  11.2 us
    ppermute x8, starting transfers between devices, chip(): return lax.ppermute(array, 'inp', [(at, at ^ 2) for at in range(4)])  9.52 us
    reduce_scatter x3, waiting for transfers between devices, scatter_units(): return lax.psum_scatter(array, 'wt', scatter_dimension=0, tiled=True)  8.85 us
  transfers between devices with their start and end apart: 43, of which 18 were waited for; matrix products, arithmetic and copies ran while one was open for 3% of the time, Pallas kernels for 24%

profile of v6, /device:TPU:0, one launch (start us, length us, event | category | flops | bytes accessed | tf_op | source)
XLA Modules:
  0.0 357.6 jit_solution(7276323253658434354)
XLA Ops:
  10.1 3.0 collective-permute-start.9
  13.1 11.9 %collective-permute-done.9 = bf16[256,1024]{1,0:T(8,128)(2,1)S(1)} collective-permute-done((bf16[256,1024]{1,0:T(8,128)(2,1)S(1)}, bf16[256,1024]{1,0:T(8,128)(2,1)S(1)}, u32[]{:S(2)}, u32[]{:S(2)}) %collective-permute-start.9) | collective-permute-done | bytes 524320 | tf_op jit(solution)/shard_map/ppermute | solution.py:163
  25.9 1.8 collective-permute-start.10
  27.8 1.5 collective-permute-start.1
  30.1 5.2 %collective-permute-done.10 = bf16[128,1024]{1,0:T(8,128)(2,1)S(1)} collective-permute-done((bf16[128,1024]{1,0:T(8,128)(2,1)S(1)}, bf16[128,1024]{1,0:T(8,128)(2,1)S(1)}, u32[]{:S(2)}, u32[]{:S(2)}) %collective-permute-start.10) | collective-permute-done | bytes 262176 | tf_op jit(solution)/shard_map/ppermute | solution.py:163
  35.3 1.7 collective-permute-start.11
  37.9 16.2 %collective-permute-done.1.refs_2_ = bf16[512,1024]{1,0:T(8,128)(2,1)S(1)} collective-permute-done((bf16[512,1024]{1,0:T(8,128)(2,1)}, bf16[512,1024]{1,0:T(8,128)(2,1)S(1)}, u32[]{:S(2)}, u32[]{:S(2)}) %collective-permute-start.1) | collective-permute-done | bytes 1048608 | tf_op jit(solution)/shard_map/ppermute | solution.py:160
  54.5 3.3 collective-permute-done.refs_1_
  57.8 1.8 collective-permute-start.3
  59.5 17.0 %collective-permute-done.12.refs_2_ = bf16[512,1024]{1,0:T(8,128)(2,1)S(1)} collective-permute-done((bf16[512,1024]{1,0:T(8,128)(2,1)}, bf16[512,1024]{1,0:T(8,128)(2,1)S(1)}, u32[]{:S(2)}, u32[]{:S(2)}) %collective-permute-start.12) | collective-permute-done | bytes 1048608 | tf_op jit(solution)/shard_map/ppermute | solution.py:160
  76.9 3.4 collective-permute-done.11.refs_1_
  81.4 10.0 %collective-permute-done.2.refs_3_ = bf16[256,1024]{1,0:T(8,128)(2,1)S(1)} collective-permute-done((bf16[256,1024]{1,0:T(8,128)(2,1)S(1)}, bf16[256,1024]{1,0:T(8,128)(2,1)S(1)}, u32[]{:S(2)}, u32[]{:S(2)}) %collective-permute-start.2) | collective-permute-done | bytes 524320 | tf_op jit(solution)/shard_map/ppermute | solution.py:163
  91.4 1.7 collective-permute-start.14
  94.0 7.2 %collective-permute-done.13.refs_3_ = bf16[256,1024]{1,0:T(8,128)(2,1)} collective-permute-done((bf16[256,1024]{1,0:T(8,128)(2,1)S(1)}, bf16[256,1024]{1,0:T(8,128)(2,1)}, u32[]{:S(2)}, u32[]{:S(2)}) %collective-permute-start.13) | collective-permute-done | bytes 524320 | tf_op jit(solution)/shard_map/ppermute | solution.py:163
  113.7 16.3 %shard_map.92 = (bf16[2048,512]{1,0:T(8,128)(2,1)}, bf16[512,2048]{1,0:T(8,128)(2,1)}, bf16[2048,512]{1,0:T(8,128)(2,1)}, bf16[2048,512]{1,0:T(8,128)(2,1)}) custom-call(bf16[512,1024]{1,0:T(8,128)(2,1)} %bitcast.refs_0_, bf16[512,1024]{1,0:T(8,128)(2,1)S(1)} %collective-permute-done.refs_1_, bf16[512,1024]{1,0:T(8,128)(2,1)S(1)} %collective-permute-done.1.refs_2_, ...), custom_call_target="tpu_custom_call" | custom-call | flops 8589934592 | bytes 20971520 | tf_op jit(solution)/shard_map/pallas_call | solution.py:38
  130.0 11.0 %shard_map.93.refs_2_ = bf16[512,2048]{1,0:T(8,128)(2,1)} custom-call(bf16[512,1024]{1,0:T(8,128)(2,1)} %bitcast.5.refs_0_, bf16[512,1024]{1,0:T(8,128)(2,1)} %collective-permute-done.11.refs_1_, bf16[512,1024]{1,0:T(8,128)(2,1)S(1)} %collective-permute-done.12.refs_2_, bf16[256,1024]{1,0:T(8,128)(2,1)} %collective-permute-done.13.refs_3_, ...), custom_call_target="tpu_custom_call" | custom-call | flops 4294967296 | bytes 12582912 | tf_op jit(solution)/shard_map/pallas_call | solution.py:38
  141.3 11.2 %all-gather.8.cloned.1.call-done.refs_1_.refs_2_.refs_10_ = bf16[512,2048]{1,0:T(8,128)(2,1)} async-done(((bf16[128,2048]{1,0:T(8,128)(2,1)}), bf16[512,2048]{1,0:T(8,128)(2,1)}) %all-gather.8.cloned.1.call-update) | async-done | bytes 2097168 | tf_op jit(solution)/shard_map/all_gather | solution.py:230
  152.5 1.6 copy-done
  154.1 1.6 copy-done.11
  157.3 2.7 shard_map.95
  161.0 13.5 %shard_map.96 = (bf16[2048,1024]{1,0:T(8,128)(2,1)}, bf16[1024,2048]{1,0:T(8,128)(2,1)}) custom-call(bf16[512,1024]{1,0:T(8,128)(2,1)} %bitcast.5.refs_0_, bf16[512,1024]{1,0:T(8,128)(2,1)} %collective-permute-done.11.refs_1_, bf16[512,1024]{1,0:T(8,128)(2,1)S(1)} %collective-permute-done.12.refs_2_, bf16[256,1024]{1,0:T(8,128)(2,1)} %collective-permute-done.13.refs_3_, ...), custom_call_target="tpu_custom_call" | custom-call | flops 4294967296 | bytes 23068672 | tf_op jit(solution)/shard_map/pallas_call | solution.py:38
  174.5 2.2 copy-done.3
  177.8 3.7 %shard_map.98 = (bf16[512,1024]{1,0:T(8,128)(2,1)S(1)}, bf16[512,1024]{1,0:T(8,128)(2,1)S(1)}, bf16[512,1024]{1,0:T(8,128)(2,1)S(1)}) custom-call(bf16[2048,512]{1,0:T(8,128)(2,1)S(1)} %copy-done.7, bf16[512,2048]{1,0:T(8,128)(2,1)S(1)} %copy-done.2, bf16[512,2048]{1,0:T(8,128)(2,1)S(1)} %copy-done.2, bf16[512,1024]{1,0:T(8,128)(2,1)S(1)} %collective-permute-done.20.refs_3_, ...), custom_call_target="tpu_custom_call" | custom-call | flops 1610612736 | bytes 12582912 | tf_op jit(solution)/shard_map/pallas_call | solution.py:38
  184.5 9.2 %shard_map.99.refs_2_.refs_0_ = bf16[1024,1024]{1,0:T(8,128)(2,1)} custom-call(bf16[512,1024]{1,0:T(8,128)(2,1)} %bitcast.refs_0_, bf16[512,1024]{1,0:T(8,128)(2,1)S(1)} %copy-done.23, bf16[512,1024]{1,0:T(8,128)(2,1)S(1)} %copy-done.20, bf16[256,1024]{1,0:T(8,128)(2,1)S(1)} %copy-done.50, bf16[256,1024]{1,0:T(8,128)(2,1)S(1)} %copy-done.54, ...), custom_call_target="tpu_custom_call" | custom-call | flops 4294967296 | bytes 14680064 | tf_op jit(solution)/shard_map/pallas_call | solution.py:38
  194.7 2.6 reduce-scatter.4.cloned.1.call-done.refs_1_
  197.3 1.6 copy-done.12
  201.8 1.5 collective-permute-start.24
  204.7 10.6 %collective-permute-done.24.refs_3_ = bf16[256,1024]{1,0:T(8,128)(2,1)S(1)} collective-permute-done((bf16[256,1024]{1,0:T(8,128)(2,1)S(1)}, bf16[256,1024]{1,0:T(8,128)(2,1)S(1)}, u32[]{:S(2)}, u32[]{:S(2)}) %collective-permute-start.24) | collective-permute-done | bytes 524320 | tf_op jit(solution)/shard_map/ppermute | solution.py:163
  216.5 2.2 copy-done.4
  218.7 2.5 shard_map.100.refs_3_.refs_11_
  222.2 3.9 %shard_map.101 = (bf16[512,1024]{1,0:T(8,128)(2,1)S(1)}, bf16[512,1024]{1,0:T(8,128)(2,1)S(1)}, bf16[512,1024]{1,0:T(8,128)(2,1)S(1)}) custom-call(bf16[2048,1024]{1,0:T(8,128)(2,1)S(1)} %copy-done.5, bf16[1024,1024]{1,0:T(8,128)(2,1)S(1)} %copy-done.25, bf16[1024,1024]{1,0:T(8,128)(2,1)S(1)} %copy-done.8, bf16[512,1024]{1,0:T(8,128)(2,1)} %shard_map.100.refs_3_.refs_11_), custom_call_target="tpu_custom_call" | custom-call | flops 3221225472 | bytes 11534336 | tf_op jit(solution)/shard_map/pallas_call | solution.py:38
  229.2 9.3 %shard_map.102.refs_3_.refs_0_ = bf16[1024,1024]{1,0:T(8,128)(2,1)} custom-call(bf16[512,1024]{1,0:T(8,128)(2,1)} %bitcast.refs_0_, bf16[512,1024]{1,0:T(8,128)(2,1)S(1)} %copy-done.24, bf16[512,1024]{1,0:T(8,128)(2,1)S(1)} %copy-done.21, bf16[256,1024]{1,0:T(8,128)(2,1)S(1)} %copy-done.51, bf16[256,1024]{1,0:T(8,128)(2,1)S(1)} %copy-done.55, ...), custom_call_target="tpu_custom_call" | custom-call | flops 4294967296 | bytes 14680064 | tf_op jit(solution)/shard_map/pallas_call | solution.py:38
  238.5 6.2 %reduce-scatter.6.cloned.1.call-done.refs_1_ = bf16[256,1024]{1,0:T(8,128)(2,1)} async-done(((bf16[1024,1024]{1,0:T(8,128)(2,1)}), bf16[256,1024]{1,0:T(8,128)(2,1)}) %reduce-scatter.6.cloned.1.call-update) | async-done | bytes 524304 | tf_op jit(solution)/shard_map/reduce_scatter | solution.py:233
  244.7 1.6 copy-done.9
  250.0 1.6 add_convert_fusion.2
  251.6 1.5 collective-permute-start.25
  253.1 1.5 add_convert_fusion.1
  256.2 1.6 copy-done.10
  257.8 1.5 shard_map.103.refs_6_
  259.9 17.8 %collective-permute-done.25.refs_7_ = bf16[512,1024]{1,0:T(8,128)(2,1)S(1)} collective-permute-done((bf16[512,1024]{1,0:T(8,128)(2,1)S(1)}, bf16[512,1024]{1,0:T(8,128)(2,1)S(1)}, u32[]{:S(2)}, u32[]{:S(2)}) %collective-permute-start.25) | collective-permute-done | bytes 1048608 | tf_op jit(solution)/shard_map/ppermute | solution.py:160
  277.7 1.9 collective-permute-done.27.refs_8_
  279.5 3.9 %shard_map.104 = (bf16[512,1024]{1,0:T(8,128)(2,1)S(1)}, bf16[512,1024]{1,0:T(8,128)(2,1)}, bf16[512,1024]{1,0:T(8,128)(2,1)S(1)}) custom-call(bf16[2048,1024]{1,0:T(8,128)(2,1)S(1)} %copy-done.6, bf16[1024,1024]{1,0:T(8,128)(2,1)S(1)} %copy-done.26, bf16[1024,1024]{1,0:T(8,128)(2,1)S(1)} %copy-done.8, ...), custom_call_target="tpu_custom_call" | custom-call | flops 3221225472 | bytes 14680064 | tf_op jit(solution)/shard_map/pallas_call | solution.py:38
  284.1 16.1 %collective-permute-done.34.refs_1_ = bf16[512,1024]{1,0:T(8,128)(2,1)S(1)} collective-permute-done((bf16[512,1024]{1,0:T(8,128)(2,1)S(1)}, bf16[512,1024]{1,0:T(8,128)(2,1)S(1)}, u32[]{:S(2)}, u32[]{:S(2)}) %collective-permute-start.34) | collective-permute-done | bytes 1048608 | tf_op jit(solution)/shard_map/ppermute | solution.py:160
  303.5 1.5 collective-permute-start.33
  305.0 2.8 add_convert_fusion
  307.8 34.0 %collective-permute-done.33.refs_2_ = bf16[128,1024]{1,0:T(8,128)(2,1)S(1)} collective-permute-done((bf16[128,1024]{1,0:T(8,128)(2,1)S(1)}, bf16[128,1024]{1,0:T(8,128)(2,1)S(1)}, u32[]{:S(2)}, u32[]{:S(2)}) %collective-permute-start.33) | collective-permute-done | bytes 262176 | tf_op jit(solution)/shard_map/ppermute | solution.py:163
  344.5 2.4 shard_map.108.refs_3_
  349.2 1.6 shard_map.110
  (219 shorter events, 52.5 us)
Async XLA Ops:
  7.2 99.9 %all-gather.4.cloned.1.call-start = ((), (), s32[]{:S(2)}) async-start(), calls=%async_computation.3 | async-start | bytes 2621440 | tf_op jit(solution)/shard_map/all_gather | solution.py:230
  9.7 97.4 %all-gather.6.cloned.1.call-start = ((), (), s32[]{:S(2)}) async-start(), calls=%async_computation.4 | async-start | bytes 2621440 | tf_op jit(solution)/shard_map/all_gather | solution.py:230
  10.1 15.0 %collective-permute-start.9 = (bf16[256,1024]{1,0:T(8,128)(2,1)S(1)}, bf16[256,1024]{1,0:T(8,128)(2,1)S(1)}, u32[]{:S(2)}, u32[]{:S(2)}) collective-permute-start(bf16[256,1024]{1,0:T(8,128)(2,1)S(1)} %pad_maximum_fusion.1), channel_id=1, source_target_pairs={{0,1},{1,0},{2,3},{3,2},{4,5},{5,4},{6,7},{7,6},{8,9},{9,8},{10,11... | collective-permute-start | bytes 1572872 | tf_op jit(solution)/shard_map/ppermute | solution.py:163
  25.8 126.6 %all-gather.8.cloned.1.call-start = ((), (), s32[]{:S(2)}) async-start(), calls=%async_computation.5 | async-start | bytes 2621440 | tf_op jit(solution)/shard_map/all_gather | solution.py:230
  25.9 9.3 %collective-permute-start.10 = (bf16[128,1024]{1,0:T(8,128)(2,1)S(1)}, bf16[128,1024]{1,0:T(8,128)(2,1)S(1)}, u32[]{:S(2)}, u32[]{:S(2)}) collective-permute-start(bf16[128,1024]{1,0:T(8,128)(2,1)S(1)} %get-tuple-element.50), channel_id=1, source_target_pairs={{0,1},{1,0},{2,3},{3,2},{4,5},{5,4},{6,7},{7,6},{8,9},{9,8},{10,11... | collective-permute-start | bytes 786440 | tf_op jit(solution)/shard_map/ppermute | solution.py:163
  27.8 26.3 %collective-permute-start.1 = (bf16[512,1024]{1,0:T(8,128)(2,1)}, bf16[512,1024]{1,0:T(8,128)(2,1)S(1)}, u32[]{:S(2)}, u32[]{:S(2)}) collective-permute-start(bf16[512,1024]{1,0:T(8,128)(2,1)} %bitcast.refs_0_), channel_id=1, source_target_pairs={{0,16},{8,24},{16,0},{24,8},{1,17},{9,25},{17,1},{25,9},{2,18},{10... | collective-permute-start | bytes 3145736 | tf_op jit(solution)/shard_map/ppermute | solution.py:160
  29.2 28.5 %collective-permute-start = (bf16[512,1024]{1,0:T(8,128)(2,1)}, bf16[512,1024]{1,0:T(8,128)(2,1)S(1)}, u32[]{:S(2)}, u32[]{:S(2)}) collective-permute-start(bf16[512,1024]{1,0:T(8,128)(2,1)} %bitcast.refs_0_), channel_id=1, source_target_pairs={{0,1},{1,0},{2,3},{3,2},{4,5},{5,4},{6,7},{7,6},{8,9},{9,8},{10,11... | collective-permute-start | bytes 3145736 | tf_op jit(solution)/shard_map/ppermute | solution.py:163
  29.8 46.8 %collective-permute-start.12 = (bf16[512,1024]{1,0:T(8,128)(2,1)}, bf16[512,1024]{1,0:T(8,128)(2,1)S(1)}, u32[]{:S(2)}, u32[]{:S(2)}) collective-permute-start(bf16[512,1024]{1,0:T(8,128)(2,1)} %bitcast.5.refs_0_), channel_id=1, source_target_pairs={{0,16},{8,24},{16,0},{24,8},{1,17},{9,25},{17,1},{25,9},{2,18},{10... | collective-permute-start | bytes 3145736 | tf_op jit(solution)/shard_map/ppermute | solution.py:160
  30.1 46.9 %collective-permute-start.4 = (bf16[512,1024]{1,0:T(8,128)(2,1)}, bf16[512,1024]{1,0:T(8,128)(2,1)}, u32[]{:S(2)}, u32[]{:S(2)}) collective-permute-start(bf16[512,1024]{1,0:T(8,128)(2,1)} %bitcast.refs_0_), channel_id=1, source_target_pairs={{0,8},{8,0},{16,24},{24,16},{1,9},{9,1},{17,25},{25,17},{2,10},{10... | collective-permute-start | bytes 3145736 | tf_op jit(solution)/shard_map/ppermute | solution.py:157
  35.3 45.0 %collective-permute-start.11 = (bf16[512,1024]{1,0:T(8,128)(2,1)}, bf16[512,1024]{1,0:T(8,128)(2,1)}, u32[]{:S(2)}, u32[]{:S(2)}) collective-permute-start(bf16[512,1024]{1,0:T(8,128)(2,1)} %bitcast.5.refs_0_), channel_id=1, source_target_pairs={{0,1},{1,0},{2,3},{3,2},{4,5},{5,4},{6,7},{7,6},{8,9},{9,8},{10,11... | collective-permute-start | bytes 3145736 | tf_op jit(solution)/shard_map/ppermute | solution.py:163
  37.9 159.4 %reduce-scatter.4.cloned.1.call-start = ((), (), s32[]{:S(2)}) async-start(), calls=%async_computation.6 | async-start | bytes 2621440 | tf_op jit(solution)/shard_map/reduce_scatter | solution.py:233
  54.1 53.0 %copy-start.19 = (bf16[512,1024]{1,0:T(8,128)(2,1)}, bf16[512,1024]{1,0:T(8,128)(2,1)S(1)}, u32[]{:S(2)}) copy-start(bf16[512,1024]{1,0:T(8,128)(2,1)S(1)} %collective-permute-done.1.refs_2_) | copy-start | bytes 3145732
  54.1 37.3 %collective-permute-start.2 = (bf16[256,1024]{1,0:T(8,128)(2,1)S(1)}, bf16[256,1024]{1,0:T(8,128)(2,1)S(1)}, u32[]{:S(2)}, u32[]{:S(2)}) collective-permute-start(bf16[256,1024]{1,0:T(8,128)(2,1)S(1)} %slice.32), channel_id=1, source_target_pairs={{0,1},{1,0},{2,3},{3,2},{4,5},{5,4},{6,7},{7,6},{8,9},{9,8},{10,11... | collective-permute-start | bytes 1572872 | tf_op jit(solution)/shard_map/ppermute | solution.py:163
  57.7 72.3 %copy-start.22 = (bf16[512,1024]{1,0:T(8,128)(2,1)}, bf16[512,1024]{1,0:T(8,128)(2,1)S(1)}, u32[]{:S(2)}) copy-start(bf16[512,1024]{1,0:T(8,128)(2,1)S(1)} %collective-permute-done.refs_1_) | copy-start | bytes 3145732
  57.8 35.4 %collective-permute-start.3 = (bf16[256,1024]{1,0:T(8,128)(2,1)S(1)}, bf16[256,1024]{1,0:T(8,128)(2,1)S(1)}, u32[]{:S(2)}, u32[]{:S(2)}) collective-permute-start(bf16[256,1024]{1,0:T(8,128)(2,1)S(1)} %slice.33), channel_id=1, source_target_pairs={{0,16},{8,24},{16,0},{24,8},{1,17},{9,25},{17,1},{25,9},{2,18},{10... | collective-permute-start | bytes 1572872 | tf_op jit(solution)/shard_map/ppermute | solution.py:160
  76.6 24.6 %collective-permute-start.13 = (bf16[256,1024]{1,0:T(8,128)(2,1)S(1)}, bf16[256,1024]{1,0:T(8,128)(2,1)}, u32[]{:S(2)}, u32[]{:S(2)}) collective-permute-start(bf16[256,1024]{1,0:T(8,128)(2,1)S(1)} %slice.34), channel_id=1, source_target_pairs={{0,1},{1,0},{2,3},{3,2},{4,5},{5,4},{6,7},{7,6},{8,9},{9,8},{10,11... | collective-permute-start | bytes 1572872 | tf_op jit(solution)/shard_map/ppermute | solution.py:163
  76.9 27.7 %collective-permute-start.5 = (bf16[512,1024]{1,0:T(8,128)(2,1)S(1)}, bf16[512,1024]{1,0:T(8,128)(2,1)S(1)}, u32[]{:S(2)}, u32[]{:S(2)}) collective-permute-start(bf16[512,1024]{1,0:T(8,128)(2,1)S(1)} %collective-permute-done.refs_1_), channel_id=1, source_target_pairs={{0,8},{8,0},{16,24},{24,16},{1,9},{9,1},{17,25},{25,17},{2,10},{10... | collective-permute-start | bytes 3145736 | tf_op jit(solution)/shard_map/ppermute | solution.py:157
  80.3 25.6 %collective-permute-start.6 = (bf16[512,1024]{1,0:T(8,128)(2,1)S(1)}, bf16[512,1024]{1,0:T(8,128)(2,1)S(1)}, u32[]{:S(2)}, u32[]{:S(2)}) collective-permute-start(bf16[512,1024]{1,0:T(8,128)(2,1)S(1)} %collective-permute-done.1.refs_2_), channel_id=1, source_target_pairs={{0,8},{8,0},{16,24},{24,16},{1,9},{9,1},{17,25},{25,17},{2,10},{10... | collective-permute-start | bytes 3145736 | tf_op jit(solution)/shard_map/ppermute | solution.py:157
  91.4 10.9 %collective-permute-start.14 = (bf16[256,1024]{1,0:T(8,128)(2,1)S(1)}, bf16[256,1024]{1,0:T(8,128)(2,1)}, u32[]{:S(2)}, u32[]{:S(2)}) collective-permute-start(bf16[256,1024]{1,0:T(8,128)(2,1)S(1)} %slice.35), channel_id=1, source_target_pairs={{0,16},{8,24},{16,0},{24,8},{1,17},{9,25},{17,1},{25,9},{2,18},{10... | collective-permute-start | bytes 1572872 | tf_op jit(solution)/shard_map/ppermute | solution.py:160
  93.1 9.3 %collective-permute-start.7 = (bf16[256,1024]{1,0:T(8,128)(2,1)S(1)}, bf16[256,1024]{1,0:T(8,128)(2,1)S(1)}, u32[]{:S(2)}, u32[]{:S(2)}) collective-permute-start(bf16[256,1024]{1,0:T(8,128)(2,1)S(1)} %collective-permute-done.2.refs_3_), channel_id=1, source_target_pairs={{0,8},{8,0},{16,24},{24,16},{1,9},{9,1},{17,25},{25,17},{2,10},{10... | collective-permute-start | bytes 1572872 | tf_op jit(solution)/shard_map/ppermute | solution.py:157
  101.1 2.5 collective-permute-start.8
  102.3 27.7 %collective-permute-start.15 = (bf16[512,1024]{1,0:T(8,128)(2,1)}, bf16[512,1024]{1,0:T(8,128)(2,1)}, u32[]{:S(2)}, u32[]{:S(2)}) collective-permute-start(bf16[512,1024]{1,0:T(8,128)(2,1)} %bitcast.5.refs_0_), channel_id=1, source_target_pairs={{0,8},{8,0},{16,24},{24,16},{1,9},{9,1},{17,25},{25,17},{2,10},{10... | collective-permute-start | bytes 3145736 | tf_op jit(solution)/shard_map/ppermute | solution.py:157
  103.3 26.8 %collective-permute-start.16 = (bf16[512,1024]{1,0:T(8,128)(2,1)}, bf16[512,1024]{1,0:T(8,128)(2,1)}, u32[]{:S(2)}, u32[]{:S(2)}) collective-permute-start(bf16[512,1024]{1,0:T(8,128)(2,1)} %collective-permute-done.11.refs_1_), channel_id=1, source_target_pairs={{0,8},{8,0},{16,24},{24,16},{1,9},{9,1},{17,25},{25,17},{2,10},{10... | collective-permute-start | bytes 3145736 | tf_op jit(solution)/shard_map/ppermute | solution.py:157
  104.4 25.6 %collective-permute-start.17 = (bf16[512,1024]{1,0:T(8,128)(2,1)S(1)}, bf16[512,1024]{1,0:T(8,128)(2,1)}, u32[]{:S(2)}, u32[]{:S(2)}) collective-permute-start(bf16[512,1024]{1,0:T(8,128)(2,1)S(1)} %collective-permute-done.12.refs_2_), channel_id=1, source_target_pairs={{0,8},{8,0},{16,24},{24,16},{1,9},{9,1},{17,25},{25,17},{2,10},{10... | collective-permute-start | bytes 3145736 | tf_op jit(solution)/shard_map/ppermute | solution.py:157
  105.6 24.4 %collective-permute-start.18 = (bf16[256,1024]{1,0:T(8,128)(2,1)}, bf16[256,1024]{1,0:T(8,128)(2,1)}, u32[]{:S(2)}, u32[]{:S(2)}) collective-permute-start(bf16[256,1024]{1,0:T(8,128)(2,1)} %collective-permute-done.13.refs_3_), channel_id=1, source_target_pairs={{0,8},{8,0},{16,24},{24,16},{1,9},{9,1},{17,25},{25,17},{2,10},{10... | collective-permute-start | bytes 1572872 | tf_op jit(solution)/shard_map/ppermute | solution.py:157
  106.9 23.1 %collective-permute-start.19 = (bf16[256,1024]{1,0:T(8,128)(2,1)}, bf16[256,1024]{1,0:T(8,128)(2,1)}, u32[]{:S(2)}, u32[]{:S(2)}) collective-permute-start(bf16[256,1024]{1,0:T(8,128)(2,1)} %collective-permute-done.14.refs_4_), channel_id=1, source_target_pairs={{0,8},{8,0},{16,24},{24,16},{1,9},{9,1},{17,25},{25,17},{2,10},{10... | collective-permute-start | bytes 1572872 | tf_op jit(solution)/shard_map/ppermute | solution.py:157
  141.1 103.6 %reduce-scatter.6.cloned.1.call-start = ((), (), s32[]{:S(2)}) async-start(), calls=%async_computation.7 | async-start | bytes 2621440 | tf_op jit(solution)/shard_map/reduce_scatter | solution.py:233
  156.6 17.8 %collective-permute-start.23 = (bf16[512,1024]{1,0:T(8,128)(2,1)S(1)}, bf16[512,1024]{1,0:T(8,128)(2,1)S(1)}, u32[]{:S(2)}, u32[]{:S(2)}) collective-permute-start(bf16[512,1024]{1,0:T(8,128)(2,1)S(1)} %shard_map.94.refs_3_.refs_13_), channel_id=1, source_target_pairs={{0,8},{8,0},{16,24},{24,16},{1,9},{9,1},{17,25},{25,17},{2,10},{10... | collective-permute-start | bytes 3145736 | tf_op jit(solution)/shard_map/ppermute | solution.py:157
  160.0 17.7 %collective-permute-start.20 = (bf16[512,1024]{1,0:T(8,128)(2,1)}, bf16[512,1024]{1,0:T(8,128)(2,1)S(1)}, u32[]{:S(2)}, u32[]{:S(2)}) collective-permute-start(bf16[512,1024]{1,0:T(8,128)(2,1)} %get-tuple-element.27.refs_14_), channel_id=1, source_target_pairs={{0,8},{8,0},{16,24},{24,16},{1,9},{9,1},{17,25},{25,17},{2,10},{10... | collective-permute-start | bytes 3145736 | tf_op jit(solution)/shard_map/ppermute | solution.py:157
  160.1 17.7 %collective-permute-start.21 = (bf16[512,1024]{1,0:T(8,128)(2,1)}, bf16[512,1024]{1,0:T(8,128)(2,1)S(1)}, u32[]{:S(2)}, u32[]{:S(2)}) collective-permute-start(bf16[512,1024]{1,0:T(8,128)(2,1)} %get-tuple-element.28.refs_15_), channel_id=1, source_target_pairs={{0,8},{8,0},{16,24},{24,16},{1,9},{9,1},{17,25},{25,17},{2,10},{10... | collective-permute-start | bytes 3145736 | tf_op jit(solution)/shard_map/ppermute | solution.py:157
  160.6 17.2 %collective-permute-start.22 = (bf16[512,1024]{1,0:T(8,128)(2,1)S(1)}, bf16[512,1024]{1,0:T(8,128)(2,1)}, u32[]{:S(2)}, u32[]{:S(2)}) collective-permute-start(bf16[512,1024]{1,0:T(8,128)(2,1)S(1)} %get-tuple-element.29.refs_16_), channel_id=1, source_target_pairs={{0,8},{8,0},{16,24},{24,16},{1,9},{9,1},{17,25},{25,17},{2,10},{10... | collective-permute-start | bytes 3145736 | tf_op jit(solution)/shard_map/ppermute | solution.py:157
  201.4 145.5 %reduce-scatter.8.cloned.1.call-start = ((), (), s32[]{:S(2)}) async-start(), calls=%async_computation.8 | async-start | bytes 2621440 | tf_op jit(solution)/shard_map/reduce_scatter | solution.py:233
  201.8 13.6 %collective-permute-start.24 = (bf16[256,1024]{1,0:T(8,128)(2,1)S(1)}, bf16[256,1024]{1,0:T(8,128)(2,1)S(1)}, u32[]{:S(2)}, u32[]{:S(2)}) collective-permute-start(bf16[256,1024]{1,0:T(8,128)(2,1)S(1)} %get-tuple-element.45), channel_id=1, source_target_pairs={{0,1},{1,0},{2,3},{3,2},{4,5},{5,4},{6,7},{7,6},{8,9},{9,8},{10,11... | collective-permute-start | bytes 1572872 | tf_op jit(solution)/shard_map/ppermute | solution.py:163
  203.3 13.2 %collective-permute-start.26 = (bf16[256,1024]{1,0:T(8,128)(2,1)S(1)}, bf16[256,1024]{1,0:T(8,128)(2,1)S(1)}, u32[]{:S(2)}, u32[]{:S(2)}) collective-permute-start(bf16[256,1024]{1,0:T(8,128)(2,1)S(1)} %get-tuple-element.46), channel_id=1, source_target_pairs={{0,16},{8,24},{16,0},{24,8},{1,17},{9,25},{17,1},{25,9},{2,18},{10... | collective-permute-start | bytes 1572872 | tf_op jit(solution)/shard_map/ppermute | solution.py:160
  248.9 5.8 %collective-permute-start.31 = (bf16[512,1024]{1,0:T(8,128)(2,1)}, bf16[512,1024]{1,0:T(8,128)(2,1)S(1)}, u32[]{:S(2)}, u32[]{:S(2)}) collective-permute-start(bf16[512,1024]{1,0:T(8,128)(2,1)} %shard_map.100.refs_3_.refs_11_), channel_id=1, source_target_pairs={{0,8},{8,0},{16,24},{24,16},{1,9},{9,1},{17,25},{25,17},{2,10},{10... | collective-permute-start | bytes 3145736 | tf_op jit(solution)/shard_map/ppermute | solution.py:157
  248.9 10.3 %collective-permute-start.28 = (bf16[512,1024]{1,0:T(8,128)(2,1)}, bf16[512,1024]{1,0:T(8,128)(2,1)S(1)}, u32[]{:S(2)}, u32[]{:S(2)}) collective-permute-start(bf16[512,1024]{1,0:T(8,128)(2,1)} %copy-done.41), channel_id=1, source_target_pairs={{0,8},{8,0},{16,24},{24,16},{1,9},{9,1},{17,25},{25,17},{2,10},{10... | collective-permute-start | bytes 3145736 | tf_op jit(solution)/shard_map/ppermute | solution.py:157
  249.4 10.4 %collective-permute-start.29 = (bf16[512,1024]{1,0:T(8,128)(2,1)}, bf16[512,1024]{1,0:T(8,128)(2,1)S(1)}, u32[]{:S(2)}, u32[]{:S(2)}) collective-permute-start(bf16[512,1024]{1,0:T(8,128)(2,1)} %copy-done.40), channel_id=1, source_target_pairs={{0,8},{8,0},{16,24},{24,16},{1,9},{9,1},{17,25},{25,17},{2,10},{10... | collective-permute-start | bytes 3145736 | tf_op jit(solution)/shard_map/ppermute | solution.py:157
  249.5 10.4 %collective-permute-start.30 = (bf16[512,1024]{1,0:T(8,128)(2,1)}, bf16[512,1024]{1,0:T(8,128)(2,1)S(1)}, u32[]{:S(2)}, u32[]{:S(2)}) collective-permute-start(bf16[512,1024]{1,0:T(8,128)(2,1)} %copy-done.39), channel_id=1, source_target_pairs={{0,8},{8,0},{16,24},{24,16},{1,9},{9,1},{17,25},{25,17},{2,10},{10... | collective-permute-start | bytes 3145736 | tf_op jit(solution)/shard_map/ppermute | solution.py:157
  251.6 26.1 %collective-permute-start.25 = (bf16[512,1024]{1,0:T(8,128)(2,1)S(1)}, bf16[512,1024]{1,0:T(8,128)(2,1)S(1)}, u32[]{:S(2)}, u32[]{:S(2)}) collective-permute-start(bf16[512,1024]{1,0:T(8,128)(2,1)S(1)} %add_convert_fusion.2), channel_id=1, source_target_pairs={{0,16},{8,24},{16,0},{24,8},{1,17},{9,25},{17,1},{25,9},{2,18},{10... | collective-permute-start | bytes 3145736 | tf_op jit(solution)/shard_map/ppermute | solution.py:160
  254.7 24.9 %collective-permute-start.27 = (bf16[512,1024]{1,0:T(8,128)(2,1)S(1)}, bf16[512,1024]{1,0:T(8,128)(2,1)S(1)}, u32[]{:S(2)}, u32[]{:S(2)}) collective-permute-start(bf16[512,1024]{1,0:T(8,128)(2,1)S(1)} %add_convert_fusion.1), channel_id=1, source_target_pairs={{0,1},{1,0},{2,3},{3,2},{4,5},{5,4},{6,7},{7,6},{8,9},{9,8},{10,11... | collective-permute-start | bytes 3145736 | tf_op jit(solution)/shard_map/ppermute | solution.py:163
  257.8 21.8 %copy-start.26 = (bf16[1024,1024]{1,0:T(8,128)(2,1)S(1)}, bf16[1024,1024]{1,0:T(8,128)(2,1)}, u32[]{:S(2)}) copy-start(bf16[1024,1024]{1,0:T(8,128)(2,1)} %all-gather.4.cloned.1.call-done.refs_10_.refs_1_) | copy-start | bytes 6291460
  259.3 40.9 %collective-permute-start.34 = (bf16[512,1024]{1,0:T(8,128)(2,1)S(1)}, bf16[512,1024]{1,0:T(8,128)(2,1)S(1)}, u32[]{:S(2)}, u32[]{:S(2)}) collective-permute-start(bf16[512,1024]{1,0:T(8,128)(2,1)S(1)} %shard_map.103.refs_6_), channel_id=1, source_target_pairs={{0,16},{8,24},{16,0},{24,8},{1,17},{9,25},{17,1},{25,9},{2,18},{10... | collective-permute-start | bytes 3145736 | tf_op jit(solution)/shard_map/ppermute | solution.py:160
  283.5 19.9 %copy-start.30 = (bf16[128,2048]{1,0:T(8,128)(2,1)S(1)}, bf16[128,2048]{1,0:T(8,128)(2,1)}, u32[]{:S(2)}) copy-start(bf16[128,2048]{1,0:T(8,128)(2,1)} %reduce-scatter.4.cloned.1.call-done.refs_1_) | copy-start | bytes 1572868
  283.5 58.4 %collective-permute-start.32 = (bf16[512,1024]{1,0:T(8,128)(2,1)}, bf16[512,1024]{1,0:T(8,128)(2,1)}, u32[]{:S(2)}, u32[]{:S(2)}) collective-permute-start(bf16[512,1024]{1,0:T(8,128)(2,1)} %get-tuple-element.41), channel_id=1, source_target_pairs={{0,16},{8,24},{16,0},{24,8},{1,17},{9,25},{17,1},{25,9},{2,18},{10... | collective-permute-start | bytes 3145736 | tf_op jit(solution)/shard_map/ppermute | solution.py:160
  301.4 43.1 %collective-permute-start.35 = (bf16[512,1024]{1,0:T(8,128)(2,1)}, bf16[512,1024]{1,0:T(8,128)(2,1)}, u32[]{:S(2)}, u32[]{:S(2)}) collective-permute-start(bf16[512,1024]{1,0:T(8,128)(2,1)} %shard_map.106), channel_id=1, source_target_pairs={{0,1},{1,0},{2,3},{3,2},{4,5},{5,4},{6,7},{7,6},{8,9},{9,8},{10,11... | collective-permute-start | bytes 3145736 | tf_op jit(solution)/shard_map/ppermute | solution.py:163
  302.8 41.7 %collective-permute-start.36 = (bf16[256,1024]{1,0:T(8,128)(2,1)}, bf16[256,1024]{1,0:T(8,128)(2,1)S(1)}, u32[]{:S(2)}, u32[]{:S(2)}) collective-permute-start(bf16[256,1024]{1,0:T(8,128)(2,1)} %reduce-scatter.6.cloned.1.call-done.refs_1_), channel_id=1, source_target_pairs={{0,1},{1,0},{2,3},{3,2},{4,5},{5,4},{6,7},{7,6},{8,9},{9,8},{10,11... | collective-permute-start | bytes 1572872 | tf_op jit(solution)/shard_map/ppermute | solution.py:163
  303.5 38.5 %copy-start.46 = (bf16[512,1024]{1,0:T(8,128)(2,1)S(1)}, bf16[512,1024]{1,0:T(8,128)(2,1)}, u32[]{:S(2)}) copy-start(bf16[512,1024]{1,0:T(8,128)(2,1)} %copy-done.45) | copy-start | bytes 3145732
  303.5 38.4 %collective-permute-start.33 = (bf16[128,1024]{1,0:T(8,128)(2,1)S(1)}, bf16[128,1024]{1,0:T(8,128)(2,1)S(1)}, u32[]{:S(2)}, u32[]{:S(2)}) collective-permute-start(bf16[128,1024]{1,0:T(8,128)(2,1)S(1)} %get-tuple-element.48), channel_id=1, source_target_pairs={{0,1},{1,0},{2,3},{3,2},{4,5},{5,4},{6,7},{7,6},{8,9},{9,8},{10,11... | collective-permute-start | bytes 786440 | tf_op jit(solution)/shard_map/ppermute | solution.py:163
  (63 other events, 254.8 us)
Sparse Core Ops, SparseCore 0:
  10.1 48.6 all-gather.3
  61.0 44.6 all-gather.5
  107.8 44.6 all-gather.7
  154.6 42.5 reduce-scatter.3
  201.5 43.1 reduce-scatter.5
  249.0 43.1 reduce-scatter.7

commit v7 on v6

--- a/solution.py
+++ b/solution.py
@@ -287,30 +287,36 @@
         corner = sums[1, 1]
         by_other, by_chip = self.other(corner[:step]), self.chip(corner[step:])
         sums |= self.near_rest(hidden, down_sides, output_far, [corner])
-        other_term = unit_term(1, [sums[0, 0]])
-        other_sum = scatter_units(call(copy_kernel, [shape(*other_term.shape)], 0, [other_term], [down_sum])[0])
+        other_term = unit_term(1, [sums[0, 0], by_other, by_chip])
+        (term,) = call(copy_kernel, [shape(*other_term.shape)], 0, [other_term], [down_sum])
+        other_sum = scatter_units(term)
+        zeros = jnp.zeros((step, half), F32)
+
+        def with_corner(sums, by_chip, by_other):
+            to_chip = sums[1, 0].astype(F32) + jnp.concatenate([by_other.astype(F32), zeros])
+            to_other = sums[0, 1].astype(F32) + jnp.concatenate([zeros, by_chip.astype(F32)])
+            return self.chip(to_chip.astype(BF16)), self.other(to_other.astype(BF16))
+
+        output_chip, output_other = with_corner(sums, by_chip, by_other)
         unit_sides = [(own_units, 0, half), (other_units, 0, half)]
-        grads_far = self.far_first(act, unit_sides, [other_term, by_other, by_chip])
+        grads_far = self.far_first(act, unit_sides, [other_term])
         grads_far |= self.far_rest(act, unit_sides, [grads_far[1, 1]])
-        zeros = jnp.zeros((step, half), F32)
-        to_chip = (sums[1, 0].astype(F32) + jnp.concatenate([by_other.astype(F32), zeros])).astype(BF16)
-        to_other = (sums[0, 1].astype(F32) + jnp.concatenate([zeros, by_chip.astype(F32)])).astype(BF16)
-        output_chip, output_other = self.chip(to_chip), self.other(to_other)
-        own_term = unit_term(0, list(grads_far.values()))
-        own_sum = scatter_units(call(copy_kernel, [shape(*own_term.shape)], 0, [own_term], [other_sum])[0])
         grads_far = {place: self.core(block) for place, block in grads_far.items()}
-        grads = self.near_first(act, unit_sides, grads_far, [own_term])
-        corner = self.chip(grads[1, 1])
+        grads = self.near_first(act, unit_sides, grads_far, [])
+        corner = grads[1, 1]
+        by_other, by_chip = self.other(corner[:step]), self.chip(corner[step:])
+        grads |= self.near_rest(act, unit_sides, grads_far, [corner])
+        own_term = unit_term(0, [grads[0, 0], output_chip, output_other])
         down_back = self.other(down_sum[:, half:])
-        grads |= self.near_rest(act, unit_sides, grads_far, [grads[1, 1], output_chip, output_other])
-        by_chip = self.chip(grads[1, 0])
-        (to_other,) = call(sum_kernel, [shape(2 * step, half)], 0, [grads[0, 1], corner])
-        by_other = self.other(to_other)
+        waits = [other_sum, by_other, by_chip, down_back]
+        (term,) = call(copy_kernel, [shape(*own_term.shape)], 0, [own_term], waits)
+        own_sum = scatter_units(term)
+        grads_chip, grads_other = with_corner(grads, by_chip, by_other)
         total = sums[0, 0].astype(F32) + output_chip.astype(F32) + output_other.astype(F32)
         output = total.astype(BF16).reshape(2, step, half)
         units_back = self.other(other_sum)
-        (partial,) = call(sum_kernel, [shape(2 * step, half)], 0, [grads[0, 0], by_chip], [down_back])
-        (total,) = call(sum_kernel, [shape(2 * step, half)], 0, [partial, by_other], [units_back])
+        (partial,) = call(sum_kernel, [shape(2 * step, half)], 0, [grads[0, 0], grads_chip])
+        (total,) = call(sum_kernel, [shape(2 * step, half)], 0, [partial, grads_other], [units_back])
         grad_tokens = total.reshape(2, step, half)
 
         at_out = lax.axis_index("out").astype(jnp.int32).reshape(1)

time: 359 us -> 325 us (0.905)
  waiting for transfers between devices: 176 us -> 138 us
  local copies, waits for them, and re-layouts: 44 us -> 48.4 us
    ppermute x11 -> x12, waiting for transfers between devices: 87.4 us -> 60.5 us  [other(): return lax.ppermute(array, 'out', [(0, 1), (1, 0)])]
    reduce_scatter x3, waiting for transfers between devices: 8.85 us -> 0.01 us  [scatter_units(): return lax.psum_scatter(array, 'wt', scatter_dimension=0, tiled=True)]
    unnamed x140 -> x152, local copies, waits for them, and re-layouts: 41.4 us -> 44.7 us
    pallas_call x19 -> x18, Pallas kernels: 86.4 us -> 85.2 us  [call(): pl.pallas_call(body, out_shape=list(outs), in_specs=[*specs, *[pl.BlockSp...]
    ppermute x11 -> x12, starting transfers between devices: 14.4 us -> 14 us  [other(): return lax.ppermute(array, 'out', [(0, 1), (1, 0)])]
  transfers between devices with their start and end apart: 43 -> 44, of which waited for: 18 -> 19; matrix products, arithmetic and copies ran while one was open for 3% -> 4% of each run, Pallas kernels for 24% -> 25%
where the time goes in v7:
time: 325 us; the launch traced here: 324 us
  waiting for transfers between devices  138 us (42%)
  Pallas kernels  85.2 us (26%)
  local copies, waits for them, and re-layouts  48.4 us (15%)
  starting transfers between devices  26.7 us (8%)
  between operations  14.7 us (5%)
  other arithmetic  11.2 us (3%)
    pallas_call x18, Pallas kernels, call(): pl.pallas_call(body, out_shape=list(outs), in_specs=[*specs, *[pl.BlockSp...  85.2 us
    ppermute x8, waiting for transfers between devices, chip(): return lax.ppermute(array, 'inp', [(at, at ^ 2) for at in range(4)])  65.7 us
    ppermute x12, waiting for transfers between devices, other(): return lax.ppermute(array, 'out', [(0, 1), (1, 0)])  60.5 us
    unnamed x152, local copies, waits for them, and re-layouts  44.7 us
    ppermute x12, starting transfers between devices, other(): return lax.ppermute(array, 'out', [(0, 1), (1, 0)])  14 us
    all_gather x3, waiting for transfers between devices, gather_units(): return lax.all_gather(array, 'wt', axis=0, tiled=True)  11.2 us
    ppermute x8, starting transfers between devices, chip(): return lax.ppermute(array, 'inp', [(at, at ^ 2) for at in range(4)])  9.4 us
  transfers between devices with their start and end apart: 44, of which 19 were waited for; matrix products, arithmetic and copies ran while one was open for 4% of the time, Pallas kernels for 25%

profile of v7, /device:TPU:0, one launch (start us, length us, event | category | flops | bytes accessed | tf_op | source)
XLA Modules:
  0.0 323.8 jit_solution(11003282194427771504)
XLA Ops:
  10.1 3.0 collective-permute-start.9
  13.1 11.9 %collective-permute-done.9 = bf16[256,1024]{1,0:T(8,128)(2,1)S(1)} collective-permute-done((bf16[256,1024]{1,0:T(8,128)(2,1)S(1)}, bf16[256,1024]{1,0:T(8,128)(2,1)S(1)}, u32[]{:S(2)}, u32[]{:S(2)}) %collective-permute-start.9) | collective-permute-done | bytes 524320 | tf_op jit(solution)/shard_map/ppermute | solution.py:163
  25.9 1.8 collective-permute-start.10
  27.7 1.5 collective-permute-start.1
  30.1 5.2 %collective-permute-done.10 = bf16[128,1024]{1,0:T(8,128)(2,1)S(1)} collective-permute-done((bf16[128,1024]{1,0:T(8,128)(2,1)S(1)}, bf16[128,1024]{1,0:T(8,128)(2,1)S(1)}, u32[]{:S(2)}, u32[]{:S(2)}) %collective-permute-start.10) | collective-permute-done | bytes 262176 | tf_op jit(solution)/shard_map/ppermute | solution.py:163
  35.2 1.7 collective-permute-start.11
  37.9 16.0 %collective-permute-done.1.refs_2_ = bf16[512,1024]{1,0:T(8,128)(2,1)S(1)} collective-permute-done((bf16[512,1024]{1,0:T(8,128)(2,1)S(1)}, bf16[512,1024]{1,0:T(8,128)(2,1)S(1)}, u32[]{:S(2)}, u32[]{:S(2)}) %collective-permute-start.1) | collective-permute-done | bytes 1048608 | tf_op jit(solution)/shard_map/ppermute | solution.py:160
  54.2 3.5 %collective-permute-done.refs_1_ = bf16[512,1024]{1,0:T(8,128)(2,1)S(1)} collective-permute-done((bf16[512,1024]{1,0:T(8,128)(2,1)S(1)}, bf16[512,1024]{1,0:T(8,128)(2,1)S(1)}, u32[]{:S(2)}, u32[]{:S(2)}) %collective-permute-start) | collective-permute-done | bytes 1048608 | tf_op jit(solution)/shard_map/ppermute | solution.py:163
  57.8 1.8 collective-permute-start.3
  59.5 16.9 %collective-permute-done.12.refs_2_ = bf16[512,1024]{1,0:T(8,128)(2,1)} collective-permute-done((bf16[512,1024]{1,0:T(8,128)(2,1)}, bf16[512,1024]{1,0:T(8,128)(2,1)}, u32[]{:S(2)}, u32[]{:S(2)}) %collective-permute-start.12) | collective-permute-done | bytes 1048608 | tf_op jit(solution)/shard_map/ppermute | solution.py:160
  77.9 2.4 collective-permute-done.11.refs_1_
  81.4 10.0 %collective-permute-done.2.refs_3_ = bf16[256,1024]{1,0:T(8,128)(2,1)S(1)} collective-permute-done((bf16[256,1024]{1,0:T(8,128)(2,1)S(1)}, bf16[256,1024]{1,0:T(8,128)(2,1)S(1)}, u32[]{:S(2)}, u32[]{:S(2)}) %collective-permute-start.2) | collective-permute-done | bytes 524320 | tf_op jit(solution)/shard_map/ppermute | solution.py:163
  91.4 1.7 collective-permute-start.14
  93.9 7.2 %collective-permute-done.13.refs_3_ = bf16[256,1024]{1,0:T(8,128)(2,1)} collective-permute-done((bf16[256,1024]{1,0:T(8,128)(2,1)S(1)}, bf16[256,1024]{1,0:T(8,128)(2,1)}, u32[]{:S(2)}, u32[]{:S(2)}) %collective-permute-start.13) | collective-permute-done | bytes 524320 | tf_op jit(solution)/shard_map/ppermute | solution.py:163
  113.7 16.0 %shard_map.92 = (bf16[2048,512]{1,0:T(8,128)(2,1)}, bf16[512,2048]{1,0:T(8,128)(2,1)}, bf16[2048,512]{1,0:T(8,128)(2,1)}, bf16[2048,512]{1,0:T(8,128)(2,1)}) custom-call(bf16[512,1024]{1,0:T(8,128)(2,1)S(1)} %bitcast.12, bf16[512,1024]{1,0:T(8,128)(2,1)S(1)} %collective-permute-done.refs_1_, bf16[512,1024]{1,0:T(8,128)(2,1)S(1)} %collective-permute-done.1.refs_2_, ...), custom_call_target="tpu_custom_call" | custom-call | flops 8589934592 | bytes 20971520 | tf_op jit(solution)/shard_map/pallas_call | solution.py:38
  129.7 11.3 %shard_map.93.refs_2_ = bf16[512,2048]{1,0:T(8,128)(2,1)} custom-call(bf16[512,1024]{1,0:T(8,128)(2,1)} %bitcast.5.refs_0_, bf16[512,1024]{1,0:T(8,128)(2,1)} %collective-permute-done.11.refs_1_, bf16[512,1024]{1,0:T(8,128)(2,1)} %collective-permute-done.12.refs_2_, bf16[256,1024]{1,0:T(8,128)(2,1)} %collective-permute-done.13.refs_3_, ...), custom_call_target="tpu_custom_call" | custom-call | flops 4294967296 | bytes 12582912 | tf_op jit(solution)/shard_map/pallas_call | solution.py:38
  141.3 11.2 %all-gather.8.cloned.1.call-done.refs_1_.refs_2_.refs_10_ = bf16[512,2048]{1,0:T(8,128)(2,1)} async-done(((bf16[128,2048]{1,0:T(8,128)(2,1)}), bf16[512,2048]{1,0:T(8,128)(2,1)}) %all-gather.8.cloned.1.call-update) | async-done | bytes 2097168 | tf_op jit(solution)/shard_map/all_gather | solution.py:230
  152.5 1.6 copy-done
  154.1 1.6 copy-done.11
  157.3 3.3 %shard_map.95 = (bf16[512,1024]{1,0:T(8,128)(2,1)}, bf16[512,1024]{1,0:T(8,128)(2,1)}, bf16[512,1024]{1,0:T(8,128)(2,1)}) custom-call(bf16[2048,512]{1,0:T(8,128)(2,1)S(1)} %copy-done.6, bf16[512,2048]{1,0:T(8,128)(2,1)S(1)} %copy-done.1, bf16[512,2048]{1,0:T(8,128)(2,1)S(1)} %copy-done.1, bf16[512,1024]{1,0:T(8,128)(2,1)S(1)} %shard_map.94.refs_3_.refs_13_), custom_call_target="tpu_custom_call" | custom-call | flops 1610612736 | bytes 9437184 | tf_op jit(solution)/shard_map/pallas_call | solution.py:38
  161.2 13.9 %shard_map.96 = (bf16[2048,1024]{1,0:T(8,128)(2,1)}, bf16[1024,2048]{1,0:T(8,128)(2,1)}) custom-call(bf16[512,1024]{1,0:T(8,128)(2,1)} %bitcast.5.refs_0_, bf16[512,1024]{1,0:T(8,128)(2,1)} %collective-permute-done.11.refs_1_, bf16[512,1024]{1,0:T(8,128)(2,1)} %collective-permute-done.12.refs_2_, bf16[256,1024]{1,0:T(8,128)(2,1)} %collective-permute-done.13.refs_3_, ...), custom_call_target="tpu_custom_call" | custom-call | flops 4294967296 | bytes 23068672 | tf_op jit(solution)/shard_map/pallas_call | solution.py:38
  175.1 2.2 copy-done.3
  178.3 1.5 collective-permute-start.24
  179.9 1.5 collective-permute-start.26
  181.4 4.5 %shard_map.98 = (bf16[512,1024]{1,0:T(8,128)(2,1)S(1)}, bf16[512,1024]{1,0:T(8,128)(2,1)S(1)}, bf16[512,1024]{1,0:T(8,128)(2,1)S(1)}) custom-call(bf16[2048,512]{1,0:T(8,128)(2,1)S(1)} %copy-done.6, bf16[512,2048]{1,0:T(8,128)(2,1)S(1)} %copy-done.2, bf16[512,2048]{1,0:T(8,128)(2,1)S(1)} %copy-done.2, bf16[512,1024]{1,0:T(8,128)(2,1)} %collective-permute-done.20.refs_3_, ...), custom_call_target="tpu_custom_call" | custom-call | flops 1610612736 | bytes 12582912 | tf_op jit(solution)/shard_map/pallas_call | solution.py:38
  188.9 3.8 %collective-permute-done.24.refs_12_ = bf16[256,1024]{1,0:T(8,128)(2,1)S(1)} collective-permute-done((bf16[256,1024]{1,0:T(8,128)(2,1)S(1)}, bf16[256,1024]{1,0:T(8,128)(2,1)S(1)}, u32[]{:S(2)}, u32[]{:S(2)}) %collective-permute-start.24) | collective-permute-done | bytes 524320 | tf_op jit(solution)/shard_map/ppermute | solution.py:163
  194.1 8.9 %shard_map.99.refs_2_.refs_0_ = bf16[1024,1024]{1,0:T(8,128)(2,1)} custom-call(bf16[512,1024]{1,0:T(8,128)(2,1)S(1)} %bitcast.13, bf16[512,1024]{1,0:T(8,128)(2,1)S(1)} %copy-done.14, bf16[512,1024]{1,0:T(8,128)(2,1)S(1)} %collective-permute-done.1.refs_2_, bf16[256,1024]{1,0:T(8,128)(2,1)S(1)} %copy-done.34, bf16[256,1024]{1,0:T(8,128)(2,1)S(1)} %copy-done.38, ...), custom_call_target="tpu_custom_call" | custom-call | flops 4294967296 | bytes 14680064 | tf_op jit(solution)/shard_map/pallas_call | solution.py:38
  204.6 1.6 copy-done.8
  210.3 2.2 copy-done.4
  212.5 1.7 copy-done.9
  214.2 1.5 shard_map.100.refs_3_
  217.0 3.9 %shard_map.101 = (bf16[512,1024]{1,0:T(8,128)(2,1)S(1)}, bf16[512,1024]{1,0:T(8,128)(2,1)S(1)}, bf16[512,1024]{1,0:T(8,128)(2,1)S(1)}) custom-call(bf16[2048,1024]{1,0:T(8,128)(2,1)S(1)} %copy-done.5, bf16[1024,1024]{1,0:T(8,128)(2,1)S(1)} %copy-done.60, bf16[1024,1024]{1,0:T(8,128)(2,1)S(1)} %copy-done.7, bf16[512,1024]{1,0:T(8,128)(2,1)S(1)} %shard_map.100.refs_3_), custom_call_target="tpu_custom_call" | custom-call | flops 3221225472 | bytes 11534336 | tf_op jit(solution)/shard_map/pallas_call | solution.py:38
  221.9 1.7 collective-permute-start.25
  224.3 1.5 shard_map.102.refs_6_
  225.9 1.7 collective-permute-start.32
  228.1 3.9 %shard_map.103 = (bf16[512,1024]{1,0:T(8,128)(2,1)S(1)}, bf16[512,1024]{1,0:T(8,128)(2,1)S(1)}, bf16[512,1024]{1,0:T(8,128)(2,1)S(1)}) custom-call(bf16[2048,1024]{1,0:T(8,128)(2,1)S(1)} %copy-done.5, bf16[1024,1024]{1,0:T(8,128)(2,1)S(1)} %copy-done.60, bf16[1024,1024]{1,0:T(8,128)(2,1)S(1)} %copy-done.7, ...), custom_call_target="tpu_custom_call" | custom-call | flops 3221225472 | bytes 14680064 | tf_op jit(solution)/shard_map/pallas_call | solution.py:38
  234.5 13.4 %collective-permute-done.25.refs_12_ = bf16[512,1024]{1,0:T(8,128)(2,1)S(1)} collective-permute-done((bf16[512,1024]{1,0:T(8,128)(2,1)S(1)}, bf16[512,1024]{1,0:T(8,128)(2,1)S(1)}, u32[]{:S(2)}, u32[]{:S(2)}) %collective-permute-start.25) | collective-permute-done | bytes 1048608 | tf_op jit(solution)/shard_map/ppermute | solution.py:160
  247.9 2.0 collective-permute-done.27.refs_13_
  250.9 8.9 %shard_map.107.refs_0_ = bf16[1024,1024]{1,0:T(8,128)(2,1)} custom-call(bf16[512,1024]{1,0:T(8,128)(2,1)S(1)} %bitcast.14, bf16[512,1024]{1,0:T(8,128)(2,1)S(1)} %copy-done.15, bf16[512,1024]{1,0:T(8,128)(2,1)S(1)} %collective-permute-done.1.refs_2_, bf16[256,1024]{1,0:T(8,128)(2,1)S(1)} %copy-done.35, bf16[256,1024]{1,0:T(8,128)(2,1)S(1)} %copy-done.39, ...), custom_call_target="tpu_custom_call" | custom-call | flops 4294967296 | bytes 14680064 | tf_op jit(solution)/shard_map/pallas_call | solution.py:38
  262.7 3.2 %collective-permute-done.37.refs_4_ = bf16[128,1024]{1,0:T(8,128)(2,1)S(1)} collective-permute-done((bf16[128,1024]{1,0:T(8,128)(2,1)S(1)}, bf16[128,1024]{1,0:T(8,128)(2,1)S(1)}, u32[]{:S(2)}, u32[]{:S(2)}) %collective-permute-start.37) | collective-permute-done | bytes 262176 | tf_op jit(solution)/shard_map/ppermute | solution.py:163
  266.0 1.6 copy-done.10
  272.1 2.5 add_convert_fusion.1
  276.8 1.5 collective-permute-start.36
  278.3 3.2 add_convert_fusion.2
  281.6 17.8 %collective-permute-done.33.refs_1_ = bf16[512,1024]{1,0:T(8,128)(2,1)} collective-permute-done((bf16[512,1024]{1,0:T(8,128)(2,1)}, bf16[512,1024]{1,0:T(8,128)(2,1)}, u32[]{:S(2)}, u32[]{:S(2)}) %collective-permute-start.33) | collective-permute-done | bytes 1048608 | tf_op jit(solution)/shard_map/ppermute | solution.py:160
  299.4 1.5 shard_map.104.refs_0_
  302.6 9.3 %collective-permute-done.36.refs_2_ = bf16[256,1024]{1,0:T(8,128)(2,1)S(1)} collective-permute-done((bf16[256,1024]{1,0:T(8,128)(2,1)}, bf16[256,1024]{1,0:T(8,128)(2,1)S(1)}, u32[]{:S(2)}, u32[]{:S(2)}) %collective-permute-start.36) | collective-permute-done | bytes 524320 | tf_op jit(solution)/shard_map/ppermute | solution.py:163
  315.4 1.6 shard_map.109
  (235 shorter events, 57.0 us)
Async XLA Ops:
  7.2 99.9 %all-gather.4.cloned.1.call-start = ((), (), s32[]{:S(2)}) async-start(), calls=%async_computation.3 | async-start | bytes 2621440 | tf_op jit(solution)/shard_map/all_gather | solution.py:230
  9.7 97.4 %all-gather.6.cloned.1.call-start = ((), (), s32[]{:S(2)}) async-start(), calls=%async_computation.4 | async-start | bytes 2621440 | tf_op jit(solution)/shard_map/all_gather | solution.py:230
  10.1 15.0 %collective-permute-start.9 = (bf16[256,1024]{1,0:T(8,128)(2,1)S(1)}, bf16[256,1024]{1,0:T(8,128)(2,1)S(1)}, u32[]{:S(2)}, u32[]{:S(2)}) collective-permute-start(bf16[256,1024]{1,0:T(8,128)(2,1)S(1)} %pad_maximum_fusion.1), channel_id=1, source_target_pairs={{0,1},{1,0},{2,3},{3,2},{4,5},{5,4},{6,7},{7,6},{8,9},{9,8},{10,11... | collective-permute-start | bytes 1572872 | tf_op jit(solution)/shard_map/ppermute | solution.py:163
  25.8 126.7 %all-gather.8.cloned.1.call-start = ((), (), s32[]{:S(2)}) async-start(), calls=%async_computation.5 | async-start | bytes 2621440 | tf_op jit(solution)/shard_map/all_gather | solution.py:230
  25.9 9.3 %collective-permute-start.10 = (bf16[128,1024]{1,0:T(8,128)(2,1)S(1)}, bf16[128,1024]{1,0:T(8,128)(2,1)S(1)}, u32[]{:S(2)}, u32[]{:S(2)}) collective-permute-start(bf16[128,1024]{1,0:T(8,128)(2,1)S(1)} %get-tuple-element.52), channel_id=1, source_target_pairs={{0,1},{1,0},{2,3},{3,2},{4,5},{5,4},{6,7},{7,6},{8,9},{9,8},{10,11... | collective-permute-start | bytes 786440 | tf_op jit(solution)/shard_map/ppermute | solution.py:163
  27.7 26.1 %collective-permute-start.1 = (bf16[512,1024]{1,0:T(8,128)(2,1)S(1)}, bf16[512,1024]{1,0:T(8,128)(2,1)S(1)}, u32[]{:S(2)}, u32[]{:S(2)}) collective-permute-start(bf16[512,1024]{1,0:T(8,128)(2,1)S(1)} %bitcast.9), channel_id=1, source_target_pairs={{0,16},{8,24},{16,0},{24,8},{1,17},{9,25},{17,1},{25,9},{2,18},{10... | collective-permute-start | bytes 3145736 | tf_op jit(solution)/shard_map/ppermute | solution.py:160
  29.2 28.5 %collective-permute-start = (bf16[512,1024]{1,0:T(8,128)(2,1)S(1)}, bf16[512,1024]{1,0:T(8,128)(2,1)S(1)}, u32[]{:S(2)}, u32[]{:S(2)}) collective-permute-start(bf16[512,1024]{1,0:T(8,128)(2,1)S(1)} %bitcast.10), channel_id=1, source_target_pairs={{0,1},{1,0},{2,3},{3,2},{4,5},{5,4},{6,7},{7,6},{8,9},{9,8},{10,11... | collective-permute-start | bytes 3145736 | tf_op jit(solution)/shard_map/ppermute | solution.py:163
  29.7 46.7 %collective-permute-start.12 = (bf16[512,1024]{1,0:T(8,128)(2,1)}, bf16[512,1024]{1,0:T(8,128)(2,1)}, u32[]{:S(2)}, u32[]{:S(2)}) collective-permute-start(bf16[512,1024]{1,0:T(8,128)(2,1)} %bitcast.5.refs_0_), channel_id=1, source_target_pairs={{0,16},{8,24},{16,0},{24,8},{1,17},{9,25},{17,1},{25,9},{2,18},{10... | collective-permute-start | bytes 3145736 | tf_op jit(solution)/shard_map/ppermute | solution.py:160
  30.1 47.8 %collective-permute-start.4 = (bf16[512,1024]{1,0:T(8,128)(2,1)S(1)}, bf16[512,1024]{1,0:T(8,128)(2,1)}, u32[]{:S(2)}, u32[]{:S(2)}) collective-permute-start(bf16[512,1024]{1,0:T(8,128)(2,1)S(1)} %bitcast.11), channel_id=1, source_target_pairs={{0,8},{8,0},{16,24},{24,16},{1,9},{9,1},{17,25},{25,17},{2,10},{10... | collective-permute-start | bytes 3145736 | tf_op jit(solution)/shard_map/ppermute | solution.py:157
  35.2 45.0 %collective-permute-start.11 = (bf16[512,1024]{1,0:T(8,128)(2,1)}, bf16[512,1024]{1,0:T(8,128)(2,1)}, u32[]{:S(2)}, u32[]{:S(2)}) collective-permute-start(bf16[512,1024]{1,0:T(8,128)(2,1)} %bitcast.5.refs_0_), channel_id=1, source_target_pairs={{0,1},{1,0},{2,3},{3,2},{4,5},{5,4},{6,7},{7,6},{8,9},{9,8},{10,11... | collective-permute-start | bytes 3145736 | tf_op jit(solution)/shard_map/ppermute | solution.py:163
  37.8 166.7 %reduce-scatter.4.cloned.1.call-start = ((), (), s32[]{:S(2)}) async-start(), calls=%async_computation.6 | async-start | bytes 2621440 | tf_op jit(solution)/shard_map/reduce_scatter | solution.py:233
  53.9 37.5 %collective-permute-start.2 = (bf16[256,1024]{1,0:T(8,128)(2,1)S(1)}, bf16[256,1024]{1,0:T(8,128)(2,1)S(1)}, u32[]{:S(2)}, u32[]{:S(2)}) collective-permute-start(bf16[256,1024]{1,0:T(8,128)(2,1)S(1)} %slice.40), channel_id=1, source_target_pairs={{0,1},{1,0},{2,3},{3,2},{4,5},{5,4},{6,7},{7,6},{8,9},{9,8},{10,11... | collective-permute-start | bytes 1572872 | tf_op jit(solution)/shard_map/ppermute | solution.py:163
  57.7 71.9 %copy-start.13 = (bf16[512,1024]{1,0:T(8,128)(2,1)}, bf16[512,1024]{1,0:T(8,128)(2,1)S(1)}, u32[]{:S(2)}) copy-start(bf16[512,1024]{1,0:T(8,128)(2,1)S(1)} %collective-permute-done.refs_1_) | copy-start | bytes 3145732
  57.8 35.4 %collective-permute-start.3 = (bf16[256,1024]{1,0:T(8,128)(2,1)S(1)}, bf16[256,1024]{1,0:T(8,128)(2,1)S(1)}, u32[]{:S(2)}, u32[]{:S(2)}) collective-permute-start(bf16[256,1024]{1,0:T(8,128)(2,1)S(1)} %slice.41), channel_id=1, source_target_pairs={{0,16},{8,24},{16,0},{24,8},{1,17},{9,25},{17,1},{25,9},{2,18},{10... | collective-permute-start | bytes 1572872 | tf_op jit(solution)/shard_map/ppermute | solution.py:160
  77.5 23.6 %collective-permute-start.13 = (bf16[256,1024]{1,0:T(8,128)(2,1)S(1)}, bf16[256,1024]{1,0:T(8,128)(2,1)}, u32[]{:S(2)}, u32[]{:S(2)}) collective-permute-start(bf16[256,1024]{1,0:T(8,128)(2,1)S(1)} %slice.42), channel_id=1, source_target_pairs={{0,1},{1,0},{2,3},{3,2},{4,5},{5,4},{6,7},{7,6},{8,9},{9,8},{10,11... | collective-permute-start | bytes 1572872 | tf_op jit(solution)/shard_map/ppermute | solution.py:163
  77.9 26.7 %collective-permute-start.5 = (bf16[512,1024]{1,0:T(8,128)(2,1)S(1)}, bf16[512,1024]{1,0:T(8,128)(2,1)S(1)}, u32[]{:S(2)}, u32[]{:S(2)}) collective-permute-start(bf16[512,1024]{1,0:T(8,128)(2,1)S(1)} %collective-permute-done.refs_1_), channel_id=1, source_target_pairs={{0,8},{8,0},{16,24},{24,16},{1,9},{9,1},{17,25},{25,17},{2,10},{10... | collective-permute-start | bytes 3145736 | tf_op jit(solution)/shard_map/ppermute | solution.py:157
  80.3 25.6 %collective-permute-start.6 = (bf16[512,1024]{1,0:T(8,128)(2,1)S(1)}, bf16[512,1024]{1,0:T(8,128)(2,1)S(1)}, u32[]{:S(2)}, u32[]{:S(2)}) collective-permute-start(bf16[512,1024]{1,0:T(8,128)(2,1)S(1)} %collective-permute-done.1.refs_2_), channel_id=1, source_target_pairs={{0,8},{8,0},{16,24},{24,16},{1,9},{9,1},{17,25},{25,17},{2,10},{10... | collective-permute-start | bytes 3145736 | tf_op jit(solution)/shard_map/ppermute | solution.py:157
  91.4 10.9 %collective-permute-start.14 = (bf16[256,1024]{1,0:T(8,128)(2,1)S(1)}, bf16[256,1024]{1,0:T(8,128)(2,1)}, u32[]{:S(2)}, u32[]{:S(2)}) collective-permute-start(bf16[256,1024]{1,0:T(8,128)(2,1)S(1)} %slice.43), channel_id=1, source_target_pairs={{0,16},{8,24},{16,0},{24,8},{1,17},{9,25},{17,1},{25,9},{2,18},{10... | collective-permute-start | bytes 1572872 | tf_op jit(solution)/shard_map/ppermute | solution.py:160
  93.1 9.3 %collective-permute-start.7 = (bf16[256,1024]{1,0:T(8,128)(2,1)S(1)}, bf16[256,1024]{1,0:T(8,128)(2,1)S(1)}, u32[]{:S(2)}, u32[]{:S(2)}) collective-permute-start(bf16[256,1024]{1,0:T(8,128)(2,1)S(1)} %collective-permute-done.2.refs_3_), channel_id=1, source_target_pairs={{0,8},{8,0},{16,24},{24,16},{1,9},{9,1},{17,25},{25,17},{2,10},{10... | collective-permute-start | bytes 1572872 | tf_op jit(solution)/shard_map/ppermute | solution.py:157
  101.1 2.5 collective-permute-start.8
  102.3 27.4 %collective-permute-start.15 = (bf16[512,1024]{1,0:T(8,128)(2,1)}, bf16[512,1024]{1,0:T(8,128)(2,1)}, u32[]{:S(2)}, u32[]{:S(2)}) collective-permute-start(bf16[512,1024]{1,0:T(8,128)(2,1)} %bitcast.5.refs_0_), channel_id=1, source_target_pairs={{0,8},{8,0},{16,24},{24,16},{1,9},{9,1},{17,25},{25,17},{2,10},{10... | collective-permute-start | bytes 3145736 | tf_op jit(solution)/shard_map/ppermute | solution.py:157
  103.3 26.4 %collective-permute-start.16 = (bf16[512,1024]{1,0:T(8,128)(2,1)}, bf16[512,1024]{1,0:T(8,128)(2,1)}, u32[]{:S(2)}, u32[]{:S(2)}) collective-permute-start(bf16[512,1024]{1,0:T(8,128)(2,1)} %collective-permute-done.11.refs_1_), channel_id=1, source_target_pairs={{0,8},{8,0},{16,24},{24,16},{1,9},{9,1},{17,25},{25,17},{2,10},{10... | collective-permute-start | bytes 3145736 | tf_op jit(solution)/shard_map/ppermute | solution.py:157
  104.4 25.3 %collective-permute-start.17 = (bf16[512,1024]{1,0:T(8,128)(2,1)}, bf16[512,1024]{1,0:T(8,128)(2,1)}, u32[]{:S(2)}, u32[]{:S(2)}) collective-permute-start(bf16[512,1024]{1,0:T(8,128)(2,1)} %collective-permute-done.12.refs_2_), channel_id=1, source_target_pairs={{0,8},{8,0},{16,24},{24,16},{1,9},{9,1},{17,25},{25,17},{2,10},{10... | collective-permute-start | bytes 3145736 | tf_op jit(solution)/shard_map/ppermute | solution.py:157
  105.5 24.1 %collective-permute-start.18 = (bf16[256,1024]{1,0:T(8,128)(2,1)}, bf16[256,1024]{1,0:T(8,128)(2,1)}, u32[]{:S(2)}, u32[]{:S(2)}) collective-permute-start(bf16[256,1024]{1,0:T(8,128)(2,1)} %collective-permute-done.13.refs_3_), channel_id=1, source_target_pairs={{0,8},{8,0},{16,24},{24,16},{1,9},{9,1},{17,25},{25,17},{2,10},{10... | collective-permute-start | bytes 1572872 | tf_op jit(solution)/shard_map/ppermute | solution.py:157
  106.9 22.8 %collective-permute-start.19 = (bf16[256,1024]{1,0:T(8,128)(2,1)}, bf16[256,1024]{1,0:T(8,128)(2,1)}, u32[]{:S(2)}, u32[]{:S(2)}) collective-permute-start(bf16[256,1024]{1,0:T(8,128)(2,1)} %collective-permute-done.14.refs_4_), channel_id=1, source_target_pairs={{0,8},{8,0},{16,24},{24,16},{1,9},{9,1},{17,25},{25,17},{2,10},{10... | collective-permute-start | bytes 1572872 | tf_op jit(solution)/shard_map/ppermute | solution.py:157
  141.0 124.9 %reduce-scatter.6.cloned.1.call-start = ((), (), s32[]{:S(2)}) async-start(), calls=%async_computation.7 | async-start | bytes 2621440 | tf_op jit(solution)/shard_map/reduce_scatter | solution.py:233
  156.6 18.4 %collective-permute-start.23 = (bf16[512,1024]{1,0:T(8,128)(2,1)S(1)}, bf16[512,1024]{1,0:T(8,128)(2,1)S(1)}, u32[]{:S(2)}, u32[]{:S(2)}) collective-permute-start(bf16[512,1024]{1,0:T(8,128)(2,1)S(1)} %shard_map.94.refs_3_.refs_13_), channel_id=1, source_target_pairs={{0,8},{8,0},{16,24},{24,16},{1,9},{9,1},{17,25},{25,17},{2,10},{10... | collective-permute-start | bytes 3145736 | tf_op jit(solution)/shard_map/ppermute | solution.py:157
  160.5 20.9 %collective-permute-start.20 = (bf16[512,1024]{1,0:T(8,128)(2,1)}, bf16[512,1024]{1,0:T(8,128)(2,1)}, u32[]{:S(2)}, u32[]{:S(2)}) collective-permute-start(bf16[512,1024]{1,0:T(8,128)(2,1)} %get-tuple-element.27.refs_14_), channel_id=1, source_target_pairs={{0,8},{8,0},{16,24},{24,16},{1,9},{9,1},{17,25},{25,17},{2,10},{10... | collective-permute-start | bytes 3145736 | tf_op jit(solution)/shard_map/ppermute | solution.py:157
  160.6 20.8 %collective-permute-start.21 = (bf16[512,1024]{1,0:T(8,128)(2,1)}, bf16[512,1024]{1,0:T(8,128)(2,1)}, u32[]{:S(2)}, u32[]{:S(2)}) collective-permute-start(bf16[512,1024]{1,0:T(8,128)(2,1)} %get-tuple-element.28.refs_15_), channel_id=1, source_target_pairs={{0,8},{8,0},{16,24},{24,16},{1,9},{9,1},{17,25},{25,17},{2,10},{10... | collective-permute-start | bytes 3145736 | tf_op jit(solution)/shard_map/ppermute | solution.py:157
  161.1 20.3 %collective-permute-start.22 = (bf16[512,1024]{1,0:T(8,128)(2,1)}, bf16[512,1024]{1,0:T(8,128)(2,1)}, u32[]{:S(2)}, u32[]{:S(2)}) collective-permute-start(bf16[512,1024]{1,0:T(8,128)(2,1)} %get-tuple-element.29.refs_16_), channel_id=1, source_target_pairs={{0,8},{8,0},{16,24},{24,16},{1,9},{9,1},{17,25},{25,17},{2,10},{10... | collective-permute-start | bytes 3145736 | tf_op jit(solution)/shard_map/ppermute | solution.py:157
  178.3 14.4 %collective-permute-start.24 = (bf16[256,1024]{1,0:T(8,128)(2,1)S(1)}, bf16[256,1024]{1,0:T(8,128)(2,1)S(1)}, u32[]{:S(2)}, u32[]{:S(2)}) collective-permute-start(bf16[256,1024]{1,0:T(8,128)(2,1)S(1)} %get-tuple-element.47), channel_id=1, source_target_pairs={{0,1},{1,0},{2,3},{3,2},{4,5},{5,4},{6,7},{7,6},{8,9},{9,8},{10,11... | collective-permute-start | bytes 1572872 | tf_op jit(solution)/shard_map/ppermute | solution.py:163
  179.9 14.1 %collective-permute-start.26 = (bf16[256,1024]{1,0:T(8,128)(2,1)S(1)}, bf16[256,1024]{1,0:T(8,128)(2,1)S(1)}, u32[]{:S(2)}, u32[]{:S(2)}) collective-permute-start(bf16[256,1024]{1,0:T(8,128)(2,1)S(1)} %get-tuple-element.48), channel_id=1, source_target_pairs={{0,16},{8,24},{16,0},{24,8},{1,17},{9,25},{17,1},{25,9},{2,18},{10... | collective-permute-start | bytes 1572872 | tf_op jit(solution)/shard_map/ppermute | solution.py:160
  208.7 104.4 %reduce-scatter.8.cloned.1.call-start = ((), (), s32[]{:S(2)}) async-start(), calls=%async_computation.8 | async-start | bytes 2621440 | tf_op jit(solution)/shard_map/reduce_scatter | solution.py:233
  215.7 8.1 %collective-permute-start.31 = (bf16[512,1024]{1,0:T(8,128)(2,1)S(1)}, bf16[512,1024]{1,0:T(8,128)(2,1)S(1)}, u32[]{:S(2)}, u32[]{:S(2)}) collective-permute-start(bf16[512,1024]{1,0:T(8,128)(2,1)S(1)} %shard_map.100.refs_3_), channel_id=1, source_target_pairs={{0,8},{8,0},{16,24},{24,16},{1,9},{9,1},{17,25},{25,17},{2,10},{10... | collective-permute-start | bytes 3145736 | tf_op jit(solution)/shard_map/ppermute | solution.py:157
  220.9 4.9 %collective-permute-start.28 = (bf16[512,1024]{1,0:T(8,128)(2,1)S(1)}, bf16[512,1024]{1,0:T(8,128)(2,1)S(1)}, u32[]{:S(2)}, u32[]{:S(2)}) collective-permute-start(bf16[512,1024]{1,0:T(8,128)(2,1)S(1)} %get-tuple-element.37), channel_id=1, source_target_pairs={{0,8},{8,0},{16,24},{24,16},{1,9},{9,1},{17,25},{25,17},{2,10},{10... | collective-permute-start | bytes 3145736 | tf_op jit(solution)/shard_map/ppermute | solution.py:157
  221.0 6.5 %collective-permute-start.29 = (bf16[512,1024]{1,0:T(8,128)(2,1)S(1)}, bf16[512,1024]{1,0:T(8,128)(2,1)S(1)}, u32[]{:S(2)}, u32[]{:S(2)}) collective-permute-start(bf16[512,1024]{1,0:T(8,128)(2,1)S(1)} %get-tuple-element.38), channel_id=1, source_target_pairs={{0,8},{8,0},{16,24},{24,16},{1,9},{9,1},{17,25},{25,17},{2,10},{10... | collective-permute-start | bytes 3145736 | tf_op jit(solution)/shard_map/ppermute | solution.py:157
  221.5 6.6 %collective-permute-start.30 = (bf16[512,1024]{1,0:T(8,128)(2,1)S(1)}, bf16[512,1024]{1,0:T(8,128)(2,1)S(1)}, u32[]{:S(2)}, u32[]{:S(2)}) collective-permute-start(bf16[512,1024]{1,0:T(8,128)(2,1)S(1)} %get-tuple-element.39), channel_id=1, source_target_pairs={{0,8},{8,0},{16,24},{24,16},{1,9},{9,1},{17,25},{25,17},{2,10},{10... | collective-permute-start | bytes 3145736 | tf_op jit(solution)/shard_map/ppermute | solution.py:157
  221.9 26.0 %collective-permute-start.25 = (bf16[512,1024]{1,0:T(8,128)(2,1)S(1)}, bf16[512,1024]{1,0:T(8,128)(2,1)S(1)}, u32[]{:S(2)}, u32[]{:S(2)}) collective-permute-start(bf16[512,1024]{1,0:T(8,128)(2,1)S(1)} %add_convert_fusion.4), channel_id=1, source_target_pairs={{0,16},{8,24},{16,0},{24,8},{1,17},{9,25},{17,1},{25,9},{2,18},{10... | collective-permute-start | bytes 3145736 | tf_op jit(solution)/shard_map/ppermute | solution.py:160
  223.8 26.1 %collective-permute-start.27 = (bf16[512,1024]{1,0:T(8,128)(2,1)S(1)}, bf16[512,1024]{1,0:T(8,128)(2,1)S(1)}, u32[]{:S(2)}, u32[]{:S(2)}) collective-permute-start(bf16[512,1024]{1,0:T(8,128)(2,1)S(1)} %add_convert_fusion.3), channel_id=1, source_target_pairs={{0,1},{1,0},{2,3},{3,2},{4,5},{5,4},{6,7},{7,6},{8,9},{9,8},{10,11... | collective-permute-start | bytes 3145736 | tf_op jit(solution)/shard_map/ppermute | solution.py:163
  225.9 35.3 %collective-permute-start.32 = (bf16[256,1024]{1,0:T(8,128)(2,1)S(1)}, bf16[256,1024]{1,0:T(8,128)(2,1)S(1)}, u32[]{:S(2)}, u32[]{:S(2)}) collective-permute-start(bf16[256,1024]{1,0:T(8,128)(2,1)S(1)} %get-tuple-element.46), channel_id=1, source_target_pairs={{0,1},{1,0},{2,3},{3,2},{4,5},{5,4},{6,7},{7,6},{8,9},{9,8},{10,11... | collective-permute-start | bytes 1572872 | tf_op jit(solution)/shard_map/ppermute | solution.py:163
  227.6 23.3 %copy-start.18 = (bf16[2,256,1024]{2,1,0:T(8,128)(2,1)S(1)}, bf16[2,256,1024]{2,1,0:T(8,128)(2,1)}, u32[]{:S(2)}) copy-start(bf16[2,256,1024]{2,1,0:T(8,128)(2,1)} %param.5) | copy-start | bytes 3145732
  227.6 34.3 %collective-permute-start.34 = (bf16[256,1024]{1,0:T(8,128)(2,1)S(1)}, bf16[256,1024]{1,0:T(8,128)(2,1)S(1)}, u32[]{:S(2)}, u32[]{:S(2)}) collective-permute-start(bf16[256,1024]{1,0:T(8,128)(2,1)S(1)} %get-tuple-element.45), channel_id=1, source_target_pairs={{0,16},{8,24},{16,0},{24,8},{1,17},{9,25},{17,1},{25,9},{2,18},{10... | collective-permute-start | bytes 1572872 | tf_op jit(solution)/shard_map/ppermute | solution.py:160
  233.0 26.8 %copy-start.27 = (bf16[512,1024]{1,0:T(8,128)(2,1)}, bf16[512,1024]{1,0:T(8,128)(2,1)S(1)}, u32[]{:S(2)}) copy-start(bf16[512,1024]{1,0:T(8,128)(2,1)S(1)} %get-tuple-element.40.refs_0_.refs_11_) | copy-start | bytes 3145732
  233.1 26.8 %copy-start.65 = (bf16[512,1024]{1,0:T(8,128)(2,1)}, bf16[512,1024]{1,0:T(8,128)(2,1)S(1)}, u32[]{:S(2)}) copy-start(bf16[512,1024]{1,0:T(8,128)(2,1)S(1)} %get-tuple-element.41) | copy-start | bytes 3145732
  234.0 32.0 %collective-permute-start.37 = (bf16[128,1024]{1,0:T(8,128)(2,1)S(1)}, bf16[128,1024]{1,0:T(8,128)(2,1)S(1)}, u32[]{:S(2)}, u32[]{:S(2)}) collective-permute-start(bf16[128,1024]{1,0:T(8,128)(2,1)S(1)} %get-tuple-element.50), channel_id=1, source_target_pairs={{0,1},{1,0},{2,3},{3,2},{4,5},{5,4},{6,7},{7,6},{8,9},{9,8},{10,11... | collective-permute-start | bytes 786440 | tf_op jit(solution)/shard_map/ppermute | solution.py:163
  274.7 24.7 %collective-permute-start.33 = (bf16[512,1024]{1,0:T(8,128)(2,1)}, bf16[512,1024]{1,0:T(8,128)(2,1)}, u32[]{:S(2)}, u32[]{:S(2)}) collective-permute-start(bf16[512,1024]{1,0:T(8,128)(2,1)} %add_convert_fusion.1), channel_id=1, source_target_pairs={{0,16},{8,24},{16,0},{24,8},{1,17},{9,25},{17,1},{25,9},{2,18},{10... | collective-permute-start | bytes 3145736 | tf_op jit(solution)/shard_map/ppermute | solution.py:160
  276.3 26.3 %collective-permute-start.35 = (bf16[512,1024]{1,0:T(8,128)(2,1)}, bf16[512,1024]{1,0:T(8,128)(2,1)S(1)}, u32[]{:S(2)}, u32[]{:S(2)}) collective-permute-start(bf16[512,1024]{1,0:T(8,128)(2,1)} %add_convert_fusion), channel_id=1, source_target_pairs={{0,1},{1,0},{2,3},{3,2},{4,5},{5,4},{6,7},{7,6},{8,9},{9,8},{10,11... | collective-permute-start | bytes 3145736 | tf_op jit(solution)/shard_map/ppermute | solution.py:163
  276.8 35.1 %collective-permute-start.36 = (bf16[256,1024]{1,0:T(8,128)(2,1)}, bf16[256,1024]{1,0:T(8,128)(2,1)S(1)}, u32[]{:S(2)}, u32[]{:S(2)}) collective-permute-start(bf16[256,1024]{1,0:T(8,128)(2,1)} %reduce-scatter.6.cloned.1.call-done.refs_1_), channel_id=1, source_target_pairs={{0,1},{1,0},{2,3},{3,2},{4,5},{5,4},{6,7},{7,6},{8,9},{9,8},{10,11... | collective-permute-start | bytes 1572872 | tf_op jit(solution)/shard_map/ppermute | solution.py:163
  (70 other events, 465.2 us)
Sparse Core Ops, SparseCore 0:
  10.1 48.6 all-gather.3
  61.0 44.6 all-gather.5
  107.8 44.6 all-gather.7
  154.6 42.5 reduce-scatter.3
  208.8 41.7 reduce-scatter.5
  271.2 41.0 reduce-scatter.7

commit v8 on v7

--- a/solution.py
+++ b/solution.py
@@ -55,24 +55,45 @@
 class Rows:
     def __init__(self, pieces, blocks, step):
         self.pieces, self.blocks, self.step = pieces, blocks, step
-
-    def read(self, refs, at, side):
-        piece, first = self.blocks[at][side]
-        return refs[piece].at[first : first + self.step]
+        self.count, self.half = len(blocks) * step, pieces[0].shape[1]
+
+    def copies(self, refs, sides, scratch, sems):
+        found = []
+        for at, pair in enumerate(self.blocks):
+            found.append([])
+            for place, side in enumerate(sides):
+                piece, first = pair[side]
+                into = scratch.at[pl.ds(at * self.step, self.step), pl.ds(place * self.half, self.half)]
+                source = refs[piece].at[pl.ds(first, self.step)]
+                found[-1].append(pltpu.make_async_copy(source, into, sems.at[at * len(sides) + place]))
+        return found
 
 
 def hidden_kernel(rows, width, *refs):
     count = len(rows.pieces)
-    pieces, (own_ref, other_ref, hidden_ref, turned_ref, silu_ref, rest_ref) = refs[:count], refs[count:]
-    groups = own_ref.shape[0] // (2 * width)
-    for at in range(len(rows.blocks)):
-        span = slice(at * rows.step, (at + 1) * rows.step)
-        sums = matmul(rows.read(pieces, at, 0)[...], own_ref[...], (1, 1))
-        sums = sums + matmul(rows.read(pieces, at, 1)[...], other_ref[...], (1, 1))
-        for group in range(groups):
-            low = 2 * group * width
-            silu_g, hidden, rest = gated(sums[:, low : low + width], sums[:, low + width : low + 2 * width])
-            cols = slice(group * width, (group + 1) * width)
+    pieces = refs[:count]
+    own_ref, other_ref, hidden_ref, turned_ref, silu_ref, rest_ref, in_ref, unit_ref, sems, unit_sems = refs[count:]
+    half = rows.half
+    loads = [
+        pltpu.make_async_copy(own_ref, unit_ref.at[:, pl.ds(0, half)], unit_sems.at[0]),
+        pltpu.make_async_copy(other_ref, unit_ref.at[:, pl.ds(half, half)], unit_sems.at[1]),
+    ]
+    copies = rows.copies(pieces, (0, 1), in_ref, sems)
+    for copy in loads + [copy for block in copies for copy in block]:
+        copy.start()
+    for copy in loads:
+        copy.wait()
+    for pair in range(len(copies) // 2):
+        for copy in copies[2 * pair] + copies[2 * pair + 1]:
+            copy.wait()
+        span = slice(2 * pair * rows.step, 2 * (pair + 1) * rows.step)
+
+        @pl.loop(0, unit_ref.shape[0] // (2 * width))
+        def _(group):
+            units = pl.ds(pl.multiple_of(group * 2 * width, 2 * width), 2 * width)
+            sums = matmul(in_ref[span], unit_ref[units], (1, 1))
+            silu_g, hidden, rest = gated(sums[:, :width], sums[:, width:])
+            cols = pl.ds(pl.multiple_of(group * width, width), width)
             hidden_ref[span, cols] = hidden.astype(BF16)
             turned_ref[cols, span] = hidden.T.astype(BF16)
             silu_ref[span, cols] = silu_g.astype(BF16)
@@ -81,36 +102,42 @@
 
 def grads_kernel(rows, width, *refs):
     count = len(rows.pieces)
-    pieces, (down_ref, silu_ref, rest_ref, act_ref, turned_ref) = refs[:count], refs[count:]
-    groups = down_ref.shape[0] // width
-    half = down_ref.shape[1] // 2
-    for at in range(len(rows.blocks)):
-        span = slice(at * rows.step, (at + 1) * rows.step)
-        back = matmul(rows.read(pieces, at, 0)[...], down_ref[:, :half], (1, 1))
-        back = back + matmul(rows.read(pieces, at, 1)[...], down_ref[:, half:], (1, 1))
-        for group in range(groups):
-            cols = slice(group * width, (group + 1) * width)
+    pieces = refs[:count]
+    down_ref, silu_ref, rest_ref, act_ref, turned_ref, cot_ref, sems = refs[count:]
+    copies = rows.copies(pieces, (0, 1), cot_ref, sems)
+    for copy in [copy for block in copies for copy in block]:
+        copy.start()
+    for pair in range(len(copies) // 2):
+        for copy in copies[2 * pair] + copies[2 * pair + 1]:
+            copy.wait()
+        span = slice(2 * pair * rows.step, 2 * (pair + 1) * rows.step)
+
+        @pl.loop(0, down_ref.shape[0] // (2 * width))
+        def _(group):
+            units = pl.ds(pl.multiple_of(group * 2 * width, 2 * width), 2 * width)
+            back = matmul(cot_ref[span], down_ref[units], (1, 1))
             for part, factor in enumerate((rest_ref, silu_ref)):
-                grad = back[:, cols] * factor[span, cols].astype(F32)
-                low = (2 * group + part) * width
-                act_ref[span, low : low + width] = grad.astype(BF16)
-                turned_ref[low : low + width, span] = grad.T.astype(BF16)
+                grads = back * factor[span, units].astype(F32)
+                for side in range(2):
+                    grad = grads[:, side * width : (side + 1) * width]
+                    low = pl.ds(pl.multiple_of((4 * group + 2 * side + part) * width, width), width)
+                    act_ref[span, low] = grad.astype(BF16)
+                    turned_ref[low, span] = grad.T.astype(BF16)
 
 
 def weight_kernel(rows, sides, tile, *refs):
     count = len(rows.pieces)
-    pieces, (turned_ref, out_ref) = refs[:count], refs[count:]
-    half = out_ref.shape[1] // len(sides)
-    for place, side in enumerate(sides):
-
-        @pl.loop(0, half // tile)
-        def _(index):
-            cols = pl.ds(pl.multiple_of(index * tile, tile), tile)
-            total = jnp.zeros((out_ref.shape[0], tile), F32)
-            for at in range(len(rows.blocks)):
-                span = slice(at * rows.step, (at + 1) * rows.step)
-                total = total + matmul(turned_ref[:, span], rows.read(pieces, at, side)[:, cols], (1, 0))
-            out_ref[:, pl.ds(pl.multiple_of(place * half + index * tile, tile), tile)] = total.astype(BF16)
+    pieces, (turned_ref, out_ref, rows_ref, sems) = refs[:count], refs[count:]
+    copies = [copy for block in rows.copies(pieces, sides, rows_ref, sems) for copy in block]
+    for copy in copies:
+        copy.start()
+    for copy in copies:
+        copy.wait()
+
+    @pl.loop(0, out_ref.shape[1] // tile)
+    def _(index):
+        cols = pl.ds(pl.multiple_of(index * tile, tile), tile)
+        out_ref[:, cols] = matmul(turned_ref[...], rows_ref[:, cols], (1, 0)).astype(BF16)
 
 
 def block_kernel(first, places, sides, added, *refs):
@@ -204,7 +231,7 @@
             2 * len(places) * quarter * depth * half,
             args,
             after,
-            specs=[ANY] * (1 + len(use)) + [VMEM] * (len(args) - 1 - len(use)),
+            specs=[HBM] * (1 + len(use)) + [VMEM] * (len(args) - 1 - len(use)),
             scratch=[
                 pltpu.VMEM((len(chips) * quarter, depth), BF16),
                 pltpu.VMEM((len(use), depth, half), BF16),
@@ -244,20 +271,31 @@
         step = rows_in.step
         count = len(rows_in.blocks) * step
         units = down.shape[0]
+        loads = len(rows_in.blocks)
+        both = pltpu.VMEM((count, 2 * half), BF16)
 
         hidden, hidden_turned, silu, rest = call(
             functools.partial(hidden_kernel, rows_in, width),
             [shape(count, units), shape(units, count), shape(count, units), shape(count, units)],
             8 * count * units * half,
             [*rows_in.pieces, own_units, other_units],
-            limit=44,
+            specs=[HBM] * (len(rows_in.pieces) + 2),
+            scratch=[
+                both,
+                pltpu.VMEM((2 * units, 2 * half), BF16),
+                pltpu.SemaphoreType.DMA((2 * loads,)),
+                pltpu.SemaphoreType.DMA((2,)),
+            ],
+            limit=32,
         )
         (down_term,) = call(
             functools.partial(weight_kernel, rows_cot, (0, 1), 256),
             [shape(units, 2 * half)],
             4 * count * units * half,
             [*rows_cot.pieces, hidden_turned],
-            limit=44,
+            specs=[HBM] * len(rows_cot.pieces) + [VMEM],
+            scratch=[both, pltpu.SemaphoreType.DMA((2 * loads,))],
+            limit=20,
         )
         down_sum = scatter_units(down_term)
         down_sides = [(down, 0, half), (down, 1, half)]
@@ -269,7 +307,9 @@
             4 * count * units * half,
             [*rows_cot.pieces, down, silu, rest],
             after=list(output_far.values()),
-            limit=44,
+            specs=[HBM] * len(rows_cot.pieces) + [VMEM] * 3,
+            scratch=[both, pltpu.SemaphoreType.DMA((2 * loads,))],
+            limit=32,
         )
 
         def unit_term(side, after):
@@ -279,7 +319,9 @@
                 4 * count * units * half,
                 [*rows_in.pieces, act_turned],
                 after,
-                limit=44,
+                specs=[HBM] * len(rows_in.pieces) + [VMEM],
+                scratch=[pltpu.VMEM((count, half), BF16), pltpu.SemaphoreType.DMA((loads,))],
+                limit=20,
             )[0]
 
         output_far = {place: self.core(block) for place, block in output_far.items()}
@@ -302,13 +344,13 @@
         grads_far = self.far_first(act, unit_sides, [other_term])
         grads_far |= self.far_rest(act, unit_sides, [grads_far[1, 1]])
         grads_far = {place: self.core(block) for place, block in grads_far.items()}
-        grads = self.near_first(act, unit_sides, grads_far, [])
+        grads = self.near_first(act, unit_sides, grads_far, [output_chip, output_other])
         corner = grads[1, 1]
         by_other, by_chip = self.other(corner[:step]), self.chip(corner[step:])
-        grads |= self.near_rest(act, unit_sides, grads_far, [corner])
-        own_term = unit_term(0, [grads[0, 0], output_chip, output_other])
+        own_term = unit_term(0, [corner])
+        grads |= self.near_rest(act, unit_sides, grads_far, [own_term])
         down_back = self.other(down_sum[:, half:])
-        waits = [other_sum, by_other, by_chip, down_back]
+        waits = [other_sum, by_other, by_chip, down_back, grads[0, 0]]
         (term,) = call(copy_kernel, [shape(*own_term.shape)], 0, [own_term], waits)
         own_sum = scatter_units(term)
         grads_chip, grads_other = with_corner(grads, by_chip, by_other)

time: 325 us -> 320 us (0.985)
  Pallas kernels: 85.2 us -> 74.9 us
  local copies, waits for them, and re-layouts: 48.4 us -> 57.6 us
    pallas_call x18, Pallas kernels: 85.2 us -> 74.9 us  [call(): pl.pallas_call(body, out_shape=list(outs), in_specs=[*specs, *[pl.BlockSp...]
    unnamed x152 -> x168, local copies, waits for them, and re-layouts: 44.7 us -> 53.9 us
    all_gather x3, waiting for transfers between devices: 11.2 us -> 3.81 us  [gather_units(): return lax.all_gather(array, 'wt', axis=0, tiled=True)]
    ppermute x8, waiting for transfers between devices: 65.7 us -> 71.6 us  [chip(): return lax.ppermute(array, 'inp', [(at, at ^ 2) for at in range(4)])]
  transfers between devices with their start and end apart: 44 -> 44, of which waited for: 19 -> 18; matrix products, arithmetic and copies ran while one was open for 4% -> 4% of each run, Pallas kernels for 25% -> 22%
where the time goes in v8:
time: 320 us; the launch traced here: 318 us
  waiting for transfers between devices  135 us (42%)
  Pallas kernels  74.9 us (23%)
  local copies, waits for them, and re-layouts  57.6 us (18%)
  starting transfers between devices  25.1 us (8%)
  between operations  14.8 us (5%)
  other arithmetic  11.1 us (3%)
    pallas_call x18, Pallas kernels, call(): pl.pallas_call(body, out_shape=list(outs), in_specs=[*specs, *[pl.BlockSp...  74.9 us
    ppermute x8, waiting for transfers between devices, chip(): return lax.ppermute(array, 'inp', [(at, at ^ 2) for at in range(4)])  71.6 us
    ppermute x12, waiting for transfers between devices, other(): return lax.ppermute(array, 'out', [(0, 1), (1, 0)])  59.4 us
    unnamed x168, local copies, waits for them, and re-layouts  53.9 us
    ppermute x12, starting transfers between devices, other(): return lax.ppermute(array, 'out', [(0, 1), (1, 0)])  12.5 us
    ppermute x8, starting transfers between devices, chip(): return lax.ppermute(array, 'inp', [(at, at ^ 2) for at in range(4)])  9.36 us
  transfers between devices with their start and end apart: 44, of which 18 were waited for; matrix products, arithmetic and copies ran while one was open for 4% of the time, Pallas kernels for 22%

profile of v8, /device:TPU:0, one launch (start us, length us, event | category | flops | bytes accessed | tf_op | source)
XLA Modules:
  0.0 318.4 jit_solution(6598162137548979951)
XLA Ops:
  10.1 3.0 collective-permute-start.9
  13.1 11.9 %collective-permute-done.9 = bf16[256,1024]{1,0:T(8,128)(2,1)S(1)} collective-permute-done((bf16[256,1024]{1,0:T(8,128)(2,1)S(1)}, bf16[256,1024]{1,0:T(8,128)(2,1)S(1)}, u32[]{:S(2)}, u32[]{:S(2)}) %collective-permute-start.9) | collective-permute-done | bytes 524320 | tf_op jit(solution)/shard_map/ppermute | solution.py:190
  25.9 1.8 collective-permute-start.10
  27.7 1.5 collective-permute-start.1
  30.1 5.2 %collective-permute-done.10 = bf16[128,1024]{1,0:T(8,128)(2,1)S(1)} collective-permute-done((bf16[128,1024]{1,0:T(8,128)(2,1)S(1)}, bf16[128,1024]{1,0:T(8,128)(2,1)S(1)}, u32[]{:S(2)}, u32[]{:S(2)}) %collective-permute-start.10) | collective-permute-done | bytes 262176 | tf_op jit(solution)/shard_map/ppermute | solution.py:190
  35.2 1.7 collective-permute-start.11
  37.9 15.9 %collective-permute-done.1.refs_2_ = bf16[512,1024]{1,0:T(8,128)(2,1)S(1)} collective-permute-done((bf16[512,1024]{1,0:T(8,128)(2,1)S(1)}, bf16[512,1024]{1,0:T(8,128)(2,1)S(1)}, u32[]{:S(2)}, u32[]{:S(2)}) %collective-permute-start.1) | collective-permute-done | bytes 1048608 | tf_op jit(solution)/shard_map/ppermute | solution.py:187
  54.2 3.5 %collective-permute-done.refs_1_ = bf16[512,1024]{1,0:T(8,128)(2,1)S(1)} collective-permute-done((bf16[512,1024]{1,0:T(8,128)(2,1)S(1)}, bf16[512,1024]{1,0:T(8,128)(2,1)S(1)}, u32[]{:S(2)}, u32[]{:S(2)}) %collective-permute-start) | collective-permute-done | bytes 1048608 | tf_op jit(solution)/shard_map/ppermute | solution.py:190
  57.8 1.8 collective-permute-start.3
  59.5 16.9 %collective-permute-done.12.refs_2_ = bf16[512,1024]{1,0:T(8,128)(2,1)} collective-permute-done((bf16[512,1024]{1,0:T(8,128)(2,1)}, bf16[512,1024]{1,0:T(8,128)(2,1)}, u32[]{:S(2)}, u32[]{:S(2)}) %collective-permute-start.12) | collective-permute-done | bytes 1048608 | tf_op jit(solution)/shard_map/ppermute | solution.py:187
  77.9 2.4 collective-permute-done.11.refs_1_
  81.4 10.0 %collective-permute-done.2.refs_3_ = bf16[256,1024]{1,0:T(8,128)(2,1)S(1)} collective-permute-done((bf16[256,1024]{1,0:T(8,128)(2,1)S(1)}, bf16[256,1024]{1,0:T(8,128)(2,1)S(1)}, u32[]{:S(2)}, u32[]{:S(2)}) %collective-permute-start.2) | collective-permute-done | bytes 524320 | tf_op jit(solution)/shard_map/ppermute | solution.py:190
  91.4 1.7 collective-permute-start.14
  93.9 7.2 %collective-permute-done.13.refs_3_ = bf16[256,1024]{1,0:T(8,128)(2,1)} collective-permute-done((bf16[256,1024]{1,0:T(8,128)(2,1)S(1)}, bf16[256,1024]{1,0:T(8,128)(2,1)}, u32[]{:S(2)}, u32[]{:S(2)}) %collective-permute-start.13) | collective-permute-done | bytes 524320 | tf_op jit(solution)/shard_map/ppermute | solution.py:190
  107.0 1.6 copy-done.5
  109.9 1.6 copy-done.41
  119.5 14.8 %shard_map.92 = (bf16[2048,512]{1,0:T(8,128)(2,1)S(1)}, bf16[512,2048]{1,0:T(8,128)(2,1)S(1)}, bf16[2048,512]{1,0:T(8,128)(2,1)S(1)}, bf16[2048,512]{1,0:T(8,128)(2,1)S(1)}) custom-call(bf16[512,1024]{1,0:T(8,128)(2,1)S(1)} %bitcast.13, bf16[512,1024]{1,0:T(8,128)(2,1)S(1)} %copy-done.23, bf16[512,1024]{1,0:T(8,128)(2,1)S(1)} %collective-permute-done.1.refs_2_, ...), custom_call_target="tpu_custom_call" | custom-call | flops 8589934592 | bytes 20971520 | tf_op jit(solution)/shard_map/pallas_call | solution.py:38
  137.1 9.5 %shard_map.93.refs_2_ = bf16[512,2048]{1,0:T(8,128)(2,1)S(1)} custom-call(bf16[512,1024]{1,0:T(8,128)(2,1)} %bitcast.5.refs_0_, bf16[512,1024]{1,0:T(8,128)(2,1)} %collective-permute-done.11.refs_1_, bf16[512,1024]{1,0:T(8,128)(2,1)} %collective-permute-done.12.refs_2_, bf16[256,1024]{1,0:T(8,128)(2,1)} %collective-permute-done.13.refs_3_, ...), custom_call_target="tpu_custom_call" | custom-call | flops 4294967296 | bytes 12582912 | tf_op jit(solution)/shard_map/pallas_call | solution.py:38
  148.1 3.8 %all-gather.8.cloned.1.call-done.refs_1_.refs_2_.refs_10_ = bf16[512,2048]{1,0:T(8,128)(2,1)} async-done(((bf16[128,2048]{1,0:T(8,128)(2,1)}), bf16[512,2048]{1,0:T(8,128)(2,1)}) %all-gather.8.cloned.1.call-update) | async-done | bytes 2097168 | tf_op jit(solution)/shard_map/all_gather | solution.py:257
  151.9 1.6 copy-done
  153.5 1.6 copy-done.10
  156.7 2.3 shard_map.95
  159.6 13.3 %shard_map.96 = (bf16[2048,1024]{1,0:T(8,128)(2,1)}, bf16[1024,2048]{1,0:T(8,128)(2,1)}) custom-call(bf16[512,1024]{1,0:T(8,128)(2,1)} %bitcast.5.refs_0_, bf16[512,1024]{1,0:T(8,128)(2,1)} %collective-permute-done.11.refs_1_, bf16[512,1024]{1,0:T(8,128)(2,1)} %collective-permute-done.12.refs_2_, bf16[256,1024]{1,0:T(8,128)(2,1)} %collective-permute-done.13.refs_3_, ...), custom_call_target="tpu_custom_call" | custom-call | flops 4294967296 | bytes 23068672 | tf_op jit(solution)/shard_map/pallas_call | solution.py:38
  173.0 2.2 copy-done.2
  176.3 1.6 collective-permute-start.24
  177.9 1.5 collective-permute-start.26
  179.4 2.3 shard_map.98
  183.7 6.9 %collective-permute-done.24.refs_12_ = bf16[256,1024]{1,0:T(8,128)(2,1)S(1)} collective-permute-done((bf16[256,1024]{1,0:T(8,128)(2,1)S(1)}, bf16[256,1024]{1,0:T(8,128)(2,1)S(1)}, u32[]{:S(2)}, u32[]{:S(2)}) %collective-permute-start.24) | collective-permute-done | bytes 524320 | tf_op jit(solution)/shard_map/ppermute | solution.py:190
  191.9 5.5 %shard_map.99.refs_2_.refs_0_ = bf16[1024,1024]{1,0:T(8,128)(2,1)S(1)} custom-call(bf16[512,1024]{1,0:T(8,128)(2,1)S(1)} %bitcast.14, bf16[512,1024]{1,0:T(8,128)(2,1)S(1)} %copy-done.24, bf16[512,1024]{1,0:T(8,128)(2,1)S(1)} %collective-permute-done.1.refs_2_, bf16[256,1024]{1,0:T(8,128)(2,1)S(1)} %copy-done.64, bf16[256,1024]{1,0:T(8,128)(2,1)S(1)} %copy-done.68, ...), custom_call_target="tpu_custom_call" | custom-call | flops 4294967296 | bytes 14680064 | tf_op jit(solution)/shard_map/pallas_call | solution.py:38
  205.4 2.2 copy-done.3
  207.6 1.7 copy-done.8
  209.4 1.5 shard_map.100.refs_3_
  211.3 1.7 collective-permute-start.25
  213.6 3.9 %shard_map.101 = (bf16[512,1024]{1,0:T(8,128)(2,1)S(1)}, bf16[512,1024]{1,0:T(8,128)(2,1)S(1)}, bf16[512,1024]{1,0:T(8,128)(2,1)S(1)}) custom-call(bf16[2048,1024]{1,0:T(8,128)(2,1)S(1)} %copy-done.4, bf16[1024,1024]{1,0:T(8,128)(2,1)S(1)} %copy-done.42, bf16[1024,1024]{1,0:T(8,128)(2,1)S(1)} %copy-done.6, bf16[512,1024]{1,0:T(8,128)(2,1)S(1)} %shard_map.100.refs_3_), custom_call_target="tpu_custom_call" | custom-call | flops 3221225472 | bytes 11534336 | tf_op jit(solution)/shard_map/pallas_call | solution.py:38
  218.1 18.7 %collective-permute-done.25.refs_3_ = bf16[512,1024]{1,0:T(8,128)(2,1)S(1)} collective-permute-done((bf16[512,1024]{1,0:T(8,128)(2,1)S(1)}, bf16[512,1024]{1,0:T(8,128)(2,1)S(1)}, u32[]{:S(2)}, u32[]{:S(2)}) %collective-permute-start.25) | collective-permute-done | bytes 1048608 | tf_op jit(solution)/shard_map/ppermute | solution.py:187
  236.9 1.6 collective-permute-done.27.refs_4_
  238.6 1.5 shard_map.102.refs_11_
  243.2 6.5 %shard_map.103.refs_6_.refs_0_ = bf16[1024,1024]{1,0:T(8,128)(2,1)S(1)} custom-call(bf16[512,1024]{1,0:T(8,128)(2,1)S(1)} %bitcast.15, bf16[512,1024]{1,0:T(8,128)(2,1)S(1)} %copy-done.25, bf16[512,1024]{1,0:T(8,128)(2,1)S(1)} %collective-permute-done.1.refs_2_, bf16[256,1024]{1,0:T(8,128)(2,1)S(1)} %copy-done.65, bf16[256,1024]{1,0:T(8,128)(2,1)S(1)} %copy-done.69, ...), custom_call_target="tpu_custom_call" | custom-call | flops 4294967296 | bytes 14680064 | tf_op jit(solution)/shard_map/pallas_call | solution.py:38
  251.0 3.9 %shard_map.104 = (bf16[512,1024]{1,0:T(8,128)(2,1)S(1)}, bf16[512,1024]{1,0:T(8,128)(2,1)S(1)}, bf16[512,1024]{1,0:T(8,128)(2,1)S(1)}) custom-call(bf16[2048,1024]{1,0:T(8,128)(2,1)S(1)} %copy-done.4, bf16[1024,1024]{1,0:T(8,128)(2,1)S(1)} %copy-done.42, bf16[1024,1024]{1,0:T(8,128)(2,1)S(1)} %copy-done.6, ...), custom_call_target="tpu_custom_call" | custom-call | flops 3221225472 | bytes 14680064 | tf_op jit(solution)/shard_map/pallas_call | solution.py:38
  259.2 1.6 copy-done.13
  262.8 1.4 shard_map.108
  264.3 2.8 add_convert_fusion.1
  270.7 2.8 add_convert_fusion.2
  273.5 18.4 %collective-permute-done.33.refs_1_ = bf16[512,1024]{1,0:T(8,128)(2,1)} collective-permute-done((bf16[512,1024]{1,0:T(8,128)(2,1)}, bf16[512,1024]{1,0:T(8,128)(2,1)}, u32[]{:S(2)}, u32[]{:S(2)}) %collective-permute-start.33) | collective-permute-done | bytes 1048608 | tf_op jit(solution)/shard_map/ppermute | solution.py:187
  291.9 1.5 shard_map.105.refs_0_
  295.0 9.3 %collective-permute-done.36.refs_2_ = bf16[256,1024]{1,0:T(8,128)(2,1)} collective-permute-done((bf16[256,1024]{1,0:T(8,128)(2,1)}, bf16[256,1024]{1,0:T(8,128)(2,1)}, u32[]{:S(2)}, u32[]{:S(2)}) %collective-permute-start.36) | collective-permute-done | bytes 524320 | tf_op jit(solution)/shard_map/ppermute | solution.py:190
  304.3 2.4 shard_map.107.refs_3_
  309.0 2.6 shard_map.109
  (251 shorter events, 63.0 us)
Async XLA Ops:
  7.2 99.9 %all-gather.4.cloned.1.call-start = ((), (), s32[]{:S(2)}) async-start(), calls=%async_computation.3 | async-start | bytes 2621440 | tf_op jit(solution)/shard_map/all_gather | solution.py:257
  8.8 17.1 %copy-start.80 = (bf16[256,1024]{1,0:T(8,128)(2,1)S(1)}, bf16[256,1024]{1,0:T(8,128)(2,1)}, u32[]{:S(2)}) copy-start(bf16[256,1024]{1,0:T(8,128)(2,1)} %param.8) | copy-start | bytes 1572868
  9.6 18.1 %copy-start.43 = (bf16[2,256,1024]{2,1,0:T(8,128)(2,1)S(1)}, bf16[2,256,1024]{2,1,0:T(8,128)(2,1)}, u32[]{:S(2)}) copy-start(bf16[2,256,1024]{2,1,0:T(8,128)(2,1)} %param.5) | copy-start | bytes 3145732
  9.7 97.4 %all-gather.6.cloned.1.call-start = ((), (), s32[]{:S(2)}) async-start(), calls=%async_computation.4 | async-start | bytes 2621440 | tf_op jit(solution)/shard_map/all_gather | solution.py:257
  10.1 15.0 %collective-permute-start.9 = (bf16[256,1024]{1,0:T(8,128)(2,1)S(1)}, bf16[256,1024]{1,0:T(8,128)(2,1)S(1)}, u32[]{:S(2)}, u32[]{:S(2)}) collective-permute-start(bf16[256,1024]{1,0:T(8,128)(2,1)S(1)} %pad_maximum_fusion.1), channel_id=1, source_target_pairs={{0,1},{1,0},{2,3},{3,2},{4,5},{5,4},{6,7},{7,6},{8,9},{9,8},{10,11... | collective-permute-start | bytes 1572872 | tf_op jit(solution)/shard_map/ppermute | solution.py:190
  25.8 126.1 %all-gather.8.cloned.1.call-start = ((), (), s32[]{:S(2)}) async-start(), calls=%async_computation.5 | async-start | bytes 2621440 | tf_op jit(solution)/shard_map/all_gather | solution.py:257
  25.9 9.3 %collective-permute-start.10 = (bf16[128,1024]{1,0:T(8,128)(2,1)S(1)}, bf16[128,1024]{1,0:T(8,128)(2,1)S(1)}, u32[]{:S(2)}, u32[]{:S(2)}) collective-permute-start(bf16[128,1024]{1,0:T(8,128)(2,1)S(1)} %get-tuple-element.52), channel_id=1, source_target_pairs={{0,1},{1,0},{2,3},{3,2},{4,5},{5,4},{6,7},{7,6},{8,9},{9,8},{10,11... | collective-permute-start | bytes 786440 | tf_op jit(solution)/shard_map/ppermute | solution.py:190
  27.7 26.1 %collective-permute-start.1 = (bf16[512,1024]{1,0:T(8,128)(2,1)S(1)}, bf16[512,1024]{1,0:T(8,128)(2,1)S(1)}, u32[]{:S(2)}, u32[]{:S(2)}) collective-permute-start(bf16[512,1024]{1,0:T(8,128)(2,1)S(1)} %bitcast.10), channel_id=1, source_target_pairs={{0,16},{8,24},{16,0},{24,8},{1,17},{9,25},{17,1},{25,9},{2,18},{10... | collective-permute-start | bytes 3145736 | tf_op jit(solution)/shard_map/ppermute | solution.py:187
  29.2 28.5 %collective-permute-start = (bf16[512,1024]{1,0:T(8,128)(2,1)S(1)}, bf16[512,1024]{1,0:T(8,128)(2,1)S(1)}, u32[]{:S(2)}, u32[]{:S(2)}) collective-permute-start(bf16[512,1024]{1,0:T(8,128)(2,1)S(1)} %bitcast.11), channel_id=1, source_target_pairs={{0,1},{1,0},{2,3},{3,2},{4,5},{5,4},{6,7},{7,6},{8,9},{9,8},{10,11... | collective-permute-start | bytes 3145736 | tf_op jit(solution)/shard_map/ppermute | solution.py:190
  29.7 46.7 %collective-permute-start.12 = (bf16[512,1024]{1,0:T(8,128)(2,1)}, bf16[512,1024]{1,0:T(8,128)(2,1)}, u32[]{:S(2)}, u32[]{:S(2)}) collective-permute-start(bf16[512,1024]{1,0:T(8,128)(2,1)} %bitcast.5.refs_0_), channel_id=1, source_target_pairs={{0,16},{8,24},{16,0},{24,8},{1,17},{9,25},{17,1},{25,9},{2,18},{10... | collective-permute-start | bytes 3145736 | tf_op jit(solution)/shard_map/ppermute | solution.py:187
  30.1 47.8 %collective-permute-start.4 = (bf16[512,1024]{1,0:T(8,128)(2,1)S(1)}, bf16[512,1024]{1,0:T(8,128)(2,1)}, u32[]{:S(2)}, u32[]{:S(2)}) collective-permute-start(bf16[512,1024]{1,0:T(8,128)(2,1)S(1)} %bitcast.12), channel_id=1, source_target_pairs={{0,8},{8,0},{16,24},{24,16},{1,9},{9,1},{17,25},{25,17},{2,10},{10... | collective-permute-start | bytes 3145736 | tf_op jit(solution)/shard_map/ppermute | solution.py:184
  35.2 45.0 %collective-permute-start.11 = (bf16[512,1024]{1,0:T(8,128)(2,1)}, bf16[512,1024]{1,0:T(8,128)(2,1)}, u32[]{:S(2)}, u32[]{:S(2)}) collective-permute-start(bf16[512,1024]{1,0:T(8,128)(2,1)} %bitcast.5.refs_0_), channel_id=1, source_target_pairs={{0,1},{1,0},{2,3},{3,2},{4,5},{5,4},{6,7},{7,6},{8,9},{9,8},{10,11... | collective-permute-start | bytes 3145736 | tf_op jit(solution)/shard_map/ppermute | solution.py:190
  37.9 162.2 %reduce-scatter.4.cloned.1.call-start = ((), (), s32[]{:S(2)}) async-start(), calls=%async_computation.6 | async-start | bytes 2621440 | tf_op jit(solution)/shard_map/reduce_scatter | solution.py:260
  53.9 37.5 %collective-permute-start.2 = (bf16[256,1024]{1,0:T(8,128)(2,1)S(1)}, bf16[256,1024]{1,0:T(8,128)(2,1)S(1)}, u32[]{:S(2)}, u32[]{:S(2)}) collective-permute-start(bf16[256,1024]{1,0:T(8,128)(2,1)S(1)} %slice.40), channel_id=1, source_target_pairs={{0,1},{1,0},{2,3},{3,2},{4,5},{5,4},{6,7},{7,6},{8,9},{9,8},{10,11... | collective-permute-start | bytes 1572872 | tf_op jit(solution)/shard_map/ppermute | solution.py:190
  57.7 49.3 %copy-start.22 = (bf16[512,1024]{1,0:T(8,128)(2,1)}, bf16[512,1024]{1,0:T(8,128)(2,1)S(1)}, u32[]{:S(2)}) copy-start(bf16[512,1024]{1,0:T(8,128)(2,1)S(1)} %collective-permute-done.refs_1_) | copy-start | bytes 3145732
  57.8 35.4 %collective-permute-start.3 = (bf16[256,1024]{1,0:T(8,128)(2,1)S(1)}, bf16[256,1024]{1,0:T(8,128)(2,1)S(1)}, u32[]{:S(2)}, u32[]{:S(2)}) collective-permute-start(bf16[256,1024]{1,0:T(8,128)(2,1)S(1)} %slice.41), channel_id=1, source_target_pairs={{0,16},{8,24},{16,0},{24,8},{1,17},{9,25},{17,1},{25,9},{2,18},{10... | collective-permute-start | bytes 1572872 | tf_op jit(solution)/shard_map/ppermute | solution.py:187
  77.5 23.6 %collective-permute-start.13 = (bf16[256,1024]{1,0:T(8,128)(2,1)S(1)}, bf16[256,1024]{1,0:T(8,128)(2,1)}, u32[]{:S(2)}, u32[]{:S(2)}) collective-permute-start(bf16[256,1024]{1,0:T(8,128)(2,1)S(1)} %slice.42), channel_id=1, source_target_pairs={{0,1},{1,0},{2,3},{3,2},{4,5},{5,4},{6,7},{7,6},{8,9},{9,8},{10,11... | collective-permute-start | bytes 1572872 | tf_op jit(solution)/shard_map/ppermute | solution.py:190
  77.9 26.7 %collective-permute-start.5 = (bf16[512,1024]{1,0:T(8,128)(2,1)S(1)}, bf16[512,1024]{1,0:T(8,128)(2,1)S(1)}, u32[]{:S(2)}, u32[]{:S(2)}) collective-permute-start(bf16[512,1024]{1,0:T(8,128)(2,1)S(1)} %collective-permute-done.refs_1_), channel_id=1, source_target_pairs={{0,8},{8,0},{16,24},{24,16},{1,9},{9,1},{17,25},{25,17},{2,10},{10... | collective-permute-start | bytes 3145736 | tf_op jit(solution)/shard_map/ppermute | solution.py:184
  80.3 25.6 %collective-permute-start.6 = (bf16[512,1024]{1,0:T(8,128)(2,1)S(1)}, bf16[512,1024]{1,0:T(8,128)(2,1)S(1)}, u32[]{:S(2)}, u32[]{:S(2)}) collective-permute-start(bf16[512,1024]{1,0:T(8,128)(2,1)S(1)} %collective-permute-done.1.refs_2_), channel_id=1, source_target_pairs={{0,8},{8,0},{16,24},{24,16},{1,9},{9,1},{17,25},{25,17},{2,10},{10... | collective-permute-start | bytes 3145736 | tf_op jit(solution)/shard_map/ppermute | solution.py:184
  91.4 10.9 %collective-permute-start.14 = (bf16[256,1024]{1,0:T(8,128)(2,1)S(1)}, bf16[256,1024]{1,0:T(8,128)(2,1)}, u32[]{:S(2)}, u32[]{:S(2)}) collective-permute-start(bf16[256,1024]{1,0:T(8,128)(2,1)S(1)} %slice.43), channel_id=1, source_target_pairs={{0,16},{8,24},{16,0},{24,8},{1,17},{9,25},{17,1},{25,9},{2,18},{10... | collective-permute-start | bytes 1572872 | tf_op jit(solution)/shard_map/ppermute | solution.py:187
  93.1 9.3 %collective-permute-start.7 = (bf16[256,1024]{1,0:T(8,128)(2,1)S(1)}, bf16[256,1024]{1,0:T(8,128)(2,1)S(1)}, u32[]{:S(2)}, u32[]{:S(2)}) collective-permute-start(bf16[256,1024]{1,0:T(8,128)(2,1)S(1)} %collective-permute-done.2.refs_3_), channel_id=1, source_target_pairs={{0,8},{8,0},{16,24},{24,16},{1,9},{9,1},{17,25},{25,17},{2,10},{10... | collective-permute-start | bytes 1572872 | tf_op jit(solution)/shard_map/ppermute | solution.py:184
  101.1 2.5 collective-permute-start.8
  102.3 34.7 %collective-permute-start.15 = (bf16[512,1024]{1,0:T(8,128)(2,1)}, bf16[512,1024]{1,0:T(8,128)(2,1)}, u32[]{:S(2)}, u32[]{:S(2)}) collective-permute-start(bf16[512,1024]{1,0:T(8,128)(2,1)} %bitcast.5.refs_0_), channel_id=1, source_target_pairs={{0,8},{8,0},{16,24},{24,16},{1,9},{9,1},{17,25},{25,17},{2,10},{10... | collective-permute-start | bytes 3145736 | tf_op jit(solution)/shard_map/ppermute | solution.py:184
  103.2 33.8 %collective-permute-start.16 = (bf16[512,1024]{1,0:T(8,128)(2,1)}, bf16[512,1024]{1,0:T(8,128)(2,1)}, u32[]{:S(2)}, u32[]{:S(2)}) collective-permute-start(bf16[512,1024]{1,0:T(8,128)(2,1)} %collective-permute-done.11.refs_1_), channel_id=1, source_target_pairs={{0,8},{8,0},{16,24},{24,16},{1,9},{9,1},{17,25},{25,17},{2,10},{10... | collective-permute-start | bytes 3145736 | tf_op jit(solution)/shard_map/ppermute | solution.py:184
  104.4 32.6 %collective-permute-start.17 = (bf16[512,1024]{1,0:T(8,128)(2,1)}, bf16[512,1024]{1,0:T(8,128)(2,1)}, u32[]{:S(2)}, u32[]{:S(2)}) collective-permute-start(bf16[512,1024]{1,0:T(8,128)(2,1)} %collective-permute-done.12.refs_2_), channel_id=1, source_target_pairs={{0,8},{8,0},{16,24},{24,16},{1,9},{9,1},{17,25},{25,17},{2,10},{10... | collective-permute-start | bytes 3145736 | tf_op jit(solution)/shard_map/ppermute | solution.py:184
  105.5 31.5 %collective-permute-start.18 = (bf16[256,1024]{1,0:T(8,128)(2,1)}, bf16[256,1024]{1,0:T(8,128)(2,1)}, u32[]{:S(2)}, u32[]{:S(2)}) collective-permute-start(bf16[256,1024]{1,0:T(8,128)(2,1)} %collective-permute-done.13.refs_3_), channel_id=1, source_target_pairs={{0,8},{8,0},{16,24},{24,16},{1,9},{9,1},{17,25},{25,17},{2,10},{10... | collective-permute-start | bytes 1572872 | tf_op jit(solution)/shard_map/ppermute | solution.py:184
  106.9 30.1 %collective-permute-start.19 = (bf16[256,1024]{1,0:T(8,128)(2,1)}, bf16[256,1024]{1,0:T(8,128)(2,1)}, u32[]{:S(2)}, u32[]{:S(2)}) collective-permute-start(bf16[256,1024]{1,0:T(8,128)(2,1)} %collective-permute-done.14.refs_4_), channel_id=1, source_target_pairs={{0,8},{8,0},{16,24},{24,16},{1,9},{9,1},{17,25},{25,17},{2,10},{10... | collective-permute-start | bytes 1572872 | tf_op jit(solution)/shard_map/ppermute | solution.py:184
  147.9 111.3 %reduce-scatter.6.cloned.1.call-start = ((), (), s32[]{:S(2)}) async-start(), calls=%async_computation.7 | async-start | bytes 2621440 | tf_op jit(solution)/shard_map/reduce_scatter | solution.py:260
  156.1 16.9 %collective-permute-start.23 = (bf16[512,1024]{1,0:T(8,128)(2,1)S(1)}, bf16[512,1024]{1,0:T(8,128)(2,1)S(1)}, u32[]{:S(2)}, u32[]{:S(2)}) collective-permute-start(bf16[512,1024]{1,0:T(8,128)(2,1)S(1)} %shard_map.94.refs_3_.refs_13_), channel_id=1, source_target_pairs={{0,8},{8,0},{16,24},{24,16},{1,9},{9,1},{17,25},{25,17},{2,10},{10... | collective-permute-start | bytes 3145736 | tf_op jit(solution)/shard_map/ppermute | solution.py:184
  159.0 20.4 %collective-permute-start.20 = (bf16[512,1024]{1,0:T(8,128)(2,1)S(1)}, bf16[512,1024]{1,0:T(8,128)(2,1)S(1)}, u32[]{:S(2)}, u32[]{:S(2)}) collective-permute-start(bf16[512,1024]{1,0:T(8,128)(2,1)S(1)} %get-tuple-element.27.refs_14_), channel_id=1, source_target_pairs={{0,8},{8,0},{16,24},{24,16},{1,9},{9,1},{17,25},{25,17},{2,10},{10... | collective-permute-start | bytes 3145736 | tf_op jit(solution)/shard_map/ppermute | solution.py:184
  159.1 20.4 %collective-permute-start.21 = (bf16[512,1024]{1,0:T(8,128)(2,1)S(1)}, bf16[512,1024]{1,0:T(8,128)(2,1)S(1)}, u32[]{:S(2)}, u32[]{:S(2)}) collective-permute-start(bf16[512,1024]{1,0:T(8,128)(2,1)S(1)} %get-tuple-element.28.refs_15_), channel_id=1, source_target_pairs={{0,8},{8,0},{16,24},{24,16},{1,9},{9,1},{17,25},{25,17},{2,10},{10... | collective-permute-start | bytes 3145736 | tf_op jit(solution)/shard_map/ppermute | solution.py:184
  159.6 19.9 %collective-permute-start.22 = (bf16[512,1024]{1,0:T(8,128)(2,1)S(1)}, bf16[512,1024]{1,0:T(8,128)(2,1)S(1)}, u32[]{:S(2)}, u32[]{:S(2)}) collective-permute-start(bf16[512,1024]{1,0:T(8,128)(2,1)S(1)} %get-tuple-element.29.refs_16_), channel_id=1, source_target_pairs={{0,8},{8,0},{16,24},{24,16},{1,9},{9,1},{17,25},{25,17},{2,10},{10... | collective-permute-start | bytes 3145736 | tf_op jit(solution)/shard_map/ppermute | solution.py:184
  176.3 14.3 %collective-permute-start.24 = (bf16[256,1024]{1,0:T(8,128)(2,1)S(1)}, bf16[256,1024]{1,0:T(8,128)(2,1)S(1)}, u32[]{:S(2)}, u32[]{:S(2)}) collective-permute-start(bf16[256,1024]{1,0:T(8,128)(2,1)S(1)} %get-tuple-element.47), channel_id=1, source_target_pairs={{0,1},{1,0},{2,3},{3,2},{4,5},{5,4},{6,7},{7,6},{8,9},{9,8},{10,11... | collective-permute-start | bytes 1572872 | tf_op jit(solution)/shard_map/ppermute | solution.py:190
  177.9 14.0 %collective-permute-start.26 = (bf16[256,1024]{1,0:T(8,128)(2,1)S(1)}, bf16[256,1024]{1,0:T(8,128)(2,1)S(1)}, u32[]{:S(2)}, u32[]{:S(2)}) collective-permute-start(bf16[256,1024]{1,0:T(8,128)(2,1)S(1)} %get-tuple-element.48), channel_id=1, source_target_pairs={{0,16},{8,24},{16,0},{24,8},{1,17},{9,25},{17,1},{25,9},{2,18},{10... | collective-permute-start | bytes 1572872 | tf_op jit(solution)/shard_map/ppermute | solution.py:187
  203.9 102.9 %reduce-scatter.8.cloned.1.call-start = ((), (), s32[]{:S(2)}) async-start(), calls=%async_computation.8 | async-start | bytes 2621440 | tf_op jit(solution)/shard_map/reduce_scatter | solution.py:260
  210.9 7.1 %collective-permute-start.31 = (bf16[512,1024]{1,0:T(8,128)(2,1)S(1)}, bf16[512,1024]{1,0:T(8,128)(2,1)S(1)}, u32[]{:S(2)}, u32[]{:S(2)}) collective-permute-start(bf16[512,1024]{1,0:T(8,128)(2,1)S(1)} %shard_map.100.refs_3_), channel_id=1, source_target_pairs={{0,8},{8,0},{16,24},{24,16},{1,9},{9,1},{17,25},{25,17},{2,10},{10... | collective-permute-start | bytes 3145736 | tf_op jit(solution)/shard_map/ppermute | solution.py:184
  211.3 25.6 %collective-permute-start.25 = (bf16[512,1024]{1,0:T(8,128)(2,1)S(1)}, bf16[512,1024]{1,0:T(8,128)(2,1)S(1)}, u32[]{:S(2)}, u32[]{:S(2)}) collective-permute-start(bf16[512,1024]{1,0:T(8,128)(2,1)S(1)} %add_convert_fusion.4), channel_id=1, source_target_pairs={{0,16},{8,24},{16,0},{24,8},{1,17},{9,25},{17,1},{25,9},{2,18},{10... | collective-permute-start | bytes 3145736 | tf_op jit(solution)/shard_map/ppermute | solution.py:187
  213.2 25.3 %collective-permute-start.27 = (bf16[512,1024]{1,0:T(8,128)(2,1)S(1)}, bf16[512,1024]{1,0:T(8,128)(2,1)S(1)}, u32[]{:S(2)}, u32[]{:S(2)}) collective-permute-start(bf16[512,1024]{1,0:T(8,128)(2,1)S(1)} %add_convert_fusion.3), channel_id=1, source_target_pairs={{0,1},{1,0},{2,3},{3,2},{4,5},{5,4},{6,7},{7,6},{8,9},{9,8},{10,11... | collective-permute-start | bytes 3145736 | tf_op jit(solution)/shard_map/ppermute | solution.py:190
  217.4 33.2 %collective-permute-start.28 = (bf16[512,1024]{1,0:T(8,128)(2,1)S(1)}, bf16[512,1024]{1,0:T(8,128)(2,1)S(1)}, u32[]{:S(2)}, u32[]{:S(2)}) collective-permute-start(bf16[512,1024]{1,0:T(8,128)(2,1)S(1)} %get-tuple-element.37), channel_id=1, source_target_pairs={{0,8},{8,0},{16,24},{24,16},{1,9},{9,1},{17,25},{25,17},{2,10},{10... | collective-permute-start | bytes 3145736 | tf_op jit(solution)/shard_map/ppermute | solution.py:184
  217.6 33.4 %collective-permute-start.29 = (bf16[512,1024]{1,0:T(8,128)(2,1)S(1)}, bf16[512,1024]{1,0:T(8,128)(2,1)S(1)}, u32[]{:S(2)}, u32[]{:S(2)}) collective-permute-start(bf16[512,1024]{1,0:T(8,128)(2,1)S(1)} %get-tuple-element.38), channel_id=1, source_target_pairs={{0,8},{8,0},{16,24},{24,16},{1,9},{9,1},{17,25},{25,17},{2,10},{10... | collective-permute-start | bytes 3145736 | tf_op jit(solution)/shard_map/ppermute | solution.py:184
  218.0 33.0 %collective-permute-start.30 = (bf16[512,1024]{1,0:T(8,128)(2,1)S(1)}, bf16[512,1024]{1,0:T(8,128)(2,1)S(1)}, u32[]{:S(2)}, u32[]{:S(2)}) collective-permute-start(bf16[512,1024]{1,0:T(8,128)(2,1)S(1)} %get-tuple-element.39), channel_id=1, source_target_pairs={{0,8},{8,0},{16,24},{24,16},{1,9},{9,1},{17,25},{25,17},{2,10},{10... | collective-permute-start | bytes 3145736 | tf_op jit(solution)/shard_map/ppermute | solution.py:184
  240.2 16.7 %collective-permute-start.32 = (bf16[256,1024]{1,0:T(8,128)(2,1)S(1)}, bf16[256,1024]{1,0:T(8,128)(2,1)S(1)}, u32[]{:S(2)}, u32[]{:S(2)}) collective-permute-start(bf16[256,1024]{1,0:T(8,128)(2,1)S(1)} %get-tuple-element.46), channel_id=1, source_target_pairs={{0,1},{1,0},{2,3},{3,2},{4,5},{5,4},{6,7},{7,6},{8,9},{9,8},{10,11... | collective-permute-start | bytes 1572872 | tf_op jit(solution)/shard_map/ppermute | solution.py:190
  240.6 17.1 %collective-permute-start.34 = (bf16[256,1024]{1,0:T(8,128)(2,1)S(1)}, bf16[256,1024]{1,0:T(8,128)(2,1)S(1)}, u32[]{:S(2)}, u32[]{:S(2)}) collective-permute-start(bf16[256,1024]{1,0:T(8,128)(2,1)S(1)} %get-tuple-element.45), channel_id=1, source_target_pairs={{0,16},{8,24},{16,0},{24,8},{1,17},{9,25},{17,1},{25,9},{2,18},{10... | collective-permute-start | bytes 1572872 | tf_op jit(solution)/shard_map/ppermute | solution.py:187
  250.7 8.5 %collective-permute-start.37 = (bf16[128,1024]{1,0:T(8,128)(2,1)S(1)}, bf16[128,1024]{1,0:T(8,128)(2,1)S(1)}, u32[]{:S(2)}, u32[]{:S(2)}) collective-permute-start(bf16[128,1024]{1,0:T(8,128)(2,1)S(1)} %get-tuple-element.50), channel_id=1, source_target_pairs={{0,1},{1,0},{2,3},{3,2},{4,5},{5,4},{6,7},{7,6},{8,9},{9,8},{10,11... | collective-permute-start | bytes 786440 | tf_op jit(solution)/shard_map/ppermute | solution.py:190
  267.1 24.7 %collective-permute-start.33 = (bf16[512,1024]{1,0:T(8,128)(2,1)}, bf16[512,1024]{1,0:T(8,128)(2,1)}, u32[]{:S(2)}, u32[]{:S(2)}) collective-permute-start(bf16[512,1024]{1,0:T(8,128)(2,1)} %add_convert_fusion.1), channel_id=1, source_target_pairs={{0,16},{8,24},{16,0},{24,8},{1,17},{9,25},{17,1},{25,9},{2,18},{10... | collective-permute-start | bytes 3145736 | tf_op jit(solution)/shard_map/ppermute | solution.py:187
  268.6 26.4 %collective-permute-start.35 = (bf16[512,1024]{1,0:T(8,128)(2,1)}, bf16[512,1024]{1,0:T(8,128)(2,1)}, u32[]{:S(2)}, u32[]{:S(2)}) collective-permute-start(bf16[512,1024]{1,0:T(8,128)(2,1)} %add_convert_fusion), channel_id=1, source_target_pairs={{0,1},{1,0},{2,3},{3,2},{4,5},{5,4},{6,7},{7,6},{8,9},{9,8},{10,11... | collective-permute-start | bytes 3145736 | tf_op jit(solution)/shard_map/ppermute | solution.py:190
  269.7 34.6 %collective-permute-start.36 = (bf16[256,1024]{1,0:T(8,128)(2,1)}, bf16[256,1024]{1,0:T(8,128)(2,1)}, u32[]{:S(2)}, u32[]{:S(2)}) collective-permute-start(bf16[256,1024]{1,0:T(8,128)(2,1)} %reduce-scatter.6.cloned.1.call-done.refs_1_), channel_id=1, source_target_pairs={{0,1},{1,0},{2,3},{3,2},{4,5},{5,4},{6,7},{7,6},{8,9},{9,8},{10,11... | collective-permute-start | bytes 1572872 | tf_op jit(solution)/shard_map/ppermute | solution.py:190
  273.5 19.9 %copy-start.79 = (f32[128,1024]{1,0:T(8,128)S(1)}, f32[128,1024]{1,0:T(8,128)}, u32[]{:S(2)}) copy-start(f32[128,1024]{1,0:T(8,128)} %get-tuple-element.49) | copy-start | bytes 1572868
  (78 other events, 268.5 us)
Sparse Core Ops, SparseCore 0:
  10.1 48.6 all-gather.3
  61.0 44.6 all-gather.5
  107.2 44.6 all-gather.7
  154.1 42.5 reduce-scatter.3
  204.0 41.8 reduce-scatter.5
  264.4 41.0 reduce-scatter.7

commit v9 on v8

--- a/solution.py
+++ b/solution.py
@@ -27,7 +27,7 @@
     return jax.ShapeDtypeStruct(dims, dtype)
 
 
-def call(kernel, outs, flops, args, after=(), specs=None, scratch=(), limit=24):
+def call(kernel, outs, flops, args, after=(), specs=None, scratch=(), limit=24, out=None):
     everything = [*args, *after]
     moved = sum(a.size * a.dtype.itemsize for a in args) + sum(o.size * o.dtype.itemsize for o in outs)
     specs = specs or [pl.BlockSpec(memory_space=pltpu.VMEM)] * len(args)
@@ -39,7 +39,7 @@
         body,
         out_shape=list(outs),
         in_specs=[*specs, *[pl.BlockSpec(memory_space=pl.ANY)] * len(after)],
-        out_specs=[pl.BlockSpec(memory_space=pltpu.VMEM)] * len(outs),
+        out_specs=[out or pl.BlockSpec(memory_space=pltpu.VMEM)] * len(outs),
         scratch_shapes=list(scratch),
         compiler_params=pltpu.CompilerParams(vmem_limit_bytes=limit * MIB),
         cost_estimate=pl.CostEstimate(flops=flops, bytes_accessed=moved, transcendentals=0),
@@ -50,6 +50,11 @@
 HBM = pl.BlockSpec(memory_space=pltpu.HBM)
 VMEM = pl.BlockSpec(memory_space=pltpu.VMEM)
 SMEM = pl.BlockSpec(memory_space=pltpu.SMEM)
+
+
+def held(array, after):
+    scratch = [pltpu.SemaphoreType.DMA]
+    return call(copy_kernel, [shape(*array.shape)], 0, [array], after, specs=[HBM], scratch=scratch, out=HBM)[0]
 
 
 class Rows:
@@ -161,8 +166,10 @@
         outs[at][...] = total.astype(BF16)
 
 
-def copy_kernel(in_ref, out_ref):
-    out_ref[...] = in_ref[...]
+def copy_kernel(in_ref, out_ref, sem):
+    copy = pltpu.make_async_copy(in_ref, out_ref, sem)
+    copy.start()
+    copy.wait()
 
 
 def sum_kernel(left_ref, right_ref, out_ref):
@@ -330,8 +337,7 @@
         by_other, by_chip = self.other(corner[:step]), self.chip(corner[step:])
         sums |= self.near_rest(hidden, down_sides, output_far, [corner])
         other_term = unit_term(1, [sums[0, 0], by_other, by_chip])
-        (term,) = call(copy_kernel, [shape(*other_term.shape)], 0, [other_term], [down_sum])
-        other_sum = scatter_units(term)
+        other_sum = scatter_units(held(other_term, [down_sum]))
         zeros = jnp.zeros((step, half), F32)
 
         def with_corner(sums, by_chip, by_other):
@@ -342,17 +348,15 @@
         output_chip, output_other = with_corner(sums, by_chip, by_other)
         unit_sides = [(own_units, 0, half), (other_units, 0, half)]
         grads_far = self.far_first(act, unit_sides, [other_term])
-        grads_far |= self.far_rest(act, unit_sides, [grads_far[1, 1]])
+        own_term = unit_term(0, [grads_far[1, 1]])
+        grads_far |= self.far_rest(act, unit_sides, [grads_far[1, 1], output_chip, output_other])
         grads_far = {place: self.core(block) for place, block in grads_far.items()}
-        grads = self.near_first(act, unit_sides, grads_far, [output_chip, output_other])
+        grads = self.near_first(act, unit_sides, grads_far, [own_term])
         corner = grads[1, 1]
         by_other, by_chip = self.other(corner[:step]), self.chip(corner[step:])
-        own_term = unit_term(0, [corner])
-        grads |= self.near_rest(act, unit_sides, grads_far, [own_term])
+        grads |= self.near_rest(act, unit_sides, grads_far, [corner])
         down_back = self.other(down_sum[:, half:])
-        waits = [other_sum, by_other, by_chip, down_back, grads[0, 0]]
-        (term,) = call(copy_kernel, [shape(*own_term.shape)], 0, [own_term], waits)
-        own_sum = scatter_units(term)
+        own_sum = scatter_units(held(own_term, [other_sum, by_other, by_chip, down_back, grads[0, 0]]))
         grads_chip, grads_other = with_corner(grads, by_chip, by_other)
         total = sums[0, 0].astype(F32) + output_chip.astype(F32) + output_other.astype(F32)
         output = total.astype(BF16).reshape(2, step, half)

time: 320 us -> 326 us (1.019)
  waiting for transfers between devices: 135 us -> 143 us
  local copies, waits for them, and re-layouts: 57.6 us -> 52.1 us
    ppermute x12, waiting for transfers between devices: 59.4 us -> 70 us  [other(): return lax.ppermute(array, 'out', [(0, 1), (1, 0)])]
    unnamed x168 -> x160, local copies, waits for them, and re-layouts: 53.9 us -> 48.4 us
  transfers between devices with their start and end apart: 44 -> 44, of which waited for: 18 -> 19; matrix products, arithmetic and copies ran while one was open for 4% -> 5% of each run, Pallas kernels for 22% -> 22%
where the time goes in v9:
time: 326 us; the launch traced here: 324 us
  waiting for transfers between devices  143 us (44%)
  Pallas kernels  73.8 us (23%)
  local copies, waits for them, and re-layouts  52.1 us (16%)
  starting transfers between devices  26.7 us (8%)
  between operations  14.9 us (5%)
  other arithmetic  14.1 us (4%)
    pallas_call x18, Pallas kernels, call(): pl.pallas_call(body, out_shape=list(outs), in_specs=[*specs, *[pl.BlockSp...  73.8 us
    ppermute x12, waiting for transfers between devices, other(): return lax.ppermute(array, 'out', [(0, 1), (1, 0)])  70 us
    ppermute x8, waiting for transfers between devices, chip(): return lax.ppermute(array, 'inp', [(at, at ^ 2) for at in range(4)])  68.9 us
    unnamed x160, local copies, waits for them, and re-layouts  48.4 us
    ppermute x12, starting transfers between devices, other(): return lax.ppermute(array, 'out', [(0, 1), (1, 0)])  13.9 us
    ppermute x8, starting transfers between devices, chip(): return lax.ppermute(array, 'inp', [(at, at ^ 2) for at in range(4)])  9.55 us
    convert_element_type x4, other arithmetic, with_corner(): return (self.chip(to_chip.astype(BF16)), self.other(to_other.astype(BF16)))  7.18 us
  transfers between devices with their start and end apart: 44, of which 19 were waited for; matrix products, arithmetic and copies ran while one was open for 5% of the time, Pallas kernels for 22%

profile of v9, /device:TPU:0, one launch (start us, length us, event | category | flops | bytes accessed | tf_op | source)
XLA Modules:
  0.0 324.4 jit_solution(17755659491384652849)
XLA Ops:
  10.1 3.0 collective-permute-start.9
  13.1 11.9 %collective-permute-done.9 = bf16[256,1024]{1,0:T(8,128)(2,1)S(1)} collective-permute-done((bf16[256,1024]{1,0:T(8,128)(2,1)S(1)}, bf16[256,1024]{1,0:T(8,128)(2,1)S(1)}, u32[]{:S(2)}, u32[]{:S(2)}) %collective-permute-start.9) | collective-permute-done | bytes 524320 | tf_op jit(solution)/shard_map/ppermute | solution.py:197
  25.9 1.8 collective-permute-start.10
  30.1 5.2 %collective-permute-done.10 = bf16[128,1024]{1,0:T(8,128)(2,1)S(1)} collective-permute-done((bf16[128,1024]{1,0:T(8,128)(2,1)S(1)}, bf16[128,1024]{1,0:T(8,128)(2,1)S(1)}, u32[]{:S(2)}, u32[]{:S(2)}) %collective-permute-start.10) | collective-permute-done | bytes 262176 | tf_op jit(solution)/shard_map/ppermute | solution.py:197
  35.2 1.7 collective-permute-start.11
  37.9 15.9 %collective-permute-done.1.refs_2_ = bf16[512,1024]{1,0:T(8,128)(2,1)S(1)} collective-permute-done((bf16[512,1024]{1,0:T(8,128)(2,1)S(1)}, bf16[512,1024]{1,0:T(8,128)(2,1)S(1)}, u32[]{:S(2)}, u32[]{:S(2)}) %collective-permute-start.1) | collective-permute-done | bytes 1048608 | tf_op jit(solution)/shard_map/ppermute | solution.py:194
  54.2 3.5 %collective-permute-done.refs_1_ = bf16[512,1024]{1,0:T(8,128)(2,1)S(1)} collective-permute-done((bf16[512,1024]{1,0:T(8,128)(2,1)S(1)}, bf16[512,1024]{1,0:T(8,128)(2,1)S(1)}, u32[]{:S(2)}, u32[]{:S(2)}) %collective-permute-start) | collective-permute-done | bytes 1048608 | tf_op jit(solution)/shard_map/ppermute | solution.py:197
  57.8 1.8 collective-permute-start.3
  59.5 16.9 %collective-permute-done.12.refs_2_ = bf16[512,1024]{1,0:T(8,128)(2,1)} collective-permute-done((bf16[512,1024]{1,0:T(8,128)(2,1)}, bf16[512,1024]{1,0:T(8,128)(2,1)}, u32[]{:S(2)}, u32[]{:S(2)}) %collective-permute-start.12) | collective-permute-done | bytes 1048608 | tf_op jit(solution)/shard_map/ppermute | solution.py:194
  77.9 2.4 collective-permute-done.11.refs_1_
  81.4 10.0 %collective-permute-done.2.refs_3_ = bf16[256,1024]{1,0:T(8,128)(2,1)S(1)} collective-permute-done((bf16[256,1024]{1,0:T(8,128)(2,1)S(1)}, bf16[256,1024]{1,0:T(8,128)(2,1)S(1)}, u32[]{:S(2)}, u32[]{:S(2)}) %collective-permute-start.2) | collective-permute-done | bytes 524320 | tf_op jit(solution)/shard_map/ppermute | solution.py:197
  91.4 1.7 collective-permute-start.14
  94.0 7.2 %collective-permute-done.13.refs_3_ = bf16[256,1024]{1,0:T(8,128)(2,1)} collective-permute-done((bf16[256,1024]{1,0:T(8,128)(2,1)S(1)}, bf16[256,1024]{1,0:T(8,128)(2,1)}, u32[]{:S(2)}, u32[]{:S(2)}) %collective-permute-start.13) | collective-permute-done | bytes 524320 | tf_op jit(solution)/shard_map/ppermute | solution.py:197
  107.1 1.6 copy-done.4
  109.9 1.6 copy-done.37
  119.5 14.8 %shard_map.92 = (bf16[2048,512]{1,0:T(8,128)(2,1)S(1)}, bf16[512,2048]{1,0:T(8,128)(2,1)S(1)}, bf16[2048,512]{1,0:T(8,128)(2,1)S(1)}, bf16[2048,512]{1,0:T(8,128)(2,1)S(1)}) custom-call(bf16[512,1024]{1,0:T(8,128)(2,1)S(1)} %bitcast.13, bf16[512,1024]{1,0:T(8,128)(2,1)S(1)} %copy-done.19, bf16[512,1024]{1,0:T(8,128)(2,1)S(1)} %collective-permute-done.1.refs_2_, ...), custom_call_target="tpu_custom_call" | custom-call | flops 8589934592 | bytes 20971520 | tf_op jit(solution)/shard_map/pallas_call | solution.py:38
  137.1 9.5 %shard_map.93.refs_2_ = bf16[512,2048]{1,0:T(8,128)(2,1)S(1)} custom-call(bf16[512,1024]{1,0:T(8,128)(2,1)} %bitcast.5.refs_0_, bf16[512,1024]{1,0:T(8,128)(2,1)} %collective-permute-done.11.refs_1_, bf16[512,1024]{1,0:T(8,128)(2,1)} %collective-permute-done.12.refs_2_, bf16[256,1024]{1,0:T(8,128)(2,1)} %collective-permute-done.13.refs_3_, ...), custom_call_target="tpu_custom_call" | custom-call | flops 4294967296 | bytes 12582912 | tf_op jit(solution)/shard_map/pallas_call | solution.py:38
  148.1 3.8 %all-gather.8.cloned.1.call-done.refs_1_.refs_2_.refs_10_ = bf16[512,2048]{1,0:T(8,128)(2,1)} async-done(((bf16[128,2048]{1,0:T(8,128)(2,1)}), bf16[512,2048]{1,0:T(8,128)(2,1)}) %all-gather.8.cloned.1.call-update) | async-done | bytes 2097168 | tf_op jit(solution)/shard_map/all_gather | solution.py:264
  151.9 1.6 copy-done
  153.5 1.6 copy-done.11
  156.7 2.3 shard_map.95
  159.6 13.3 %shard_map.96 = (bf16[2048,1024]{1,0:T(8,128)(2,1)}, bf16[1024,2048]{1,0:T(8,128)(2,1)}) custom-call(bf16[512,1024]{1,0:T(8,128)(2,1)} %bitcast.5.refs_0_, bf16[512,1024]{1,0:T(8,128)(2,1)} %collective-permute-done.11.refs_1_, bf16[512,1024]{1,0:T(8,128)(2,1)} %collective-permute-done.12.refs_2_, bf16[256,1024]{1,0:T(8,128)(2,1)} %collective-permute-done.13.refs_3_, ...), custom_call_target="tpu_custom_call" | custom-call | flops 4294967296 | bytes 23068672 | tf_op jit(solution)/shard_map/pallas_call | solution.py:38
  173.0 2.2 copy-done.2
  176.3 1.6 collective-permute-start.24
  177.9 1.5 collective-permute-start.26
  179.4 2.3 shard_map.98
  183.7 6.9 %collective-permute-done.24.refs_12_ = bf16[256,1024]{1,0:T(8,128)(2,1)S(1)} collective-permute-done((bf16[256,1024]{1,0:T(8,128)(2,1)S(1)}, bf16[256,1024]{1,0:T(8,128)(2,1)S(1)}, u32[]{:S(2)}, u32[]{:S(2)}) %collective-permute-start.24) | collective-permute-done | bytes 524320 | tf_op jit(solution)/shard_map/ppermute | solution.py:197
  192.0 5.5 %shard_map.99.refs_2_.refs_0_ = bf16[1024,1024]{1,0:T(8,128)(2,1)S(1)} custom-call(bf16[512,1024]{1,0:T(8,128)(2,1)S(1)} %bitcast.14, bf16[512,1024]{1,0:T(8,128)(2,1)S(1)} %copy-done.20, bf16[512,1024]{1,0:T(8,128)(2,1)S(1)} %collective-permute-done.1.refs_2_, bf16[256,1024]{1,0:T(8,128)(2,1)S(1)} %copy-done.60, bf16[256,1024]{1,0:T(8,128)(2,1)S(1)} %copy-done.64, ...), custom_call_target="tpu_custom_call" | custom-call | flops 4294967296 | bytes 14680064 | tf_op jit(solution)/shard_map/pallas_call | solution.py:38
  203.3 1.8 add_convert_fusion.4
  205.0 1.5 collective-permute-start.25
  206.6 1.6 add_convert_fusion.3
  208.7 1.6 copy-done.7
  211.9 17.6 %collective-permute-done.25.refs_4_ = bf16[512,1024]{1,0:T(8,128)(2,1)S(1)} collective-permute-done((bf16[512,1024]{1,0:T(8,128)(2,1)S(1)}, bf16[512,1024]{1,0:T(8,128)(2,1)S(1)}, u32[]{:S(2)}, u32[]{:S(2)}) %collective-permute-start.25) | collective-permute-done | bytes 1048608 | tf_op jit(solution)/shard_map/ppermute | solution.py:194
  229.5 2.7 collective-permute-done.27.refs_5_
  232.2 3.9 %shard_map.101 = (bf16[512,1024]{1,0:T(8,128)(2,1)S(1)}, bf16[512,1024]{1,0:T(8,128)(2,1)S(1)}, bf16[512,1024]{1,0:T(8,128)(2,1)S(1)}) custom-call(bf16[2048,1024]{1,0:T(8,128)(2,1)S(1)} %copy-done.3, bf16[1024,1024]{1,0:T(8,128)(2,1)S(1)} %copy-done.38, bf16[1024,1024]{1,0:T(8,128)(2,1)S(1)} %copy-done.5, ...), custom_call_target="tpu_custom_call" | custom-call | flops 3221225472 | bytes 11534336 | tf_op jit(solution)/shard_map/pallas_call | solution.py:38
  236.9 6.5 %shard_map.102.refs_3_.refs_0_ = bf16[1024,1024]{1,0:T(8,128)(2,1)S(1)} custom-call(bf16[512,1024]{1,0:T(8,128)(2,1)S(1)} %bitcast.15, bf16[512,1024]{1,0:T(8,128)(2,1)S(1)} %copy-done.21, bf16[512,1024]{1,0:T(8,128)(2,1)S(1)} %collective-permute-done.1.refs_2_, bf16[256,1024]{1,0:T(8,128)(2,1)S(1)} %copy-done.61, bf16[256,1024]{1,0:T(8,128)(2,1)S(1)} %copy-done.65, ...), custom_call_target="tpu_custom_call" | custom-call | flops 4294967296 | bytes 14680064 | tf_op jit(solution)/shard_map/pallas_call | solution.py:38
  243.4 1.5 shard_map.103.refs_6_
  248.6 3.9 %shard_map.104 = (bf16[512,1024]{1,0:T(8,128)(2,1)S(1)}, bf16[512,1024]{1,0:T(8,128)(2,1)S(1)}, bf16[512,1024]{1,0:T(8,128)(2,1)S(1)}) custom-call(bf16[2048,1024]{1,0:T(8,128)(2,1)S(1)} %copy-done.3, bf16[1024,1024]{1,0:T(8,128)(2,1)S(1)} %copy-done.38, bf16[1024,1024]{1,0:T(8,128)(2,1)S(1)} %copy-done.5, ...), custom_call_target="tpu_custom_call" | custom-call | flops 3221225472 | bytes 14680064 | tf_op jit(solution)/shard_map/pallas_call | solution.py:38
  254.4 5.4 %collective-permute-done.32.refs_2_ = bf16[256,1024]{1,0:T(8,128)(2,1)S(1)} collective-permute-done((bf16[256,1024]{1,0:T(8,128)(2,1)S(1)}, bf16[256,1024]{1,0:T(8,128)(2,1)S(1)}, u32[]{:S(2)}, u32[]{:S(2)}) %collective-permute-start.32) | collective-permute-done | bytes 524320 | tf_op jit(solution)/shard_map/ppermute | solution.py:197
  261.4 3.5 %collective-permute-done.37.refs_4_ = bf16[128,1024]{1,0:T(8,128)(2,1)S(1)} collective-permute-done((bf16[128,1024]{1,0:T(8,128)(2,1)S(1)}, bf16[128,1024]{1,0:T(8,128)(2,1)S(1)}, u32[]{:S(2)}, u32[]{:S(2)}) %collective-permute-start.37) | collective-permute-done | bytes 262176 | tf_op jit(solution)/shard_map/ppermute | solution.py:197
  265.0 1.6 copy-done.9
  271.0 2.5 add_convert_fusion.1
  277.4 3.2 add_convert_fusion.2
  281.7 16.9 %collective-permute-done.33.refs_1_ = bf16[512,1024]{1,0:T(8,128)(2,1)} collective-permute-done((bf16[512,1024]{1,0:T(8,128)(2,1)}, bf16[512,1024]{1,0:T(8,128)(2,1)}, u32[]{:S(2)}, u32[]{:S(2)}) %collective-permute-start.33) | collective-permute-done | bytes 1048608 | tf_op jit(solution)/shard_map/ppermute | solution.py:194
  300.1 1.7 collective-permute-done.35.refs_1_
  301.8 9.5 %collective-permute-done.36.refs_2_ = bf16[256,1024]{1,0:T(8,128)(2,1)S(1)} collective-permute-done((bf16[256,1024]{1,0:T(8,128)(2,1)}, bf16[256,1024]{1,0:T(8,128)(2,1)S(1)}, u32[]{:S(2)}, u32[]{:S(2)}) %collective-permute-start.36) | collective-permute-done | bytes 524320 | tf_op jit(solution)/shard_map/ppermute | solution.py:197
  311.2 2.4 shard_map.107.refs_3_
  315.9 1.6 shard_map.109
  (243 shorter events, 65.4 us)
Async XLA Ops:
  7.2 99.9 %all-gather.4.cloned.1.call-start = ((), (), s32[]{:S(2)}) async-start(), calls=%async_computation.3 | async-start | bytes 2621440 | tf_op jit(solution)/shard_map/all_gather | solution.py:264
  9.7 97.4 %all-gather.6.cloned.1.call-start = ((), (), s32[]{:S(2)}) async-start(), calls=%async_computation.4 | async-start | bytes 2621440 | tf_op jit(solution)/shard_map/all_gather | solution.py:264
  10.1 15.0 %collective-permute-start.9 = (bf16[256,1024]{1,0:T(8,128)(2,1)S(1)}, bf16[256,1024]{1,0:T(8,128)(2,1)S(1)}, u32[]{:S(2)}, u32[]{:S(2)}) collective-permute-start(bf16[256,1024]{1,0:T(8,128)(2,1)S(1)} %pad_maximum_fusion.1), channel_id=1, source_target_pairs={{0,1},{1,0},{2,3},{3,2},{4,5},{5,4},{6,7},{7,6},{8,9},{9,8},{10,11... | collective-permute-start | bytes 1572872 | tf_op jit(solution)/shard_map/ppermute | solution.py:197
  25.8 126.1 %all-gather.8.cloned.1.call-start = ((), (), s32[]{:S(2)}) async-start(), calls=%async_computation.5 | async-start | bytes 2621440 | tf_op jit(solution)/shard_map/all_gather | solution.py:264
  25.9 9.3 %collective-permute-start.10 = (bf16[128,1024]{1,0:T(8,128)(2,1)S(1)}, bf16[128,1024]{1,0:T(8,128)(2,1)S(1)}, u32[]{:S(2)}, u32[]{:S(2)}) collective-permute-start(bf16[128,1024]{1,0:T(8,128)(2,1)S(1)} %get-tuple-element.52), channel_id=1, source_target_pairs={{0,1},{1,0},{2,3},{3,2},{4,5},{5,4},{6,7},{7,6},{8,9},{9,8},{10,11... | collective-permute-start | bytes 786440 | tf_op jit(solution)/shard_map/ppermute | solution.py:197
  27.7 26.1 %collective-permute-start.1 = (bf16[512,1024]{1,0:T(8,128)(2,1)S(1)}, bf16[512,1024]{1,0:T(8,128)(2,1)S(1)}, u32[]{:S(2)}, u32[]{:S(2)}) collective-permute-start(bf16[512,1024]{1,0:T(8,128)(2,1)S(1)} %bitcast.10), channel_id=1, source_target_pairs={{0,16},{8,24},{16,0},{24,8},{1,17},{9,25},{17,1},{25,9},{2,18},{10... | collective-permute-start | bytes 3145736 | tf_op jit(solution)/shard_map/ppermute | solution.py:194
  29.2 28.5 %collective-permute-start = (bf16[512,1024]{1,0:T(8,128)(2,1)S(1)}, bf16[512,1024]{1,0:T(8,128)(2,1)S(1)}, u32[]{:S(2)}, u32[]{:S(2)}) collective-permute-start(bf16[512,1024]{1,0:T(8,128)(2,1)S(1)} %bitcast.11), channel_id=1, source_target_pairs={{0,1},{1,0},{2,3},{3,2},{4,5},{5,4},{6,7},{7,6},{8,9},{9,8},{10,11... | collective-permute-start | bytes 3145736 | tf_op jit(solution)/shard_map/ppermute | solution.py:197
  29.7 46.7 %collective-permute-start.12 = (bf16[512,1024]{1,0:T(8,128)(2,1)}, bf16[512,1024]{1,0:T(8,128)(2,1)}, u32[]{:S(2)}, u32[]{:S(2)}) collective-permute-start(bf16[512,1024]{1,0:T(8,128)(2,1)} %bitcast.5.refs_0_), channel_id=1, source_target_pairs={{0,16},{8,24},{16,0},{24,8},{1,17},{9,25},{17,1},{25,9},{2,18},{10... | collective-permute-start | bytes 3145736 | tf_op jit(solution)/shard_map/ppermute | solution.py:194
  30.1 47.8 %collective-permute-start.4 = (bf16[512,1024]{1,0:T(8,128)(2,1)S(1)}, bf16[512,1024]{1,0:T(8,128)(2,1)}, u32[]{:S(2)}, u32[]{:S(2)}) collective-permute-start(bf16[512,1024]{1,0:T(8,128)(2,1)S(1)} %bitcast.12), channel_id=1, source_target_pairs={{0,8},{8,0},{16,24},{24,16},{1,9},{9,1},{17,25},{25,17},{2,10},{10... | collective-permute-start | bytes 3145736 | tf_op jit(solution)/shard_map/ppermute | solution.py:191
  35.2 45.0 %collective-permute-start.11 = (bf16[512,1024]{1,0:T(8,128)(2,1)}, bf16[512,1024]{1,0:T(8,128)(2,1)}, u32[]{:S(2)}, u32[]{:S(2)}) collective-permute-start(bf16[512,1024]{1,0:T(8,128)(2,1)} %bitcast.5.refs_0_), channel_id=1, source_target_pairs={{0,1},{1,0},{2,3},{3,2},{4,5},{5,4},{6,7},{7,6},{8,9},{9,8},{10,11... | collective-permute-start | bytes 3145736 | tf_op jit(solution)/shard_map/ppermute | solution.py:197
  37.9 162.2 %reduce-scatter.4.cloned.1.call-start = ((), (), s32[]{:S(2)}) async-start(), calls=%async_computation.6 | async-start | bytes 2621440 | tf_op jit(solution)/shard_map/reduce_scatter | solution.py:267
  53.9 37.5 %collective-permute-start.2 = (bf16[256,1024]{1,0:T(8,128)(2,1)S(1)}, bf16[256,1024]{1,0:T(8,128)(2,1)S(1)}, u32[]{:S(2)}, u32[]{:S(2)}) collective-permute-start(bf16[256,1024]{1,0:T(8,128)(2,1)S(1)} %slice.40), channel_id=1, source_target_pairs={{0,1},{1,0},{2,3},{3,2},{4,5},{5,4},{6,7},{7,6},{8,9},{9,8},{10,11... | collective-permute-start | bytes 1572872 | tf_op jit(solution)/shard_map/ppermute | solution.py:197
  57.7 49.3 %copy-start.18 = (bf16[512,1024]{1,0:T(8,128)(2,1)}, bf16[512,1024]{1,0:T(8,128)(2,1)S(1)}, u32[]{:S(2)}) copy-start(bf16[512,1024]{1,0:T(8,128)(2,1)S(1)} %collective-permute-done.refs_1_) | copy-start | bytes 3145732
  57.8 35.4 %collective-permute-start.3 = (bf16[256,1024]{1,0:T(8,128)(2,1)S(1)}, bf16[256,1024]{1,0:T(8,128)(2,1)S(1)}, u32[]{:S(2)}, u32[]{:S(2)}) collective-permute-start(bf16[256,1024]{1,0:T(8,128)(2,1)S(1)} %slice.41), channel_id=1, source_target_pairs={{0,16},{8,24},{16,0},{24,8},{1,17},{9,25},{17,1},{25,9},{2,18},{10... | collective-permute-start | bytes 1572872 | tf_op jit(solution)/shard_map/ppermute | solution.py:194
  77.5 23.6 %collective-permute-start.13 = (bf16[256,1024]{1,0:T(8,128)(2,1)S(1)}, bf16[256,1024]{1,0:T(8,128)(2,1)}, u32[]{:S(2)}, u32[]{:S(2)}) collective-permute-start(bf16[256,1024]{1,0:T(8,128)(2,1)S(1)} %slice.42), channel_id=1, source_target_pairs={{0,1},{1,0},{2,3},{3,2},{4,5},{5,4},{6,7},{7,6},{8,9},{9,8},{10,11... | collective-permute-start | bytes 1572872 | tf_op jit(solution)/shard_map/ppermute | solution.py:197
  77.9 26.7 %collective-permute-start.5 = (bf16[512,1024]{1,0:T(8,128)(2,1)S(1)}, bf16[512,1024]{1,0:T(8,128)(2,1)S(1)}, u32[]{:S(2)}, u32[]{:S(2)}) collective-permute-start(bf16[512,1024]{1,0:T(8,128)(2,1)S(1)} %collective-permute-done.refs_1_), channel_id=1, source_target_pairs={{0,8},{8,0},{16,24},{24,16},{1,9},{9,1},{17,25},{25,17},{2,10},{10... | collective-permute-start | bytes 3145736 | tf_op jit(solution)/shard_map/ppermute | solution.py:191
  80.3 25.6 %collective-permute-start.6 = (bf16[512,1024]{1,0:T(8,128)(2,1)S(1)}, bf16[512,1024]{1,0:T(8,128)(2,1)S(1)}, u32[]{:S(2)}, u32[]{:S(2)}) collective-permute-start(bf16[512,1024]{1,0:T(8,128)(2,1)S(1)} %collective-permute-done.1.refs_2_), channel_id=1, source_target_pairs={{0,8},{8,0},{16,24},{24,16},{1,9},{9,1},{17,25},{25,17},{2,10},{10... | collective-permute-start | bytes 3145736 | tf_op jit(solution)/shard_map/ppermute | solution.py:191
  91.4 10.9 %collective-permute-start.14 = (bf16[256,1024]{1,0:T(8,128)(2,1)S(1)}, bf16[256,1024]{1,0:T(8,128)(2,1)}, u32[]{:S(2)}, u32[]{:S(2)}) collective-permute-start(bf16[256,1024]{1,0:T(8,128)(2,1)S(1)} %slice.43), channel_id=1, source_target_pairs={{0,16},{8,24},{16,0},{24,8},{1,17},{9,25},{17,1},{25,9},{2,18},{10... | collective-permute-start | bytes 1572872 | tf_op jit(solution)/shard_map/ppermute | solution.py:194
  93.1 9.3 %collective-permute-start.7 = (bf16[256,1024]{1,0:T(8,128)(2,1)S(1)}, bf16[256,1024]{1,0:T(8,128)(2,1)S(1)}, u32[]{:S(2)}, u32[]{:S(2)}) collective-permute-start(bf16[256,1024]{1,0:T(8,128)(2,1)S(1)} %collective-permute-done.2.refs_3_), channel_id=1, source_target_pairs={{0,8},{8,0},{16,24},{24,16},{1,9},{9,1},{17,25},{25,17},{2,10},{10... | collective-permute-start | bytes 1572872 | tf_op jit(solution)/shard_map/ppermute | solution.py:191
  101.1 2.5 collective-permute-start.8
  102.3 34.7 %collective-permute-start.15 = (bf16[512,1024]{1,0:T(8,128)(2,1)}, bf16[512,1024]{1,0:T(8,128)(2,1)}, u32[]{:S(2)}, u32[]{:S(2)}) collective-permute-start(bf16[512,1024]{1,0:T(8,128)(2,1)} %bitcast.5.refs_0_), channel_id=1, source_target_pairs={{0,8},{8,0},{16,24},{24,16},{1,9},{9,1},{17,25},{25,17},{2,10},{10... | collective-permute-start | bytes 3145736 | tf_op jit(solution)/shard_map/ppermute | solution.py:191
  103.2 33.8 %collective-permute-start.16 = (bf16[512,1024]{1,0:T(8,128)(2,1)}, bf16[512,1024]{1,0:T(8,128)(2,1)}, u32[]{:S(2)}, u32[]{:S(2)}) collective-permute-start(bf16[512,1024]{1,0:T(8,128)(2,1)} %collective-permute-done.11.refs_1_), channel_id=1, source_target_pairs={{0,8},{8,0},{16,24},{24,16},{1,9},{9,1},{17,25},{25,17},{2,10},{10... | collective-permute-start | bytes 3145736 | tf_op jit(solution)/shard_map/ppermute | solution.py:191
  104.4 32.6 %collective-permute-start.17 = (bf16[512,1024]{1,0:T(8,128)(2,1)}, bf16[512,1024]{1,0:T(8,128)(2,1)}, u32[]{:S(2)}, u32[]{:S(2)}) collective-permute-start(bf16[512,1024]{1,0:T(8,128)(2,1)} %collective-permute-done.12.refs_2_), channel_id=1, source_target_pairs={{0,8},{8,0},{16,24},{24,16},{1,9},{9,1},{17,25},{25,17},{2,10},{10... | collective-permute-start | bytes 3145736 | tf_op jit(solution)/shard_map/ppermute | solution.py:191
  105.6 31.5 %collective-permute-start.18 = (bf16[256,1024]{1,0:T(8,128)(2,1)}, bf16[256,1024]{1,0:T(8,128)(2,1)}, u32[]{:S(2)}, u32[]{:S(2)}) collective-permute-start(bf16[256,1024]{1,0:T(8,128)(2,1)} %collective-permute-done.13.refs_3_), channel_id=1, source_target_pairs={{0,8},{8,0},{16,24},{24,16},{1,9},{9,1},{17,25},{25,17},{2,10},{10... | collective-permute-start | bytes 1572872 | tf_op jit(solution)/shard_map/ppermute | solution.py:191
  106.9 30.1 %collective-permute-start.19 = (bf16[256,1024]{1,0:T(8,128)(2,1)}, bf16[256,1024]{1,0:T(8,128)(2,1)}, u32[]{:S(2)}, u32[]{:S(2)}) collective-permute-start(bf16[256,1024]{1,0:T(8,128)(2,1)} %collective-permute-done.14.refs_4_), channel_id=1, source_target_pairs={{0,8},{8,0},{16,24},{24,16},{1,9},{9,1},{17,25},{25,17},{2,10},{10... | collective-permute-start | bytes 1572872 | tf_op jit(solution)/shard_map/ppermute | solution.py:191
  147.9 117.1 %reduce-scatter.6.cloned.1.call-start = ((), (), s32[]{:S(2)}) async-start(), calls=%async_computation.7 | async-start | bytes 2621440 | tf_op jit(solution)/shard_map/reduce_scatter | solution.py:267
  156.1 16.9 %collective-permute-start.23 = (bf16[512,1024]{1,0:T(8,128)(2,1)S(1)}, bf16[512,1024]{1,0:T(8,128)(2,1)S(1)}, u32[]{:S(2)}, u32[]{:S(2)}) collective-permute-start(bf16[512,1024]{1,0:T(8,128)(2,1)S(1)} %shard_map.94.refs_3_.refs_13_), channel_id=1, source_target_pairs={{0,8},{8,0},{16,24},{24,16},{1,9},{9,1},{17,25},{25,17},{2,10},{10... | collective-permute-start | bytes 3145736 | tf_op jit(solution)/shard_map/ppermute | solution.py:191
  159.0 20.5 %collective-permute-start.20 = (bf16[512,1024]{1,0:T(8,128)(2,1)S(1)}, bf16[512,1024]{1,0:T(8,128)(2,1)S(1)}, u32[]{:S(2)}, u32[]{:S(2)}) collective-permute-start(bf16[512,1024]{1,0:T(8,128)(2,1)S(1)} %get-tuple-element.27.refs_14_), channel_id=1, source_target_pairs={{0,8},{8,0},{16,24},{24,16},{1,9},{9,1},{17,25},{25,17},{2,10},{10... | collective-permute-start | bytes 3145736 | tf_op jit(solution)/shard_map/ppermute | solution.py:191
  159.1 20.4 %collective-permute-start.21 = (bf16[512,1024]{1,0:T(8,128)(2,1)S(1)}, bf16[512,1024]{1,0:T(8,128)(2,1)S(1)}, u32[]{:S(2)}, u32[]{:S(2)}) collective-permute-start(bf16[512,1024]{1,0:T(8,128)(2,1)S(1)} %get-tuple-element.28.refs_15_), channel_id=1, source_target_pairs={{0,8},{8,0},{16,24},{24,16},{1,9},{9,1},{17,25},{25,17},{2,10},{10... | collective-permute-start | bytes 3145736 | tf_op jit(solution)/shard_map/ppermute | solution.py:191
  159.6 19.9 %collective-permute-start.22 = (bf16[512,1024]{1,0:T(8,128)(2,1)S(1)}, bf16[512,1024]{1,0:T(8,128)(2,1)S(1)}, u32[]{:S(2)}, u32[]{:S(2)}) collective-permute-start(bf16[512,1024]{1,0:T(8,128)(2,1)S(1)} %get-tuple-element.29.refs_16_), channel_id=1, source_target_pairs={{0,8},{8,0},{16,24},{24,16},{1,9},{9,1},{17,25},{25,17},{2,10},{10... | collective-permute-start | bytes 3145736 | tf_op jit(solution)/shard_map/ppermute | solution.py:191
  176.3 14.3 %collective-permute-start.24 = (bf16[256,1024]{1,0:T(8,128)(2,1)S(1)}, bf16[256,1024]{1,0:T(8,128)(2,1)S(1)}, u32[]{:S(2)}, u32[]{:S(2)}) collective-permute-start(bf16[256,1024]{1,0:T(8,128)(2,1)S(1)} %get-tuple-element.47), channel_id=1, source_target_pairs={{0,1},{1,0},{2,3},{3,2},{4,5},{5,4},{6,7},{7,6},{8,9},{9,8},{10,11... | collective-permute-start | bytes 1572872 | tf_op jit(solution)/shard_map/ppermute | solution.py:197
  177.9 14.0 %collective-permute-start.26 = (bf16[256,1024]{1,0:T(8,128)(2,1)S(1)}, bf16[256,1024]{1,0:T(8,128)(2,1)S(1)}, u32[]{:S(2)}, u32[]{:S(2)}) collective-permute-start(bf16[256,1024]{1,0:T(8,128)(2,1)S(1)} %get-tuple-element.48), channel_id=1, source_target_pairs={{0,16},{8,24},{16,0},{24,8},{1,17},{9,25},{17,1},{25,9},{2,18},{10... | collective-permute-start | bytes 1572872 | tf_op jit(solution)/shard_map/ppermute | solution.py:194
  203.0 110.7 %reduce-scatter.8.cloned.1.call-start = ((), (), s32[]{:S(2)}) async-start(), calls=%async_computation.8 | async-start | bytes 2621440 | tf_op jit(solution)/shard_map/reduce_scatter | solution.py:267
  205.0 24.5 %collective-permute-start.25 = (bf16[512,1024]{1,0:T(8,128)(2,1)S(1)}, bf16[512,1024]{1,0:T(8,128)(2,1)S(1)}, u32[]{:S(2)}, u32[]{:S(2)}) collective-permute-start(bf16[512,1024]{1,0:T(8,128)(2,1)S(1)} %add_convert_fusion.4), channel_id=1, source_target_pairs={{0,16},{8,24},{16,0},{24,8},{1,17},{9,25},{17,1},{25,9},{2,18},{10... | collective-permute-start | bytes 3145736 | tf_op jit(solution)/shard_map/ppermute | solution.py:194
  208.2 24.0 %collective-permute-start.27 = (bf16[512,1024]{1,0:T(8,128)(2,1)S(1)}, bf16[512,1024]{1,0:T(8,128)(2,1)S(1)}, u32[]{:S(2)}, u32[]{:S(2)}) collective-permute-start(bf16[512,1024]{1,0:T(8,128)(2,1)S(1)} %add_convert_fusion.3), channel_id=1, source_target_pairs={{0,1},{1,0},{2,3},{3,2},{4,5},{5,4},{6,7},{7,6},{8,9},{9,8},{10,11... | collective-permute-start | bytes 3145736 | tf_op jit(solution)/shard_map/ppermute | solution.py:197
  211.8 25.0 %copy-start.17 = (bf16[1024,2048]{1,0:T(8,128)(2,1)S(1)}, bf16[1024,2048]{1,0:T(8,128)(2,1)}, u32[]{:S(2)}) copy-start(bf16[1024,2048]{1,0:T(8,128)(2,1)} %get-tuple-element.36.refs_10_) | copy-start | bytes 12582916
  211.8 25.0 %copy-start.21 = (bf16[512,1024]{1,0:T(8,128)(2,1)S(1)}, bf16[512,1024]{1,0:T(8,128)(2,1)}, u32[]{:S(2)}) copy-start(bf16[512,1024]{1,0:T(8,128)(2,1)} %copy-done.18) | copy-start | bytes 3145732
  211.8 25.0 %copy-start.42 = (bf16[2,256,1024]{2,1,0:T(8,128)(2,1)S(1)}, bf16[2,256,1024]{2,1,0:T(8,128)(2,1)}, u32[]{:S(2)}) copy-start(bf16[2,256,1024]{2,1,0:T(8,128)(2,1)} %param.5) | copy-start | bytes 3145732
  211.9 31.5 %collective-permute-start.31 = (bf16[512,1024]{1,0:T(8,128)(2,1)S(1)}, bf16[512,1024]{1,0:T(8,128)(2,1)S(1)}, u32[]{:S(2)}, u32[]{:S(2)}) collective-permute-start(bf16[512,1024]{1,0:T(8,128)(2,1)S(1)} %shard_map.100.refs_3_.refs_11_), channel_id=1, source_target_pairs={{0,8},{8,0},{16,24},{24,16},{1,9},{9,1},{17,25},{25,17},{2,10},{10... | collective-permute-start | bytes 3145736 | tf_op jit(solution)/shard_map/ppermute | solution.py:191
  236.1 11.1 %collective-permute-start.28 = (bf16[512,1024]{1,0:T(8,128)(2,1)S(1)}, bf16[512,1024]{1,0:T(8,128)(2,1)S(1)}, u32[]{:S(2)}, u32[]{:S(2)}) collective-permute-start(bf16[512,1024]{1,0:T(8,128)(2,1)S(1)} %get-tuple-element.37), channel_id=1, source_target_pairs={{0,8},{8,0},{16,24},{24,16},{1,9},{9,1},{17,25},{25,17},{2,10},{10... | collective-permute-start | bytes 3145736 | tf_op jit(solution)/shard_map/ppermute | solution.py:191
  236.2 12.4 %collective-permute-start.29 = (bf16[512,1024]{1,0:T(8,128)(2,1)S(1)}, bf16[512,1024]{1,0:T(8,128)(2,1)S(1)}, u32[]{:S(2)}, u32[]{:S(2)}) collective-permute-start(bf16[512,1024]{1,0:T(8,128)(2,1)S(1)} %get-tuple-element.38), channel_id=1, source_target_pairs={{0,8},{8,0},{16,24},{24,16},{1,9},{9,1},{17,25},{25,17},{2,10},{10... | collective-permute-start | bytes 3145736 | tf_op jit(solution)/shard_map/ppermute | solution.py:191
  236.7 11.9 %collective-permute-start.30 = (bf16[512,1024]{1,0:T(8,128)(2,1)S(1)}, bf16[512,1024]{1,0:T(8,128)(2,1)S(1)}, u32[]{:S(2)}, u32[]{:S(2)}) collective-permute-start(bf16[512,1024]{1,0:T(8,128)(2,1)S(1)} %get-tuple-element.39), channel_id=1, source_target_pairs={{0,8},{8,0},{16,24},{24,16},{1,9},{9,1},{17,25},{25,17},{2,10},{10... | collective-permute-start | bytes 3145736 | tf_op jit(solution)/shard_map/ppermute | solution.py:191
  245.0 14.8 %collective-permute-start.32 = (bf16[256,1024]{1,0:T(8,128)(2,1)S(1)}, bf16[256,1024]{1,0:T(8,128)(2,1)S(1)}, u32[]{:S(2)}, u32[]{:S(2)}) collective-permute-start(bf16[256,1024]{1,0:T(8,128)(2,1)S(1)} %get-tuple-element.46), channel_id=1, source_target_pairs={{0,1},{1,0},{2,3},{3,2},{4,5},{5,4},{6,7},{7,6},{8,9},{9,8},{10,11... | collective-permute-start | bytes 1572872 | tf_op jit(solution)/shard_map/ppermute | solution.py:197
  245.7 14.9 %collective-permute-start.34 = (bf16[256,1024]{1,0:T(8,128)(2,1)S(1)}, bf16[256,1024]{1,0:T(8,128)(2,1)S(1)}, u32[]{:S(2)}, u32[]{:S(2)}) collective-permute-start(bf16[256,1024]{1,0:T(8,128)(2,1)S(1)} %get-tuple-element.45), channel_id=1, source_target_pairs={{0,16},{8,24},{16,0},{24,8},{1,17},{9,25},{17,1},{25,9},{2,18},{10... | collective-permute-start | bytes 1572872 | tf_op jit(solution)/shard_map/ppermute | solution.py:194
  247.2 17.8 %collective-permute-start.37 = (bf16[128,1024]{1,0:T(8,128)(2,1)S(1)}, bf16[128,1024]{1,0:T(8,128)(2,1)S(1)}, u32[]{:S(2)}, u32[]{:S(2)}) collective-permute-start(bf16[128,1024]{1,0:T(8,128)(2,1)S(1)} %get-tuple-element.50), channel_id=1, source_target_pairs={{0,1},{1,0},{2,3},{3,2},{4,5},{5,4},{6,7},{7,6},{8,9},{9,8},{10,11... | collective-permute-start | bytes 786440 | tf_op jit(solution)/shard_map/ppermute | solution.py:197
  273.6 25.0 %collective-permute-start.33 = (bf16[512,1024]{1,0:T(8,128)(2,1)}, bf16[512,1024]{1,0:T(8,128)(2,1)}, u32[]{:S(2)}, u32[]{:S(2)}) collective-permute-start(bf16[512,1024]{1,0:T(8,128)(2,1)} %add_convert_fusion.1), channel_id=1, source_target_pairs={{0,16},{8,24},{16,0},{24,8},{1,17},{9,25},{17,1},{25,9},{2,18},{10... | collective-permute-start | bytes 3145736 | tf_op jit(solution)/shard_map/ppermute | solution.py:194
  275.4 26.4 %collective-permute-start.35 = (bf16[512,1024]{1,0:T(8,128)(2,1)}, bf16[512,1024]{1,0:T(8,128)(2,1)}, u32[]{:S(2)}, u32[]{:S(2)}) collective-permute-start(bf16[512,1024]{1,0:T(8,128)(2,1)} %add_convert_fusion), channel_id=1, source_target_pairs={{0,1},{1,0},{2,3},{3,2},{4,5},{5,4},{6,7},{7,6},{8,9},{9,8},{10,11... | collective-permute-start | bytes 3145736 | tf_op jit(solution)/shard_map/ppermute | solution.py:197
  276.0 35.2 %collective-permute-start.36 = (bf16[256,1024]{1,0:T(8,128)(2,1)}, bf16[256,1024]{1,0:T(8,128)(2,1)S(1)}, u32[]{:S(2)}, u32[]{:S(2)}) collective-permute-start(bf16[256,1024]{1,0:T(8,128)(2,1)} %reduce-scatter.6.cloned.1.call-done.refs_1_), channel_id=1, source_target_pairs={{0,1},{1,0},{2,3},{3,2},{4,5},{5,4},{6,7},{7,6},{8,9},{9,8},{10,11... | collective-permute-start | bytes 1572872 | tf_op jit(solution)/shard_map/ppermute | solution.py:197
  (74 other events, 436.9 us)
Sparse Core Ops, SparseCore 0:
  10.1 48.6 all-gather.3
  61.0 44.6 all-gather.5
  107.2 44.6 all-gather.7
  154.1 42.5 reduce-scatter.3
  203.1 41.8 reduce-scatter.5
  270.1 41.0 reduce-scatter.7

commit v10 on v0

--- a/solution.py
+++ b/solution.py
@@ -100,6 +100,16 @@
             out_ref[:, pl.ds(pl.multiple_of(place * half + index * tile, tile), tile)] = total.astype(BF16)
 
 
+def finish_kernel(at_ref, mine_ref, theirs_ref, gate_ref, up_ref):
+    width = mine_ref.shape[0] // 2
+    for part, out_ref in enumerate((gate_ref, up_ref)):
+        span = slice(part * width, (part + 1) * width)
+        mine, theirs = mine_ref[span].astype(F32).T, theirs_ref[span].astype(F32).T
+        first = at_ref[0] == 0
+        out_ref[:, :width] = jnp.where(first, mine, theirs)
+        out_ref[:, width:] = jnp.where(first, theirs, mine)
+
+
 class Square:
     def core(self, array):
         return lax.ppermute(array, "inp", [(at, at ^ 1) for at in range(4)])
@@ -136,7 +146,7 @@
             blocks += [((base + 2, 0), (base + 3, 0)), ((base + 2, step), (base + 4, 0))]
         return Rows(pieces, blocks, step)
 
-    def scatter(self, product, rows, cols):
+    def scatter(self, product, rows, cols, split):
         half, quarter = rows // 2, rows // 4
         far = {}
         for chip in (1, 0):
@@ -150,11 +160,15 @@
                 sums[chip, other] = product(at, other) + far[chip, other].astype(F32)
         batch = quarter // 2
         corner = sums[1, 1].astype(BF16)
-        from_other = self.other(corner[:batch]).astype(F32)
-        from_chip = self.chip(corner[batch:]).astype(F32)
-        zeros = jnp.zeros_like(from_other)
-        to_chip = sums[1, 0] + jnp.concatenate([from_other, zeros])
-        to_other = sums[0, 1] + jnp.concatenate([zeros, from_chip])
+        if split:
+            from_other = self.other(corner[:batch]).astype(F32)
+            from_chip = self.chip(corner[batch:]).astype(F32)
+            zeros = jnp.zeros_like(from_other)
+            to_chip = sums[1, 0] + jnp.concatenate([from_other, zeros])
+            to_other = sums[0, 1] + jnp.concatenate([zeros, from_chip])
+        else:
+            to_chip = sums[1, 0]
+            to_other = sums[0, 1] + self.chip(corner).astype(F32)
         total = sums[0, 0] + self.chip(to_chip.astype(BF16)).astype(F32) + self.other(to_other.astype(BF16)).astype(F32)
         return total.astype(BF16).reshape(2, batch, cols // 2)
 
@@ -216,8 +230,14 @@
         down_back = self.other(down_sum[:, half:])
         units_back = self.other(other_sum)
         grad_down = self.in_order(down_sum[:, :half], down_back)
-        grad_gate = self.in_order(own_sum[:width], units_back[:width]).T
-        grad_up = self.in_order(own_sum[width:], units_back[width:]).T
+        grad_gate, grad_up = pl.pallas_call(
+            finish_kernel,
+            out_shape=[jax.ShapeDtypeStruct((half, 2 * width), F32)] * 2,
+            in_specs=[pl.BlockSpec(memory_space=pltpu.SMEM)] + [pl.BlockSpec(memory_space=pltpu.VMEM)] * 2,
+            out_specs=[pl.BlockSpec(memory_space=pltpu.VMEM)] * 2,
+            compiler_params=pltpu.CompilerParams(vmem_limit_bytes=16 * MIB),
+            cost_estimate=pl.CostEstimate(flops=0, bytes_accessed=5 * MIB, transcendentals=0),
+        )(lax.axis_index("out").astype(jnp.int32).reshape(1), own_sum, units_back)
 
         def output_block(at, other):
             return matmul(hidden[at], down[:, other * half : (other + 1) * half], (1, 0))
@@ -225,8 +245,8 @@
         def input_block(at, other):
             return matmul(act[at], other_units if other else own_units, (1, 0))
 
-        output = self.scatter(output_block, count, 2 * half)
-        grad_tokens = self.scatter(input_block, count, 2 * half)
+        output = self.scatter(output_block, count, 2 * half, True)
+        grad_tokens = self.scatter(input_block, count, 2 * half, False)
         return (output, grad_tokens, grad_gate, grad_up, grad_down)
 
 

time: 310 us -> 310 us (level)
    ppermute x8, waiting for transfers between devices: 67 us -> 78.7 us  [chip(): return lax.ppermute(array, 'inp', [(at, at ^ 2) for at in range(4)])]
    ppermute x12 -> x11, waiting for transfers between devices: 59.3 us -> 48.8 us  [other(): return lax.ppermute(array, 'out', [(0, 1), (1, 0)])]
    ppermute x12 -> x11, starting transfers between devices: 14.8 us -> 14.5 us  [other(): return lax.ppermute(array, 'out', [(0, 1), (1, 0)])]
  transfers between devices with their start and end apart: 44 -> 43, of which waited for: 16 -> 14; matrix products, arithmetic and copies ran while one was open for 16% -> 15% of each run, Pallas kernels for 19% -> 19%
where the time goes in v10:
time: 310 us; the launch traced here: 309 us
  waiting for transfers between devices  139 us (45%)
  Pallas kernels  61 us (20%)
  matrix products  41.8 us (13%)
  starting transfers between devices  28 us (9%)
  local copies, waits for them, and re-layouts  20.3 us (7%)
  between operations  14.6 us (5%)
  other arithmetic  4.44 us (1%)
    ppermute x8, waiting for transfers between devices, chip(): return lax.ppermute(array, 'inp', [(at, at ^ 2) for at in range(4)])  78.7 us
    pallas_call x5, Pallas kernels, call(): pl.pallas_call(kernel, out_shape=outs, in_specs=[pl.BlockSpec(memory_spac...  59.4 us
    ppermute x11, waiting for transfers between devices, other(): return lax.ppermute(array, 'out', [(0, 1), (1, 0)])  48.8 us
    dot_general x16, matrix products, matmul(): lax.dot_general(a, b, ((contract[:1], contract[1:]), ((), ())), preferred...  41.8 us
    unnamed x78, local copies, waits for them, and re-layouts  17.8 us
    ppermute x11, starting transfers between devices, other(): return lax.ppermute(array, 'out', [(0, 1), (1, 0)])  14.5 us
    all_gather x3, waiting for transfers between devices, gather_units(): return lax.all_gather(array, 'wt', axis=0, tiled=True)  11.3 us
    ppermute x8, starting transfers between devices, chip(): return lax.ppermute(array, 'inp', [(at, at ^ 2) for at in range(4)])  10.5 us
  transfers between devices with their start and end apart: 43, of which 14 were waited for; matrix products, arithmetic and copies ran while one was open for 15% of the time, Pallas kernels for 19%

profile of v10, /device:TPU:0, one launch (start us, length us, event | category | flops | bytes accessed | tf_op | source)
XLA Modules:
  0.0 309.1 jit_solution(523298181782240827)
XLA Ops:
  7.2 1.3 constant_dynamic-slice_fusion.2
  10.1 3.0 collective-permute-start.9
  13.1 11.9 %collective-permute-done.9 = bf16[256,1024]{1,0:T(8,128)(2,1)S(1)} collective-permute-done((bf16[256,1024]{1,0:T(8,128)(2,1)S(1)}, bf16[256,1024]{1,0:T(8,128)(2,1)S(1)}, u32[]{:S(2)}, u32[]{:S(2)}) %collective-permute-start.9) | collective-permute-done | bytes 524320 | tf_op jit(solution)/shard_map/ppermute | solution.py:121
  25.9 1.8 collective-permute-start.10
  27.8 1.5 collective-permute-start.1
  30.1 5.2 %collective-permute-done.10 = bf16[128,1024]{1,0:T(8,128)(2,1)S(1)} collective-permute-done((bf16[128,1024]{1,0:T(8,128)(2,1)S(1)}, bf16[128,1024]{1,0:T(8,128)(2,1)S(1)}, u32[]{:S(2)}, u32[]{:S(2)}) %collective-permute-start.10) | collective-permute-done | bytes 262176 | tf_op jit(solution)/shard_map/ppermute | solution.py:121
  35.3 1.7 collective-permute-start.19
  37.9 16.2 %collective-permute-done.1.refs_2_ = bf16[512,1024]{1,0:T(8,128)(2,1)S(1)} collective-permute-done((bf16[512,1024]{1,0:T(8,128)(2,1)}, bf16[512,1024]{1,0:T(8,128)(2,1)S(1)}, u32[]{:S(2)}, u32[]{:S(2)}) %collective-permute-start.1) | collective-permute-done | bytes 1048608 | tf_op jit(solution)/shard_map/ppermute | solution.py:118
  54.4 3.3 %collective-permute-done.refs_1_ = bf16[512,1024]{1,0:T(8,128)(2,1)S(1)} collective-permute-done((bf16[512,1024]{1,0:T(8,128)(2,1)}, bf16[512,1024]{1,0:T(8,128)(2,1)S(1)}, u32[]{:S(2)}, u32[]{:S(2)}) %collective-permute-start) | collective-permute-done | bytes 1048608 | tf_op jit(solution)/shard_map/ppermute | solution.py:121
  57.8 1.8 collective-permute-start.3
  59.5 17.0 %collective-permute-done.20.refs_2_ = bf16[512,1024]{1,0:T(8,128)(2,1)S(1)} collective-permute-done((bf16[512,1024]{1,0:T(8,128)(2,1)}, bf16[512,1024]{1,0:T(8,128)(2,1)S(1)}, u32[]{:S(2)}, u32[]{:S(2)}) %collective-permute-start.20) | collective-permute-done | bytes 1048608 | tf_op jit(solution)/shard_map/ppermute | solution.py:118
  76.9 3.4 %collective-permute-done.19.refs_1_ = bf16[512,1024]{1,0:T(8,128)(2,1)} collective-permute-done((bf16[512,1024]{1,0:T(8,128)(2,1)}, bf16[512,1024]{1,0:T(8,128)(2,1)}, u32[]{:S(2)}, u32[]{:S(2)}) %collective-permute-start.19) | collective-permute-done | bytes 1048608 | tf_op jit(solution)/shard_map/ppermute | solution.py:121
  81.4 10.0 %collective-permute-done.2.refs_3_ = bf16[256,1024]{1,0:T(8,128)(2,1)S(1)} collective-permute-done((bf16[256,1024]{1,0:T(8,128)(2,1)S(1)}, bf16[256,1024]{1,0:T(8,128)(2,1)S(1)}, u32[]{:S(2)}, u32[]{:S(2)}) %collective-permute-start.2) | collective-permute-done | bytes 524320 | tf_op jit(solution)/shard_map/ppermute | solution.py:121
  91.4 1.7 collective-permute-start.22
  94.0 7.2 %collective-permute-done.21.refs_3_ = bf16[256,1024]{1,0:T(8,128)(2,1)} collective-permute-done((bf16[256,1024]{1,0:T(8,128)(2,1)S(1)}, bf16[256,1024]{1,0:T(8,128)(2,1)}, u32[]{:S(2)}, u32[]{:S(2)}) %collective-permute-start.21) | collective-permute-done | bytes 524320 | tf_op jit(solution)/shard_map/ppermute | solution.py:121
  113.7 16.1 %shard_map.92 = (bf16[2048,512]{1,0:T(8,128)(2,1)}, bf16[512,2048]{1,0:T(8,128)(2,1)}, bf16[2048,512]{1,0:T(8,128)(2,1)}, bf16[2048,512]{1,0:T(8,128)(2,1)}) custom-call(bf16[512,1024]{1,0:T(8,128)(2,1)} %bitcast.refs_0_, bf16[512,1024]{1,0:T(8,128)(2,1)S(1)} %collective-permute-done.refs_1_, bf16[512,1024]{1,0:T(8,128)(2,1)S(1)} %collective-permute-done.1.refs_2_, ...), custom_call_target="tpu_custom_call" | custom-call | flops 8589934592 | bytes 20971520 | tf_op jit(solution)/shard_map/pallas_call | solution.py:28
  129.8 11.1 %shard_map.97 = bf16[512,2048]{1,0:T(8,128)(2,1)} custom-call(bf16[512,1024]{1,0:T(8,128)(2,1)} %bitcast.6.refs_0_, bf16[512,1024]{1,0:T(8,128)(2,1)} %collective-permute-done.19.refs_1_, bf16[512,1024]{1,0:T(8,128)(2,1)S(1)} %collective-permute-done.20.refs_2_, bf16[256,1024]{1,0:T(8,128)(2,1)} %collective-permute-done.21.refs_3_, ...), custom_call_target="tpu_custom_call" | custom-call | flops 4294967296 | bytes 12582912 | tf_op jit(solution)/shard_map/pallas_call | solution.py:28
  141.2 11.3 %all-gather.8.cloned.1.call-done.refs_10_ = bf16[512,2048]{1,0:T(8,128)(2,1)} async-done(((bf16[128,2048]{1,0:T(8,128)(2,1)}), bf16[512,2048]{1,0:T(8,128)(2,1)}) %all-gather.8.cloned.1.call-update) | async-done | bytes 2097168 | tf_op jit(solution)/shard_map/all_gather | solution.py:177
  152.5 13.5 %shard_map.93 = (bf16[2048,1024]{1,0:T(8,128)(2,1)}, bf16[1024,2048]{1,0:T(8,128)(2,1)}) custom-call(bf16[512,1024]{1,0:T(8,128)(2,1)} %bitcast.6.refs_0_, bf16[512,1024]{1,0:T(8,128)(2,1)} %collective-permute-done.19.refs_1_, bf16[512,1024]{1,0:T(8,128)(2,1)S(1)} %collective-permute-done.20.refs_2_, bf16[256,1024]{1,0:T(8,128)(2,1)} %collective-permute-done.21.refs_3_, ...), custom_call_target="tpu_custom_call" | custom-call | flops 4294967296 | bytes 23068672 | tf_op jit(solution)/shard_map/pallas_call | solution.py:28
  166.1 9.2 %shard_map.95 = bf16[1024,1024]{1,0:T(8,128)(2,1)} custom-call(bf16[512,1024]{1,0:T(8,128)(2,1)} %bitcast.refs_0_, bf16[512,1024]{1,0:T(8,128)(2,1)S(1)} %collective-permute-done.refs_1_, bf16[512,1024]{1,0:T(8,128)(2,1)S(1)} %collective-permute-done.1.refs_2_, bf16[256,1024]{1,0:T(8,128)(2,1)S(1)} %copy-done.11, bf16[256,1024]{1,0:T(8,128)(2,1)S(1)} %copy-done.15, ...), custom_call_target="tpu_custom_call" | custom-call | flops 4294967296 | bytes 14680064 | tf_op jit(solution)/shard_map/pallas_call | solution.py:28
  175.4 4.3 %convolution_convert_fusion.2 = bf16[512,1024]{1,0:T(8,128)(2,1)} fusion(bf16[1024,1024]{1,0:T(8,128)(2,1)} %all-gather.4.cloned.1.call-done.refs_10_, bf16[2048,1024]{1,0:T(8,128)(2,1)} %get-tuple-element.16), kind=kOutput, calls=%fused_computation.10 | convolution fusion | flops 1074266112 | bytes 4194304 | tf_op jit(solution)/shard_map/dot_general | solution.py:16
  179.7 3.6 %convolution_convert_fusion = bf16[512,1024]{1,0:T(8,128)(2,1)} fusion(bf16[1024,1024]{1,0:T(8,128)(2,1)S(1)} %copy-done.30, bf16[2048,1024]{1,0:T(8,128)(2,1)} %get-tuple-element.16), kind=kOutput, calls=%fused_computation.8 | convolution fusion | flops 1074266112 | bytes 4194304 | tf_op jit(solution)/shard_map/dot_general | solution.py:16
  184.0 1.7 convolution_convert_fusion.5
  187.1 1.7 convolution_convert_fusion.4
  188.9 9.5 %shard_map.94 = bf16[1024,1024]{1,0:T(8,128)(2,1)} custom-call(bf16[512,1024]{1,0:T(8,128)(2,1)} %bitcast.refs_0_, bf16[512,1024]{1,0:T(8,128)(2,1)S(1)} %collective-permute-done.refs_1_, bf16[512,1024]{1,0:T(8,128)(2,1)S(1)} %collective-permute-done.1.refs_2_, bf16[256,1024]{1,0:T(8,128)(2,1)S(1)} %copy-done.12, bf16[256,1024]{1,0:T(8,128)(2,1)S(1)} %copy-done.16, ...), custom_call_target="tpu_custom_call" | custom-call | flops 4294967296 | bytes 14680064 | tf_op jit(solution)/shard_map/pallas_call | solution.py:28
  198.4 1.6 copy-done.31
  199.9 2.6 convolution_convert_fusion.1
  202.6 1.3 fusion.6
  204.2 2.2 convolution_convert_fusion.3
  207.0 1.9 add_convert_fusion.7
  209.1 1.6 collective-permute-start.14
  211.4 1.5 collective-permute-start.17
  213.0 2.5 add_convert_fusion.2
  215.6 7.9 %collective-permute-done.14 = bf16[256,1024]{1,0:T(8,128)(2,1)S(1)} collective-permute-done((bf16[256,1024]{1,0:T(8,128)(2,1)S(1)}, bf16[256,1024]{1,0:T(8,128)(2,1)S(1)}, u32[]{:S(2)}, u32[]{:S(2)}) %collective-permute-start.14) | collective-permute-done | bytes 524320 | tf_op jit(solution)/shard_map/ppermute | solution.py:121
  223.4 1.6 collective-permute-start.33
  225.0 3.0 add_convert_fusion.6
  228.4 2.9 add_convert_fusion.5
  231.4 1.6 collective-permute-start.18
  233.0 3.5 %add_convert_fusion.3 = bf16[512,1024]{1,0:T(8,128)(2,1)} fusion(bf16[512,1024]{1,0:T(8,128)(2,1)} %collective-permute-done.29, bf16[1024,1024]{1,0:T(8,128)(2,1)S(1)} %copy-done.27, bf16[2048,1024]{1,0:T(8,128)(2,1)S(1)} %copy-done.36), kind=kOutput, calls=%fused_computation.3 | convolution fusion | flops 1075314688 | bytes 5242880 | tf_op jit(solution)/shard_map/dot_general | solution.py:16
  236.5 13.0 %collective-permute-done.33 = bf16[512,1024]{1,0:T(8,128)(2,1)S(1)} collective-permute-done((bf16[512,1024]{1,0:T(8,128)(2,1)S(1)}, bf16[512,1024]{1,0:T(8,128)(2,1)S(1)}, u32[]{:S(2)}, u32[]{:S(2)}) %collective-permute-start.33) | collective-permute-done | bytes 1048608 | tf_op jit(solution)/shard_map/ppermute | solution.py:118
  249.5 1.6 collective-permute-start.30
  252.6 1.5 collective-permute-start.34
  254.0 18.0 %collective-permute-done.15 = bf16[512,1024]{1,0:T(8,128)(2,1)} collective-permute-done((bf16[512,1024]{1,0:T(8,128)(2,1)}, bf16[512,1024]{1,0:T(8,128)(2,1)}, u32[]{:S(2)}, u32[]{:S(2)}) %collective-permute-start.15) | collective-permute-done | bytes 1048608 | tf_op jit(solution)/shard_map/ppermute | solution.py:118
  272.0 3.9 %add_convert_fusion.4 = bf16[512,1024]{1,0:T(8,128)(2,1)} fusion(bf16[512,1024]{1,0:T(8,128)(2,1)} %collective-permute-done.18, bf16[512,1024]{1,0:T(8,128)(2,1)} %collective-permute-done.15, bf16[512,1024]{1,0:T(8,128)(2,1)} %copy-done.33, bf16[512,2048]{1,0:T(8,128)(2,1)S(1)} %copy-done.29, bf16[2048,512]{1,0:T(8,128)(2,1)} %get-tuple-element.13), kind=kOutput, calls=%fused_computation.4 | convolution fusion | flops 540540928 | bytes 5767168 | tf_op jit(solution)/shard_map/dot_general | solution.py:16
  277.0 1.6 collective-permute-start.36
  279.1 14.1 %collective-permute-done.30 = bf16[512,1024]{1,0:T(8,128)(2,1)} collective-permute-done((bf16[512,1024]{1,0:T(8,128)(2,1)}, bf16[512,1024]{1,0:T(8,128)(2,1)}, u32[]{:S(2)}, u32[]{:S(2)}) %collective-permute-start.30) | collective-permute-done | bytes 1048608 | tf_op jit(solution)/shard_map/ppermute | solution.py:118
  293.3 5.2 %add_convert_fusion = bf16[512,1024]{1,0:T(8,128)(2,1)} fusion(bf16[512,1024]{1,0:T(8,128)(2,1)} %collective-permute-done.34, bf16[512,1024]{1,0:T(8,128)(2,1)} %collective-permute-done.30, bf16[512,1024]{1,0:T(8,128)(2,1)} %collective-permute-done.28, bf16[1024,1024]{1,0:T(8,128)(2,1)} %all-gather.4.cloned.1.call-done.refs_10_, ...), kind=kOutput, calls=%fused_computation | convolution fusion | flops 1077411840 | bytes 7340032 | tf_op jit(solution)/shard_map/dot_general | solution.py:16
  300.6 1.6 shard_map.96
  (158 shorter events, 29.3 us)
Async XLA Ops:
  7.2 99.8 %all-gather.4.cloned.1.call-start = ((), (), s32[]{:S(2)}) async-start(), calls=%async_computation.3 | async-start | bytes 2621440 | tf_op jit(solution)/shard_map/all_gather | solution.py:177
  8.8 17.1 %copy-start.25 = (bf16[256,1024]{1,0:T(8,128)(2,1)S(1)}, bf16[256,1024]{1,0:T(8,128)(2,1)}, u32[]{:S(2)}) copy-start(bf16[256,1024]{1,0:T(8,128)(2,1)} %param.8) | copy-start | bytes 1572868
  9.7 97.3 %all-gather.6.cloned.1.call-start = ((), (), s32[]{:S(2)}) async-start(), calls=%async_computation.4 | async-start | bytes 2621440 | tf_op jit(solution)/shard_map/all_gather | solution.py:177
  10.1 15.0 %collective-permute-start.9 = (bf16[256,1024]{1,0:T(8,128)(2,1)S(1)}, bf16[256,1024]{1,0:T(8,128)(2,1)S(1)}, u32[]{:S(2)}, u32[]{:S(2)}) collective-permute-start(bf16[256,1024]{1,0:T(8,128)(2,1)S(1)} %pad_maximum_fusion.1), channel_id=1, source_target_pairs={{0,1},{1,0},{2,3},{3,2},{4,5},{5,4},{6,7},{7,6},{8,9},{9,8},{10,11... | collective-permute-start | bytes 1572872 | tf_op jit(solution)/shard_map/ppermute | solution.py:121
  25.8 126.6 %all-gather.8.cloned.1.call-start = ((), (), s32[]{:S(2)}) async-start(), calls=%async_computation.5 | async-start | bytes 2621440 | tf_op jit(solution)/shard_map/all_gather | solution.py:177
  25.9 9.3 %collective-permute-start.10 = (bf16[128,1024]{1,0:T(8,128)(2,1)S(1)}, bf16[128,1024]{1,0:T(8,128)(2,1)S(1)}, u32[]{:S(2)}, u32[]{:S(2)}) collective-permute-start(bf16[128,1024]{1,0:T(8,128)(2,1)S(1)} %get-tuple-element.30), channel_id=1, source_target_pairs={{0,1},{1,0},{2,3},{3,2},{4,5},{5,4},{6,7},{7,6},{8,9},{9,8},{10,11... | collective-permute-start | bytes 786440 | tf_op jit(solution)/shard_map/ppermute | solution.py:121
  27.8 26.3 %collective-permute-start.1 = (bf16[512,1024]{1,0:T(8,128)(2,1)}, bf16[512,1024]{1,0:T(8,128)(2,1)S(1)}, u32[]{:S(2)}, u32[]{:S(2)}) collective-permute-start(bf16[512,1024]{1,0:T(8,128)(2,1)} %bitcast.refs_0_), channel_id=1, source_target_pairs={{0,16},{8,24},{16,0},{24,8},{1,17},{9,25},{17,1},{25,9},{2,18},{10... | collective-permute-start | bytes 3145736 | tf_op jit(solution)/shard_map/ppermute | solution.py:118
  29.2 28.5 %collective-permute-start = (bf16[512,1024]{1,0:T(8,128)(2,1)}, bf16[512,1024]{1,0:T(8,128)(2,1)S(1)}, u32[]{:S(2)}, u32[]{:S(2)}) collective-permute-start(bf16[512,1024]{1,0:T(8,128)(2,1)} %bitcast.refs_0_), channel_id=1, source_target_pairs={{0,1},{1,0},{2,3},{3,2},{4,5},{5,4},{6,7},{7,6},{8,9},{9,8},{10,11... | collective-permute-start | bytes 3145736 | tf_op jit(solution)/shard_map/ppermute | solution.py:121
  29.8 46.8 %collective-permute-start.20 = (bf16[512,1024]{1,0:T(8,128)(2,1)}, bf16[512,1024]{1,0:T(8,128)(2,1)S(1)}, u32[]{:S(2)}, u32[]{:S(2)}) collective-permute-start(bf16[512,1024]{1,0:T(8,128)(2,1)} %bitcast.6.refs_0_), channel_id=1, source_target_pairs={{0,16},{8,24},{16,0},{24,8},{1,17},{9,25},{17,1},{25,9},{2,18},{10... | collective-permute-start | bytes 3145736 | tf_op jit(solution)/shard_map/ppermute | solution.py:118
  30.1 46.9 %collective-permute-start.4 = (bf16[512,1024]{1,0:T(8,128)(2,1)}, bf16[512,1024]{1,0:T(8,128)(2,1)}, u32[]{:S(2)}, u32[]{:S(2)}) collective-permute-start(bf16[512,1024]{1,0:T(8,128)(2,1)} %bitcast.refs_0_), channel_id=1, source_target_pairs={{0,8},{8,0},{16,24},{24,16},{1,9},{9,1},{17,25},{25,17},{2,10},{10... | collective-permute-start | bytes 3145736 | tf_op jit(solution)/shard_map/ppermute | solution.py:115
  35.3 45.0 %collective-permute-start.19 = (bf16[512,1024]{1,0:T(8,128)(2,1)}, bf16[512,1024]{1,0:T(8,128)(2,1)}, u32[]{:S(2)}, u32[]{:S(2)}) collective-permute-start(bf16[512,1024]{1,0:T(8,128)(2,1)} %bitcast.6.refs_0_), channel_id=1, source_target_pairs={{0,1},{1,0},{2,3},{3,2},{4,5},{5,4},{6,7},{7,6},{8,9},{9,8},{10,11... | collective-permute-start | bytes 3145736 | tf_op jit(solution)/shard_map/ppermute | solution.py:121
  37.8 238.1 %reduce-scatter.8.cloned.1.call-start = ((), (), s32[]{:S(2)}) async-start(), calls=%async_computation.8 | async-start | bytes 2621440 | tf_op jit(solution)/shard_map/reduce_scatter | solution.py:180
  54.1 37.3 %collective-permute-start.2 = (bf16[256,1024]{1,0:T(8,128)(2,1)S(1)}, bf16[256,1024]{1,0:T(8,128)(2,1)S(1)}, u32[]{:S(2)}, u32[]{:S(2)}) collective-permute-start(bf16[256,1024]{1,0:T(8,128)(2,1)S(1)} %slice.86), channel_id=1, source_target_pairs={{0,1},{1,0},{2,3},{3,2},{4,5},{5,4},{6,7},{7,6},{8,9},{9,8},{10,11... | collective-permute-start | bytes 1572872 | tf_op jit(solution)/shard_map/ppermute | solution.py:121
  57.8 35.4 %collective-permute-start.3 = (bf16[256,1024]{1,0:T(8,128)(2,1)S(1)}, bf16[256,1024]{1,0:T(8,128)(2,1)S(1)}, u32[]{:S(2)}, u32[]{:S(2)}) collective-permute-start(bf16[256,1024]{1,0:T(8,128)(2,1)S(1)} %slice.87), channel_id=1, source_target_pairs={{0,16},{8,24},{16,0},{24,8},{1,17},{9,25},{17,1},{25,9},{2,18},{10... | collective-permute-start | bytes 1572872 | tf_op jit(solution)/shard_map/ppermute | solution.py:118
  76.6 24.6 %collective-permute-start.21 = (bf16[256,1024]{1,0:T(8,128)(2,1)S(1)}, bf16[256,1024]{1,0:T(8,128)(2,1)}, u32[]{:S(2)}, u32[]{:S(2)}) collective-permute-start(bf16[256,1024]{1,0:T(8,128)(2,1)S(1)} %slice.92), channel_id=1, source_target_pairs={{0,1},{1,0},{2,3},{3,2},{4,5},{5,4},{6,7},{7,6},{8,9},{9,8},{10,11... | collective-permute-start | bytes 1572872 | tf_op jit(solution)/shard_map/ppermute | solution.py:121
  76.9 27.6 %collective-permute-start.5 = (bf16[512,1024]{1,0:T(8,128)(2,1)S(1)}, bf16[512,1024]{1,0:T(8,128)(2,1)S(1)}, u32[]{:S(2)}, u32[]{:S(2)}) collective-permute-start(bf16[512,1024]{1,0:T(8,128)(2,1)S(1)} %collective-permute-done.refs_1_), channel_id=1, source_target_pairs={{0,8},{8,0},{16,24},{24,16},{1,9},{9,1},{17,25},{25,17},{2,10},{10... | collective-permute-start | bytes 3145736 | tf_op jit(solution)/shard_map/ppermute | solution.py:115
  80.3 25.6 %collective-permute-start.6 = (bf16[512,1024]{1,0:T(8,128)(2,1)S(1)}, bf16[512,1024]{1,0:T(8,128)(2,1)S(1)}, u32[]{:S(2)}, u32[]{:S(2)}) collective-permute-start(bf16[512,1024]{1,0:T(8,128)(2,1)S(1)} %collective-permute-done.1.refs_2_), channel_id=1, source_target_pairs={{0,8},{8,0},{16,24},{24,16},{1,9},{9,1},{17,25},{25,17},{2,10},{10... | collective-permute-start | bytes 3145736 | tf_op jit(solution)/shard_map/ppermute | solution.py:115
  91.4 10.9 %collective-permute-start.22 = (bf16[256,1024]{1,0:T(8,128)(2,1)S(1)}, bf16[256,1024]{1,0:T(8,128)(2,1)}, u32[]{:S(2)}, u32[]{:S(2)}) collective-permute-start(bf16[256,1024]{1,0:T(8,128)(2,1)S(1)} %slice.93), channel_id=1, source_target_pairs={{0,16},{8,24},{16,0},{24,8},{1,17},{9,25},{17,1},{25,9},{2,18},{10... | collective-permute-start | bytes 1572872 | tf_op jit(solution)/shard_map/ppermute | solution.py:118
  93.1 9.3 %collective-permute-start.7 = (bf16[256,1024]{1,0:T(8,128)(2,1)S(1)}, bf16[256,1024]{1,0:T(8,128)(2,1)S(1)}, u32[]{:S(2)}, u32[]{:S(2)}) collective-permute-start(bf16[256,1024]{1,0:T(8,128)(2,1)S(1)} %collective-permute-done.2.refs_3_), channel_id=1, source_target_pairs={{0,8},{8,0},{16,24},{24,16},{1,9},{9,1},{17,25},{25,17},{2,10},{10... | collective-permute-start | bytes 1572872 | tf_op jit(solution)/shard_map/ppermute | solution.py:115
  101.1 2.5 collective-permute-start.8
  102.3 27.5 %collective-permute-start.23 = (bf16[512,1024]{1,0:T(8,128)(2,1)}, bf16[512,1024]{1,0:T(8,128)(2,1)}, u32[]{:S(2)}, u32[]{:S(2)}) collective-permute-start(bf16[512,1024]{1,0:T(8,128)(2,1)} %bitcast.6.refs_0_), channel_id=1, source_target_pairs={{0,8},{8,0},{16,24},{24,16},{1,9},{9,1},{17,25},{25,17},{2,10},{10... | collective-permute-start | bytes 3145736 | tf_op jit(solution)/shard_map/ppermute | solution.py:115
  103.2 26.6 %collective-permute-start.24 = (bf16[512,1024]{1,0:T(8,128)(2,1)}, bf16[512,1024]{1,0:T(8,128)(2,1)}, u32[]{:S(2)}, u32[]{:S(2)}) collective-permute-start(bf16[512,1024]{1,0:T(8,128)(2,1)} %collective-permute-done.19.refs_1_), channel_id=1, source_target_pairs={{0,8},{8,0},{16,24},{24,16},{1,9},{9,1},{17,25},{25,17},{2,10},{10... | collective-permute-start | bytes 3145736 | tf_op jit(solution)/shard_map/ppermute | solution.py:115
  104.4 25.4 %collective-permute-start.25 = (bf16[512,1024]{1,0:T(8,128)(2,1)S(1)}, bf16[512,1024]{1,0:T(8,128)(2,1)}, u32[]{:S(2)}, u32[]{:S(2)}) collective-permute-start(bf16[512,1024]{1,0:T(8,128)(2,1)S(1)} %collective-permute-done.20.refs_2_), channel_id=1, source_target_pairs={{0,8},{8,0},{16,24},{24,16},{1,9},{9,1},{17,25},{25,17},{2,10},{10... | collective-permute-start | bytes 3145736 | tf_op jit(solution)/shard_map/ppermute | solution.py:115
  105.5 24.3 %collective-permute-start.26 = (bf16[256,1024]{1,0:T(8,128)(2,1)}, bf16[256,1024]{1,0:T(8,128)(2,1)}, u32[]{:S(2)}, u32[]{:S(2)}) collective-permute-start(bf16[256,1024]{1,0:T(8,128)(2,1)} %collective-permute-done.21.refs_3_), channel_id=1, source_target_pairs={{0,8},{8,0},{16,24},{24,16},{1,9},{9,1},{17,25},{25,17},{2,10},{10... | collective-permute-start | bytes 1572872 | tf_op jit(solution)/shard_map/ppermute | solution.py:115
  106.9 22.9 %collective-permute-start.27 = (bf16[256,1024]{1,0:T(8,128)(2,1)}, bf16[256,1024]{1,0:T(8,128)(2,1)}, u32[]{:S(2)}, u32[]{:S(2)}) collective-permute-start(bf16[256,1024]{1,0:T(8,128)(2,1)} %collective-permute-done.22.refs_4_), channel_id=1, source_target_pairs={{0,8},{8,0},{16,24},{24,16},{1,9},{9,1},{17,25},{25,17},{2,10},{10... | collective-permute-start | bytes 1572872 | tf_op jit(solution)/shard_map/ppermute | solution.py:115
  140.9 137.7 %reduce-scatter.6.cloned.1.call-start = ((), (), s32[]{:S(2)}) async-start(), calls=%async_computation.7 | async-start | bytes 2621440 | tf_op jit(solution)/shard_map/reduce_scatter | solution.py:180
  152.5 13.6 %copy-start.11 = (bf16[256,1024]{1,0:T(8,128)(2,1)S(1)}, bf16[256,1024]{1,0:T(8,128)(2,1)}, u32[]{:S(2)}) copy-start(bf16[256,1024]{1,0:T(8,128)(2,1)} %copy-done.9) | copy-start | bytes 1572868
  152.5 13.6 %copy-start.15 = (bf16[256,1024]{1,0:T(8,128)(2,1)S(1)}, bf16[256,1024]{1,0:T(8,128)(2,1)}, u32[]{:S(2)}) copy-start(bf16[256,1024]{1,0:T(8,128)(2,1)} %copy-done.13) | copy-start | bytes 1572868
  152.5 13.6 %copy-start.19 = (bf16[256,1024]{1,0:T(8,128)(2,1)S(1)}, bf16[256,1024]{1,0:T(8,128)(2,1)}, u32[]{:S(2)}) copy-start(bf16[256,1024]{1,0:T(8,128)(2,1)} %copy-done.17) | copy-start | bytes 1572868
  152.5 13.6 %copy-start.23 = (bf16[256,1024]{1,0:T(8,128)(2,1)S(1)}, bf16[256,1024]{1,0:T(8,128)(2,1)}, u32[]{:S(2)}) copy-start(bf16[256,1024]{1,0:T(8,128)(2,1)} %copy-done.21) | copy-start | bytes 1572868
  175.3 124.3 %reduce-scatter.4.cloned.1.call-start = ((), (), s32[]{:S(2)}) async-start(), calls=%async_computation.6 | async-start | bytes 2621440 | tf_op jit(solution)/shard_map/reduce_scatter | solution.py:180
  179.7 51.7 %collective-permute-start.29 = (bf16[512,1024]{1,0:T(8,128)(2,1)}, bf16[512,1024]{1,0:T(8,128)(2,1)}, u32[]{:S(2)}, u32[]{:S(2)}) collective-permute-start(bf16[512,1024]{1,0:T(8,128)(2,1)} %convolution_convert_fusion.2), channel_id=1, source_target_pairs={{0,8},{8,0},{16,24},{24,16},{1,9},{9,1},{17,25},{25,17},{2,10},{10... | collective-permute-start | bytes 3145736 | tf_op jit(solution)/shard_map/ppermute | solution.py:115
  183.3 28.1 %collective-permute-start.32 = (bf16[512,1024]{1,0:T(8,128)(2,1)}, bf16[512,1024]{1,0:T(8,128)(2,1)}, u32[]{:S(2)}, u32[]{:S(2)}) collective-permute-start(bf16[512,1024]{1,0:T(8,128)(2,1)} %convolution_convert_fusion), channel_id=1, source_target_pairs={{0,8},{8,0},{16,24},{24,16},{1,9},{9,1},{17,25},{25,17},{2,10},{10... | collective-permute-start | bytes 3145736 | tf_op jit(solution)/shard_map/ppermute | solution.py:115
  185.7 20.7 %collective-permute-start.13 = (bf16[512,1024]{1,0:T(8,128)(2,1)}, bf16[512,1024]{1,0:T(8,128)(2,1)}, u32[]{:S(2)}, u32[]{:S(2)}) collective-permute-start(bf16[512,1024]{1,0:T(8,128)(2,1)} %convolution_convert_fusion.5), channel_id=1, source_target_pairs={{0,8},{8,0},{16,24},{24,16},{1,9},{9,1},{17,25},{25,17},{2,10},{10... | collective-permute-start | bytes 3145736 | tf_op jit(solution)/shard_map/ppermute | solution.py:115
  186.5 28.9 %collective-permute-start.12 = (bf16[512,1024]{1,0:T(8,128)(2,1)S(1)}, bf16[512,1024]{1,0:T(8,128)(2,1)}, u32[]{:S(2)}, u32[]{:S(2)}) collective-permute-start(bf16[512,1024]{1,0:T(8,128)(2,1)S(1)} %convolution_convert_fusion.6), channel_id=1, source_target_pairs={{0,8},{8,0},{16,24},{24,16},{1,9},{9,1},{17,25},{25,17},{2,10},{10... | collective-permute-start | bytes 3145736 | tf_op jit(solution)/shard_map/ppermute | solution.py:115
  188.8 39.1 %collective-permute-start.16 = (bf16[512,1024]{1,0:T(8,128)(2,1)}, bf16[512,1024]{1,0:T(8,128)(2,1)}, u32[]{:S(2)}, u32[]{:S(2)}) collective-permute-start(bf16[512,1024]{1,0:T(8,128)(2,1)} %convolution_convert_fusion.4), channel_id=1, source_target_pairs={{0,8},{8,0},{16,24},{24,16},{1,9},{9,1},{17,25},{25,17},{2,10},{10... | collective-permute-start | bytes 3145736 | tf_op jit(solution)/shard_map/ppermute | solution.py:115
  209.1 14.3 %collective-permute-start.14 = (bf16[256,1024]{1,0:T(8,128)(2,1)S(1)}, bf16[256,1024]{1,0:T(8,128)(2,1)S(1)}, u32[]{:S(2)}, u32[]{:S(2)}) collective-permute-start(bf16[256,1024]{1,0:T(8,128)(2,1)S(1)} %get-tuple-element.21), channel_id=1, source_target_pairs={{0,1},{1,0},{2,3},{3,2},{4,5},{5,4},{6,7},{7,6},{8,9},{9,8},{10,11... | collective-permute-start | bytes 1572872 | tf_op jit(solution)/shard_map/ppermute | solution.py:121
  211.4 16.5 %collective-permute-start.17 = (bf16[256,1024]{1,0:T(8,128)(2,1)S(1)}, bf16[256,1024]{1,0:T(8,128)(2,1)S(1)}, u32[]{:S(2)}, u32[]{:S(2)}) collective-permute-start(bf16[256,1024]{1,0:T(8,128)(2,1)S(1)} %get-tuple-element.22), channel_id=1, source_target_pairs={{0,16},{8,24},{16,0},{24,8},{1,17},{9,25},{17,1},{25,9},{2,18},{10... | collective-permute-start | bytes 1572872 | tf_op jit(solution)/shard_map/ppermute | solution.py:118
  215.5 21.0 %collective-permute-start.31 = (bf16[512,1024]{1,0:T(8,128)(2,1)S(1)}, bf16[512,1024]{1,0:T(8,128)(2,1)S(1)}, u32[]{:S(2)}, u32[]{:S(2)}) collective-permute-start(bf16[512,1024]{1,0:T(8,128)(2,1)S(1)} %convolution_convert_fusion.1), channel_id=1, source_target_pairs={{0,8},{8,0},{16,24},{24,16},{1,9},{9,1},{17,25},{25,17},{2,10},{10... | collective-permute-start | bytes 3145736 | tf_op jit(solution)/shard_map/ppermute | solution.py:115
  223.4 26.1 %collective-permute-start.33 = (bf16[512,1024]{1,0:T(8,128)(2,1)S(1)}, bf16[512,1024]{1,0:T(8,128)(2,1)S(1)}, u32[]{:S(2)}, u32[]{:S(2)}) collective-permute-start(bf16[512,1024]{1,0:T(8,128)(2,1)S(1)} %add_convert_fusion.2), channel_id=1, source_target_pairs={{0,16},{8,24},{16,0},{24,8},{1,17},{9,25},{17,1},{25,9},{2,18},{10... | collective-permute-start | bytes 3145736 | tf_op jit(solution)/shard_map/ppermute | solution.py:118
  227.9 23.7 %collective-permute-start.11 = (bf16[512,1024]{1,0:T(8,128)(2,1)S(1)}, bf16[512,1024]{1,0:T(8,128)(2,1)S(1)}, u32[]{:S(2)}, u32[]{:S(2)}) collective-permute-start(bf16[512,1024]{1,0:T(8,128)(2,1)S(1)} %convolution_convert_fusion.7), channel_id=1, source_target_pairs={{0,8},{8,0},{16,24},{24,16},{1,9},{9,1},{17,25},{25,17},{2,10},{10... | collective-permute-start | bytes 3145736 | tf_op jit(solution)/shard_map/ppermute | solution.py:115
  227.9 44.1 %collective-permute-start.15 = (bf16[512,1024]{1,0:T(8,128)(2,1)}, bf16[512,1024]{1,0:T(8,128)(2,1)}, u32[]{:S(2)}, u32[]{:S(2)}) collective-permute-start(bf16[512,1024]{1,0:T(8,128)(2,1)} %add_convert_fusion.6), channel_id=1, source_target_pairs={{0,16},{8,24},{16,0},{24,8},{1,17},{9,25},{17,1},{25,9},{2,18},{10... | collective-permute-start | bytes 3145736 | tf_op jit(solution)/shard_map/ppermute | solution.py:118
  231.4 40.6 %collective-permute-start.18 = (bf16[512,1024]{1,0:T(8,128)(2,1)}, bf16[512,1024]{1,0:T(8,128)(2,1)}, u32[]{:S(2)}, u32[]{:S(2)}) collective-permute-start(bf16[512,1024]{1,0:T(8,128)(2,1)} %add_convert_fusion.5), channel_id=1, source_target_pairs={{0,1},{1,0},{2,3},{3,2},{4,5},{5,4},{6,7},{7,6},{8,9},{9,8},{10,11... | collective-permute-start | bytes 3145736 | tf_op jit(solution)/shard_map/ppermute | solution.py:121
  236.4 42.7 %collective-permute-start.28 = (bf16[512,1024]{1,0:T(8,128)(2,1)}, bf16[512,1024]{1,0:T(8,128)(2,1)}, u32[]{:S(2)}, u32[]{:S(2)}) collective-permute-start(bf16[512,1024]{1,0:T(8,128)(2,1)} %convolution_convert_fusion.3), channel_id=1, source_target_pairs={{0,8},{8,0},{16,24},{24,16},{1,9},{9,1},{17,25},{25,17},{2,10},{10... | collective-permute-start | bytes 3145736 | tf_op jit(solution)/shard_map/ppermute | solution.py:115
  249.5 43.8 %collective-permute-start.30 = (bf16[512,1024]{1,0:T(8,128)(2,1)}, bf16[512,1024]{1,0:T(8,128)(2,1)}, u32[]{:S(2)}, u32[]{:S(2)}) collective-permute-start(bf16[512,1024]{1,0:T(8,128)(2,1)} %add_convert_fusion.3), channel_id=1, source_target_pairs={{0,16},{8,24},{16,0},{24,8},{1,17},{9,25},{17,1},{25,9},{2,18},{10... | collective-permute-start | bytes 3145736 | tf_op jit(solution)/shard_map/ppermute | solution.py:118
  252.6 40.7 %collective-permute-start.34 = (bf16[512,1024]{1,0:T(8,128)(2,1)S(1)}, bf16[512,1024]{1,0:T(8,128)(2,1)}, u32[]{:S(2)}, u32[]{:S(2)}) collective-permute-start(bf16[512,1024]{1,0:T(8,128)(2,1)S(1)} %add_convert_fusion.1), channel_id=1, source_target_pairs={{0,1},{1,0},{2,3},{3,2},{4,5},{5,4},{6,7},{7,6},{8,9},{9,8},{10,11... | collective-permute-start | bytes 3145736 | tf_op jit(solution)/shard_map/ppermute | solution.py:121
  277.0 21.4 %collective-permute-start.36 = (bf16[128,1024]{1,0:T(8,128)(2,1)S(1)}, bf16[128,1024]{1,0:T(8,128)(2,1)S(1)}, u32[]{:S(2)}, u32[]{:S(2)}) collective-permute-start(bf16[128,1024]{1,0:T(8,128)(2,1)S(1)} %get-tuple-element.24), channel_id=1, source_target_pairs={{0,1},{1,0},{2,3},{3,2},{4,5},{5,4},{6,7},{7,6},{8,9},{9,8},{10,11... | collective-permute-start | bytes 786440 | tf_op jit(solution)/shard_map/ppermute | solution.py:121
  278.7 20.9 %collective-permute-start.35 = (bf16[256,1024]{1,0:T(8,128)(2,1)}, bf16[256,1024]{1,0:T(8,128)(2,1)S(1)}, u32[]{:S(2)}, u32[]{:S(2)}) collective-permute-start(bf16[256,1024]{1,0:T(8,128)(2,1)} %reduce-scatter.6.cloned.1.call-done), channel_id=1, source_target_pairs={{0,1},{1,0},{2,3},{3,2},{4,5},{5,4},{6,7},{7,6},{8,9},{9,8},{10,11... | collective-permute-start | bytes 1572872 | tf_op jit(solution)/shard_map/ppermute | solution.py:121
  (32 other events, 85.1 us)
Sparse Core Ops, SparseCore 0:
  10.1 48.6 all-gather.3
  61.0 44.6 all-gather.5
  107.8 44.6 all-gather.7
  154.6 42.5 reduce-scatter.7
  199.5 43.1 reduce-scatter.5
  244.8 43.1 reduce-scatter.3

commit v11 on v10

--- a/solution.py
+++ b/solution.py
@@ -37,6 +37,29 @@
 
 def shape(*dims):
     return jax.ShapeDtypeStruct(dims, BF16)
+
+
+def run(kernel, outs, flops, args, after=(), specs=None, scratch=(), limit=24):
+    everything = [*args, *after]
+    moved = sum(a.size * a.dtype.itemsize for a in args) + sum(o.size * o.dtype.itemsize for o in outs)
+    specs = specs or [pl.BlockSpec(memory_space=pltpu.VMEM)] * len(args)
+
+    def body(*refs):
+        kernel(*refs[: len(args)], *refs[len(everything) :])
+
+    return pl.pallas_call(
+        body,
+        out_shape=list(outs),
+        in_specs=[*specs, *[pl.BlockSpec(memory_space=pl.ANY)] * len(after)],
+        out_specs=[pl.BlockSpec(memory_space=pltpu.VMEM)] * len(outs),
+        scratch_shapes=list(scratch),
+        compiler_params=pltpu.CompilerParams(vmem_limit_bytes=limit * MIB),
+        cost_estimate=pl.CostEstimate(flops=flops, bytes_accessed=moved, transcendentals=0),
+    )(*everything)
+
+
+ANY = pl.BlockSpec(memory_space=pl.ANY)
+VMEM = pl.BlockSpec(memory_space=pltpu.VMEM)
 
 
 class Rows:
@@ -100,6 +123,27 @@
             out_ref[:, pl.ds(pl.multiple_of(place * half + index * tile, tile), tile)] = total.astype(BF16)
 
 
+def block_kernel(first, places, sides, added, *refs):
+    rights, many = len(sides), len(places)
+    left_any, right_any, refs = refs[0], refs[1 : 1 + rights], refs[1 + rights :]
+    adds, refs = refs[: many * added], refs[many * added :]
+    outs, (left_ref, right_ref, sems) = refs[:many], refs[many:]
+    depth, half = right_ref.shape[1:]
+    copies = [pltpu.make_async_copy(left_any.at[pl.ds(first, left_ref.shape[0])], left_ref, sems.at[0])]
+    for at, side in enumerate(sides):
+        source = right_any[at].at[:, pl.ds(side * half, half)]
+        copies.append(pltpu.make_async_copy(source, right_ref.at[at], sems.at[1 + at]))
+    for copy in copies:
+        copy.start()
+    for copy in copies:
+        copy.wait()
+    for at, (row, right) in enumerate(places):
+        total = matmul(left_ref[row : row + outs[at].shape[0]], right_ref[right], (1, 0))
+        if added:
+            total = total + adds[at][...].astype(F32)
+        outs[at][...] = total.astype(BF16)
+
+
 def finish_kernel(at_ref, mine_ref, theirs_ref, gate_ref, up_ref):
     width = mine_ref.shape[0] // 2
     for part, out_ref in enumerate((gate_ref, up_ref)):
@@ -146,13 +190,40 @@
             blocks += [((base + 2, 0), (base + 3, 0)), ((base + 2, step), (base + 4, 0))]
         return Rows(pieces, blocks, step)
 
-    def scatter(self, product, rows, cols, split):
+    def products(self, left, rights, places, adds=(), after=()):
+        far = int(not adds)
+        quarter, depth = left.shape[0] // 4, left.shape[1]
+        half = rights[0][2]
+        outs = [shape(quarter, half)] * len(places)
+        use = sorted({other for _, other in places})
+        chips = sorted({chip for chip, _ in places})
+        first = 2 * far * quarter + chips[0] * quarter
+        wanted = [((chip - chips[0]) * quarter, use.index(other)) for chip, other in places]
+        args = [left] + [rights[other][0] for other in use] + [adds[place] for place in places if adds]
+        blocks = run(
+            functools.partial(block_kernel, first, wanted, [rights[other][1] for other in use], bool(adds)),
+            outs,
+            2 * len(places) * quarter * depth * half,
+            args,
+            after,
+            specs=[ANY] * (1 + len(use)) + [VMEM] * (len(args) - 1 - len(use)),
+            scratch=[
+                pltpu.VMEM((len(chips) * quarter, depth), BF16),
+                pltpu.VMEM((len(use), depth, half), BF16),
+                pltpu.SemaphoreType.DMA((1 + len(use),)),
+            ],
+        )
+        return dict(zip(places, blocks))
+
+    def scatter(self, product, rows, cols, split, far=None):
         half, quarter = rows // 2, rows // 4
-        far = {}
-        for chip in (1, 0):
-            for other in (1, 0):
-                at = slice(half + chip * quarter, half + (chip + 1) * quarter)
-                far[chip, other] = self.core(product(at, other).astype(BF16))
+        if far is None:
+            far = {}
+            for chip in (1, 0):
+                for other in (1, 0):
+                    at = slice(half + chip * quarter, half + (chip + 1) * quarter)
+                    far[chip, other] = product(at, other).astype(BF16)
+        far = {place: self.core(block) for place, block in far.items()}
         sums = {}
         for chip in (1, 0):
             for other in (1, 0):
@@ -207,24 +278,27 @@
             hidden_turned,
         )
         down_sum = scatter_units(down_term)
-        act, act_turned = call(
+        down_sides = [(down, 0, half), (down, 1, half)]
+        far = self.products(hidden, down_sides, [(1, 1)], after=[down_term])
+        far |= self.products(hidden, down_sides, [(0, 1), (1, 0), (0, 0)], after=[far[1, 1]])
+        act, act_turned = run(
             functools.partial(grads_kernel, rows_cot, width),
             [shape(count, 2 * units), shape(2 * units, count)],
             4 * count * units * half,
-            *rows_cot.pieces,
-            down,
-            silu,
-            rest,
+            [*rows_cot.pieces, down, silu, rest],
+            after=list(far.values()),
+            limit=44,
         )
         terms = [
-            call(
+            run(
                 functools.partial(weight_kernel, rows_in, (side,), 256),
                 [shape(2 * units, half)],
                 4 * count * units * half,
-                *rows_in.pieces,
-                act_turned,
+                [*rows_in.pieces, act_turned],
+                after=after,
+                limit=44,
             )[0]
-            for side in (1, 0)
+            for side, after in ((1, []), (0, [down_sum]))
         ]
         other_sum, own_sum = scatter_units(terms[0]), scatter_units(terms[1])
         down_back = self.other(down_sum[:, half:])
@@ -245,7 +319,7 @@
         def input_block(at, other):
             return matmul(act[at], other_units if other else own_units, (1, 0))
 
-        output = self.scatter(output_block, count, 2 * half, True)
+        output = self.scatter(output_block, count, 2 * half, True, far)
         grad_tokens = self.scatter(input_block, count, 2 * half, False)
         return (output, grad_tokens, grad_gate, grad_up, grad_down)
 

time: 310 us -> 316 us (1.019)
  local copies, waits for them, and re-layouts: 20.3 us -> 30.8 us
  matrix products: 41.8 us -> 36.9 us
  Pallas kernels: 61 us -> 65.5 us
  waiting for transfers between devices: 139 us -> 135 us
    pallas_call x0 -> x5, Pallas kernels: none -> 36.8 us  [run(): pl.pallas_call(body, out_shape=list(outs), in_specs=[*specs, *[pl.BlockSp...]
    pallas_call x5 -> x2, Pallas kernels: 59.4 us -> 27.1 us  [call(): pl.pallas_call(kernel, out_shape=outs, in_specs=[pl.BlockSpec(memory_spac...]
    ppermute x11, waiting for transfers between devices: 48.8 us -> 39.1 us  [other(): return lax.ppermute(array, 'out', [(0, 1), (1, 0)])]
    unnamed x78 -> x104, local copies, waits for them, and re-layouts: 17.8 us -> 26.9 us
    ppermute x8, waiting for transfers between devices: 78.7 us -> 83.9 us  [chip(): return lax.ppermute(array, 'inp', [(at, at ^ 2) for at in range(4)])]
    dot_general x16 -> x12, matrix products: 41.8 us -> 36.9 us  [matmul(): lax.dot_general(a, b, ((contract[:1], contract[1:]), ((), ())), preferred...]
  transfers between devices with their start and end apart: 43 -> 43, of which waited for: 14 -> 16; matrix products, arithmetic and copies ran while one was open for 15% -> 13% of each run, Pallas kernels for 19% -> 20%
where the time goes in v11:
time: 316 us; the launch traced here: 315 us
  waiting for transfers between devices  135 us (43%)
  Pallas kernels  65.5 us (21%)
  matrix products  36.9 us (12%)
  local copies, waits for them, and re-layouts  30.8 us (10%)
  starting transfers between devices  28.6 us (9%)
  between operations  14.6 us (5%)
  other arithmetic  3.42 us (1%)
    ppermute x8, waiting for transfers between devices, chip(): return lax.ppermute(array, 'inp', [(at, at ^ 2) for at in range(4)])  83.9 us
    ppermute x11, waiting for transfers between devices, other(): return lax.ppermute(array, 'out', [(0, 1), (1, 0)])  39.1 us
    dot_general x12, matrix products, matmul(): lax.dot_general(a, b, ((contract[:1], contract[1:]), ((), ())), preferred...  36.9 us
    pallas_call x5, Pallas kernels, run(): pl.pallas_call(body, out_shape=list(outs), in_specs=[*specs, *[pl.BlockSp...  36.8 us
    pallas_call x2, Pallas kernels, call(): pl.pallas_call(kernel, out_shape=outs, in_specs=[pl.BlockSpec(memory_spac...  27.1 us
    unnamed x104, local copies, waits for them, and re-layouts  26.9 us
    ppermute x11, starting transfers between devices, other(): return lax.ppermute(array, 'out', [(0, 1), (1, 0)])  15.7 us
    all_gather x3, waiting for transfers between devices, gather_units(): return lax.all_gather(array, 'wt', axis=0, tiled=True)  11.4 us
  transfers between devices with their start and end apart: 43, of which 16 were waited for; matrix products, arithmetic and copies ran while one was open for 13% of the time, Pallas kernels for 20%

profile of v11, /device:TPU:0, one launch (start us, length us, event | category | flops | bytes accessed | tf_op | source)
XLA Modules:
  0.0 315.0 jit_solution(15775737879951688518)
XLA Ops:
  10.1 3.0 collective-permute-start.9
  13.1 11.9 %collective-permute-done.9 = bf16[256,1024]{1,0:T(8,128)(2,1)S(1)} collective-permute-done((bf16[256,1024]{1,0:T(8,128)(2,1)S(1)}, bf16[256,1024]{1,0:T(8,128)(2,1)S(1)}, u32[]{:S(2)}, u32[]{:S(2)}) %collective-permute-start.9) | collective-permute-done | bytes 524320 | tf_op jit(solution)/shard_map/ppermute | solution.py:165
  25.9 1.8 collective-permute-start.10
  27.8 1.5 collective-permute-start.1
  30.1 5.2 %collective-permute-done.10 = bf16[128,1024]{1,0:T(8,128)(2,1)S(1)} collective-permute-done((bf16[128,1024]{1,0:T(8,128)(2,1)S(1)}, bf16[128,1024]{1,0:T(8,128)(2,1)S(1)}, u32[]{:S(2)}, u32[]{:S(2)}) %collective-permute-start.10) | collective-permute-done | bytes 262176 | tf_op jit(solution)/shard_map/ppermute | solution.py:165
  35.3 1.7 collective-permute-start.11
  37.9 16.3 %collective-permute-done.1.refs_2_ = bf16[512,1024]{1,0:T(8,128)(2,1)} collective-permute-done((bf16[512,1024]{1,0:T(8,128)(2,1)}, bf16[512,1024]{1,0:T(8,128)(2,1)}, u32[]{:S(2)}, u32[]{:S(2)}) %collective-permute-start.1) | collective-permute-done | bytes 1048608 | tf_op jit(solution)/shard_map/ppermute | solution.py:162
  55.6 2.2 collective-permute-done.refs_1_
  57.8 16.5 %collective-permute-done.12.refs_2_ = bf16[512,1024]{1,0:T(8,128)(2,1)S(1)} collective-permute-done((bf16[512,1024]{1,0:T(8,128)(2,1)S(1)}, bf16[512,1024]{1,0:T(8,128)(2,1)S(1)}, u32[]{:S(2)}, u32[]{:S(2)}) %collective-permute-start.12) | collective-permute-done | bytes 1048608 | tf_op jit(solution)/shard_map/ppermute | solution.py:162
  74.3 1.4 slice.73
  75.8 1.6 collective-permute-start.3
  77.3 2.9 collective-permute-done.11.refs_1_
  80.2 1.7 collective-permute-start.13
  82.0 9.5 %collective-permute-done.2.refs_3_ = bf16[256,1024]{1,0:T(8,128)(2,1)S(1)} collective-permute-done((bf16[256,1024]{1,0:T(8,128)(2,1)S(1)}, bf16[256,1024]{1,0:T(8,128)(2,1)S(1)}, u32[]{:S(2)}, u32[]{:S(2)}) %collective-permute-start.2) | collective-permute-done | bytes 524320 | tf_op jit(solution)/shard_map/ppermute | solution.py:165
  91.4 1.7 collective-permute-start.14
  94.0 7.2 %collective-permute-done.13.refs_3_ = bf16[256,1024]{1,0:T(8,128)(2,1)} collective-permute-done((bf16[256,1024]{1,0:T(8,128)(2,1)S(1)}, bf16[256,1024]{1,0:T(8,128)(2,1)}, u32[]{:S(2)}, u32[]{:S(2)}) %collective-permute-start.13) | collective-permute-done | bytes 524320 | tf_op jit(solution)/shard_map/ppermute | solution.py:165
  113.7 16.7 %shard_map.92 = (bf16[2048,512]{1,0:T(8,128)(2,1)}, bf16[512,2048]{1,0:T(8,128)(2,1)}, bf16[2048,512]{1,0:T(8,128)(2,1)}, bf16[2048,512]{1,0:T(8,128)(2,1)}) custom-call(bf16[512,1024]{1,0:T(8,128)(2,1)} %bitcast.refs_0_, bf16[512,1024]{1,0:T(8,128)(2,1)} %collective-permute-done.refs_1_, bf16[512,1024]{1,0:T(8,128)(2,1)} %collective-permute-done.1.refs_2_, ...), custom_call_target="tpu_custom_call" | custom-call | flops 8589934592 | bytes 20971520 | tf_op jit(solution)/shard_map/pallas_call | solution.py:28
  130.4 10.4 %shard_map.93.refs_2_ = bf16[512,2048]{1,0:T(8,128)(2,1)} custom-call(bf16[512,1024]{1,0:T(8,128)(2,1)S(1)} %bitcast.20, bf16[512,1024]{1,0:T(8,128)(2,1)S(1)} %collective-permute-done.11.refs_1_, bf16[512,1024]{1,0:T(8,128)(2,1)S(1)} %collective-permute-done.12.refs_2_, bf16[256,1024]{1,0:T(8,128)(2,1)} %collective-permute-done.13.refs_3_, ...), custom_call_target="tpu_custom_call" | custom-call | flops 4294967296 | bytes 12582912 | tf_op jit(solution)/shard_map/pallas_call | solution.py:28
  141.1 11.4 %all-gather.8.cloned.1.call-done.refs_1_.refs_2_.refs_10_ = bf16[512,2048]{1,0:T(8,128)(2,1)} async-done(((bf16[128,2048]{1,0:T(8,128)(2,1)}), bf16[512,2048]{1,0:T(8,128)(2,1)}) %all-gather.8.cloned.1.call-update) | async-done | bytes 2097168 | tf_op jit(solution)/shard_map/all_gather | solution.py:248
  152.5 1.6 copy-done
  154.1 1.6 copy-done.5
  157.3 2.7 shard_map.95
  161.0 12.9 %shard_map.96 = (bf16[2048,1024]{1,0:T(8,128)(2,1)}, bf16[1024,2048]{1,0:T(8,128)(2,1)}) custom-call(bf16[512,1024]{1,0:T(8,128)(2,1)S(1)} %bitcast.21, bf16[512,1024]{1,0:T(8,128)(2,1)S(1)} %copy-done.9, bf16[512,1024]{1,0:T(8,128)(2,1)S(1)} %copy-done.7, bf16[256,1024]{1,0:T(8,128)(2,1)} %collective-permute-done.13.refs_3_, ...), custom_call_target="tpu_custom_call" | custom-call | flops 4294967296 | bytes 23068672 | tf_op jit(solution)/shard_map/pallas_call | solution.py:50
  174.0 9.9 %shard_map.98 = bf16[1024,1024]{1,0:T(8,128)(2,1)} custom-call(bf16[512,1024]{1,0:T(8,128)(2,1)} %bitcast.refs_0_, bf16[512,1024]{1,0:T(8,128)(2,1)} %collective-permute-done.refs_1_, bf16[512,1024]{1,0:T(8,128)(2,1)} %collective-permute-done.1.refs_2_, bf16[256,1024]{1,0:T(8,128)(2,1)S(1)} %copy-done.25, bf16[256,1024]{1,0:T(8,128)(2,1)S(1)} %copy-done.29, ...), custom_call_target="tpu_custom_call" | custom-call | flops 4294967296 | bytes 14680064 | tf_op jit(solution)/shard_map/pallas_call | solution.py:50
  184.7 4.3 %convolution_convert_fusion = bf16[512,1024]{1,0:T(8,128)(2,1)} fusion(bf16[1024,1024]{1,0:T(8,128)(2,1)} %all-gather.6.cloned.1.call-done.refs_11_, bf16[2048,1024]{1,0:T(8,128)(2,1)} %get-tuple-element.23), kind=kOutput, calls=%fused_computation.8 | convolution fusion | flops 1074266112 | bytes 4194304 | tf_op jit(solution)/shard_map/dot_general | solution.py:16
  189.4 2.3 convolution_convert_fusion.2
  191.7 2.6 fusion.10
  194.3 2.2 convolution_convert_fusion.1
  202.4 10.3 %shard_map.97 = bf16[1024,1024]{1,0:T(8,128)(2,1)} custom-call(bf16[512,1024]{1,0:T(8,128)(2,1)} %bitcast.refs_0_, bf16[512,1024]{1,0:T(8,128)(2,1)} %collective-permute-done.refs_1_, bf16[512,1024]{1,0:T(8,128)(2,1)} %collective-permute-done.1.refs_2_, bf16[256,1024]{1,0:T(8,128)(2,1)S(1)} %copy-done.26, bf16[256,1024]{1,0:T(8,128)(2,1)S(1)} %copy-done.30, ...), custom_call_target="tpu_custom_call" | custom-call | flops 4294967296 | bytes 14680064 | tf_op jit(solution)/shard_map/pallas_call | solution.py:50
  212.7 1.6 copy-done.2
  214.3 2.2 add_convert_fusion.7
  216.6 1.5 collective-permute-start.26
  218.3 2.3 convolution_convert_fusion.3
  220.6 1.5 collective-permute-start.23
  222.0 2.5 add_convert_fusion.2
  224.7 5.5 %collective-permute-done.26 = bf16[256,1024]{1,0:T(8,128)(2,1)S(1)} collective-permute-done((bf16[256,1024]{1,0:T(8,128)(2,1)S(1)}, bf16[256,1024]{1,0:T(8,128)(2,1)S(1)}, u32[]{:S(2)}, u32[]{:S(2)}) %collective-permute-start.26) | collective-permute-done | bytes 524320 | tf_op jit(solution)/shard_map/ppermute | solution.py:162
  231.5 3.0 add_convert_fusion.5
  234.5 1.5 collective-permute-start.27
  236.0 3.0 add_convert_fusion.6
  239.8 3.5 %add_convert_fusion.3 = bf16[512,1024]{1,0:T(8,128)(2,1)} fusion(bf16[512,1024]{1,0:T(8,128)(2,1)} %collective-permute-done.29, bf16[1024,1024]{1,0:T(8,128)(2,1)S(1)} %copy-done.45, bf16[2048,1024]{1,0:T(8,128)(2,1)S(1)} %copy-done.43), kind=kOutput, calls=%fused_computation.3 | convolution fusion | flops 1075314688 | bytes 5242880 | tf_op jit(solution)/shard_map/dot_general | solution.py:16
  243.2 13.0 %collective-permute-done.33 = bf16[512,1024]{1,0:T(8,128)(2,1)S(1)} collective-permute-done((bf16[512,1024]{1,0:T(8,128)(2,1)S(1)}, bf16[512,1024]{1,0:T(8,128)(2,1)S(1)}, u32[]{:S(2)}, u32[]{:S(2)}) %collective-permute-start.33) | collective-permute-done | bytes 1048608 | tf_op jit(solution)/shard_map/ppermute | solution.py:162
  259.1 1.4 collective-permute-start.34
  260.8 18.0 %collective-permute-done.24 = bf16[512,1024]{1,0:T(8,128)(2,1)} collective-permute-done((bf16[512,1024]{1,0:T(8,128)(2,1)}, bf16[512,1024]{1,0:T(8,128)(2,1)}, u32[]{:S(2)}, u32[]{:S(2)}) %collective-permute-start.24) | collective-permute-done | bytes 1048608 | tf_op jit(solution)/shard_map/ppermute | solution.py:162
  278.9 3.9 %add_convert_fusion.4 = bf16[512,1024]{1,0:T(8,128)(2,1)} fusion(bf16[512,1024]{1,0:T(8,128)(2,1)} %collective-permute-done.27, bf16[512,1024]{1,0:T(8,128)(2,1)} %collective-permute-done.24, bf16[512,1024]{1,0:T(8,128)(2,1)} %copy-done.49, bf16[512,2048]{1,0:T(8,128)(2,1)S(1)} %copy-done.2, bf16[2048,512]{1,0:T(8,128)(2,1)} %get-tuple-element.16.refs_0_), kind=kOutput, calls=%fused_computation.4 | convolution fusion | flops 540540928 | bytes 5767168 | tf_op jit(solution)/shard_map/dot_general | solution.py:16
  282.9 1.4 collective-permute-start.36
  285.0 14.2 %collective-permute-done.30 = bf16[512,1024]{1,0:T(8,128)(2,1)} collective-permute-done((bf16[512,1024]{1,0:T(8,128)(2,1)}, bf16[512,1024]{1,0:T(8,128)(2,1)}, u32[]{:S(2)}, u32[]{:S(2)}) %collective-permute-start.30) | collective-permute-done | bytes 1048608 | tf_op jit(solution)/shard_map/ppermute | solution.py:162
  299.2 5.2 %add_convert_fusion = bf16[512,1024]{1,0:T(8,128)(2,1)} fusion(bf16[512,1024]{1,0:T(8,128)(2,1)} %collective-permute-done.34, bf16[512,1024]{1,0:T(8,128)(2,1)} %collective-permute-done.30, bf16[512,1024]{1,0:T(8,128)(2,1)} %collective-permute-done.28, bf16[1024,1024]{1,0:T(8,128)(2,1)} %all-gather.4.cloned.1.call-done.refs_10_, ...), kind=kOutput, calls=%fused_computation | convolution fusion | flops 1077411840 | bytes 7340032 | tf_op jit(solution)/shard_map/dot_general | solution.py:16
  306.5 1.6 shard_map.99
  (182 shorter events, 38.6 us)
Async XLA Ops:
  7.2 99.8 %all-gather.4.cloned.1.call-start = ((), (), s32[]{:S(2)}) async-start(), calls=%async_computation.3 | async-start | bytes 2621440 | tf_op jit(solution)/shard_map/all_gather | solution.py:248
  9.6 20.1 %copy-start.10 = (bf16[2,256,1024]{2,1,0:T(8,128)(2,1)S(1)}, bf16[2,256,1024]{2,1,0:T(8,128)(2,1)}, u32[]{:S(2)}) copy-start(bf16[2,256,1024]{2,1,0:T(8,128)(2,1)} %param.9) | copy-start | bytes 3145732
  9.7 97.3 %all-gather.6.cloned.1.call-start = ((), (), s32[]{:S(2)}) async-start(), calls=%async_computation.4 | async-start | bytes 2621440 | tf_op jit(solution)/shard_map/all_gather | solution.py:248
  10.1 15.0 %collective-permute-start.9 = (bf16[256,1024]{1,0:T(8,128)(2,1)S(1)}, bf16[256,1024]{1,0:T(8,128)(2,1)S(1)}, u32[]{:S(2)}, u32[]{:S(2)}) collective-permute-start(bf16[256,1024]{1,0:T(8,128)(2,1)S(1)} %pad_maximum_fusion.1), channel_id=1, source_target_pairs={{0,1},{1,0},{2,3},{3,2},{4,5},{5,4},{6,7},{7,6},{8,9},{9,8},{10,11... | collective-permute-start | bytes 1572872 | tf_op jit(solution)/shard_map/ppermute | solution.py:165
  25.8 126.6 %all-gather.8.cloned.1.call-start = ((), (), s32[]{:S(2)}) async-start(), calls=%async_computation.5 | async-start | bytes 2621440 | tf_op jit(solution)/shard_map/all_gather | solution.py:248
  25.9 9.3 %collective-permute-start.10 = (bf16[128,1024]{1,0:T(8,128)(2,1)S(1)}, bf16[128,1024]{1,0:T(8,128)(2,1)S(1)}, u32[]{:S(2)}, u32[]{:S(2)}) collective-permute-start(bf16[128,1024]{1,0:T(8,128)(2,1)S(1)} %get-tuple-element.32), channel_id=1, source_target_pairs={{0,1},{1,0},{2,3},{3,2},{4,5},{5,4},{6,7},{7,6},{8,9},{9,8},{10,11... | collective-permute-start | bytes 786440 | tf_op jit(solution)/shard_map/ppermute | solution.py:165
  27.8 26.4 %collective-permute-start.1 = (bf16[512,1024]{1,0:T(8,128)(2,1)}, bf16[512,1024]{1,0:T(8,128)(2,1)}, u32[]{:S(2)}, u32[]{:S(2)}) collective-permute-start(bf16[512,1024]{1,0:T(8,128)(2,1)} %bitcast.refs_0_), channel_id=1, source_target_pairs={{0,16},{8,24},{16,0},{24,8},{1,17},{9,25},{17,1},{25,9},{2,18},{10... | collective-permute-start | bytes 3145736 | tf_op jit(solution)/shard_map/ppermute | solution.py:162
  29.2 28.6 %collective-permute-start = (bf16[512,1024]{1,0:T(8,128)(2,1)}, bf16[512,1024]{1,0:T(8,128)(2,1)}, u32[]{:S(2)}, u32[]{:S(2)}) collective-permute-start(bf16[512,1024]{1,0:T(8,128)(2,1)} %bitcast.refs_0_), channel_id=1, source_target_pairs={{0,1},{1,0},{2,3},{3,2},{4,5},{5,4},{6,7},{7,6},{8,9},{9,8},{10,11... | collective-permute-start | bytes 3145736 | tf_op jit(solution)/shard_map/ppermute | solution.py:165
  29.8 44.5 %collective-permute-start.12 = (bf16[512,1024]{1,0:T(8,128)(2,1)S(1)}, bf16[512,1024]{1,0:T(8,128)(2,1)S(1)}, u32[]{:S(2)}, u32[]{:S(2)}) collective-permute-start(bf16[512,1024]{1,0:T(8,128)(2,1)S(1)} %bitcast.17), channel_id=1, source_target_pairs={{0,16},{8,24},{16,0},{24,8},{1,17},{9,25},{17,1},{25,9},{2,18},{10... | collective-permute-start | bytes 3145736 | tf_op jit(solution)/shard_map/ppermute | solution.py:162
  30.1 45.7 %collective-permute-start.4 = (bf16[512,1024]{1,0:T(8,128)(2,1)}, bf16[512,1024]{1,0:T(8,128)(2,1)}, u32[]{:S(2)}, u32[]{:S(2)}) collective-permute-start(bf16[512,1024]{1,0:T(8,128)(2,1)} %bitcast.refs_0_), channel_id=1, source_target_pairs={{0,8},{8,0},{16,24},{24,16},{1,9},{9,1},{17,25},{25,17},{2,10},{10... | collective-permute-start | bytes 3145736 | tf_op jit(solution)/shard_map/ppermute | solution.py:159
  35.3 44.9 %collective-permute-start.11 = (bf16[512,1024]{1,0:T(8,128)(2,1)S(1)}, bf16[512,1024]{1,0:T(8,128)(2,1)S(1)}, u32[]{:S(2)}, u32[]{:S(2)}) collective-permute-start(bf16[512,1024]{1,0:T(8,128)(2,1)S(1)} %bitcast.18), channel_id=1, source_target_pairs={{0,1},{1,0},{2,3},{3,2},{4,5},{5,4},{6,7},{7,6},{8,9},{9,8},{10,11... | collective-permute-start | bytes 3145736 | tf_op jit(solution)/shard_map/ppermute | solution.py:165
  37.9 159.4 %reduce-scatter.4.cloned.1.call-start = ((), (), s32[]{:S(2)}) async-start(), calls=%async_computation.6 | async-start | bytes 2621440 | tf_op jit(solution)/shard_map/reduce_scatter | solution.py:251
  55.2 36.2 %collective-permute-start.2 = (bf16[256,1024]{1,0:T(8,128)(2,1)S(1)}, bf16[256,1024]{1,0:T(8,128)(2,1)S(1)}, u32[]{:S(2)}, u32[]{:S(2)}) collective-permute-start(bf16[256,1024]{1,0:T(8,128)(2,1)S(1)} %slice.72), channel_id=1, source_target_pairs={{0,1},{1,0},{2,3},{3,2},{4,5},{5,4},{6,7},{7,6},{8,9},{9,8},{10,11... | collective-permute-start | bytes 1572872 | tf_op jit(solution)/shard_map/ppermute | solution.py:165
  57.8 44.6 %collective-permute-start.5 = (bf16[512,1024]{1,0:T(8,128)(2,1)}, bf16[512,1024]{1,0:T(8,128)(2,1)S(1)}, u32[]{:S(2)}, u32[]{:S(2)}) collective-permute-start(bf16[512,1024]{1,0:T(8,128)(2,1)} %collective-permute-done.refs_1_), channel_id=1, source_target_pairs={{0,8},{8,0},{16,24},{24,16},{1,9},{9,1},{17,25},{25,17},{2,10},{10... | collective-permute-start | bytes 3145736 | tf_op jit(solution)/shard_map/ppermute | solution.py:159
  74.3 56.1 %copy-start.6 = (bf16[512,1024]{1,0:T(8,128)(2,1)}, bf16[512,1024]{1,0:T(8,128)(2,1)S(1)}, u32[]{:S(2)}) copy-start(bf16[512,1024]{1,0:T(8,128)(2,1)S(1)} %collective-permute-done.12.refs_2_) | copy-start | bytes 3145732
  74.3 29.5 %collective-permute-start.6 = (bf16[512,1024]{1,0:T(8,128)(2,1)}, bf16[512,1024]{1,0:T(8,128)(2,1)S(1)}, u32[]{:S(2)}, u32[]{:S(2)}) collective-permute-start(bf16[512,1024]{1,0:T(8,128)(2,1)} %collective-permute-done.1.refs_2_), channel_id=1, source_target_pairs={{0,8},{8,0},{16,24},{24,16},{1,9},{9,1},{17,25},{25,17},{2,10},{10... | collective-permute-start | bytes 3145736 | tf_op jit(solution)/shard_map/ppermute | solution.py:159
  75.8 17.4 %collective-permute-start.3 = (bf16[256,1024]{1,0:T(8,128)(2,1)S(1)}, bf16[256,1024]{1,0:T(8,128)(2,1)S(1)}, u32[]{:S(2)}, u32[]{:S(2)}) collective-permute-start(bf16[256,1024]{1,0:T(8,128)(2,1)S(1)} %slice.73), channel_id=1, source_target_pairs={{0,16},{8,24},{16,0},{24,8},{1,17},{9,25},{17,1},{25,9},{2,18},{10... | collective-permute-start | bytes 1572872 | tf_op jit(solution)/shard_map/ppermute | solution.py:162
  80.2 50.2 %copy-start.8 = (bf16[512,1024]{1,0:T(8,128)(2,1)}, bf16[512,1024]{1,0:T(8,128)(2,1)S(1)}, u32[]{:S(2)}) copy-start(bf16[512,1024]{1,0:T(8,128)(2,1)S(1)} %collective-permute-done.11.refs_1_) | copy-start | bytes 3145732
  80.2 20.9 %collective-permute-start.13 = (bf16[256,1024]{1,0:T(8,128)(2,1)S(1)}, bf16[256,1024]{1,0:T(8,128)(2,1)}, u32[]{:S(2)}, u32[]{:S(2)}) collective-permute-start(bf16[256,1024]{1,0:T(8,128)(2,1)S(1)} %slice.75), channel_id=1, source_target_pairs={{0,1},{1,0},{2,3},{3,2},{4,5},{5,4},{6,7},{7,6},{8,9},{9,8},{10,11... | collective-permute-start | bytes 1572872 | tf_op jit(solution)/shard_map/ppermute | solution.py:165
  91.4 10.9 %collective-permute-start.14 = (bf16[256,1024]{1,0:T(8,128)(2,1)S(1)}, bf16[256,1024]{1,0:T(8,128)(2,1)}, u32[]{:S(2)}, u32[]{:S(2)}) collective-permute-start(bf16[256,1024]{1,0:T(8,128)(2,1)S(1)} %slice.76), channel_id=1, source_target_pairs={{0,16},{8,24},{16,0},{24,8},{1,17},{9,25},{17,1},{25,9},{2,18},{10... | collective-permute-start | bytes 1572872 | tf_op jit(solution)/shard_map/ppermute | solution.py:162
  93.1 11.8 %collective-permute-start.7 = (bf16[256,1024]{1,0:T(8,128)(2,1)S(1)}, bf16[256,1024]{1,0:T(8,128)(2,1)S(1)}, u32[]{:S(2)}, u32[]{:S(2)}) collective-permute-start(bf16[256,1024]{1,0:T(8,128)(2,1)S(1)} %collective-permute-done.2.refs_3_), channel_id=1, source_target_pairs={{0,8},{8,0},{16,24},{24,16},{1,9},{9,1},{17,25},{25,17},{2,10},{10... | collective-permute-start | bytes 1572872 | tf_op jit(solution)/shard_map/ppermute | solution.py:159
  101.1 4.9 %collective-permute-start.8 = (bf16[256,1024]{1,0:T(8,128)(2,1)S(1)}, bf16[256,1024]{1,0:T(8,128)(2,1)S(1)}, u32[]{:S(2)}, u32[]{:S(2)}) collective-permute-start(bf16[256,1024]{1,0:T(8,128)(2,1)S(1)} %collective-permute-done.3.refs_4_), channel_id=1, source_target_pairs={{0,8},{8,0},{16,24},{24,16},{1,9},{9,1},{17,25},{25,17},{2,10},{10... | collective-permute-start | bytes 1572872 | tf_op jit(solution)/shard_map/ppermute | solution.py:159
  102.3 28.1 %collective-permute-start.15 = (bf16[512,1024]{1,0:T(8,128)(2,1)S(1)}, bf16[512,1024]{1,0:T(8,128)(2,1)}, u32[]{:S(2)}, u32[]{:S(2)}) collective-permute-start(bf16[512,1024]{1,0:T(8,128)(2,1)S(1)} %bitcast.19), channel_id=1, source_target_pairs={{0,8},{8,0},{16,24},{24,16},{1,9},{9,1},{17,25},{25,17},{2,10},{10... | collective-permute-start | bytes 3145736 | tf_op jit(solution)/shard_map/ppermute | solution.py:159
  103.4 27.0 %collective-permute-start.16 = (bf16[512,1024]{1,0:T(8,128)(2,1)S(1)}, bf16[512,1024]{1,0:T(8,128)(2,1)}, u32[]{:S(2)}, u32[]{:S(2)}) collective-permute-start(bf16[512,1024]{1,0:T(8,128)(2,1)S(1)} %collective-permute-done.11.refs_1_), channel_id=1, source_target_pairs={{0,8},{8,0},{16,24},{24,16},{1,9},{9,1},{17,25},{25,17},{2,10},{10... | collective-permute-start | bytes 3145736 | tf_op jit(solution)/shard_map/ppermute | solution.py:159
  104.8 25.6 %collective-permute-start.17 = (bf16[512,1024]{1,0:T(8,128)(2,1)S(1)}, bf16[512,1024]{1,0:T(8,128)(2,1)}, u32[]{:S(2)}, u32[]{:S(2)}) collective-permute-start(bf16[512,1024]{1,0:T(8,128)(2,1)S(1)} %collective-permute-done.12.refs_2_), channel_id=1, source_target_pairs={{0,8},{8,0},{16,24},{24,16},{1,9},{9,1},{17,25},{25,17},{2,10},{10... | collective-permute-start | bytes 3145736 | tf_op jit(solution)/shard_map/ppermute | solution.py:159
  105.7 24.7 %collective-permute-start.18 = (bf16[256,1024]{1,0:T(8,128)(2,1)}, bf16[256,1024]{1,0:T(8,128)(2,1)}, u32[]{:S(2)}, u32[]{:S(2)}) collective-permute-start(bf16[256,1024]{1,0:T(8,128)(2,1)} %collective-permute-done.13.refs_3_), channel_id=1, source_target_pairs={{0,8},{8,0},{16,24},{24,16},{1,9},{9,1},{17,25},{25,17},{2,10},{10... | collective-permute-start | bytes 1572872 | tf_op jit(solution)/shard_map/ppermute | solution.py:159
  106.8 23.6 %collective-permute-start.19 = (bf16[256,1024]{1,0:T(8,128)(2,1)}, bf16[256,1024]{1,0:T(8,128)(2,1)}, u32[]{:S(2)}, u32[]{:S(2)}) collective-permute-start(bf16[256,1024]{1,0:T(8,128)(2,1)} %collective-permute-done.14.refs_4_), channel_id=1, source_target_pairs={{0,8},{8,0},{16,24},{24,16},{1,9},{9,1},{17,25},{25,17},{2,10},{10... | collective-permute-start | bytes 1572872 | tf_op jit(solution)/shard_map/ppermute | solution.py:159
  140.9 143.4 %reduce-scatter.8.cloned.1.call-start = ((), (), s32[]{:S(2)}) async-start(), calls=%async_computation.8 | async-start | bytes 2621440 | tf_op jit(solution)/shard_map/reduce_scatter | solution.py:251
  183.9 121.5 %reduce-scatter.6.cloned.1.call-start = ((), (), s32[]{:S(2)}) async-start(), calls=%async_computation.7 | async-start | bytes 2621440 | tf_op jit(solution)/shard_map/reduce_scatter | solution.py:251
  184.0 40.6 %collective-permute-start.25 = (bf16[512,1024]{1,0:T(8,128)(2,1)}, bf16[512,1024]{1,0:T(8,128)(2,1)}, u32[]{:S(2)}, u32[]{:S(2)}) collective-permute-start(bf16[512,1024]{1,0:T(8,128)(2,1)} %get-tuple-element.20.refs_14_), channel_id=1, source_target_pairs={{0,8},{8,0},{16,24},{24,16},{1,9},{9,1},{17,25},{25,17},{2,10},{10... | collective-permute-start | bytes 3145736 | tf_op jit(solution)/shard_map/ppermute | solution.py:159
  184.1 28.6 %collective-permute-start.22 = (bf16[512,1024]{1,0:T(8,128)(2,1)S(1)}, bf16[512,1024]{1,0:T(8,128)(2,1)}, u32[]{:S(2)}, u32[]{:S(2)}) collective-permute-start(bf16[512,1024]{1,0:T(8,128)(2,1)S(1)} %shard_map.94.refs_3_.refs_13_), channel_id=1, source_target_pairs={{0,8},{8,0},{16,24},{24,16},{1,9},{9,1},{17,25},{25,17},{2,10},{10... | collective-permute-start | bytes 3145736 | tf_op jit(solution)/shard_map/ppermute | solution.py:159
  184.6 49.9 %collective-permute-start.21 = (bf16[512,1024]{1,0:T(8,128)(2,1)}, bf16[512,1024]{1,0:T(8,128)(2,1)}, u32[]{:S(2)}, u32[]{:S(2)}) collective-permute-start(bf16[512,1024]{1,0:T(8,128)(2,1)} %get-tuple-element.19.refs_15_), channel_id=1, source_target_pairs={{0,8},{8,0},{16,24},{24,16},{1,9},{9,1},{17,25},{25,17},{2,10},{10... | collective-permute-start | bytes 3145736 | tf_op jit(solution)/shard_map/ppermute | solution.py:159
  188.9 31.6 %collective-permute-start.32 = (bf16[512,1024]{1,0:T(8,128)(2,1)}, bf16[512,1024]{1,0:T(8,128)(2,1)}, u32[]{:S(2)}, u32[]{:S(2)}) collective-permute-start(bf16[512,1024]{1,0:T(8,128)(2,1)} %convolution_convert_fusion), channel_id=1, source_target_pairs={{0,8},{8,0},{16,24},{24,16},{1,9},{9,1},{17,25},{25,17},{2,10},{10... | collective-permute-start | bytes 3145736 | tf_op jit(solution)/shard_map/ppermute | solution.py:159
  191.6 47.3 %collective-permute-start.29 = (bf16[512,1024]{1,0:T(8,128)(2,1)}, bf16[512,1024]{1,0:T(8,128)(2,1)}, u32[]{:S(2)}, u32[]{:S(2)}) collective-permute-start(bf16[512,1024]{1,0:T(8,128)(2,1)} %convolution_convert_fusion.2), channel_id=1, source_target_pairs={{0,8},{8,0},{16,24},{24,16},{1,9},{9,1},{17,25},{25,17},{2,10},{10... | collective-permute-start | bytes 3145736 | tf_op jit(solution)/shard_map/ppermute | solution.py:159
  216.6 13.5 %collective-permute-start.26 = (bf16[256,1024]{1,0:T(8,128)(2,1)S(1)}, bf16[256,1024]{1,0:T(8,128)(2,1)S(1)}, u32[]{:S(2)}, u32[]{:S(2)}) collective-permute-start(bf16[256,1024]{1,0:T(8,128)(2,1)S(1)} %get-tuple-element.28), channel_id=1, source_target_pairs={{0,16},{8,24},{16,0},{24,8},{1,17},{9,25},{17,1},{25,9},{2,18},{10... | collective-permute-start | bytes 1572872 | tf_op jit(solution)/shard_map/ppermute | solution.py:162
  220.6 13.9 %collective-permute-start.23 = (bf16[256,1024]{1,0:T(8,128)(2,1)S(1)}, bf16[256,1024]{1,0:T(8,128)(2,1)S(1)}, u32[]{:S(2)}, u32[]{:S(2)}) collective-permute-start(bf16[256,1024]{1,0:T(8,128)(2,1)S(1)} %get-tuple-element.27), channel_id=1, source_target_pairs={{0,1},{1,0},{2,3},{3,2},{4,5},{5,4},{6,7},{7,6},{8,9},{9,8},{10,11... | collective-permute-start | bytes 1572872 | tf_op jit(solution)/shard_map/ppermute | solution.py:165
  224.6 18.6 %collective-permute-start.31 = (bf16[512,1024]{1,0:T(8,128)(2,1)S(1)}, bf16[512,1024]{1,0:T(8,128)(2,1)S(1)}, u32[]{:S(2)}, u32[]{:S(2)}) collective-permute-start(bf16[512,1024]{1,0:T(8,128)(2,1)S(1)} %copy-done.48), channel_id=1, source_target_pairs={{0,8},{8,0},{16,24},{24,16},{1,9},{9,1},{17,25},{25,17},{2,10},{10... | collective-permute-start | bytes 3145736 | tf_op jit(solution)/shard_map/ppermute | solution.py:159
  230.2 26.1 %collective-permute-start.33 = (bf16[512,1024]{1,0:T(8,128)(2,1)S(1)}, bf16[512,1024]{1,0:T(8,128)(2,1)S(1)}, u32[]{:S(2)}, u32[]{:S(2)}) collective-permute-start(bf16[512,1024]{1,0:T(8,128)(2,1)S(1)} %add_convert_fusion.2), channel_id=1, source_target_pairs={{0,16},{8,24},{16,0},{24,8},{1,17},{9,25},{17,1},{25,9},{2,18},{10... | collective-permute-start | bytes 3145736 | tf_op jit(solution)/shard_map/ppermute | solution.py:162
  234.5 23.7 %collective-permute-start.20 = (bf16[512,1024]{1,0:T(8,128)(2,1)S(1)}, bf16[512,1024]{1,0:T(8,128)(2,1)S(1)}, u32[]{:S(2)}, u32[]{:S(2)}) collective-permute-start(bf16[512,1024]{1,0:T(8,128)(2,1)S(1)} %copy-done.13), channel_id=1, source_target_pairs={{0,8},{8,0},{16,24},{24,16},{1,9},{9,1},{17,25},{25,17},{2,10},{10... | collective-permute-start | bytes 3145736 | tf_op jit(solution)/shard_map/ppermute | solution.py:159
  234.5 26.3 %collective-permute-start.27 = (bf16[512,1024]{1,0:T(8,128)(2,1)}, bf16[512,1024]{1,0:T(8,128)(2,1)}, u32[]{:S(2)}, u32[]{:S(2)}) collective-permute-start(bf16[512,1024]{1,0:T(8,128)(2,1)} %add_convert_fusion.5), channel_id=1, source_target_pairs={{0,1},{1,0},{2,3},{3,2},{4,5},{5,4},{6,7},{7,6},{8,9},{9,8},{10,11... | collective-permute-start | bytes 3145736 | tf_op jit(solution)/shard_map/ppermute | solution.py:165
  239.0 18.6 %copy-start.39 = (f32[512,1024]{1,0:T(8,128)S(1)}, f32[512,1024]{1,0:T(8,128)}, u32[]{:S(2)}) copy-start(f32[512,1024]{1,0:T(8,128)} %fusion.10) | copy-start | bytes 6291460
  239.0 39.9 %collective-permute-start.24 = (bf16[512,1024]{1,0:T(8,128)(2,1)}, bf16[512,1024]{1,0:T(8,128)(2,1)}, u32[]{:S(2)}, u32[]{:S(2)}) collective-permute-start(bf16[512,1024]{1,0:T(8,128)(2,1)} %add_convert_fusion.6), channel_id=1, source_target_pairs={{0,16},{8,24},{16,0},{24,8},{1,17},{9,25},{17,1},{25,9},{2,18},{10... | collective-permute-start | bytes 3145736 | tf_op jit(solution)/shard_map/ppermute | solution.py:162
  243.2 41.7 %collective-permute-start.28 = (bf16[512,1024]{1,0:T(8,128)(2,1)}, bf16[512,1024]{1,0:T(8,128)(2,1)}, u32[]{:S(2)}, u32[]{:S(2)}) collective-permute-start(bf16[512,1024]{1,0:T(8,128)(2,1)} %convolution_convert_fusion.3), channel_id=1, source_target_pairs={{0,8},{8,0},{16,24},{24,16},{1,9},{9,1},{17,25},{25,17},{2,10},{10... | collective-permute-start | bytes 3145736 | tf_op jit(solution)/shard_map/ppermute | solution.py:159
  256.3 42.9 %collective-permute-start.30 = (bf16[512,1024]{1,0:T(8,128)(2,1)}, bf16[512,1024]{1,0:T(8,128)(2,1)}, u32[]{:S(2)}, u32[]{:S(2)}) collective-permute-start(bf16[512,1024]{1,0:T(8,128)(2,1)} %add_convert_fusion.3), channel_id=1, source_target_pairs={{0,16},{8,24},{16,0},{24,8},{1,17},{9,25},{17,1},{25,9},{2,18},{10... | collective-permute-start | bytes 3145736 | tf_op jit(solution)/shard_map/ppermute | solution.py:162
  259.1 40.0 %collective-permute-start.34 = (bf16[512,1024]{1,0:T(8,128)(2,1)S(1)}, bf16[512,1024]{1,0:T(8,128)(2,1)}, u32[]{:S(2)}, u32[]{:S(2)}) collective-permute-start(bf16[512,1024]{1,0:T(8,128)(2,1)S(1)} %add_convert_fusion.1), channel_id=1, source_target_pairs={{0,1},{1,0},{2,3},{3,2},{4,5},{5,4},{6,7},{7,6},{8,9},{9,8},{10,11... | collective-permute-start | bytes 3145736 | tf_op jit(solution)/shard_map/ppermute | solution.py:165
  260.6 22.2 %copy-start.15 = (bf16[128,2048]{1,0:T(8,128)(2,1)S(1)}, bf16[128,2048]{1,0:T(8,128)(2,1)}, u32[]{:S(2)}) copy-start(bf16[128,2048]{1,0:T(8,128)(2,1)} %reduce-scatter.4.cloned.1.call-done.refs_11_) | copy-start | bytes 1572868
  282.9 21.5 %collective-permute-start.36 = (bf16[128,1024]{1,0:T(8,128)(2,1)S(1)}, bf16[128,1024]{1,0:T(8,128)(2,1)S(1)}, u32[]{:S(2)}, u32[]{:S(2)}) collective-permute-start(bf16[128,1024]{1,0:T(8,128)(2,1)S(1)} %get-tuple-element.30), channel_id=1, source_target_pairs={{0,1},{1,0},{2,3},{3,2},{4,5},{5,4},{6,7},{7,6},{8,9},{9,8},{10,11... | collective-permute-start | bytes 786440 | tf_op jit(solution)/shard_map/ppermute | solution.py:165
  284.2 21.2 %collective-permute-start.35 = (bf16[256,1024]{1,0:T(8,128)(2,1)}, bf16[256,1024]{1,0:T(8,128)(2,1)S(1)}, u32[]{:S(2)}, u32[]{:S(2)}) collective-permute-start(bf16[256,1024]{1,0:T(8,128)(2,1)} %reduce-scatter.8.cloned.1.call-done), channel_id=1, source_target_pairs={{0,1},{1,0},{2,3},{3,2},{4,5},{5,4},{6,7},{7,6},{8,9},{9,8},{10,11... | collective-permute-start | bytes 1572872 | tf_op jit(solution)/shard_map/ppermute | solution.py:165
  (45 other events, 193.1 us)
Sparse Core Ops, SparseCore 0:
  10.1 48.6 all-gather.3
  61.0 44.6 all-gather.5
  107.8 44.6 all-gather.7
  154.6 42.5 reduce-scatter.3
  199.5 43.1 reduce-scatter.7
  244.8 43.1 reduce-scatter.5

commit v12 on v10

--- a/solution.py
+++ b/solution.py
@@ -37,6 +37,25 @@
 
 def shape(*dims):
     return jax.ShapeDtypeStruct(dims, BF16)
+
+
+def run(kernel, outs, flops, args, after=(), specs=None, scratch=(), limit=24):
+    everything = [*args, *after]
+    moved = sum(a.size * a.dtype.itemsize for a in args) + sum(o.size * o.dtype.itemsize for o in outs)
+    specs = specs or [pl.BlockSpec(memory_space=pltpu.VMEM)] * len(args)
+
+    def body(*refs):
+        kernel(*refs[: len(args)], *refs[len(everything) :])
+
+    return pl.pallas_call(
+        body,
+        out_shape=list(outs),
+        in_specs=[*specs, *[pl.BlockSpec(memory_space=pl.ANY)] * len(after)],
+        out_specs=[pl.BlockSpec(memory_space=pltpu.VMEM)] * len(outs),
+        scratch_shapes=list(scratch),
+        compiler_params=pltpu.CompilerParams(vmem_limit_bytes=limit * MIB),
+        cost_estimate=pl.CostEstimate(flops=flops, bytes_accessed=moved, transcendentals=0),
+    )(*everything)
 
 
 class Rows:
@@ -161,8 +180,8 @@
         batch = quarter // 2
         corner = sums[1, 1].astype(BF16)
         if split:
-            from_other = self.other(corner[:batch]).astype(F32)
-            from_chip = self.chip(corner[batch:]).astype(F32)
+            self.came = [self.other(corner[:batch]), self.chip(corner[batch:])]
+            from_other, from_chip = [piece.astype(F32) for piece in self.came]
             zeros = jnp.zeros_like(from_other)
             to_chip = sums[1, 0] + jnp.concatenate([from_other, zeros])
             to_other = sums[0, 1] + jnp.concatenate([zeros, from_chip])
@@ -207,24 +226,27 @@
             hidden_turned,
         )
         down_sum = scatter_units(down_term)
-        act, act_turned = call(
+        act, act_turned = run(
             functools.partial(grads_kernel, rows_cot, width),
             [shape(count, 2 * units), shape(2 * units, count)],
             4 * count * units * half,
-            *rows_cot.pieces,
-            down,
-            silu,
-            rest,
+            [*rows_cot.pieces, down, silu, rest],
+            limit=44,
         )
+        def output_block(at, other):
+            return matmul(hidden[at], down[:, other * half : (other + 1) * half], (1, 0))
+
+        output = self.scatter(output_block, count, 2 * half, True)
         terms = [
-            call(
+            run(
                 functools.partial(weight_kernel, rows_in, (side,), 256),
                 [shape(2 * units, half)],
                 4 * count * units * half,
-                *rows_in.pieces,
-                act_turned,
+                [*rows_in.pieces, act_turned],
+                after=after,
+                limit=44,
             )[0]
-            for side in (1, 0)
+            for side, after in ((1, []), (0, self.came))
         ]
         other_sum, own_sum = scatter_units(terms[0]), scatter_units(terms[1])
         down_back = self.other(down_sum[:, half:])
@@ -239,13 +261,9 @@
             cost_estimate=pl.CostEstimate(flops=0, bytes_accessed=5 * MIB, transcendentals=0),
         )(lax.axis_index("out").astype(jnp.int32).reshape(1), own_sum, units_back)
 
-        def output_block(at, other):
-            return matmul(hidden[at], down[:, other * half : (other + 1) * half], (1, 0))
-
         def input_block(at, other):
             return matmul(act[at], other_units if other else own_units, (1, 0))
 
-        output = self.scatter(output_block, count, 2 * half, True)
         grad_tokens = self.scatter(input_block, count, 2 * half, False)
         return (output, grad_tokens, grad_gate, grad_up, grad_down)
 

time: 310 us -> 311 us (level)
    pallas_call x5 -> x2, Pallas kernels: 59.4 us -> 27.3 us  [call(): pl.pallas_call(kernel, out_shape=outs, in_specs=[pl.BlockSpec(memory_spac...]
    pallas_call x0 -> x3, Pallas kernels: none -> 32.1 us  [run(): pl.pallas_call(body, out_shape=list(outs), in_specs=[*specs, *[pl.BlockSp...]
    unnamed x78 -> x80, local copies, waits for them, and re-layouts: 17.8 us -> 16.2 us
  transfers between devices with their start and end apart: 43 -> 43, of which waited for: 14 -> 15; matrix products, arithmetic and copies ran while one was open for 15% -> 16% of each run, Pallas kernels for 19% -> 19%
where the time goes in v12:
time: 311 us; the launch traced here: 310 us
  waiting for transfers between devices  140 us (45%)
  Pallas kernels  61 us (20%)
  matrix products  43.4 us (14%)
  starting transfers between devices  27 us (9%)
  local copies, waits for them, and re-layouts  18.8 us (6%)
  between operations  14.5 us (5%)
  other arithmetic  5.7 us (2%)
    ppermute x8, waiting for transfers between devices, chip(): return lax.ppermute(array, 'inp', [(at, at ^ 2) for at in range(4)])  80.7 us
    ppermute x11, waiting for transfers between devices, other(): return lax.ppermute(array, 'out', [(0, 1), (1, 0)])  47.6 us
    dot_general x16, matrix products, matmul(): lax.dot_general(a, b, ((contract[:1], contract[1:]), ((), ())), preferred...  43.4 us
    pallas_call x3, Pallas kernels, run(): pl.pallas_call(body, out_shape=list(outs), in_specs=[*specs, *[pl.BlockSp...  32.1 us
    pallas_call x2, Pallas kernels, call(): pl.pallas_call(kernel, out_shape=outs, in_specs=[pl.BlockSpec(memory_spac...  27.3 us
    unnamed x80, local copies, waits for them, and re-layouts  16.2 us
    ppermute x11, starting transfers between devices, other(): return lax.ppermute(array, 'out', [(0, 1), (1, 0)])  13.4 us
    all_gather x3, waiting for transfers between devices, gather_units(): return lax.all_gather(array, 'wt', axis=0, tiled=True)  11.2 us
  transfers between devices with their start and end apart: 43, of which 15 were waited for; matrix products, arithmetic and copies ran while one was open for 16% of the time, Pallas kernels for 19%

profile of v12, /device:TPU:0, one launch (start us, length us, event | category | flops | bytes accessed | tf_op | source)
XLA Modules:
  0.0 310.1 jit_solution(10778415055719986422)
XLA Ops:
  7.2 1.3 constant_dynamic-slice_fusion.2
  10.1 3.0 collective-permute-start.9
  13.1 11.9 %collective-permute-done.9 = bf16[256,1024]{1,0:T(8,128)(2,1)S(1)} collective-permute-done((bf16[256,1024]{1,0:T(8,128)(2,1)S(1)}, bf16[256,1024]{1,0:T(8,128)(2,1)S(1)}, u32[]{:S(2)}, u32[]{:S(2)}) %collective-permute-start.9) | collective-permute-done | bytes 524320 | tf_op jit(solution)/shard_map/ppermute | solution.py:140
  25.9 1.8 collective-permute-start.10
  27.8 1.5 collective-permute-start.1
  30.1 5.2 %collective-permute-done.10 = bf16[128,1024]{1,0:T(8,128)(2,1)S(1)} collective-permute-done((bf16[128,1024]{1,0:T(8,128)(2,1)S(1)}, bf16[128,1024]{1,0:T(8,128)(2,1)S(1)}, u32[]{:S(2)}, u32[]{:S(2)}) %collective-permute-start.10) | collective-permute-done | bytes 262176 | tf_op jit(solution)/shard_map/ppermute | solution.py:140
  35.3 1.7 collective-permute-start.19
  37.9 16.2 %collective-permute-done.1.refs_2_ = bf16[512,1024]{1,0:T(8,128)(2,1)S(1)} collective-permute-done((bf16[512,1024]{1,0:T(8,128)(2,1)}, bf16[512,1024]{1,0:T(8,128)(2,1)S(1)}, u32[]{:S(2)}, u32[]{:S(2)}) %collective-permute-start.1) | collective-permute-done | bytes 1048608 | tf_op jit(solution)/shard_map/ppermute | solution.py:137
  54.4 3.3 %collective-permute-done.refs_1_ = bf16[512,1024]{1,0:T(8,128)(2,1)S(1)} collective-permute-done((bf16[512,1024]{1,0:T(8,128)(2,1)}, bf16[512,1024]{1,0:T(8,128)(2,1)S(1)}, u32[]{:S(2)}, u32[]{:S(2)}) %collective-permute-start) | collective-permute-done | bytes 1048608 | tf_op jit(solution)/shard_map/ppermute | solution.py:140
  57.8 1.8 collective-permute-start.3
  59.5 17.0 %collective-permute-done.20.refs_2_ = bf16[512,1024]{1,0:T(8,128)(2,1)S(1)} collective-permute-done((bf16[512,1024]{1,0:T(8,128)(2,1)}, bf16[512,1024]{1,0:T(8,128)(2,1)S(1)}, u32[]{:S(2)}, u32[]{:S(2)}) %collective-permute-start.20) | collective-permute-done | bytes 1048608 | tf_op jit(solution)/shard_map/ppermute | solution.py:137
  76.9 3.4 %collective-permute-done.19.refs_1_ = bf16[512,1024]{1,0:T(8,128)(2,1)} collective-permute-done((bf16[512,1024]{1,0:T(8,128)(2,1)}, bf16[512,1024]{1,0:T(8,128)(2,1)}, u32[]{:S(2)}, u32[]{:S(2)}) %collective-permute-start.19) | collective-permute-done | bytes 1048608 | tf_op jit(solution)/shard_map/ppermute | solution.py:140
  81.4 10.0 %collective-permute-done.2.refs_3_ = bf16[256,1024]{1,0:T(8,128)(2,1)S(1)} collective-permute-done((bf16[256,1024]{1,0:T(8,128)(2,1)S(1)}, bf16[256,1024]{1,0:T(8,128)(2,1)S(1)}, u32[]{:S(2)}, u32[]{:S(2)}) %collective-permute-start.2) | collective-permute-done | bytes 524320 | tf_op jit(solution)/shard_map/ppermute | solution.py:140
  91.4 1.7 collective-permute-start.22
  94.0 7.2 %collective-permute-done.21.refs_3_ = bf16[256,1024]{1,0:T(8,128)(2,1)} collective-permute-done((bf16[256,1024]{1,0:T(8,128)(2,1)S(1)}, bf16[256,1024]{1,0:T(8,128)(2,1)}, u32[]{:S(2)}, u32[]{:S(2)}) %collective-permute-start.21) | collective-permute-done | bytes 524320 | tf_op jit(solution)/shard_map/ppermute | solution.py:140
  107.0 1.2 copy-done.2
  108.3 1.2 copy-done.6
  113.7 16.2 %shard_map.92 = (bf16[2048,512]{1,0:T(8,128)(2,1)}, bf16[512,2048]{1,0:T(8,128)(2,1)}, bf16[2048,512]{1,0:T(8,128)(2,1)}, bf16[2048,512]{1,0:T(8,128)(2,1)}) custom-call(bf16[512,1024]{1,0:T(8,128)(2,1)} %bitcast.refs_0_, bf16[512,1024]{1,0:T(8,128)(2,1)S(1)} %collective-permute-done.refs_1_, bf16[512,1024]{1,0:T(8,128)(2,1)S(1)} %collective-permute-done.1.refs_2_, ...), custom_call_target="tpu_custom_call" | custom-call | flops 8589934592 | bytes 20971520 | tf_op jit(solution)/shard_map/pallas_call | solution.py:28
  129.9 11.1 %shard_map.97 = bf16[512,2048]{1,0:T(8,128)(2,1)} custom-call(bf16[512,1024]{1,0:T(8,128)(2,1)} %bitcast.6.refs_0_, bf16[512,1024]{1,0:T(8,128)(2,1)} %collective-permute-done.19.refs_1_, bf16[512,1024]{1,0:T(8,128)(2,1)S(1)} %collective-permute-done.20.refs_2_, bf16[256,1024]{1,0:T(8,128)(2,1)} %collective-permute-done.21.refs_3_, ...), custom_call_target="tpu_custom_call" | custom-call | flops 4294967296 | bytes 12582912 | tf_op jit(solution)/shard_map/pallas_call | solution.py:28
  141.2 11.2 %all-gather.8.cloned.1.call-done.refs_10_ = bf16[512,2048]{1,0:T(8,128)(2,1)} async-done(((bf16[128,2048]{1,0:T(8,128)(2,1)}), bf16[512,2048]{1,0:T(8,128)(2,1)}) %all-gather.8.cloned.1.call-update) | async-done | bytes 2097168 | tf_op jit(solution)/shard_map/all_gather | solution.py:196
  152.5 13.5 %shard_map.93 = (bf16[2048,1024]{1,0:T(8,128)(2,1)}, bf16[1024,2048]{1,0:T(8,128)(2,1)}) custom-call(bf16[512,1024]{1,0:T(8,128)(2,1)} %bitcast.6.refs_0_, bf16[512,1024]{1,0:T(8,128)(2,1)} %collective-permute-done.19.refs_1_, bf16[512,1024]{1,0:T(8,128)(2,1)S(1)} %collective-permute-done.20.refs_2_, bf16[256,1024]{1,0:T(8,128)(2,1)} %collective-permute-done.21.refs_3_, ...), custom_call_target="tpu_custom_call" | custom-call | flops 4294967296 | bytes 23068672 | tf_op jit(solution)/shard_map/pallas_call | solution.py:50
  166.1 9.2 %shard_map.95 = bf16[1024,1024]{1,0:T(8,128)(2,1)} custom-call(bf16[512,1024]{1,0:T(8,128)(2,1)} %bitcast.refs_0_, bf16[512,1024]{1,0:T(8,128)(2,1)S(1)} %collective-permute-done.refs_1_, bf16[512,1024]{1,0:T(8,128)(2,1)S(1)} %collective-permute-done.1.refs_2_, bf16[256,1024]{1,0:T(8,128)(2,1)S(1)} %copy-done.11, bf16[256,1024]{1,0:T(8,128)(2,1)S(1)} %copy-done.15, ...), custom_call_target="tpu_custom_call" | custom-call | flops 4294967296 | bytes 14680064 | tf_op jit(solution)/shard_map/pallas_call | solution.py:50
  175.4 2.2 convolution_convert_fusion.5
  177.8 3.6 %convolution_convert_fusion.2 = bf16[512,1024]{1,0:T(8,128)(2,1)} fusion(bf16[1024,1024]{1,0:T(8,128)(2,1)S(1)} %copy-done.28, bf16[2048,1024]{1,0:T(8,128)(2,1)} %get-tuple-element.16), kind=kOutput, calls=%fused_computation.10 | convolution fusion | flops 1074266112 | bytes 4194304 | tf_op jit(solution)/shard_map/dot_general | solution.py:16
  181.9 2.3 convolution_convert_fusion.1
  184.2 2.3 convolution_convert_fusion
  186.9 1.7 convolution_convert_fusion.6
  189.4 1.5 collective-permute-start.14
  191.0 1.4 collective-permute-start.17
  192.4 1.7 convolution_convert_fusion.4
  194.1 2.6 fusion.6
  196.8 6.6 %collective-permute-done.14.refs_11_ = bf16[256,1024]{1,0:T(8,128)(2,1)S(1)} collective-permute-done((bf16[256,1024]{1,0:T(8,128)(2,1)S(1)}, bf16[256,1024]{1,0:T(8,128)(2,1)S(1)}, u32[]{:S(2)}, u32[]{:S(2)}) %collective-permute-start.14) | collective-permute-done | bytes 524320 | tf_op jit(solution)/shard_map/ppermute | solution.py:140
  204.6 9.4 %shard_map.94 = bf16[1024,1024]{1,0:T(8,128)(2,1)} custom-call(bf16[512,1024]{1,0:T(8,128)(2,1)} %bitcast.refs_0_, bf16[512,1024]{1,0:T(8,128)(2,1)S(1)} %collective-permute-done.refs_1_, bf16[512,1024]{1,0:T(8,128)(2,1)S(1)} %collective-permute-done.1.refs_2_, bf16[256,1024]{1,0:T(8,128)(2,1)S(1)} %copy-done.12, bf16[256,1024]{1,0:T(8,128)(2,1)S(1)} %copy-done.16, ...), custom_call_target="tpu_custom_call" | custom-call | flops 4294967296 | bytes 14680064 | tf_op jit(solution)/shard_map/pallas_call | solution.py:50
  214.0 1.6 copy-done.29
  215.6 3.6 %convolution_convert_fusion.3 = bf16[512,1024]{1,0:T(8,128)(2,1)} fusion(bf16[1024,1024]{1,0:T(8,128)(2,1)S(1)} %copy-done.29, bf16[2048,1024]{1,0:T(8,128)(2,1)} %get-tuple-element.16), kind=kOutput, calls=%fused_computation.11 | convolution fusion | flops 1074266112 | bytes 4194304 | tf_op jit(solution)/shard_map/dot_general | solution.py:16
  220.8 2.8 add_convert_fusion.2
  223.7 1.7 collective-permute-start.33
  225.3 3.0 add_convert_fusion.6
  228.7 3.2 %add_convert_fusion.5 = bf16[512,1024]{1,0:T(8,128)(2,1)} fusion(bf16[512,1024]{1,0:T(8,128)(2,1)} %collective-permute-done.16, bf16[256,1024]{1,0:T(8,128)(2,1)S(1)} %collective-permute-done.17.refs_12_, bf16[512,2048]{1,0:T(8,128)(2,1)S(1)} %copy-done.32, bf16[2048,512]{1,0:T(8,128)(2,1)S(1)} %copy-done.36), kind=kOutput, calls=%fused_computation.5 | convolution fusion | flops 539492352 | bytes 4194304 | tf_op jit(solution)/shard_map/dot_general | solution.py:16
  232.9 3.8 %add_convert_fusion.3 = bf16[512,1024]{1,0:T(8,128)(2,1)} fusion(bf16[512,1024]{1,0:T(8,128)(2,1)} %collective-permute-done.29, bf16[1024,1024]{1,0:T(8,128)(2,1)S(1)} %copy-done.30, bf16[2048,1024]{1,0:T(8,128)(2,1)} %get-tuple-element.16), kind=kOutput, calls=%fused_computation.3 | convolution fusion | flops 1075314688 | bytes 5242880 | tf_op jit(solution)/shard_map/dot_general | solution.py:16
  236.7 13.0 %collective-permute-done.33 = bf16[512,1024]{1,0:T(8,128)(2,1)S(1)} collective-permute-done((bf16[512,1024]{1,0:T(8,128)(2,1)S(1)}, bf16[512,1024]{1,0:T(8,128)(2,1)S(1)}, u32[]{:S(2)}, u32[]{:S(2)}) %collective-permute-start.33) | collective-permute-done | bytes 1048608 | tf_op jit(solution)/shard_map/ppermute | solution.py:137
  249.7 1.6 collective-permute-start.30
  251.3 1.8 add_convert_fusion.1
  254.2 18.1 %collective-permute-done.15 = bf16[512,1024]{1,0:T(8,128)(2,1)} collective-permute-done((bf16[512,1024]{1,0:T(8,128)(2,1)}, bf16[512,1024]{1,0:T(8,128)(2,1)}, u32[]{:S(2)}, u32[]{:S(2)}) %collective-permute-start.15) | collective-permute-done | bytes 1048608 | tf_op jit(solution)/shard_map/ppermute | solution.py:137
  272.3 3.9 %add_convert_fusion.4 = bf16[512,1024]{1,0:T(8,128)(2,1)} fusion(bf16[512,1024]{1,0:T(8,128)(2,1)S(1)} %collective-permute-done.18, bf16[512,1024]{1,0:T(8,128)(2,1)} %collective-permute-done.15, bf16[512,1024]{1,0:T(8,128)(2,1)} %collective-permute-done.11, bf16[512,2048]{1,0:T(8,128)(2,1)} %all-gather.8.cloned.1.call-done.refs_10_, ...), kind=kOutput, calls=%fused_computation.4 | convolution fusion | flops 540540928 | bytes 5767168 | tf_op jit(solution)/shard_map/dot_general | solution.py:16
  279.3 14.9 %collective-permute-done.30 = bf16[512,1024]{1,0:T(8,128)(2,1)} collective-permute-done((bf16[512,1024]{1,0:T(8,128)(2,1)}, bf16[512,1024]{1,0:T(8,128)(2,1)}, u32[]{:S(2)}, u32[]{:S(2)}) %collective-permute-start.30) | collective-permute-done | bytes 1048608 | tf_op jit(solution)/shard_map/ppermute | solution.py:137
  294.3 5.2 %add_convert_fusion = bf16[512,1024]{1,0:T(8,128)(2,1)} fusion(bf16[512,1024]{1,0:T(8,128)(2,1)} %collective-permute-done.34, bf16[512,1024]{1,0:T(8,128)(2,1)} %collective-permute-done.30, bf16[512,1024]{1,0:T(8,128)(2,1)} %collective-permute-done.28, bf16[1024,1024]{1,0:T(8,128)(2,1)} %all-gather.4.cloned.1.call-done.refs_10_, ...), kind=kOutput, calls=%fused_computation | convolution fusion | flops 1077411840 | bytes 7340032 | tf_op jit(solution)/shard_map/dot_general | solution.py:16
  301.6 1.6 shard_map.96
  (160 shorter events, 29.8 us)
Async XLA Ops:
  7.2 99.9 %all-gather.4.cloned.1.call-start = ((), (), s32[]{:S(2)}) async-start(), calls=%async_computation.3 | async-start | bytes 2621440 | tf_op jit(solution)/shard_map/all_gather | solution.py:196
  8.8 17.1 %copy-start.26 = (bf16[256,1024]{1,0:T(8,128)(2,1)S(1)}, bf16[256,1024]{1,0:T(8,128)(2,1)}, u32[]{:S(2)}) copy-start(bf16[256,1024]{1,0:T(8,128)(2,1)} %param.8) | copy-start | bytes 1572868
  9.7 97.4 %all-gather.6.cloned.1.call-start = ((), (), s32[]{:S(2)}) async-start(), calls=%async_computation.4 | async-start | bytes 2621440 | tf_op jit(solution)/shard_map/all_gather | solution.py:196
  10.1 15.0 %collective-permute-start.9 = (bf16[256,1024]{1,0:T(8,128)(2,1)S(1)}, bf16[256,1024]{1,0:T(8,128)(2,1)S(1)}, u32[]{:S(2)}, u32[]{:S(2)}) collective-permute-start(bf16[256,1024]{1,0:T(8,128)(2,1)S(1)} %pad_maximum_fusion.1), channel_id=1, source_target_pairs={{0,1},{1,0},{2,3},{3,2},{4,5},{5,4},{6,7},{7,6},{8,9},{9,8},{10,11... | collective-permute-start | bytes 1572872 | tf_op jit(solution)/shard_map/ppermute | solution.py:140
  25.8 126.6 %all-gather.8.cloned.1.call-start = ((), (), s32[]{:S(2)}) async-start(), calls=%async_computation.5 | async-start | bytes 2621440 | tf_op jit(solution)/shard_map/all_gather | solution.py:196
  25.9 9.3 %collective-permute-start.10 = (bf16[128,1024]{1,0:T(8,128)(2,1)S(1)}, bf16[128,1024]{1,0:T(8,128)(2,1)S(1)}, u32[]{:S(2)}, u32[]{:S(2)}) collective-permute-start(bf16[128,1024]{1,0:T(8,128)(2,1)S(1)} %get-tuple-element.30), channel_id=1, source_target_pairs={{0,1},{1,0},{2,3},{3,2},{4,5},{5,4},{6,7},{7,6},{8,9},{9,8},{10,11... | collective-permute-start | bytes 786440 | tf_op jit(solution)/shard_map/ppermute | solution.py:140
  27.8 26.3 %collective-permute-start.1 = (bf16[512,1024]{1,0:T(8,128)(2,1)}, bf16[512,1024]{1,0:T(8,128)(2,1)S(1)}, u32[]{:S(2)}, u32[]{:S(2)}) collective-permute-start(bf16[512,1024]{1,0:T(8,128)(2,1)} %bitcast.refs_0_), channel_id=1, source_target_pairs={{0,16},{8,24},{16,0},{24,8},{1,17},{9,25},{17,1},{25,9},{2,18},{10... | collective-permute-start | bytes 3145736 | tf_op jit(solution)/shard_map/ppermute | solution.py:137
  29.2 28.5 %collective-permute-start = (bf16[512,1024]{1,0:T(8,128)(2,1)}, bf16[512,1024]{1,0:T(8,128)(2,1)S(1)}, u32[]{:S(2)}, u32[]{:S(2)}) collective-permute-start(bf16[512,1024]{1,0:T(8,128)(2,1)} %bitcast.refs_0_), channel_id=1, source_target_pairs={{0,1},{1,0},{2,3},{3,2},{4,5},{5,4},{6,7},{7,6},{8,9},{9,8},{10,11... | collective-permute-start | bytes 3145736 | tf_op jit(solution)/shard_map/ppermute | solution.py:140
  29.8 46.8 %collective-permute-start.20 = (bf16[512,1024]{1,0:T(8,128)(2,1)}, bf16[512,1024]{1,0:T(8,128)(2,1)S(1)}, u32[]{:S(2)}, u32[]{:S(2)}) collective-permute-start(bf16[512,1024]{1,0:T(8,128)(2,1)} %bitcast.6.refs_0_), channel_id=1, source_target_pairs={{0,16},{8,24},{16,0},{24,8},{1,17},{9,25},{17,1},{25,9},{2,18},{10... | collective-permute-start | bytes 3145736 | tf_op jit(solution)/shard_map/ppermute | solution.py:137
  30.1 46.9 %collective-permute-start.4 = (bf16[512,1024]{1,0:T(8,128)(2,1)}, bf16[512,1024]{1,0:T(8,128)(2,1)}, u32[]{:S(2)}, u32[]{:S(2)}) collective-permute-start(bf16[512,1024]{1,0:T(8,128)(2,1)} %bitcast.refs_0_), channel_id=1, source_target_pairs={{0,8},{8,0},{16,24},{24,16},{1,9},{9,1},{17,25},{25,17},{2,10},{10... | collective-permute-start | bytes 3145736 | tf_op jit(solution)/shard_map/ppermute | solution.py:134
  35.3 45.0 %collective-permute-start.19 = (bf16[512,1024]{1,0:T(8,128)(2,1)}, bf16[512,1024]{1,0:T(8,128)(2,1)}, u32[]{:S(2)}, u32[]{:S(2)}) collective-permute-start(bf16[512,1024]{1,0:T(8,128)(2,1)} %bitcast.6.refs_0_), channel_id=1, source_target_pairs={{0,1},{1,0},{2,3},{3,2},{4,5},{5,4},{6,7},{7,6},{8,9},{9,8},{10,11... | collective-permute-start | bytes 3145736 | tf_op jit(solution)/shard_map/ppermute | solution.py:140
  37.8 238.3 %reduce-scatter.8.cloned.1.call-start = ((), (), s32[]{:S(2)}) async-start(), calls=%async_computation.8 | async-start | bytes 2621440 | tf_op jit(solution)/shard_map/reduce_scatter | solution.py:199
  54.1 37.3 %collective-permute-start.2 = (bf16[256,1024]{1,0:T(8,128)(2,1)S(1)}, bf16[256,1024]{1,0:T(8,128)(2,1)S(1)}, u32[]{:S(2)}, u32[]{:S(2)}) collective-permute-start(bf16[256,1024]{1,0:T(8,128)(2,1)S(1)} %slice.86), channel_id=1, source_target_pairs={{0,1},{1,0},{2,3},{3,2},{4,5},{5,4},{6,7},{7,6},{8,9},{9,8},{10,11... | collective-permute-start | bytes 1572872 | tf_op jit(solution)/shard_map/ppermute | solution.py:140
  57.8 35.4 %collective-permute-start.3 = (bf16[256,1024]{1,0:T(8,128)(2,1)S(1)}, bf16[256,1024]{1,0:T(8,128)(2,1)S(1)}, u32[]{:S(2)}, u32[]{:S(2)}) collective-permute-start(bf16[256,1024]{1,0:T(8,128)(2,1)S(1)} %slice.87), channel_id=1, source_target_pairs={{0,16},{8,24},{16,0},{24,8},{1,17},{9,25},{17,1},{25,9},{2,18},{10... | collective-permute-start | bytes 1572872 | tf_op jit(solution)/shard_map/ppermute | solution.py:137
  76.6 24.6 %collective-permute-start.21 = (bf16[256,1024]{1,0:T(8,128)(2,1)S(1)}, bf16[256,1024]{1,0:T(8,128)(2,1)}, u32[]{:S(2)}, u32[]{:S(2)}) collective-permute-start(bf16[256,1024]{1,0:T(8,128)(2,1)S(1)} %slice.92), channel_id=1, source_target_pairs={{0,1},{1,0},{2,3},{3,2},{4,5},{5,4},{6,7},{7,6},{8,9},{9,8},{10,11... | collective-permute-start | bytes 1572872 | tf_op jit(solution)/shard_map/ppermute | solution.py:140
  76.9 27.6 %collective-permute-start.5 = (bf16[512,1024]{1,0:T(8,128)(2,1)S(1)}, bf16[512,1024]{1,0:T(8,128)(2,1)S(1)}, u32[]{:S(2)}, u32[]{:S(2)}) collective-permute-start(bf16[512,1024]{1,0:T(8,128)(2,1)S(1)} %collective-permute-done.refs_1_), channel_id=1, source_target_pairs={{0,8},{8,0},{16,24},{24,16},{1,9},{9,1},{17,25},{25,17},{2,10},{10... | collective-permute-start | bytes 3145736 | tf_op jit(solution)/shard_map/ppermute | solution.py:134
  80.3 25.6 %collective-permute-start.6 = (bf16[512,1024]{1,0:T(8,128)(2,1)S(1)}, bf16[512,1024]{1,0:T(8,128)(2,1)S(1)}, u32[]{:S(2)}, u32[]{:S(2)}) collective-permute-start(bf16[512,1024]{1,0:T(8,128)(2,1)S(1)} %collective-permute-done.1.refs_2_), channel_id=1, source_target_pairs={{0,8},{8,0},{16,24},{24,16},{1,9},{9,1},{17,25},{25,17},{2,10},{10... | collective-permute-start | bytes 3145736 | tf_op jit(solution)/shard_map/ppermute | solution.py:134
  91.4 10.9 %collective-permute-start.22 = (bf16[256,1024]{1,0:T(8,128)(2,1)S(1)}, bf16[256,1024]{1,0:T(8,128)(2,1)}, u32[]{:S(2)}, u32[]{:S(2)}) collective-permute-start(bf16[256,1024]{1,0:T(8,128)(2,1)S(1)} %slice.93), channel_id=1, source_target_pairs={{0,16},{8,24},{16,0},{24,8},{1,17},{9,25},{17,1},{25,9},{2,18},{10... | collective-permute-start | bytes 1572872 | tf_op jit(solution)/shard_map/ppermute | solution.py:137
  93.1 9.3 %collective-permute-start.7 = (bf16[256,1024]{1,0:T(8,128)(2,1)S(1)}, bf16[256,1024]{1,0:T(8,128)(2,1)S(1)}, u32[]{:S(2)}, u32[]{:S(2)}) collective-permute-start(bf16[256,1024]{1,0:T(8,128)(2,1)S(1)} %collective-permute-done.2.refs_3_), channel_id=1, source_target_pairs={{0,8},{8,0},{16,24},{24,16},{1,9},{9,1},{17,25},{25,17},{2,10},{10... | collective-permute-start | bytes 1572872 | tf_op jit(solution)/shard_map/ppermute | solution.py:134
  101.1 2.5 collective-permute-start.8
  102.3 27.5 %collective-permute-start.23 = (bf16[512,1024]{1,0:T(8,128)(2,1)}, bf16[512,1024]{1,0:T(8,128)(2,1)}, u32[]{:S(2)}, u32[]{:S(2)}) collective-permute-start(bf16[512,1024]{1,0:T(8,128)(2,1)} %bitcast.6.refs_0_), channel_id=1, source_target_pairs={{0,8},{8,0},{16,24},{24,16},{1,9},{9,1},{17,25},{25,17},{2,10},{10... | collective-permute-start | bytes 3145736 | tf_op jit(solution)/shard_map/ppermute | solution.py:134
  103.2 26.6 %collective-permute-start.24 = (bf16[512,1024]{1,0:T(8,128)(2,1)}, bf16[512,1024]{1,0:T(8,128)(2,1)}, u32[]{:S(2)}, u32[]{:S(2)}) collective-permute-start(bf16[512,1024]{1,0:T(8,128)(2,1)} %collective-permute-done.19.refs_1_), channel_id=1, source_target_pairs={{0,8},{8,0},{16,24},{24,16},{1,9},{9,1},{17,25},{25,17},{2,10},{10... | collective-permute-start | bytes 3145736 | tf_op jit(solution)/shard_map/ppermute | solution.py:134
  104.4 25.4 %collective-permute-start.25 = (bf16[512,1024]{1,0:T(8,128)(2,1)S(1)}, bf16[512,1024]{1,0:T(8,128)(2,1)}, u32[]{:S(2)}, u32[]{:S(2)}) collective-permute-start(bf16[512,1024]{1,0:T(8,128)(2,1)S(1)} %collective-permute-done.20.refs_2_), channel_id=1, source_target_pairs={{0,8},{8,0},{16,24},{24,16},{1,9},{9,1},{17,25},{25,17},{2,10},{10... | collective-permute-start | bytes 3145736 | tf_op jit(solution)/shard_map/ppermute | solution.py:134
  105.5 24.3 %collective-permute-start.26 = (bf16[256,1024]{1,0:T(8,128)(2,1)}, bf16[256,1024]{1,0:T(8,128)(2,1)}, u32[]{:S(2)}, u32[]{:S(2)}) collective-permute-start(bf16[256,1024]{1,0:T(8,128)(2,1)} %collective-permute-done.21.refs_3_), channel_id=1, source_target_pairs={{0,8},{8,0},{16,24},{24,16},{1,9},{9,1},{17,25},{25,17},{2,10},{10... | collective-permute-start | bytes 1572872 | tf_op jit(solution)/shard_map/ppermute | solution.py:134
  106.9 23.0 %collective-permute-start.27 = (bf16[256,1024]{1,0:T(8,128)(2,1)}, bf16[256,1024]{1,0:T(8,128)(2,1)}, u32[]{:S(2)}, u32[]{:S(2)}) collective-permute-start(bf16[256,1024]{1,0:T(8,128)(2,1)} %collective-permute-done.22.refs_4_), channel_id=1, source_target_pairs={{0,8},{8,0},{16,24},{24,16},{1,9},{9,1},{17,25},{25,17},{2,10},{10... | collective-permute-start | bytes 1572872 | tf_op jit(solution)/shard_map/ppermute | solution.py:134
  141.0 137.4 %reduce-scatter.6.cloned.1.call-start = ((), (), s32[]{:S(2)}) async-start(), calls=%async_computation.7 | async-start | bytes 2621440 | tf_op jit(solution)/shard_map/reduce_scatter | solution.py:199
  152.5 13.6 %copy-start.15 = (bf16[256,1024]{1,0:T(8,128)(2,1)S(1)}, bf16[256,1024]{1,0:T(8,128)(2,1)}, u32[]{:S(2)}) copy-start(bf16[256,1024]{1,0:T(8,128)(2,1)} %copy-done.13) | copy-start | bytes 1572868
  152.5 13.6 %copy-start.19 = (bf16[256,1024]{1,0:T(8,128)(2,1)S(1)}, bf16[256,1024]{1,0:T(8,128)(2,1)}, u32[]{:S(2)}) copy-start(bf16[256,1024]{1,0:T(8,128)(2,1)} %copy-done.17) | copy-start | bytes 1572868
  152.5 13.6 %copy-start.23 = (bf16[256,1024]{1,0:T(8,128)(2,1)S(1)}, bf16[256,1024]{1,0:T(8,128)(2,1)}, u32[]{:S(2)}) copy-start(bf16[256,1024]{1,0:T(8,128)(2,1)} %copy-done.21) | copy-start | bytes 1572868
  175.3 125.3 %reduce-scatter.4.cloned.1.call-start = ((), (), s32[]{:S(2)}) async-start(), calls=%async_computation.6 | async-start | bytes 2621440 | tf_op jit(solution)/shard_map/reduce_scatter | solution.py:199
  177.6 11.0 %collective-permute-start.13 = (bf16[512,1024]{1,0:T(8,128)(2,1)S(1)}, bf16[512,1024]{1,0:T(8,128)(2,1)S(1)}, u32[]{:S(2)}, u32[]{:S(2)}) collective-permute-start(bf16[512,1024]{1,0:T(8,128)(2,1)S(1)} %convolution_convert_fusion.5), channel_id=1, source_target_pairs={{0,8},{8,0},{16,24},{24,16},{1,9},{9,1},{17,25},{25,17},{2,10},{10... | collective-permute-start | bytes 3145736 | tf_op jit(solution)/shard_map/ppermute | solution.py:134
  181.4 50.5 %collective-permute-start.29 = (bf16[512,1024]{1,0:T(8,128)(2,1)}, bf16[512,1024]{1,0:T(8,128)(2,1)}, u32[]{:S(2)}, u32[]{:S(2)}) collective-permute-start(bf16[512,1024]{1,0:T(8,128)(2,1)} %convolution_convert_fusion.2), channel_id=1, source_target_pairs={{0,8},{8,0},{16,24},{24,16},{1,9},{9,1},{17,25},{25,17},{2,10},{10... | collective-permute-start | bytes 3145736 | tf_op jit(solution)/shard_map/ppermute | solution.py:134
  184.2 52.5 %collective-permute-start.31 = (bf16[512,1024]{1,0:T(8,128)(2,1)}, bf16[512,1024]{1,0:T(8,128)(2,1)}, u32[]{:S(2)}, u32[]{:S(2)}) collective-permute-start(bf16[512,1024]{1,0:T(8,128)(2,1)} %convolution_convert_fusion.1), channel_id=1, source_target_pairs={{0,8},{8,0},{16,24},{24,16},{1,9},{9,1},{17,25},{25,17},{2,10},{10... | collective-permute-start | bytes 3145736 | tf_op jit(solution)/shard_map/ppermute | solution.py:134
  186.5 33.5 %collective-permute-start.32 = (bf16[512,1024]{1,0:T(8,128)(2,1)}, bf16[512,1024]{1,0:T(8,128)(2,1)}, u32[]{:S(2)}, u32[]{:S(2)}) collective-permute-start(bf16[512,1024]{1,0:T(8,128)(2,1)} %convolution_convert_fusion), channel_id=1, source_target_pairs={{0,8},{8,0},{16,24},{24,16},{1,9},{9,1},{17,25},{25,17},{2,10},{10... | collective-permute-start | bytes 3145736 | tf_op jit(solution)/shard_map/ppermute | solution.py:134
  189.4 13.9 %collective-permute-start.14 = (bf16[256,1024]{1,0:T(8,128)(2,1)S(1)}, bf16[256,1024]{1,0:T(8,128)(2,1)S(1)}, u32[]{:S(2)}, u32[]{:S(2)}) collective-permute-start(bf16[256,1024]{1,0:T(8,128)(2,1)S(1)} %get-tuple-element.21), channel_id=1, source_target_pairs={{0,1},{1,0},{2,3},{3,2},{4,5},{5,4},{6,7},{7,6},{8,9},{9,8},{10,11... | collective-permute-start | bytes 1572872 | tf_op jit(solution)/shard_map/ppermute | solution.py:140
  191.0 13.6 %collective-permute-start.17 = (bf16[256,1024]{1,0:T(8,128)(2,1)S(1)}, bf16[256,1024]{1,0:T(8,128)(2,1)S(1)}, u32[]{:S(2)}, u32[]{:S(2)}) collective-permute-start(bf16[256,1024]{1,0:T(8,128)(2,1)S(1)} %get-tuple-element.22), channel_id=1, source_target_pairs={{0,16},{8,24},{16,0},{24,8},{1,17},{9,25},{17,1},{25,9},{2,18},{10... | collective-permute-start | bytes 1572872 | tf_op jit(solution)/shard_map/ppermute | solution.py:137
  203.4 20.3 %collective-permute-start.12 = (bf16[512,1024]{1,0:T(8,128)(2,1)}, bf16[512,1024]{1,0:T(8,128)(2,1)}, u32[]{:S(2)}, u32[]{:S(2)}) collective-permute-start(bf16[512,1024]{1,0:T(8,128)(2,1)} %convolution_convert_fusion.6), channel_id=1, source_target_pairs={{0,8},{8,0},{16,24},{24,16},{1,9},{9,1},{17,25},{25,17},{2,10},{10... | collective-permute-start | bytes 3145736 | tf_op jit(solution)/shard_map/ppermute | solution.py:134
  204.5 23.8 %collective-permute-start.16 = (bf16[512,1024]{1,0:T(8,128)(2,1)}, bf16[512,1024]{1,0:T(8,128)(2,1)}, u32[]{:S(2)}, u32[]{:S(2)}) collective-permute-start(bf16[512,1024]{1,0:T(8,128)(2,1)} %convolution_convert_fusion.4), channel_id=1, source_target_pairs={{0,8},{8,0},{16,24},{24,16},{1,9},{9,1},{17,25},{25,17},{2,10},{10... | collective-permute-start | bytes 3145736 | tf_op jit(solution)/shard_map/ppermute | solution.py:134
  219.9 33.2 %collective-permute-start.11 = (bf16[512,1024]{1,0:T(8,128)(2,1)S(1)}, bf16[512,1024]{1,0:T(8,128)(2,1)}, u32[]{:S(2)}, u32[]{:S(2)}) collective-permute-start(bf16[512,1024]{1,0:T(8,128)(2,1)S(1)} %convolution_convert_fusion.7), channel_id=1, source_target_pairs={{0,8},{8,0},{16,24},{24,16},{1,9},{9,1},{17,25},{25,17},{2,10},{10... | collective-permute-start | bytes 3145736 | tf_op jit(solution)/shard_map/ppermute | solution.py:134
  223.7 26.0 %collective-permute-start.33 = (bf16[512,1024]{1,0:T(8,128)(2,1)S(1)}, bf16[512,1024]{1,0:T(8,128)(2,1)S(1)}, u32[]{:S(2)}, u32[]{:S(2)}) collective-permute-start(bf16[512,1024]{1,0:T(8,128)(2,1)S(1)} %add_convert_fusion.2), channel_id=1, source_target_pairs={{0,16},{8,24},{16,0},{24,8},{1,17},{9,25},{17,1},{25,9},{2,18},{10... | collective-permute-start | bytes 3145736 | tf_op jit(solution)/shard_map/ppermute | solution.py:137
  228.3 43.9 %collective-permute-start.15 = (bf16[512,1024]{1,0:T(8,128)(2,1)}, bf16[512,1024]{1,0:T(8,128)(2,1)}, u32[]{:S(2)}, u32[]{:S(2)}) collective-permute-start(bf16[512,1024]{1,0:T(8,128)(2,1)} %add_convert_fusion.6), channel_id=1, source_target_pairs={{0,16},{8,24},{16,0},{24,8},{1,17},{9,25},{17,1},{25,9},{2,18},{10... | collective-permute-start | bytes 3145736 | tf_op jit(solution)/shard_map/ppermute | solution.py:137
  231.9 19.4 %copy-start.25 = (f32[512,1024]{1,0:T(8,128)S(1)}, f32[512,1024]{1,0:T(8,128)}, u32[]{:S(2)}) copy-start(f32[512,1024]{1,0:T(8,128)} %fusion.6) | copy-start | bytes 6291460
  231.9 40.4 %collective-permute-start.18 = (bf16[512,1024]{1,0:T(8,128)(2,1)}, bf16[512,1024]{1,0:T(8,128)(2,1)S(1)}, u32[]{:S(2)}, u32[]{:S(2)}) collective-permute-start(bf16[512,1024]{1,0:T(8,128)(2,1)} %add_convert_fusion.5), channel_id=1, source_target_pairs={{0,1},{1,0},{2,3},{3,2},{4,5},{5,4},{6,7},{7,6},{8,9},{9,8},{10,11... | collective-permute-start | bytes 3145736 | tf_op jit(solution)/shard_map/ppermute | solution.py:140
  236.7 42.6 %collective-permute-start.28 = (bf16[512,1024]{1,0:T(8,128)(2,1)}, bf16[512,1024]{1,0:T(8,128)(2,1)}, u32[]{:S(2)}, u32[]{:S(2)}) collective-permute-start(bf16[512,1024]{1,0:T(8,128)(2,1)} %convolution_convert_fusion.3), channel_id=1, source_target_pairs={{0,8},{8,0},{16,24},{24,16},{1,9},{9,1},{17,25},{25,17},{2,10},{10... | collective-permute-start | bytes 3145736 | tf_op jit(solution)/shard_map/ppermute | solution.py:134
  249.7 44.6 %collective-permute-start.30 = (bf16[512,1024]{1,0:T(8,128)(2,1)}, bf16[512,1024]{1,0:T(8,128)(2,1)}, u32[]{:S(2)}, u32[]{:S(2)}) collective-permute-start(bf16[512,1024]{1,0:T(8,128)(2,1)} %add_convert_fusion.3), channel_id=1, source_target_pairs={{0,16},{8,24},{16,0},{24,8},{1,17},{9,25},{17,1},{25,9},{2,18},{10... | collective-permute-start | bytes 3145736 | tf_op jit(solution)/shard_map/ppermute | solution.py:137
  253.1 41.1 %collective-permute-start.34 = (bf16[512,1024]{1,0:T(8,128)(2,1)S(1)}, bf16[512,1024]{1,0:T(8,128)(2,1)}, u32[]{:S(2)}, u32[]{:S(2)}) collective-permute-start(bf16[512,1024]{1,0:T(8,128)(2,1)S(1)} %add_convert_fusion.1), channel_id=1, source_target_pairs={{0,1},{1,0},{2,3},{3,2},{4,5},{5,4},{6,7},{7,6},{8,9},{9,8},{10,11... | collective-permute-start | bytes 3145736 | tf_op jit(solution)/shard_map/ppermute | solution.py:140
  277.3 22.2 %collective-permute-start.36 = (bf16[128,1024]{1,0:T(8,128)(2,1)S(1)}, bf16[128,1024]{1,0:T(8,128)(2,1)S(1)}, u32[]{:S(2)}, u32[]{:S(2)}) collective-permute-start(bf16[128,1024]{1,0:T(8,128)(2,1)S(1)} %get-tuple-element.24), channel_id=1, source_target_pairs={{0,1},{1,0},{2,3},{3,2},{4,5},{5,4},{6,7},{7,6},{8,9},{9,8},{10,11... | collective-permute-start | bytes 786440 | tf_op jit(solution)/shard_map/ppermute | solution.py:140
  278.4 22.2 %collective-permute-start.35 = (bf16[256,1024]{1,0:T(8,128)(2,1)}, bf16[256,1024]{1,0:T(8,128)(2,1)S(1)}, u32[]{:S(2)}, u32[]{:S(2)}) collective-permute-start(bf16[256,1024]{1,0:T(8,128)(2,1)} %reduce-scatter.6.cloned.1.call-done), channel_id=1, source_target_pairs={{0,1},{1,0},{2,3},{3,2},{4,5},{5,4},{6,7},{7,6},{8,9},{9,8},{10,11... | collective-permute-start | bytes 1572872 | tf_op jit(solution)/shard_map/ppermute | solution.py:140
  (33 other events, 148.3 us)
Sparse Core Ops, SparseCore 0:
  10.1 48.6 all-gather.3
  61.0 44.6 all-gather.5
  107.8 44.6 all-gather.7
  154.6 42.5 reduce-scatter.7
  199.5 43.1 reduce-scatter.5
  244.8 43.1 reduce-scatter.3

commit v13 on v10

--- a/solution.py
+++ b/solution.py
@@ -146,7 +146,7 @@
             blocks += [((base + 2, 0), (base + 3, 0)), ((base + 2, step), (base + 4, 0))]
         return Rows(pieces, blocks, step)
 
-    def scatter(self, product, rows, cols, split):
+    def scatter(self, product, rows, cols, over_y):
         half, quarter = rows // 2, rows // 4
         far = {}
         for chip in (1, 0):
@@ -160,12 +160,9 @@
                 sums[chip, other] = product(at, other) + far[chip, other].astype(F32)
         batch = quarter // 2
         corner = sums[1, 1].astype(BF16)
-        if split:
-            from_other = self.other(corner[:batch]).astype(F32)
-            from_chip = self.chip(corner[batch:]).astype(F32)
-            zeros = jnp.zeros_like(from_other)
-            to_chip = sums[1, 0] + jnp.concatenate([from_other, zeros])
-            to_other = sums[0, 1] + jnp.concatenate([zeros, from_chip])
+        if over_y:
+            to_chip = sums[1, 0] + self.other(corner).astype(F32)
+            to_other = sums[0, 1]
         else:
             to_chip = sums[1, 0]
             to_other = sums[0, 1] + self.chip(corner).astype(F32)

time: 310 us -> 308 us (level)
    ppermute x11, waiting for transfers between devices: 48.8 us -> 68.8 us  [other(): return lax.ppermute(array, 'out', [(0, 1), (1, 0)])]
    ppermute x8 -> x7, waiting for transfers between devices: 78.7 us -> 61.8 us  [chip(): return lax.ppermute(array, 'inp', [(at, at ^ 2) for at in range(4)])]
    ppermute x8 -> x7, starting transfers between devices: 10.5 us -> 9.47 us  [chip(): return lax.ppermute(array, 'inp', [(at, at ^ 2) for at in range(4)])]
    unnamed x78 -> x80, local copies, waits for them, and re-layouts: 17.8 us -> 16.8 us
  transfers between devices with their start and end apart: 43 -> 42, of which waited for: 14 -> 16; matrix products, arithmetic and copies ran while one was open for 15% -> 15% of each run, Pallas kernels for 19% -> 19%
where the time goes in v13:
time: 308 us; the launch traced here: 307 us
  waiting for transfers between devices  142 us (46%)
  Pallas kernels  60.7 us (20%)
  matrix products  40.1 us (13%)
  starting transfers between devices  26.1 us (8%)
  local copies, waits for them, and re-layouts  19.3 us (6%)
  between operations  14.5 us (5%)
  other arithmetic  4.47 us (1%)
    ppermute x11, waiting for transfers between devices, other(): return lax.ppermute(array, 'out', [(0, 1), (1, 0)])  68.8 us
    ppermute x7, waiting for transfers between devices, chip(): return lax.ppermute(array, 'inp', [(at, at ^ 2) for at in range(4)])  61.8 us
    pallas_call x5, Pallas kernels, call(): pl.pallas_call(kernel, out_shape=outs, in_specs=[pl.BlockSpec(memory_spac...  59.1 us
    dot_general x16, matrix products, matmul(): lax.dot_general(a, b, ((contract[:1], contract[1:]), ((), ())), preferred...  40.1 us
    unnamed x80, local copies, waits for them, and re-layouts  16.8 us
    ppermute x11, starting transfers between devices, other(): return lax.ppermute(array, 'out', [(0, 1), (1, 0)])  13.6 us
    all_gather x3, waiting for transfers between devices, gather_units(): return lax.all_gather(array, 'wt', axis=0, tiled=True)  11.4 us
    ppermute x7, starting transfers between devices, chip(): return lax.ppermute(array, 'inp', [(at, at ^ 2) for at in range(4)])  9.47 us
  transfers between devices with their start and end apart: 42, of which 16 were waited for; matrix products, arithmetic and copies ran while one was open for 15% of the time, Pallas kernels for 19%

profile of v13, /device:TPU:0, one launch (start us, length us, event | category | flops | bytes accessed | tf_op | source)
XLA Modules:
  0.0 307.5 jit_solution(12012981225451978107)
XLA Ops:
  10.1 3.0 collective-permute-start.9
  13.1 11.9 %collective-permute-done.9 = bf16[256,1024]{1,0:T(8,128)(2,1)S(1)} collective-permute-done((bf16[256,1024]{1,0:T(8,128)(2,1)S(1)}, bf16[256,1024]{1,0:T(8,128)(2,1)S(1)}, u32[]{:S(2)}, u32[]{:S(2)}) %collective-permute-start.9) | collective-permute-done | bytes 524320 | tf_op jit(solution)/shard_map/ppermute | solution.py:121
  25.9 1.8 collective-permute-start.10
  27.8 1.5 collective-permute-start.1
  30.1 5.2 %collective-permute-done.10 = bf16[128,1024]{1,0:T(8,128)(2,1)S(1)} collective-permute-done((bf16[128,1024]{1,0:T(8,128)(2,1)S(1)}, bf16[128,1024]{1,0:T(8,128)(2,1)S(1)}, u32[]{:S(2)}, u32[]{:S(2)}) %collective-permute-start.10) | collective-permute-done | bytes 262176 | tf_op jit(solution)/shard_map/ppermute | solution.py:121
  35.3 1.7 collective-permute-start.18
  37.9 16.2 %collective-permute-done.1.refs_2_ = bf16[512,1024]{1,0:T(8,128)(2,1)S(1)} collective-permute-done((bf16[512,1024]{1,0:T(8,128)(2,1)}, bf16[512,1024]{1,0:T(8,128)(2,1)S(1)}, u32[]{:S(2)}, u32[]{:S(2)}) %collective-permute-start.1) | collective-permute-done | bytes 1048608 | tf_op jit(solution)/shard_map/ppermute | solution.py:118
  54.5 3.3 %collective-permute-done.refs_1_ = bf16[512,1024]{1,0:T(8,128)(2,1)S(1)} collective-permute-done((bf16[512,1024]{1,0:T(8,128)(2,1)}, bf16[512,1024]{1,0:T(8,128)(2,1)S(1)}, u32[]{:S(2)}, u32[]{:S(2)}) %collective-permute-start) | collective-permute-done | bytes 1048608 | tf_op jit(solution)/shard_map/ppermute | solution.py:121
  57.8 1.8 collective-permute-start.3
  59.5 17.0 %collective-permute-done.19.refs_2_ = bf16[512,1024]{1,0:T(8,128)(2,1)S(1)} collective-permute-done((bf16[512,1024]{1,0:T(8,128)(2,1)}, bf16[512,1024]{1,0:T(8,128)(2,1)S(1)}, u32[]{:S(2)}, u32[]{:S(2)}) %collective-permute-start.19) | collective-permute-done | bytes 1048608 | tf_op jit(solution)/shard_map/ppermute | solution.py:118
  76.9 3.4 %collective-permute-done.18.refs_1_ = bf16[512,1024]{1,0:T(8,128)(2,1)} collective-permute-done((bf16[512,1024]{1,0:T(8,128)(2,1)}, bf16[512,1024]{1,0:T(8,128)(2,1)}, u32[]{:S(2)}, u32[]{:S(2)}) %collective-permute-start.18) | collective-permute-done | bytes 1048608 | tf_op jit(solution)/shard_map/ppermute | solution.py:121
  81.4 10.0 %collective-permute-done.2.refs_3_ = bf16[256,1024]{1,0:T(8,128)(2,1)S(1)} collective-permute-done((bf16[256,1024]{1,0:T(8,128)(2,1)S(1)}, bf16[256,1024]{1,0:T(8,128)(2,1)S(1)}, u32[]{:S(2)}, u32[]{:S(2)}) %collective-permute-start.2) | collective-permute-done | bytes 524320 | tf_op jit(solution)/shard_map/ppermute | solution.py:121
  91.4 1.7 collective-permute-start.21
  94.0 7.1 %collective-permute-done.20.refs_3_ = bf16[256,1024]{1,0:T(8,128)(2,1)} collective-permute-done((bf16[256,1024]{1,0:T(8,128)(2,1)S(1)}, bf16[256,1024]{1,0:T(8,128)(2,1)}, u32[]{:S(2)}, u32[]{:S(2)}) %collective-permute-start.20) | collective-permute-done | bytes 524320 | tf_op jit(solution)/shard_map/ppermute | solution.py:121
  113.7 16.1 %shard_map.92 = (bf16[2048,512]{1,0:T(8,128)(2,1)}, bf16[512,2048]{1,0:T(8,128)(2,1)}, bf16[2048,512]{1,0:T(8,128)(2,1)}, bf16[2048,512]{1,0:T(8,128)(2,1)}) custom-call(bf16[512,1024]{1,0:T(8,128)(2,1)} %bitcast.refs_0_, bf16[512,1024]{1,0:T(8,128)(2,1)S(1)} %collective-permute-done.refs_1_, bf16[512,1024]{1,0:T(8,128)(2,1)S(1)} %collective-permute-done.1.refs_2_, ...), custom_call_target="tpu_custom_call" | custom-call | flops 8589934592 | bytes 20971520 | tf_op jit(solution)/shard_map/pallas_call | solution.py:28
  129.8 11.0 %shard_map.97 = bf16[512,2048]{1,0:T(8,128)(2,1)} custom-call(bf16[512,1024]{1,0:T(8,128)(2,1)} %bitcast.6.refs_0_, bf16[512,1024]{1,0:T(8,128)(2,1)} %collective-permute-done.18.refs_1_, bf16[512,1024]{1,0:T(8,128)(2,1)S(1)} %collective-permute-done.19.refs_2_, bf16[256,1024]{1,0:T(8,128)(2,1)} %collective-permute-done.20.refs_3_, ...), custom_call_target="tpu_custom_call" | custom-call | flops 4294967296 | bytes 12582912 | tf_op jit(solution)/shard_map/pallas_call | solution.py:28
  141.1 11.4 %all-gather.8.cloned.1.call-done.refs_10_ = bf16[512,2048]{1,0:T(8,128)(2,1)} async-done(((bf16[128,2048]{1,0:T(8,128)(2,1)}), bf16[512,2048]{1,0:T(8,128)(2,1)}) %all-gather.8.cloned.1.call-update) | async-done | bytes 2097168 | tf_op jit(solution)/shard_map/all_gather | solution.py:174
  152.5 13.5 %shard_map.93 = (bf16[2048,1024]{1,0:T(8,128)(2,1)}, bf16[1024,2048]{1,0:T(8,128)(2,1)}) custom-call(bf16[512,1024]{1,0:T(8,128)(2,1)} %bitcast.6.refs_0_, bf16[512,1024]{1,0:T(8,128)(2,1)} %collective-permute-done.18.refs_1_, bf16[512,1024]{1,0:T(8,128)(2,1)S(1)} %collective-permute-done.19.refs_2_, bf16[256,1024]{1,0:T(8,128)(2,1)} %collective-permute-done.20.refs_3_, ...), custom_call_target="tpu_custom_call" | custom-call | flops 4294967296 | bytes 23068672 | tf_op jit(solution)/shard_map/pallas_call | solution.py:28
  166.0 9.2 %shard_map.95 = bf16[1024,1024]{1,0:T(8,128)(2,1)} custom-call(bf16[512,1024]{1,0:T(8,128)(2,1)} %bitcast.refs_0_, bf16[512,1024]{1,0:T(8,128)(2,1)S(1)} %collective-permute-done.refs_1_, bf16[512,1024]{1,0:T(8,128)(2,1)S(1)} %collective-permute-done.1.refs_2_, bf16[256,1024]{1,0:T(8,128)(2,1)S(1)} %copy-done.11, bf16[256,1024]{1,0:T(8,128)(2,1)S(1)} %copy-done.15, ...), custom_call_target="tpu_custom_call" | custom-call | flops 4294967296 | bytes 14680064 | tf_op jit(solution)/shard_map/pallas_call | solution.py:28
  175.3 4.3 %convolution_convert_fusion.2 = bf16[512,1024]{1,0:T(8,128)(2,1)} fusion(bf16[1024,1024]{1,0:T(8,128)(2,1)} %all-gather.4.cloned.1.call-done.refs_10_, bf16[2048,1024]{1,0:T(8,128)(2,1)} %get-tuple-element.16), kind=kOutput, calls=%fused_computation.10 | convolution fusion | flops 1074266112 | bytes 4194304 | tf_op jit(solution)/shard_map/dot_general | solution.py:16
  179.7 2.3 convolution_convert_fusion.1
  182.5 2.3 convolution_convert_fusion
  184.7 1.7 convolution_convert_fusion.5
  187.0 1.7 convolution_convert_fusion.6
  188.8 9.3 %shard_map.94 = bf16[1024,1024]{1,0:T(8,128)(2,1)} custom-call(bf16[512,1024]{1,0:T(8,128)(2,1)} %bitcast.refs_0_, bf16[512,1024]{1,0:T(8,128)(2,1)S(1)} %collective-permute-done.refs_1_, bf16[512,1024]{1,0:T(8,128)(2,1)S(1)} %collective-permute-done.1.refs_2_, bf16[256,1024]{1,0:T(8,128)(2,1)S(1)} %copy-done.12, bf16[256,1024]{1,0:T(8,128)(2,1)S(1)} %copy-done.16, ...), custom_call_target="tpu_custom_call" | custom-call | flops 4294967296 | bytes 14680064 | tf_op jit(solution)/shard_map/pallas_call | solution.py:28
  198.1 1.6 copy-done.32
  199.6 2.6 fusion.6
  202.3 2.6 add_convert_fusion.2
  205.0 1.5 collective-permute-start.32
  206.5 1.3 convolution_convert_fusion.3
  208.8 2.0 add_convert_fusion.7
  210.8 1.5 collective-permute-start.14
  212.3 3.5 %add_convert_fusion.3 = bf16[512,1024]{1,0:T(8,128)(2,1)} fusion(bf16[512,1024]{1,0:T(8,128)(2,1)} %collective-permute-done.28, bf16[1024,1024]{1,0:T(8,128)(2,1)S(1)} %copy-done.27, bf16[2048,1024]{1,0:T(8,128)(2,1)S(1)} %copy-done.37), kind=kOutput, calls=%fused_computation.3 | convolution fusion | flops 1075314688 | bytes 5242880 | tf_op jit(solution)/shard_map/dot_general | solution.py:16
  215.8 14.8 %collective-permute-done.32 = bf16[512,1024]{1,0:T(8,128)(2,1)S(1)} collective-permute-done((bf16[512,1024]{1,0:T(8,128)(2,1)S(1)}, bf16[512,1024]{1,0:T(8,128)(2,1)S(1)}, u32[]{:S(2)}, u32[]{:S(2)}) %collective-permute-start.32) | collective-permute-done | bytes 1048608 | tf_op jit(solution)/shard_map/ppermute | solution.py:118
  230.6 1.5 collective-permute-start.29
  232.7 1.5 collective-permute-start.33
  234.2 1.7 convolution_convert_fusion.7
  235.9 1.7 add_convert_fusion.5
  238.3 3.0 add_convert_fusion.6
  243.5 13.5 %collective-permute-done.29 = bf16[512,1024]{1,0:T(8,128)(2,1)} collective-permute-done((bf16[512,1024]{1,0:T(8,128)(2,1)}, bf16[512,1024]{1,0:T(8,128)(2,1)}, u32[]{:S(2)}, u32[]{:S(2)}) %collective-permute-start.29) | collective-permute-done | bytes 1048608 | tf_op jit(solution)/shard_map/ppermute | solution.py:118
  257.0 2.5 collective-permute-done.33
  259.5 4.6 %add_convert_fusion = bf16[512,1024]{1,0:T(8,128)(2,1)} fusion(bf16[512,1024]{1,0:T(8,128)(2,1)} %collective-permute-done.33, bf16[512,1024]{1,0:T(8,128)(2,1)} %collective-permute-done.29, bf16[512,1024]{1,0:T(8,128)(2,1)} %copy-done.33, bf16[1024,1024]{1,0:T(8,128)(2,1)S(1)} %copy-done.28, bf16[2048,1024]{1,0:T(8,128)(2,1)} %get-tuple-element.16), kind=kOutput, calls=%fused_computation | convolution fusion | flops 1077411840 | bytes 7340032 | tf_op jit(solution)/shard_map/dot_general | solution.py:16
  265.2 1.5 collective-permute-start.35
  267.3 14.7 %collective-permute-done.17 = bf16[512,1024]{1,0:T(8,128)(2,1)} collective-permute-done((bf16[512,1024]{1,0:T(8,128)(2,1)}, bf16[512,1024]{1,0:T(8,128)(2,1)}, u32[]{:S(2)}, u32[]{:S(2)}) %collective-permute-start.17) | collective-permute-done | bytes 1048608 | tf_op jit(solution)/shard_map/ppermute | solution.py:121
  281.9 4.2 %add_convert_fusion.4 = bf16[512,1024]{1,0:T(8,128)(2,1)} fusion(bf16[512,1024]{1,0:T(8,128)(2,1)} %collective-permute-done.17, bf16[512,1024]{1,0:T(8,128)(2,1)} %collective-permute-done.15, bf16[512,1024]{1,0:T(8,128)(2,1)} %collective-permute-done.11, bf16[512,2048]{1,0:T(8,128)(2,1)} %all-gather.8.cloned.1.call-done.refs_10_, ...), kind=kOutput, calls=%fused_computation.4 | convolution fusion | flops 540540928 | bytes 5767168 | tf_op jit(solution)/shard_map/dot_general | solution.py:16
  286.1 1.3 collective-permute-done.35
  288.6 9.4 %collective-permute-done.34.theirs_ref = bf16[256,1024]{1,0:T(8,128)(2,1)S(1)} collective-permute-done((bf16[256,1024]{1,0:T(8,128)(2,1)}, bf16[256,1024]{1,0:T(8,128)(2,1)S(1)}, u32[]{:S(2)}, u32[]{:S(2)}) %collective-permute-start.34) | collective-permute-done | bytes 524320 | tf_op jit(solution)/shard_map/ppermute | solution.py:121
  299.0 1.6 shard_map.96
  (157 shorter events, 30.5 us)
Async XLA Ops:
  7.2 99.9 %all-gather.4.cloned.1.call-start = ((), (), s32[]{:S(2)}) async-start(), calls=%async_computation.3 | async-start | bytes 2621440 | tf_op jit(solution)/shard_map/all_gather | solution.py:174
  8.8 17.1 %copy-start.25 = (bf16[256,1024]{1,0:T(8,128)(2,1)S(1)}, bf16[256,1024]{1,0:T(8,128)(2,1)}, u32[]{:S(2)}) copy-start(bf16[256,1024]{1,0:T(8,128)(2,1)} %param.8) | copy-start | bytes 1572868
  9.7 97.4 %all-gather.6.cloned.1.call-start = ((), (), s32[]{:S(2)}) async-start(), calls=%async_computation.4 | async-start | bytes 2621440 | tf_op jit(solution)/shard_map/all_gather | solution.py:174
  10.1 15.0 %collective-permute-start.9 = (bf16[256,1024]{1,0:T(8,128)(2,1)S(1)}, bf16[256,1024]{1,0:T(8,128)(2,1)S(1)}, u32[]{:S(2)}, u32[]{:S(2)}) collective-permute-start(bf16[256,1024]{1,0:T(8,128)(2,1)S(1)} %pad_maximum_fusion.1), channel_id=1, source_target_pairs={{0,1},{1,0},{2,3},{3,2},{4,5},{5,4},{6,7},{7,6},{8,9},{9,8},{10,11... | collective-permute-start | bytes 1572872 | tf_op jit(solution)/shard_map/ppermute | solution.py:121
  25.8 126.6 %all-gather.8.cloned.1.call-start = ((), (), s32[]{:S(2)}) async-start(), calls=%async_computation.5 | async-start | bytes 2621440 | tf_op jit(solution)/shard_map/all_gather | solution.py:174
  25.9 9.3 %collective-permute-start.10 = (bf16[128,1024]{1,0:T(8,128)(2,1)S(1)}, bf16[128,1024]{1,0:T(8,128)(2,1)S(1)}, u32[]{:S(2)}, u32[]{:S(2)}) collective-permute-start(bf16[128,1024]{1,0:T(8,128)(2,1)S(1)} %get-tuple-element.28), channel_id=1, source_target_pairs={{0,1},{1,0},{2,3},{3,2},{4,5},{5,4},{6,7},{7,6},{8,9},{9,8},{10,11... | collective-permute-start | bytes 786440 | tf_op jit(solution)/shard_map/ppermute | solution.py:121
  27.8 26.3 %collective-permute-start.1 = (bf16[512,1024]{1,0:T(8,128)(2,1)}, bf16[512,1024]{1,0:T(8,128)(2,1)S(1)}, u32[]{:S(2)}, u32[]{:S(2)}) collective-permute-start(bf16[512,1024]{1,0:T(8,128)(2,1)} %bitcast.refs_0_), channel_id=1, source_target_pairs={{0,16},{8,24},{16,0},{24,8},{1,17},{9,25},{17,1},{25,9},{2,18},{10... | collective-permute-start | bytes 3145736 | tf_op jit(solution)/shard_map/ppermute | solution.py:118
  29.2 28.5 %collective-permute-start = (bf16[512,1024]{1,0:T(8,128)(2,1)}, bf16[512,1024]{1,0:T(8,128)(2,1)S(1)}, u32[]{:S(2)}, u32[]{:S(2)}) collective-permute-start(bf16[512,1024]{1,0:T(8,128)(2,1)} %bitcast.refs_0_), channel_id=1, source_target_pairs={{0,1},{1,0},{2,3},{3,2},{4,5},{5,4},{6,7},{7,6},{8,9},{9,8},{10,11... | collective-permute-start | bytes 3145736 | tf_op jit(solution)/shard_map/ppermute | solution.py:121
  29.8 46.8 %collective-permute-start.19 = (bf16[512,1024]{1,0:T(8,128)(2,1)}, bf16[512,1024]{1,0:T(8,128)(2,1)S(1)}, u32[]{:S(2)}, u32[]{:S(2)}) collective-permute-start(bf16[512,1024]{1,0:T(8,128)(2,1)} %bitcast.6.refs_0_), channel_id=1, source_target_pairs={{0,16},{8,24},{16,0},{24,8},{1,17},{9,25},{17,1},{25,9},{2,18},{10... | collective-permute-start | bytes 3145736 | tf_op jit(solution)/shard_map/ppermute | solution.py:118
  30.1 46.9 %collective-permute-start.4 = (bf16[512,1024]{1,0:T(8,128)(2,1)}, bf16[512,1024]{1,0:T(8,128)(2,1)}, u32[]{:S(2)}, u32[]{:S(2)}) collective-permute-start(bf16[512,1024]{1,0:T(8,128)(2,1)} %bitcast.refs_0_), channel_id=1, source_target_pairs={{0,8},{8,0},{16,24},{24,16},{1,9},{9,1},{17,25},{25,17},{2,10},{10... | collective-permute-start | bytes 3145736 | tf_op jit(solution)/shard_map/ppermute | solution.py:115
  35.3 45.0 %collective-permute-start.18 = (bf16[512,1024]{1,0:T(8,128)(2,1)}, bf16[512,1024]{1,0:T(8,128)(2,1)}, u32[]{:S(2)}, u32[]{:S(2)}) collective-permute-start(bf16[512,1024]{1,0:T(8,128)(2,1)} %bitcast.6.refs_0_), channel_id=1, source_target_pairs={{0,1},{1,0},{2,3},{3,2},{4,5},{5,4},{6,7},{7,6},{8,9},{9,8},{10,11... | collective-permute-start | bytes 3145736 | tf_op jit(solution)/shard_map/ppermute | solution.py:121
  37.9 226.2 %reduce-scatter.8.cloned.1.call-start = ((), (), s32[]{:S(2)}) async-start(), calls=%async_computation.8 | async-start | bytes 2621440 | tf_op jit(solution)/shard_map/reduce_scatter | solution.py:177
  54.1 37.3 %collective-permute-start.2 = (bf16[256,1024]{1,0:T(8,128)(2,1)S(1)}, bf16[256,1024]{1,0:T(8,128)(2,1)S(1)}, u32[]{:S(2)}, u32[]{:S(2)}) collective-permute-start(bf16[256,1024]{1,0:T(8,128)(2,1)S(1)} %slice.78), channel_id=1, source_target_pairs={{0,1},{1,0},{2,3},{3,2},{4,5},{5,4},{6,7},{7,6},{8,9},{9,8},{10,11... | collective-permute-start | bytes 1572872 | tf_op jit(solution)/shard_map/ppermute | solution.py:121
  57.8 35.4 %collective-permute-start.3 = (bf16[256,1024]{1,0:T(8,128)(2,1)S(1)}, bf16[256,1024]{1,0:T(8,128)(2,1)S(1)}, u32[]{:S(2)}, u32[]{:S(2)}) collective-permute-start(bf16[256,1024]{1,0:T(8,128)(2,1)S(1)} %slice.79), channel_id=1, source_target_pairs={{0,16},{8,24},{16,0},{24,8},{1,17},{9,25},{17,1},{25,9},{2,18},{10... | collective-permute-start | bytes 1572872 | tf_op jit(solution)/shard_map/ppermute | solution.py:118
  76.6 24.6 %collective-permute-start.20 = (bf16[256,1024]{1,0:T(8,128)(2,1)S(1)}, bf16[256,1024]{1,0:T(8,128)(2,1)}, u32[]{:S(2)}, u32[]{:S(2)}) collective-permute-start(bf16[256,1024]{1,0:T(8,128)(2,1)S(1)} %slice.82), channel_id=1, source_target_pairs={{0,1},{1,0},{2,3},{3,2},{4,5},{5,4},{6,7},{7,6},{8,9},{9,8},{10,11... | collective-permute-start | bytes 1572872 | tf_op jit(solution)/shard_map/ppermute | solution.py:121
  76.9 27.6 %collective-permute-start.5 = (bf16[512,1024]{1,0:T(8,128)(2,1)S(1)}, bf16[512,1024]{1,0:T(8,128)(2,1)S(1)}, u32[]{:S(2)}, u32[]{:S(2)}) collective-permute-start(bf16[512,1024]{1,0:T(8,128)(2,1)S(1)} %collective-permute-done.refs_1_), channel_id=1, source_target_pairs={{0,8},{8,0},{16,24},{24,16},{1,9},{9,1},{17,25},{25,17},{2,10},{10... | collective-permute-start | bytes 3145736 | tf_op jit(solution)/shard_map/ppermute | solution.py:115
  80.3 25.6 %collective-permute-start.6 = (bf16[512,1024]{1,0:T(8,128)(2,1)S(1)}, bf16[512,1024]{1,0:T(8,128)(2,1)S(1)}, u32[]{:S(2)}, u32[]{:S(2)}) collective-permute-start(bf16[512,1024]{1,0:T(8,128)(2,1)S(1)} %collective-permute-done.1.refs_2_), channel_id=1, source_target_pairs={{0,8},{8,0},{16,24},{24,16},{1,9},{9,1},{17,25},{25,17},{2,10},{10... | collective-permute-start | bytes 3145736 | tf_op jit(solution)/shard_map/ppermute | solution.py:115
  91.4 10.9 %collective-permute-start.21 = (bf16[256,1024]{1,0:T(8,128)(2,1)S(1)}, bf16[256,1024]{1,0:T(8,128)(2,1)}, u32[]{:S(2)}, u32[]{:S(2)}) collective-permute-start(bf16[256,1024]{1,0:T(8,128)(2,1)S(1)} %slice.83), channel_id=1, source_target_pairs={{0,16},{8,24},{16,0},{24,8},{1,17},{9,25},{17,1},{25,9},{2,18},{10... | collective-permute-start | bytes 1572872 | tf_op jit(solution)/shard_map/ppermute | solution.py:118
  93.1 9.3 %collective-permute-start.7 = (bf16[256,1024]{1,0:T(8,128)(2,1)S(1)}, bf16[256,1024]{1,0:T(8,128)(2,1)S(1)}, u32[]{:S(2)}, u32[]{:S(2)}) collective-permute-start(bf16[256,1024]{1,0:T(8,128)(2,1)S(1)} %collective-permute-done.2.refs_3_), channel_id=1, source_target_pairs={{0,8},{8,0},{16,24},{24,16},{1,9},{9,1},{17,25},{25,17},{2,10},{10... | collective-permute-start | bytes 1572872 | tf_op jit(solution)/shard_map/ppermute | solution.py:115
  101.1 2.5 collective-permute-start.8
  102.3 27.5 %collective-permute-start.22 = (bf16[512,1024]{1,0:T(8,128)(2,1)}, bf16[512,1024]{1,0:T(8,128)(2,1)}, u32[]{:S(2)}, u32[]{:S(2)}) collective-permute-start(bf16[512,1024]{1,0:T(8,128)(2,1)} %bitcast.6.refs_0_), channel_id=1, source_target_pairs={{0,8},{8,0},{16,24},{24,16},{1,9},{9,1},{17,25},{25,17},{2,10},{10... | collective-permute-start | bytes 3145736 | tf_op jit(solution)/shard_map/ppermute | solution.py:115
  103.2 26.6 %collective-permute-start.23 = (bf16[512,1024]{1,0:T(8,128)(2,1)}, bf16[512,1024]{1,0:T(8,128)(2,1)}, u32[]{:S(2)}, u32[]{:S(2)}) collective-permute-start(bf16[512,1024]{1,0:T(8,128)(2,1)} %collective-permute-done.18.refs_1_), channel_id=1, source_target_pairs={{0,8},{8,0},{16,24},{24,16},{1,9},{9,1},{17,25},{25,17},{2,10},{10... | collective-permute-start | bytes 3145736 | tf_op jit(solution)/shard_map/ppermute | solution.py:115
  104.4 25.4 %collective-permute-start.24 = (bf16[512,1024]{1,0:T(8,128)(2,1)S(1)}, bf16[512,1024]{1,0:T(8,128)(2,1)}, u32[]{:S(2)}, u32[]{:S(2)}) collective-permute-start(bf16[512,1024]{1,0:T(8,128)(2,1)S(1)} %collective-permute-done.19.refs_2_), channel_id=1, source_target_pairs={{0,8},{8,0},{16,24},{24,16},{1,9},{9,1},{17,25},{25,17},{2,10},{10... | collective-permute-start | bytes 3145736 | tf_op jit(solution)/shard_map/ppermute | solution.py:115
  105.5 24.3 %collective-permute-start.25 = (bf16[256,1024]{1,0:T(8,128)(2,1)}, bf16[256,1024]{1,0:T(8,128)(2,1)}, u32[]{:S(2)}, u32[]{:S(2)}) collective-permute-start(bf16[256,1024]{1,0:T(8,128)(2,1)} %collective-permute-done.20.refs_3_), channel_id=1, source_target_pairs={{0,8},{8,0},{16,24},{24,16},{1,9},{9,1},{17,25},{25,17},{2,10},{10... | collective-permute-start | bytes 1572872 | tf_op jit(solution)/shard_map/ppermute | solution.py:115
  106.9 22.9 %collective-permute-start.26 = (bf16[256,1024]{1,0:T(8,128)(2,1)}, bf16[256,1024]{1,0:T(8,128)(2,1)}, u32[]{:S(2)}, u32[]{:S(2)}) collective-permute-start(bf16[256,1024]{1,0:T(8,128)(2,1)} %collective-permute-done.21.refs_4_), channel_id=1, source_target_pairs={{0,8},{8,0},{16,24},{24,16},{1,9},{9,1},{17,25},{25,17},{2,10},{10... | collective-permute-start | bytes 1572872 | tf_op jit(solution)/shard_map/ppermute | solution.py:115
  140.9 125.8 %reduce-scatter.6.cloned.1.call-start = ((), (), s32[]{:S(2)}) async-start(), calls=%async_computation.7 | async-start | bytes 2621440 | tf_op jit(solution)/shard_map/reduce_scatter | solution.py:177
  152.5 13.5 %copy-start.11 = (bf16[256,1024]{1,0:T(8,128)(2,1)S(1)}, bf16[256,1024]{1,0:T(8,128)(2,1)}, u32[]{:S(2)}) copy-start(bf16[256,1024]{1,0:T(8,128)(2,1)} %copy-done.9) | copy-start | bytes 1572868
  152.5 13.5 %copy-start.15 = (bf16[256,1024]{1,0:T(8,128)(2,1)S(1)}, bf16[256,1024]{1,0:T(8,128)(2,1)}, u32[]{:S(2)}) copy-start(bf16[256,1024]{1,0:T(8,128)(2,1)} %copy-done.13) | copy-start | bytes 1572868
  152.5 13.5 %copy-start.19 = (bf16[256,1024]{1,0:T(8,128)(2,1)S(1)}, bf16[256,1024]{1,0:T(8,128)(2,1)}, u32[]{:S(2)}) copy-start(bf16[256,1024]{1,0:T(8,128)(2,1)} %copy-done.17) | copy-start | bytes 1572868
  152.5 13.5 %copy-start.23 = (bf16[256,1024]{1,0:T(8,128)(2,1)S(1)}, bf16[256,1024]{1,0:T(8,128)(2,1)}, u32[]{:S(2)}) copy-start(bf16[256,1024]{1,0:T(8,128)(2,1)} %copy-done.21) | copy-start | bytes 1572868
  175.3 113.3 %reduce-scatter.4.cloned.1.call-start = ((), (), s32[]{:S(2)}) async-start(), calls=%async_computation.6 | async-start | bytes 2621440 | tf_op jit(solution)/shard_map/reduce_scatter | solution.py:177
  179.7 31.1 %collective-permute-start.28 = (bf16[512,1024]{1,0:T(8,128)(2,1)}, bf16[512,1024]{1,0:T(8,128)(2,1)}, u32[]{:S(2)}, u32[]{:S(2)}) collective-permute-start(bf16[512,1024]{1,0:T(8,128)(2,1)} %convolution_convert_fusion.2), channel_id=1, source_target_pairs={{0,8},{8,0},{16,24},{24,16},{1,9},{9,1},{17,25},{25,17},{2,10},{10... | collective-permute-start | bytes 3145736 | tf_op jit(solution)/shard_map/ppermute | solution.py:115
  182.0 33.9 %collective-permute-start.30 = (bf16[512,1024]{1,0:T(8,128)(2,1)}, bf16[512,1024]{1,0:T(8,128)(2,1)S(1)}, u32[]{:S(2)}, u32[]{:S(2)}) collective-permute-start(bf16[512,1024]{1,0:T(8,128)(2,1)} %convolution_convert_fusion.1), channel_id=1, source_target_pairs={{0,8},{8,0},{16,24},{24,16},{1,9},{9,1},{17,25},{25,17},{2,10},{10... | collective-permute-start | bytes 3145736 | tf_op jit(solution)/shard_map/ppermute | solution.py:115
  184.7 17.6 %collective-permute-start.31 = (bf16[512,1024]{1,0:T(8,128)(2,1)}, bf16[512,1024]{1,0:T(8,128)(2,1)}, u32[]{:S(2)}, u32[]{:S(2)}) collective-permute-start(bf16[512,1024]{1,0:T(8,128)(2,1)} %convolution_convert_fusion), channel_id=1, source_target_pairs={{0,8},{8,0},{16,24},{24,16},{1,9},{9,1},{17,25},{25,17},{2,10},{10... | collective-permute-start | bytes 3145736 | tf_op jit(solution)/shard_map/ppermute | solution.py:115
  186.5 22.1 %collective-permute-start.13 = (bf16[512,1024]{1,0:T(8,128)(2,1)}, bf16[512,1024]{1,0:T(8,128)(2,1)}, u32[]{:S(2)}, u32[]{:S(2)}) collective-permute-start(bf16[512,1024]{1,0:T(8,128)(2,1)} %convolution_convert_fusion.5), channel_id=1, source_target_pairs={{0,8},{8,0},{16,24},{24,16},{1,9},{9,1},{17,25},{25,17},{2,10},{10... | collective-permute-start | bytes 3145736 | tf_op jit(solution)/shard_map/ppermute | solution.py:115
  188.7 48.8 %collective-permute-start.12 = (bf16[512,1024]{1,0:T(8,128)(2,1)}, bf16[512,1024]{1,0:T(8,128)(2,1)}, u32[]{:S(2)}, u32[]{:S(2)}) collective-permute-start(bf16[512,1024]{1,0:T(8,128)(2,1)} %convolution_convert_fusion.6), channel_id=1, source_target_pairs={{0,8},{8,0},{16,24},{24,16},{1,9},{9,1},{17,25},{25,17},{2,10},{10... | collective-permute-start | bytes 3145736 | tf_op jit(solution)/shard_map/ppermute | solution.py:115
  205.0 25.7 %collective-permute-start.32 = (bf16[512,1024]{1,0:T(8,128)(2,1)S(1)}, bf16[512,1024]{1,0:T(8,128)(2,1)S(1)}, u32[]{:S(2)}, u32[]{:S(2)}) collective-permute-start(bf16[512,1024]{1,0:T(8,128)(2,1)S(1)} %add_convert_fusion.2), channel_id=1, source_target_pairs={{0,16},{8,24},{16,0},{24,8},{1,17},{9,25},{17,1},{25,9},{2,18},{10... | collective-permute-start | bytes 3145736 | tf_op jit(solution)/shard_map/ppermute | solution.py:118
  208.5 24.2 %collective-permute-start.16 = (bf16[512,1024]{1,0:T(8,128)(2,1)S(1)}, bf16[512,1024]{1,0:T(8,128)(2,1)S(1)}, u32[]{:S(2)}, u32[]{:S(2)}) collective-permute-start(bf16[512,1024]{1,0:T(8,128)(2,1)S(1)} %convolution_convert_fusion.4), channel_id=1, source_target_pairs={{0,8},{8,0},{16,24},{24,16},{1,9},{9,1},{17,25},{25,17},{2,10},{10... | collective-permute-start | bytes 3145736 | tf_op jit(solution)/shard_map/ppermute | solution.py:115
  210.8 26.8 %collective-permute-start.14 = (bf16[512,1024]{1,0:T(8,128)(2,1)S(1)}, bf16[512,1024]{1,0:T(8,128)(2,1)S(1)}, u32[]{:S(2)}, u32[]{:S(2)}) collective-permute-start(bf16[512,1024]{1,0:T(8,128)(2,1)S(1)} %add_convert_fusion.7), channel_id=1, source_target_pairs={{0,1},{1,0},{2,3},{3,2},{4,5},{5,4},{6,7},{7,6},{8,9},{9,8},{10,11... | collective-permute-start | bytes 3145736 | tf_op jit(solution)/shard_map/ppermute | solution.py:121
  215.8 25.5 %collective-permute-start.27 = (bf16[512,1024]{1,0:T(8,128)(2,1)S(1)}, bf16[512,1024]{1,0:T(8,128)(2,1)S(1)}, u32[]{:S(2)}, u32[]{:S(2)}) collective-permute-start(bf16[512,1024]{1,0:T(8,128)(2,1)S(1)} %convolution_convert_fusion.3), channel_id=1, source_target_pairs={{0,8},{8,0},{16,24},{24,16},{1,9},{9,1},{17,25},{25,17},{2,10},{10... | collective-permute-start | bytes 3145736 | tf_op jit(solution)/shard_map/ppermute | solution.py:115
  230.6 26.4 %collective-permute-start.29 = (bf16[512,1024]{1,0:T(8,128)(2,1)}, bf16[512,1024]{1,0:T(8,128)(2,1)}, u32[]{:S(2)}, u32[]{:S(2)}) collective-permute-start(bf16[512,1024]{1,0:T(8,128)(2,1)} %add_convert_fusion.3), channel_id=1, source_target_pairs={{0,16},{8,24},{16,0},{24,8},{1,17},{9,25},{17,1},{25,9},{2,18},{10... | collective-permute-start | bytes 3145736 | tf_op jit(solution)/shard_map/ppermute | solution.py:118
  232.7 26.8 %collective-permute-start.33 = (bf16[512,1024]{1,0:T(8,128)(2,1)S(1)}, bf16[512,1024]{1,0:T(8,128)(2,1)}, u32[]{:S(2)}, u32[]{:S(2)}) collective-permute-start(bf16[512,1024]{1,0:T(8,128)(2,1)S(1)} %add_convert_fusion.1), channel_id=1, source_target_pairs={{0,1},{1,0},{2,3},{3,2},{4,5},{5,4},{6,7},{7,6},{8,9},{9,8},{10,11... | collective-permute-start | bytes 3145736 | tf_op jit(solution)/shard_map/ppermute | solution.py:121
  237.6 21.9 %copy-start.28 = (bf16[1024,1024]{1,0:T(8,128)(2,1)S(1)}, bf16[1024,1024]{1,0:T(8,128)(2,1)}, u32[]{:S(2)}) copy-start(bf16[1024,1024]{1,0:T(8,128)(2,1)} %all-gather.4.cloned.1.call-done.refs_10_) | copy-start | bytes 6291460
  237.6 29.7 %collective-permute-start.11 = (bf16[512,1024]{1,0:T(8,128)(2,1)}, bf16[512,1024]{1,0:T(8,128)(2,1)}, u32[]{:S(2)}, u32[]{:S(2)}) collective-permute-start(bf16[512,1024]{1,0:T(8,128)(2,1)} %convolution_convert_fusion.7), channel_id=1, source_target_pairs={{0,8},{8,0},{16,24},{24,16},{1,9},{9,1},{17,25},{25,17},{2,10},{10... | collective-permute-start | bytes 3145736 | tf_op jit(solution)/shard_map/ppermute | solution.py:115
  237.6 44.3 %collective-permute-start.17 = (bf16[512,1024]{1,0:T(8,128)(2,1)}, bf16[512,1024]{1,0:T(8,128)(2,1)}, u32[]{:S(2)}, u32[]{:S(2)}) collective-permute-start(bf16[512,1024]{1,0:T(8,128)(2,1)} %add_convert_fusion.5), channel_id=1, source_target_pairs={{0,1},{1,0},{2,3},{3,2},{4,5},{5,4},{6,7},{7,6},{8,9},{9,8},{10,11... | collective-permute-start | bytes 3145736 | tf_op jit(solution)/shard_map/ppermute | solution.py:121
  242.3 39.6 %collective-permute-start.15 = (bf16[512,1024]{1,0:T(8,128)(2,1)}, bf16[512,1024]{1,0:T(8,128)(2,1)}, u32[]{:S(2)}, u32[]{:S(2)}) collective-permute-start(bf16[512,1024]{1,0:T(8,128)(2,1)} %add_convert_fusion.6), channel_id=1, source_target_pairs={{0,16},{8,24},{16,0},{24,8},{1,17},{9,25},{17,1},{25,9},{2,18},{10... | collective-permute-start | bytes 3145736 | tf_op jit(solution)/shard_map/ppermute | solution.py:118
  265.2 22.3 %collective-permute-start.35 = (bf16[128,1024]{1,0:T(8,128)(2,1)S(1)}, bf16[128,1024]{1,0:T(8,128)(2,1)S(1)}, u32[]{:S(2)}, u32[]{:S(2)}) collective-permute-start(bf16[128,1024]{1,0:T(8,128)(2,1)S(1)} %get-tuple-element.22), channel_id=1, source_target_pairs={{0,1},{1,0},{2,3},{3,2},{4,5},{5,4},{6,7},{7,6},{8,9},{9,8},{10,11... | collective-permute-start | bytes 786440 | tf_op jit(solution)/shard_map/ppermute | solution.py:121
  266.7 31.3 %collective-permute-start.34 = (bf16[256,1024]{1,0:T(8,128)(2,1)}, bf16[256,1024]{1,0:T(8,128)(2,1)S(1)}, u32[]{:S(2)}, u32[]{:S(2)}) collective-permute-start(bf16[256,1024]{1,0:T(8,128)(2,1)} %reduce-scatter.6.cloned.1.call-done), channel_id=1, source_target_pairs={{0,1},{1,0},{2,3},{3,2},{4,5},{5,4},{6,7},{7,6},{8,9},{9,8},{10,11... | collective-permute-start | bytes 1572872 | tf_op jit(solution)/shard_map/ppermute | solution.py:121
  (32 other events, 87.3 us)
Sparse Core Ops, SparseCore 0:
  10.1 48.6 all-gather.3
  61.0 44.6 all-gather.5
  107.8 44.6 all-gather.7
  154.6 42.5 reduce-scatter.7
  199.5 43.1 reduce-scatter.5
  244.8 43.1 reduce-scatter.3
